TPU v7x, 256 devices: a whole 4x4x8 slice. The times are simulated.
256 devices in a mesh: leaf: 64 (over z, x, core), chan: 4 (over y).
Axes of the slice: x: 4, y: 4, z: 8, core: 2. Of those that a mesh axis runs over, the one named last changes fastest.
Arguments:
- features: bfloat16 [192, 65536], P('chan', 'leaf'), may hold values from -6 to 6
- in_factor: bfloat16 [192, 48], P('chan'), may hold values from -0.4375 to 0.4375
- core: bfloat16 [27, 48, 48], P(None, 'chan'), may hold values from -0.15625 to 0.15625
- out_factor: bfloat16 [48, 192], P(None, 'chan'), may hold values from -0.875 to 0.875
- neighbours: int32 [27, 65536], P(None, 'leaf'), may hold values from -1 to 5119, as said below
- halo_blocks: int32 [64, 8, 8], P('leaf'), may hold values from -1 to 1023, as said below
- row_mask: int32 [65536], P('leaf'), may hold values 0 or 1
- cotangent: bfloat16 [192, 65536], P('chan', 'leaf'), may hold values from -6 to 6
Outputs:
- output: bfloat16 [192, 65536], P('chan', 'leaf')
- grad_features: bfloat16 [192, 65536], P('chan', 'leaf')
- grad_in: float32 [192, 48], P('chan')
- grad_core: float32 [27, 48, 48], P(None, 'chan')
- grad_out: float32 [48, 192], P(None, 'chan')
Inputs may be any that keep to these rules, and one draw needn't show every extreme that they name: Peer slot s of leaf device d stands for device p = d + s - 4 for s < 4 and p = d + s - 3 otherwise. If 0 <= p < 64, halo_blocks[d, s, :] are 8 consecutive blocks owned by p, ids p * 16 to p * 16 + 15; otherwise they are -1. `neighbours`: offset 13 is the octant itself (e equals its local row); -1 marks a missing neighbour; every other entry is a local row or a received slot as in the first step, whose peer slot stands for a device of the axis.
All inputs are finite; a program needn't handle non-finite values. No bound on the sum of `row_mask` on one device may be relied on, other than what follows from the above.
Results may differ from a plain program's by a relative error of at most 0.0057.
Values may be sent and summed in bfloat16 or wider, within the bound.
No kernel may reach another device: no remote copies, remote signals or barrier semaphores. Data moves between devices by JAX's collectives and lax.ppermute only.
A program may use at most 64 MiB of HBM per device.

v0:
```python
import jax
import jax.numpy as jnp
from jax import lax
from jax.sharding import PartitionSpec as P


def passed_along(block, axis, distance):
    devices = range(lax.axis_size(axis))
    route = [(i - distance, i) for i in devices if i - distance in devices]
    return lax.ppermute(block, axis, route)


def chan_round(total):
    result = lax.psum(total, "chan").astype(jnp.bfloat16)
    return result


def peer_steps(span_count, near_count):
    return [
        slot - span_count if slot < span_count else slot - span_count + 1
        for slot in range(near_count)
    ]


def body(features, in_factor, core, out_factor, neighbours, halo_blocks, row_mask, cotangent):
    row_count = features.shape[1]
    block_count = row_count // 64
    group_count = lax.axis_size("chan")
    leaf_index = lax.axis_index("leaf")
    group_index = lax.axis_index("chan")
    rank_width = in_factor.shape[1]
    slab_width = rank_width // group_count
    near_count = halo_blocks.shape[1]
    slot_count = halo_blocks.shape[2]
    offset_count = neighbours.shape[0]
    distances = peer_steps(near_count // 2, near_count)
    keep_rows = row_mask.astype(jnp.float32)[:, None]
    partial_reduced = lax.dot_general(
        features, in_factor, (((0,), (0,)), ((), ())), preferred_element_type=jnp.float32
    )
    sent_rows = chan_round(partial_reduced) * keep_rows.astype(jnp.bfloat16)
    core_used = lax.all_gather(core, "chan", axis=1, tiled=True)
    width = sent_rows.shape[1]
    block_rows = sent_rows.reshape(block_count, 64 * width)
    wanted_lists = []
    received = []
    for slot_index in range(near_count):
        distance = distances[slot_index]
        asked = passed_along(halo_blocks[0, slot_index], "leaf", distance)
        wanted = jnp.clip(asked - leaf_index * block_count, 0, block_count - 1)
        wanted_lists.append(wanted)
        outgoing = jnp.take(block_rows, wanted, axis=0)
        received.append(passed_along(outgoing, "leaf", -distance))
    incoming = jnp.concatenate(received, axis=0)
    table = jnp.concatenate([sent_rows, incoming.reshape(-1, width)], axis=0)
    present = neighbours >= 0
    safe_index = jnp.where(present, neighbours, 0)
    step_rows = min(2048, row_count)
    step_count = row_count // step_rows
    index_steps = jnp.transpose(safe_index.reshape(offset_count, step_count, step_rows), (1, 2, 0))
    present_steps = jnp.transpose(present.reshape(offset_count, step_count, step_rows), (1, 2, 0))
    core_flat = core_used.reshape(offset_count * width, rank_width)

    def collect(index_block, present_block):
        picked = jnp.take(table, index_block, axis=0)
        picked = jnp.where(present_block[:, :, None], picked, jnp.zeros((), jnp.bfloat16))
        return picked.reshape(step_rows, offset_count * width)

    def forward_step(pieces):
        return jnp.dot(collect(pieces[0], pieces[1]), core_flat, preferred_element_type=jnp.float32)

    mixed_steps = lax.map(forward_step, (index_steps, present_steps))
    mixed_sum = mixed_steps.reshape(row_count, rank_width)
    mixed = mixed_sum.astype(jnp.bfloat16)
    output = lax.dot_general(
        out_factor, mixed, (((0,), (1,)), ((), ())), preferred_element_type=jnp.float32
    ).astype(jnp.bfloat16)
    grad_mixed = chan_round(
        lax.dot_general(
            cotangent, out_factor, (((0,), (1,)), ((), ())), preferred_element_type=jnp.float32
        )
    )
    grad_right = lax.dot_general(
        mixed, cotangent, (((0,), (1,)), ((), ())), preferred_element_type=jnp.float32
    )
    grad_steps = grad_mixed.reshape(step_count, step_rows, rank_width)
    core_back = core_flat.T

    def backward_step(carry, pieces):
        grad_sum, grad_table = carry
        index_block, present_block, grad_block = pieces
        flat = collect(index_block, present_block)
        own_flat = lax.dynamic_slice_in_dim(
            flat.reshape(step_rows, offset_count, width), group_index * slab_width, slab_width, 2
        )
        own_flat = own_flat.reshape(step_rows, offset_count * slab_width)
        grad_sum = grad_sum + lax.dot_general(
            own_flat, grad_block, (((0,), (0,)), ((), ())), preferred_element_type=jnp.float32
        )
        back_terms = jnp.dot(grad_block, core_back, preferred_element_type=jnp.float32).reshape(
            step_rows * offset_count, width
        )
        back_terms = jnp.where(
            present_block.reshape(-1)[:, None], back_terms, jnp.zeros((), jnp.float32)
        )
        grad_table = grad_table.at[index_block.reshape(-1)].add(back_terms)
        return ((grad_sum, grad_table), None)

    init = (
        jnp.zeros((offset_count * slab_width, rank_width), jnp.float32),
        jnp.zeros((table.shape[0], width), jnp.float32),
    )
    (grad_sum, grad_table), unused = lax.scan(
        backward_step, init, (index_steps, present_steps, grad_steps)
    )
    remote_terms = grad_table[row_count:].reshape(near_count, slot_count, 64 * width)
    grad_blocks = grad_table[:row_count].reshape(block_count, 64 * width)
    for slot_index in range(near_count):
        returned = passed_along(remote_terms[slot_index], "leaf", distances[slot_index])
        grad_blocks = grad_blocks.at[wanted_lists[slot_index]].add(returned)
    grad_rows = (grad_blocks.reshape(row_count, width) * keep_rows).astype(jnp.bfloat16)
    grad_features = lax.dot_general(
        in_factor, grad_rows, (((1,), (1,)), ((), ())), preferred_element_type=jnp.float32
    ).astype(jnp.bfloat16)
    grad_left = jnp.dot(features, grad_rows, preferred_element_type=jnp.float32)
    grad_left, grad_sum, grad_right = lax.psum((grad_left, grad_sum, grad_right), "leaf")
    factor = float(row_count * lax.axis_size("leaf")) ** (-0.5)
    grad_core = grad_sum.reshape(offset_count, slab_width, rank_width) * factor
    return (output, grad_features, grad_left * factor, grad_core, grad_right * factor)


def solution(mesh):
    placed = (
        P("chan", "leaf"),
        P("chan", None),
        P(None, "chan", None),
        P(None, "chan"),
        P(None, "leaf"),
        P("leaf", None, None),
        P("leaf"),
        P("chan", "leaf"),
    )
    return jax.shard_map(
        body,
        mesh=mesh,
        in_specs=placed,
        out_specs=(
            P("chan", "leaf"),
            P("chan", "leaf"),
            P("chan", None),
            P(None, "chan", None),
            P(None, "chan"),
        ),
        check_vma=False,
    )
```

profile of v0, /device:TPU:1, one launch (start us, length us, event | category | flops | bytes accessed | tf_op | source)
XLA Modules:
  0.0 745.8 jit_solution(8978023612030671671)
XLA Ops:
  13.9 12.2 %all_gather.3 = bf16[27,48,48]{2,0,1:T(8,128)(2,1)S(1)} all-gather(bf16[27,12,48]{2,0,1:T(8,128)(2,1)} %param.14), channel_id=1, replica_groups=mesh['leaf'=64,'chan'=4] {'chan'}, dimensions={1}, use_global_device_ids=true | all-gather | bytes 155520 | tf_op jit(solution)/shard_map/all_gather | solution.py:42
  27.4 16.0 %all-reduce.6 = (bf16[1024,48]{0,1:T(8,128)(2,1)S(1)}, bf16[1024,48]{0,1:T(8,128)(2,1)S(1)}) all-reduce(f32[1024,48]{0,1:T(8,128)S(1)} %fusion.16, f32[1024,48]{0,1:T(8,128)S(1)} %fusion.18), channel_id=1, replica_groups=mesh['leaf'=64,'chan'=4] {'chan'}, use_global_device_ids=true, to_apply=%region_0.0 | all-reduce | flops 98304 | bytes 589824 | tf_op jit(solution)/shard_map/psum | solution.py:14
  43.4 3.4 fusion.20
  46.8 13.3 %reshape.126 = f32[27648,48]{1,0:T(8,128)} reshape(f32[1024,1296]{1,0:T(8,128)} %fusion.20) | data formatting | bytes 10616832 | tf_op jit(solution)/shard_map/while/body/eval_jaxpr/reshape | solution.py:100
  61.6 164.1 %scatter_custom_fusion = f32[5120,48]{1,0:T(8,128)S(1)} fusion(s32[27648]{0:T(1024)S(1)} %bitcast.65, f32[27648,48]{1,0:T(8,128)} %reshape.126, f32[]{:T(128)} %constant.51.clone.1, pred[27648]{0:T(1024)(128)(4,1)S(1)} %broadcast_in_dim.107), kind=kCustom, calls=%fused_computation.18 | custom fusion | flops 2654208 | bytes 15167488 | tf_op jit(solution)/shard_map/while/body/eval_jaxpr/scatter-add | solution.py:106
  237.9 1.8 squeeze.74
  252.7 9.0 %collective-permute-start.6 = (s32[8]{0:T(128)}, s32[8]{0:T(128)S(1)}, u32[]{:S(2)}, u32[]{:S(2)}) collective-permute-start(s32[8]{0:T(128)} %get-tuple-element.113), channel_id=1, source_target_pairs={{4,0},{8,4},{12,8},{16,12},{20,16},{24,20},{28,24},{32,28},{36,32}... | collective-permute-start | bytes 104 | tf_op jit(solution)/shard_map/ppermute | solution.py:10
  263.5 1.9 collective-permute-start.19
  266.0 4.8 collective-permute-start.8
  272.1 5.6 collective-permute-start.10
  278.5 7.0 collective-permute-start.12
  286.8 11.0 %collective-permute-start.14 = (s32[8]{0:T(128)}, s32[8]{0:T(128)S(1)}, u32[]{:S(2)}, u32[]{:S(2)}) collective-permute-start(s32[8]{0:T(128)} %get-tuple-element.110), channel_id=1, source_target_pairs={{0,16},{4,20},{8,24},{12,28},{16,32},{20,36},{24,40},{28,44},{32,4... | collective-permute-start | bytes 104 | tf_op jit(solution)/shard_map/ppermute | solution.py:10
  298.6 5.1 collective-permute-start.1
  305.5 8.5 %collective-permute-start.3 = (bf16[8,3072]{1,0:T(8,128)(2,1)S(1)}, bf16[8,3072]{1,0:T(8,128)(2,1)S(1)}, u32[]{:S(2)}, u32[]{:S(2)}) collective-permute-start(bf16[8,3072]{1,0:T(8,128)(2,1)S(1)} %broadcast_select_fusion.6), channel_id=1, source_target_pairs={{0,12},{4,16},{8,20},{12,24},{16,28},{20,32},{24,36},{28,40},{32,4... | collective-permute-start | bytes 147464 | tf_op jit(solution)/shard_map/ppermute | solution.py:10
  317.6 7.2 collective-permute-start.7
  326.0 1.9 collective-permute-start.9
  327.9 4.1 collective-permute-done.9
  333.3 4.3 collective-permute-done.11
  338.9 8.5 %collective-permute-done.13 = bf16[8,3072]{1,0:T(8,128)(2,1)S(1)} collective-permute-done((bf16[8,3072]{1,0:T(8,128)(2,1)S(1)}, bf16[8,3072]{1,0:T(8,128)(2,1)S(1)}, u32[]{:S(2)}, u32[]{:S(2)}) %collective-permute-start.13) | collective-permute-done | bytes 49184 | tf_op jit(solution)/shard_map/ppermute | solution.py:10
  348.7 11.2 %collective-permute-done.15 = bf16[8,3072]{1,0:T(8,128)(2,1)S(1)} collective-permute-done((bf16[8,3072]{1,0:T(8,128)(2,1)S(1)}, bf16[8,3072]{1,0:T(8,128)(2,1)S(1)}, u32[]{:S(2)}, u32[]{:S(2)}) %collective-permute-start.15) | collective-permute-done | bytes 49184 | tf_op jit(solution)/shard_map/ppermute | solution.py:10
  359.9 1.9 collective-permute-start.20
  364.2 97.1 %gather_fusion.8 = bf16[27648,48]{1,0:T(8,128)(2,1)} fusion(bf16[5120,48]{1,0:T(8,128)(2,1)S(1)} %pad_maximum_fusion, s32[27648]{0:T(1024)S(1)} %broadcast_clamp_fusion), kind=kCustom, calls=%fused_computation.1.clone | custom fusion | bytes 5419008 | tf_op jit(solution)/shard_map/while/body/eval_jaxpr/jit(_take)/gather | solution.py:65
  461.3 6.5 copy.77
  467.8 33.4 %reshape.311 = bf16[1024,27,48]{1,0,2:T(8,128)(2,1)} reshape(bf16[27648,48]{0,1:T(8,128)(2,1)S(1)} %copy.77) | data formatting | bytes 5308416 | tf_op jit(solution)/shard_map/while/body/eval_jaxpr/jit(_take)/gather | solution.py:65
  501.2 7.4 select_select_fusion
  508.6 3.8 fusion.5
  512.7 3.2 copy.83
  517.2 1.9 fusion.19
  519.8 5.7 collective-permute-start.21
  525.6 5.4 collective-permute-start.22
  530.9 5.0 collective-permute-start.23
  547.7 186.7 %all-reduce.5.cloned.1.call-done = (f32[48,48]{0,1:T(8,128)}, f32[324,48]{0,1:T(8,128)}, f32[48,48]{0,1:T(8,128)}) async-done(((f32[48,48]{0,1:T(8,128)}, f32[324,48]{0,1:T(8,128)}, f32[48,48]{0,1:T(8,128)}), (f32[48,48]{0,1:T(8,128)}, f32[324,48]{0,1:T(8,128)}, f32[48,48]{0,1:T(8,128)})) %all-reduce.5.cloned.1.call-update) | async-done | bytes 80656 | tf_op jit(solution)/shard_map/psum | solution.py:126
  (168 shorter events, 72.1 us)
Async XLA Ops:
  7.2 727.1 %all-reduce.5.cloned.1.call-start = ((), (), s32[]{:S(2)}) async-start(), calls=%async_computation | async-start | bytes 245760 | tf_op jit(solution)/shard_map/psum | solution.py:126
  8.8 241.9 %collective-permute-start = (s32[8]{0:T(128)}, s32[8]{0:T(128)}, u32[]{:S(2)}, u32[]{:S(2)}) collective-permute-start(s32[8]{0:T(128)} %get-tuple-element.116), channel_id=1, source_target_pairs={{16,0},{20,4},{24,8},{28,12},{32,16},{36,20},{40,24},{44,28},{48,3... | collective-permute-start | bytes 104 | tf_op jit(solution)/shard_map/ppermute | solution.py:10
  61.6 175.0 %copy-start.2 = (s32[27,1024]{1,0:T(8,128)S(1)}, s32[27,1024]{1,0:T(8,128)}, u32[]{:S(2)}) copy-start(s32[27,1024]{1,0:T(8,128)} %param.16) | copy-start | bytes 331780
  228.8 291.0 %collective-permute-start.16 = (f32[8,3072]{1,0:T(8,128)}, f32[8,3072]{1,0:T(8,128)}, u32[]{:S(2)}, u32[]{:S(2)}) collective-permute-start(f32[8,3072]{1,0:T(8,128)} %squeeze.72), channel_id=1, source_target_pairs={{16,0},{20,4},{24,8},{28,12},{32,16},{36,20},{40,24},{44,28},{48,3... | collective-permute-start | bytes 294920 | tf_op jit(solution)/shard_map/ppermute | solution.py:10
  230.1 22.6 %collective-permute-start.2 = (s32[8]{0:T(128)}, s32[8]{0:T(128)}, u32[]{:S(2)}, u32[]{:S(2)}) collective-permute-start(s32[8]{0:T(128)} %get-tuple-element.115), channel_id=1, source_target_pairs={{12,0},{16,4},{20,8},{24,12},{28,16},{32,20},{36,24},{40,28},{44,3... | collective-permute-start | bytes 104 | tf_op jit(solution)/shard_map/ppermute | solution.py:10
  233.1 292.4 %collective-permute-start.17 = (f32[8,3072]{1,0:T(8,128)}, f32[8,3072]{1,0:T(8,128)}, u32[]{:S(2)}, u32[]{:S(2)}) collective-permute-start(f32[8,3072]{1,0:T(8,128)} %squeeze.73), channel_id=1, source_target_pairs={{12,0},{16,4},{20,8},{24,12},{28,16},{32,20},{36,24},{40,28},{44,3... | collective-permute-start | bytes 294920 | tf_op jit(solution)/shard_map/ppermute | solution.py:10
  234.4 29.1 %collective-permute-start.4 = (s32[8]{0:T(128)}, s32[8]{0:T(128)}, u32[]{:S(2)}, u32[]{:S(2)}) collective-permute-start(s32[8]{0:T(128)} %get-tuple-element.114), channel_id=1, source_target_pairs={{8,0},{12,4},{16,8},{20,12},{24,16},{28,20},{32,24},{36,28},{40,32... | collective-permute-start | bytes 104 | tf_op jit(solution)/shard_map/ppermute | solution.py:10
  248.6 113.2 %copy-start.1 = (bf16[1024,48]{1,0:T(8,128)(2,1)}, bf16[1024,48]{1,0:T(8,128)(2,1)S(1)}, u32[]{:S(2)}) copy-start(bf16[1024,48]{1,0:T(8,128)(2,1)S(1)} %copy.75) | copy-start | bytes 294916
  250.7 280.2 %collective-permute-start.18 = (f32[8,3072]{1,0:T(8,128)}, f32[8,3072]{1,0:T(8,128)}, u32[]{:S(2)}, u32[]{:S(2)}) collective-permute-start(f32[8,3072]{1,0:T(8,128)} %squeeze.74), channel_id=1, source_target_pairs={{8,0},{12,4},{16,8},{20,12},{24,16},{28,20},{32,24},{36,28},{40,32... | collective-permute-start | bytes 294920 | tf_op jit(solution)/shard_map/ppermute | solution.py:10
  252.7 208.6 %copy-start.7 = (s32[8]{0:T(128)}, s32[8]{0:T(128)S(1)}, u32[]{:S(2)}) copy-start(s32[8]{0:T(128)S(1)} %get-tuple-element.97) | copy-start | bytes 100
  252.7 13.3 %collective-permute-start.6 = (s32[8]{0:T(128)}, s32[8]{0:T(128)S(1)}, u32[]{:S(2)}, u32[]{:S(2)}) collective-permute-start(s32[8]{0:T(128)} %get-tuple-element.113), channel_id=1, source_target_pairs={{4,0},{8,4},{12,8},{16,12},{20,16},{24,20},{28,24},{32,28},{36,32}... | collective-permute-start | bytes 104 | tf_op jit(solution)/shard_map/ppermute | solution.py:10
  262.3 199.0 %copy-start.8 = (s32[8]{0:T(128)}, s32[8]{0:T(128)S(1)}, u32[]{:S(2)}) copy-start(s32[8]{0:T(128)S(1)} %get-tuple-element.95) | copy-start | bytes 100
  263.5 276.9 %collective-permute-start.19 = (f32[8,3072]{1,0:T(8,128)}, f32[8,3072]{1,0:T(8,128)}, u32[]{:S(2)}, u32[]{:S(2)}) collective-permute-start(f32[8,3072]{1,0:T(8,128)} %squeeze.75), channel_id=1, source_target_pairs={{4,0},{8,4},{12,8},{16,12},{20,16},{24,20},{28,24},{32,28},{36,32}... | collective-permute-start | bytes 294920 | tf_op jit(solution)/shard_map/ppermute | solution.py:10
  266.0 195.3 %copy-start.9 = (s32[8]{0:T(128)}, s32[8]{0:T(128)S(1)}, u32[]{:S(2)}) copy-start(s32[8]{0:T(128)S(1)} %get-tuple-element.93) | copy-start | bytes 100
  266.0 6.0 collective-permute-start.8
  270.9 190.5 %copy-start.10 = (s32[8]{0:T(128)}, s32[8]{0:T(128)S(1)}, u32[]{:S(2)}) copy-start(s32[8]{0:T(128)S(1)} %get-tuple-element.91) | copy-start | bytes 100
  272.1 6.4 collective-permute-start.10
  277.7 86.4 %copy-start.12 = (s32[8]{0:T(128)}, s32[8]{0:T(128)S(1)}, u32[]{:S(2)}) copy-start(s32[8]{0:T(128)S(1)} %get-tuple-element.89) | copy-start | bytes 100
  278.5 8.3 %collective-permute-start.12 = (s32[8]{0:T(128)}, s32[8]{0:T(128)S(1)}, u32[]{:S(2)}, u32[]{:S(2)}) collective-permute-start(s32[8]{0:T(128)} %get-tuple-element.117), channel_id=1, source_target_pairs={{0,12},{4,16},{8,20},{12,24},{16,28},{20,32},{24,36},{28,40},{32,4... | collective-permute-start | bytes 104 | tf_op jit(solution)/shard_map/ppermute | solution.py:10
  286.8 11.8 %collective-permute-start.14 = (s32[8]{0:T(128)}, s32[8]{0:T(128)S(1)}, u32[]{:S(2)}, u32[]{:S(2)}) collective-permute-start(s32[8]{0:T(128)} %get-tuple-element.110), channel_id=1, source_target_pairs={{0,16},{4,20},{8,24},{12,28},{16,32},{20,36},{24,40},{28,44},{32,4... | collective-permute-start | bytes 104 | tf_op jit(solution)/shard_map/ppermute | solution.py:10
  298.6 6.8 collective-permute-start.1
  305.5 9.7 %collective-permute-start.3 = (bf16[8,3072]{1,0:T(8,128)(2,1)S(1)}, bf16[8,3072]{1,0:T(8,128)(2,1)S(1)}, u32[]{:S(2)}, u32[]{:S(2)}) collective-permute-start(bf16[8,3072]{1,0:T(8,128)(2,1)S(1)} %broadcast_select_fusion.6), channel_id=1, source_target_pairs={{0,12},{4,16},{8,20},{12,24},{16,28},{20,32},{24,36},{28,40},{32,4... | collective-permute-start | bytes 147464 | tf_op jit(solution)/shard_map/ppermute | solution.py:10
  315.1 2.4 collective-permute-start.5
  317.6 8.4 %collective-permute-start.7 = (bf16[8,3072]{1,0:T(8,128)(2,1)S(1)}, bf16[8,3072]{1,0:T(8,128)(2,1)S(1)}, u32[]{:S(2)}, u32[]{:S(2)}) collective-permute-start(bf16[8,3072]{1,0:T(8,128)(2,1)S(1)} %broadcast_select_fusion.4), channel_id=1, source_target_pairs={{0,4},{4,8},{8,12},{12,16},{16,20},{20,24},{24,28},{28,32},{32,36}... | collective-permute-start | bytes 147464 | tf_op jit(solution)/shard_map/ppermute | solution.py:10
  326.0 6.0 collective-permute-start.9
  332.0 5.6 collective-permute-start.11
  337.6 9.8 %collective-permute-start.13 = (bf16[8,3072]{1,0:T(8,128)(2,1)S(1)}, bf16[8,3072]{1,0:T(8,128)(2,1)S(1)}, u32[]{:S(2)}, u32[]{:S(2)}) collective-permute-start(bf16[8,3072]{1,0:T(8,128)(2,1)S(1)} %broadcast_select_fusion.1), channel_id=1, source_target_pairs={{12,0},{16,4},{20,8},{24,12},{28,16},{32,20},{36,24},{40,28},{44,3... | collective-permute-start | bytes 147464 | tf_op jit(solution)/shard_map/ppermute | solution.py:10
  347.4 12.6 %collective-permute-start.15 = (bf16[8,3072]{1,0:T(8,128)(2,1)S(1)}, bf16[8,3072]{1,0:T(8,128)(2,1)S(1)}, u32[]{:S(2)}, u32[]{:S(2)}) collective-permute-start(bf16[8,3072]{1,0:T(8,128)(2,1)S(1)} %broadcast_select_fusion), channel_id=1, source_target_pairs={{16,0},{20,4},{24,8},{28,12},{32,16},{36,20},{40,24},{44,28},{48,3... | collective-permute-start | bytes 147464 | tf_op jit(solution)/shard_map/ppermute | solution.py:10
  359.9 181.7 %collective-permute-start.20 = (f32[8,3072]{1,0:T(8,128)}, f32[8,3072]{1,0:T(8,128)}, u32[]{:S(2)}, u32[]{:S(2)}) collective-permute-start(f32[8,3072]{1,0:T(8,128)} %squeeze.76), channel_id=1, source_target_pairs={{0,4},{4,8},{8,12},{12,16},{16,20},{20,24},{24,28},{28,32},{32,36}... | collective-permute-start | bytes 294920 | tf_op jit(solution)/shard_map/ppermute | solution.py:10
  519.8 23.0 %collective-permute-start.21 = (f32[8,3072]{1,0:T(8,128)}, f32[8,3072]{1,0:T(8,128)S(1)}, u32[]{:S(2)}, u32[]{:S(2)}) collective-permute-start(f32[8,3072]{1,0:T(8,128)} %squeeze.77), channel_id=1, source_target_pairs={{0,8},{4,12},{8,16},{12,20},{16,24},{20,28},{24,32},{28,36},{32,40... | collective-permute-start | bytes 294920 | tf_op jit(solution)/shard_map/ppermute | solution.py:10
  525.6 18.1 %collective-permute-start.22 = (f32[8,3072]{1,0:T(8,128)}, f32[8,3072]{1,0:T(8,128)S(1)}, u32[]{:S(2)}, u32[]{:S(2)}) collective-permute-start(f32[8,3072]{1,0:T(8,128)} %squeeze.78), channel_id=1, source_target_pairs={{0,12},{4,16},{8,20},{12,24},{16,28},{20,32},{24,36},{28,40},{32,4... | collective-permute-start | bytes 294920 | tf_op jit(solution)/shard_map/ppermute | solution.py:10
  530.9 13.6 %collective-permute-start.23 = (f32[8,3072]{1,0:T(8,128)}, f32[8,3072]{1,0:T(8,128)S(1)}, u32[]{:S(2)}, u32[]{:S(2)}) collective-permute-start(f32[8,3072]{1,0:T(8,128)} %squeeze.79), channel_id=1, source_target_pairs={{0,16},{4,20},{8,24},{12,28},{16,32},{20,36},{24,40},{28,44},{32,4... | collective-permute-start | bytes 294920 | tf_op jit(solution)/shard_map/ppermute | solution.py:10
  (14 other events, 426.6 us)
Sparse Core Ops, SparseCore 0:
  546.8 187.4 all-reduce.4
where the time goes:
time: 748 us; the launch traced here: 746 us
  waiting for transfers between devices  220 us (29%)
  other arithmetic  188 us (25%)
  local copies, waits for them, and re-layouts  187 us (25%)
  starting transfers between devices  92.8 us (12%)
  blocking collectives  28.3 us (4%)
  between operations  15 us (2%)
  matrix products  14.6 us (2%)
    psum x1, waiting for transfers between devices, body(): lax.psum((grad_left, grad_sum, grad_right), 'leaf')  187 us
    scatter-add x1, other arithmetic, backward_step(): grad_table = grad_table.at[index_block.reshape(-1)].add(back_terms)  164 us
    gather x3, local copies, waits for them, and re-layouts, collect(): picked = jnp.take(table, index_block, axis=0)  137 us
    ppermute x24, starting transfers between devices, passed_along(): return lax.ppermute(block, axis, route)  92.7 us
    ppermute x24, waiting for transfers between devices, passed_along(): return lax.ppermute(block, axis, route)  33.2 us
    psum x1, blocking collectives, chan_round(): result = lax.psum(total, 'chan').astype(jnp.bfloat16)  16 us
  transfers between devices with their start and end apart: 25, of which 10 were waited for; matrix products, arithmetic and copies ran while one was open for 51% of the time, Pallas kernels for 0%

commit v1 on v0

v1 whole, which is shorter than its diff:
```python
import jax
import jax.numpy as jnp
from jax import lax
from jax.experimental import pallas as pl
from jax.experimental.pallas import tpu as pltpu
from jax.sharding import PartitionSpec as P

BF = jnp.bfloat16
F32 = jnp.float32
LOW = 256
SLAB = 16
VMEM = pl.BlockSpec(memory_space=pltpu.VMEM)
SMEM = pl.BlockSpec(memory_space=pltpu.SMEM)
ROOMY = pltpu.CompilerParams(vmem_limit_bytes=40 * 2**20)


def dot(a, b, contract=((1,), (0,))):
    return lax.dot_general(a, b, (contract, ((), ())), preferred_element_type=F32)


NT = ((1,), (1,))
TN = ((0,), (0,))


def rank_picker(shape, slab_dim, group, group_count, width, sign):
    padded = lax.broadcasted_iota(jnp.int32, shape, slab_dim)
    rank = lax.broadcasted_iota(jnp.int32, shape, 1 - slab_dim)
    step = padded // SLAB
    lane = padded % SLAB
    slab = lax.rem(group + sign * step + group_count, group_count)
    hit = (rank == slab * width + lane) & (lane < width)
    return jnp.where(hit, 1.0, 0.0).astype(BF)


def project_kernel(group_ref, feat_ref, in_ref, cot_ref, outf_ref, *payload_refs):
    group_count = len(payload_refs)
    rank = in_ref.shape[1]
    width = rank // group_count
    pick = rank_picker((group_count * SLAB, rank), 0, group_ref[0], group_count, width, 1)
    weights = dot(pick, in_ref[...], NT).astype(BF)
    reduced = dot(weights, feat_ref[...]).astype(BF)
    grad_mixed = dot(outf_ref[...], cot_ref[...]).astype(BF)
    for j in range(group_count):
        payload_refs[j][0:SLAB, :] = reduced[j * SLAB : (j + 1) * SLAB]
        payload_refs[j][SLAB:, :] = grad_mixed


def low_onehot(low):
    shape = (LOW, low.shape[1])
    want = jnp.broadcast_to(low.astype(F32), shape).astype(BF)
    have = lax.broadcasted_iota(jnp.int32, shape, 0).astype(F32).astype(BF)
    return jnp.where(have == want, jnp.ones((), BF), jnp.zeros((), BF))


def scatter_kernel(halo_ref, p0, p1, p2, p3, core_ref, nbr_ref, gm_ref, own_ref, left_ref, right_ref,
                   far_left_ref, far_right_ref, terms_ref, acc_ref):
    rows = nbr_ref.shape[1]
    tiles = acc_ref.shape[0] // SLAB
    total = (p0[SLAB:, :].astype(F32) + p1[SLAB:, :].astype(F32)) + (
        p2[SLAB:, :].astype(F32) + p3[SLAB:, :].astype(F32)
    )
    grad_mixed = total.astype(BF)
    gm_ref[...] = grad_mixed
    terms_ref[...] = dot(core_ref[...], grad_mixed).astype(BF)
    acc_ref[...] = jnp.zeros_like(acc_ref)

    def step(k, carry):
        index = nbr_ref[pl.ds(k, 1), :]
        onehot = low_onehot(index & (LOW - 1))
        high = jnp.broadcast_to((index >> 8).astype(F32), (SLAB, rows)).astype(BF)
        terms = terms_ref[pl.ds(pl.multiple_of(k * SLAB, SLAB), SLAB), :]
        spread = jnp.concatenate(
            [jnp.where(high == jnp.full((), t, BF), terms, jnp.zeros((), BF)) for t in range(tiles)], 0
        )
        acc_ref[...] += dot(spread, onehot, NT)
        return carry

    lax.fori_loop(0, nbr_ref.shape[0], step, 0, unroll=9)

    def tile(t):
        return acc_ref[t * SLAB : (t + 1) * SLAB, :]

    own_tiles = rows // LOW
    own_ref[...] = jnp.concatenate([tile(t) for t in range(own_tiles)], 1)
    near = halo_ref.shape[0]
    per_peer = (tiles - own_tiles) // near
    for s in range(near):
        first = jnp.clip(halo_ref[s, 0] & 15, 0, 8) * 64
        start = own_tiles + s * per_peer
        window = jnp.concatenate(
            [tile(start + i) for i in range(per_peer)]
            + [jnp.zeros((SLAB, rows - per_peer * LOW), F32)],
            1,
        )
        block = pltpu.roll(window, first, 1).astype(BF)
        if s < 3:
            far_left_ref[s * SLAB : (s + 1) * SLAB, :] = block
        elif s == 3:
            left_ref[...] = block
        elif s == 4:
            right_ref[...] = block
        else:
            far_right_ref[(s - 5) * SLAB : (s - 4) * SLAB, :] = block


def gather_kernel(halo_ref, own_ref, u_ref, v_ref, p_ref, q_ref, gm_ref, core_ref, nbr_ref,
                  mix_ref, gc_ref, table_ref, ga_ref):
    rows = nbr_ref.shape[1]
    tiles = table_ref.shape[0] // SLAB
    own_tiles = rows // LOW
    near = halo_ref.shape[0]
    per_peer = (tiles - own_tiles) // near
    for t in range(own_tiles):
        table_ref[t * SLAB : (t + 1) * SLAB, :] = own_ref[:, t * LOW : (t + 1) * LOW]
    for s in range(near):
        if s < 3:
            block = p_ref[s * SLAB : (s + 1) * SLAB, :]
        elif s == 3:
            block = u_ref[...]
        elif s == 4:
            block = v_ref[...]
        else:
            block = q_ref[(s - 5) * SLAB : (s - 4) * SLAB, :]
        first = jnp.clip(halo_ref[s, 0] & 15, 0, 8) * 64
        window = pltpu.roll(block.astype(F32), rows - first, 1).astype(BF)
        for i in range(per_peer):
            t = own_tiles + s * per_peer + i
            table_ref[t * SLAB : (t + 1) * SLAB, :] = window[:, i * LOW : (i + 1) * LOW]

    def step(k, carry):
        index = nbr_ref[pl.ds(k, 1), :]
        onehot = low_onehot(index & (LOW - 1))
        high = jnp.broadcast_to(index >> 8, (SLAB, rows))
        picked = dot(table_ref[...], onehot)
        found = jnp.zeros((SLAB, rows), F32)
        for t in range(tiles):
            found = jnp.where(high == t, picked[t * SLAB : (t + 1) * SLAB], found)
        ga_ref[pl.ds(pl.multiple_of(k * SLAB, SLAB), SLAB), :] = found.astype(BF)
        return carry

    lax.fori_loop(0, nbr_ref.shape[0], step, 0, unroll=9)
    gathered = ga_ref[...]
    mix_ref[...] = dot(core_ref[...], gathered, TN).astype(BF)
    gc_ref[...] = dot(gm_ref[...], gathered, NT)


def output_kernel(m0, m1, m2, m3, outf_ref, mixed_ref, out_ref):
    total = (m0[...].astype(F32) + m1[...].astype(F32)) + (m2[...].astype(F32) + m3[...].astype(F32))
    mixed = total.astype(BF)
    mixed_ref[...] = mixed
    out_ref[...] = dot(outf_ref[...], mixed, TN).astype(BF)


def gradient_kernel(group_ref, g0, g1, g2, g3, in_ref, feat_ref, mixed_ref, cot_ref, gc_ref,
                    gf_ref, packed_ref):
    rank = in_ref.shape[1]
    rows = feat_ref.shape[1]
    pick = rank_picker((rank, 4 * SLAB), 1, group_ref[0], 4, rank // 4, -1)
    slabs = jnp.concatenate([g0[...], g1[...], g2[...], g3[...]], 0)
    grad_rows = dot(pick, slabs).astype(BF)
    gf_ref[...] = dot(in_ref[...], grad_rows).astype(BF)
    wide = gc_ref.shape[1]
    right = jnp.concatenate([cot_ref[...], jnp.zeros((80, rows), BF)], 0)
    left = jnp.concatenate([jnp.zeros((64, rows), BF), grad_rows, jnp.zeros((16, rows), BF)], 0)
    packed_ref[:, 0:128] = dot(mixed_ref[...], right, NT) + dot(feat_ref[...], left, NT)
    packed_ref[:, 128 : 128 + wide] = gc_ref[...]
    packed_ref[:, 128 + wide :] = jnp.zeros_like(packed_ref[:, 128 + wide :])


def unpack_kernel(factor, packed_ref, left_ref, core_ref, right_ref):
    tail = packed_ref[:, 0:128] * factor
    right_ref[...] = tail[:, 0:48]
    left_ref[...] = tail[:, 64:112]
    flat = (packed_ref[:, 128:] * factor).T
    for k in range(core_ref.shape[0]):
        core_ref[k] = flat[k * SLAB : k * SLAB + core_ref.shape[1], :]


def shifted(block, axis, distance):
    count = lax.axis_size(axis)
    return lax.ppermute(block, axis, [(i, (i + distance) % count) for i in range(count)])


def leaf_sum(total):
    for bit in (1, 2, 4, 8, 16, 32):
        total = total + lax.ppermute(total, "leaf", [(i, i ^ bit) for i in range(lax.axis_size("leaf"))])
    return total


def struct(shape, dtype):
    return jax.ShapeDtypeStruct(shape, dtype)


def body(features, in_factor, core, out_factor, neighbours, halo_blocks, row_mask, cotangent):
    channels, rows = features.shape
    offsets, width, rank = core.shape
    near, slots = halo_blocks.shape[1:]
    table_rows = (rows + near * slots * 64) // LOW * SLAB
    group = lax.axis_index("chan").astype(jnp.int32).reshape(1)
    keep = row_mask.astype(F32).reshape(1, rows)
    halo = halo_blocks[0]
    core_rows = jnp.pad(core, ((0, 0), (0, SLAB - width), (0, 0))).reshape(offsets * SLAB, rank)

    payload = pl.pallas_call(
        project_kernel,
        out_shape=[struct((SLAB + rank, rows), BF)] * 4,
        in_specs=[SMEM] + [VMEM] * 4,
        out_specs=[VMEM] * 4,
        name="project",
    )(group, features, in_factor, cotangent, out_factor)
    parts = [payload[0]] + [shifted(payload[j], "chan", j) for j in (1, 2, 3)]
    reduced = sum(part[:SLAB].astype(F32) for part in parts) * keep
    reduced = reduced.astype(BF)

    from_left = shifted(reduced, "leaf", 1)
    from_right = shifted(reduced, "leaf", -1)
    bundle = jnp.concatenate([from_left, reduced, from_right], 0)
    far_from_left = shifted(bundle, "leaf", 3)
    far_from_right = shifted(bundle, "leaf", -3)

    slab = struct((SLAB, rows), BF)
    triple = struct((3 * SLAB, rows), BF)
    grad_mixed, own, to_left, to_right, far_left, far_right = pl.pallas_call(
        scatter_kernel,
        out_shape=[struct((rank, rows), BF), struct((SLAB, rows), F32), slab, slab, triple, triple],
        in_specs=[SMEM] + [VMEM] * 6,
        out_specs=[VMEM] * 6,
        scratch_shapes=[pltpu.VMEM((offsets * SLAB, rows), BF), pltpu.VMEM((table_rows, LOW), F32)],
        compiler_params=ROOMY,
        cost_estimate=pl.CostEstimate(flops=5 * 10**9, bytes_accessed=2**20, transcendentals=0),
        name="scatter",
    )(halo, *parts, core_rows, neighbours)

    back_right = shifted(far_left, "leaf", -3)
    back_left = shifted(far_right, "leaf", 3)
    back = back_right.astype(F32) + back_left.astype(F32)
    near_left = shifted((to_left.astype(F32) + back[:SLAB]).astype(BF), "leaf", -1)
    near_right = shifted((to_right.astype(F32) + back[2 * SLAB :]).astype(BF), "leaf", 1)

    mixed_part, grad_core = pl.pallas_call(
        gather_kernel,
        out_shape=[struct((rank, rows), BF), struct((rank, offsets * SLAB), F32)],
        in_specs=[SMEM] + [VMEM] * 8,
        out_specs=[VMEM] * 2,
        scratch_shapes=[pltpu.VMEM((table_rows, LOW), BF), pltpu.VMEM((offsets * SLAB, rows), BF)],
        compiler_params=ROOMY,
        cost_estimate=pl.CostEstimate(flops=5 * 10**9, bytes_accessed=2**20, transcendentals=0),
        name="gather",
    )(halo, reduced, from_left, from_right, far_from_left, far_from_right, grad_mixed, core_rows, neighbours)
    mixed_parts = [mixed_part] + [shifted(mixed_part, "chan", j) for j in (1, 2, 3)]

    grad_slab = own + back[SLAB : 2 * SLAB] + near_left.astype(F32) + near_right.astype(F32)
    grad_slab = (grad_slab * keep).astype(BF)
    slabs = [grad_slab] + [shifted(grad_slab, "chan", j) for j in (1, 2, 3)]

    mixed, output = pl.pallas_call(
        output_kernel,
        out_shape=[struct((rank, rows), BF), struct((channels, rows), BF)],
        in_specs=[VMEM] * 5,
        out_specs=[VMEM] * 2,
        name="output",
    )(*mixed_parts, out_factor)

    packed_width = 128 + (offsets * SLAB + 127) // 128 * 128
    grad_features, packed = pl.pallas_call(
        gradient_kernel,
        out_shape=[struct((channels, rows), BF), struct((rank, packed_width), F32)],
        in_specs=[SMEM] + [VMEM] * 9,
        out_specs=[VMEM] * 2,
        name="gradient",
    )(group, *slabs, in_factor, features, mixed, cotangent, grad_core)
    packed = leaf_sum(packed)

    factor = float(rows * lax.axis_size("leaf")) ** (-0.5)
    grad_in, grad_core, grad_out = pl.pallas_call(
        lambda *refs: unpack_kernel(factor, *refs),
        out_shape=[struct((channels, rank), F32), struct((offsets, width, rank), F32), struct((rank, channels), F32)],
        in_specs=[VMEM],
        out_specs=[VMEM] * 3,
        name="unpack",
    )(packed)
    return (output, grad_features, grad_in, grad_core, grad_out)


def solution(mesh):
    placed = (
        P("chan", "leaf"),
        P("chan", None),
        P(None, "chan", None),
        P(None, "chan"),
        P(None, "leaf"),
        P("leaf", None, None),
        P("leaf"),
        P("chan", "leaf"),
    )
    return jax.shard_map(
        body,
        mesh=mesh,
        in_specs=placed,
        out_specs=(
            P("chan", "leaf"),
            P("chan", "leaf"),
            P("chan", None),
            P(None, "chan", None),
            P(None, "chan"),
        ),
        check_vma=False,
    )
```

time: 748 us -> 117 us (0.16)
  the two profiles are of different devices: /device:TPU:1 before, /device:TPU:2 now
where the time goes in v1:
time: 117 us
  waiting for transfers between devices  50.8 us (43%)
  starting transfers between devices  38.6 us (33%)
  Pallas kernels  20.6 us (18%)
  local copies, waits for them, and re-layouts  4.28 us (4%)
  other arithmetic  1.74 us (1%)
    ppermute x17, starting transfers between devices, shifted(): lax.ppermute(block, axis, [(i, (i + distance) % count) for i in range(cou...  34.9 us
    ppermute x6, waiting for transfers between devices, leaf_sum(): lax.ppermute(total, 'leaf', [(i, i ^ bit) for i in range(lax.axis_size('l...  31.1 us
    ppermute x17, waiting for transfers between devices, shifted(): lax.ppermute(block, axis, [(i, (i + distance) % count) for i in range(cou...  19.7 us
    pallas_call x1, Pallas kernels, body(): pl.pallas_call(gather_kernel, out_shape=[struct((rank, rows), BF), struct...  6.4 us
    pallas_call x1, Pallas kernels, body(): pl.pallas_call(scatter_kernel, out_shape=[struct((rank, rows), BF), struc...  6.33 us
    unnamed x30, local copies, waits for them, and re-layouts  4.25 us
    ppermute x6, starting transfers between devices, leaf_sum(): lax.ppermute(total, 'leaf', [(i, i ^ bit) for i in range(lax.axis_size('l...  3.7 us
  transfers between devices with their start and end apart: 23, of which 16 were waited for; matrix products, arithmetic and copies ran while one was open for 0% of the time, Pallas kernels for 2%

profile of v1, /device:TPU:2, one launch (start us, length us, event | category | flops | bytes accessed | tf_op | source)
XLA Modules:
  0.0 116.9 jit_solution(17114756415957498928)
XLA Ops:
  0.6 2.1 %project.1 = (bf16[64,1024]{1,0:T(8,128)(2,1)}, bf16[64,1024]{1,0:T(8,128)(2,1)}, bf16[64,1024]{1,0:T(8,128)(2,1)}, bf16[64,1024]{1,0:T(8,128)(2,1)}) custom-call(s32[1]{0:T(128)} %bitcast.1.group_ref, bf16[48,1024]{1,0:T(8,128)(2,1)} %feat_ref.3, bf16[48,48]{1,0:T(8,128)(2,1)} %in_ref.3, bf16[48,1024]{1,0:T(8,128)(2,1)} %cot_ref.3, bf16[48,48]{1,0:T(8,128)(2,1)} %outf_ref.3), custom_call_target="tpu_custom_call" | custom-call | tf_op jit(solution)/shard_map/project/pallas_call | solution.py:204
  2.8 1.6 %collective-permute-start = (bf16[64,1024]{1,0:T(8,128)(2,1)}, bf16[64,1024]{1,0:T(8,128)(2,1)S(1)}, u32[]{:S(2)}, u32[]{:S(2)}) collective-permute-start(bf16[64,1024]{1,0:T(8,128)(2,1)} %get-tuple-element.25), channel_id=1, source_target_pairs={{0,1},{1,2},{2,3},{3,0},{4,5},{5,6},{6,7},{7,4},{8,9},{9,10},{10,1... | collective-permute-start | bytes 393224 | tf_op jit(solution)/shard_map/ppermute | solution.py:181
  4.3 2.9 %collective-permute-start.1 = (bf16[64,1024]{1,0:T(8,128)(2,1)}, bf16[64,1024]{1,0:T(8,128)(2,1)S(1)}, u32[]{:S(2)}, u32[]{:S(2)}) collective-permute-start(bf16[64,1024]{1,0:T(8,128)(2,1)} %get-tuple-element.26), channel_id=1, source_target_pairs={{0,2},{1,3},{2,0},{3,1},{4,6},{5,7},{6,4},{7,5},{8,10},{9,11},{10,... | collective-permute-start | bytes 393224 | tf_op jit(solution)/shard_map/ppermute | solution.py:181
  7.2 1.3 %collective-permute-start.2 = (bf16[64,1024]{1,0:T(8,128)(2,1)}, bf16[64,1024]{1,0:T(8,128)(2,1)S(1)}, u32[]{:S(2)}, u32[]{:S(2)}) collective-permute-start(bf16[64,1024]{1,0:T(8,128)(2,1)} %get-tuple-element.27), channel_id=1, source_target_pairs={{0,3},{1,0},{2,1},{3,2},{4,7},{5,4},{6,5},{7,6},{8,11},{9,8},{10,9... | collective-permute-start | bytes 393224 | tf_op jit(solution)/shard_map/ppermute | solution.py:181
  9.5 4.0 %collective-permute-done.1.p2 = bf16[64,1024]{1,0:T(8,128)(2,1)S(1)} collective-permute-done((bf16[64,1024]{1,0:T(8,128)(2,1)}, bf16[64,1024]{1,0:T(8,128)(2,1)S(1)}, u32[]{:S(2)}, u32[]{:S(2)}) %collective-permute-start.1) | collective-permute-done | bytes 131104 | tf_op jit(solution)/shard_map/ppermute | solution.py:181
  13.5 6.3 %scatter.1 = (bf16[48,1024]{1,0:T(8,128)(2,1)S(1)}, f32[16,1024]{1,0:T(8,128)S(1)}, bf16[16,1024]{1,0:T(8,128)(2,1)S(1)}, bf16[16,1024]{1,0:T(8,128)(2,1)S(1)}, ...) custom-call(s32[8,8]{1,0:T(8,128)S(1)} %bitcast.5, bf16[64,1024]{1,0:T(8,128)(2,1)S(1)} %copy-done.2, ...), custom_call_target="tpu_custom_call" | custom-call | flops 5000000000 | bytes 1048576 | tf_op jit(solution)/shard_map/scatter/pallas_call | solution.py:223
  19.8 6.1 %collective-permute-start.10 = (bf16[48,1024]{1,0:T(8,128)(2,1)S(1)}, bf16[48,1024]{1,0:T(8,128)(2,1)S(1)}, u32[]{:S(2)}, u32[]{:S(2)}) collective-permute-start(bf16[48,1024]{1,0:T(8,128)(2,1)S(1)} %get-tuple-element.32), channel_id=1, source_target_pairs={{0,244},{4,248},{8,252},{12,0},{16,4},{20,8},{24,12},{28,16},{32,2... | collective-permute-start | bytes 294920 | tf_op jit(solution)/shard_map/ppermute | solution.py:181
  25.9 2.2 %collective-permute-done.10 = bf16[48,1024]{1,0:T(8,128)(2,1)S(1)} collective-permute-done((bf16[48,1024]{1,0:T(8,128)(2,1)S(1)}, bf16[48,1024]{1,0:T(8,128)(2,1)S(1)}, u32[]{:S(2)}, u32[]{:S(2)}) %collective-permute-start.10) | collective-permute-done | bytes 98336 | tf_op jit(solution)/shard_map/ppermute | solution.py:181
  28.1 5.5 %collective-permute-done.11 = bf16[48,1024]{1,0:T(8,128)(2,1)S(1)} collective-permute-done((bf16[48,1024]{1,0:T(8,128)(2,1)S(1)}, bf16[48,1024]{1,0:T(8,128)(2,1)S(1)}, u32[]{:S(2)}, u32[]{:S(2)}) %collective-permute-start.11) | collective-permute-done | bytes 98336 | tf_op jit(solution)/shard_map/ppermute | solution.py:181
  33.7 2.1 %collective-permute-start.12 = (bf16[16,1024]{1,0:T(8,128)(2,1)S(1)}, bf16[16,1024]{1,0:T(8,128)(2,1)S(1)}, u32[]{:S(2)}, u32[]{:S(2)}) collective-permute-start(bf16[16,1024]{1,0:T(8,128)(2,1)S(1)} %get-tuple-element.48), channel_id=1, source_target_pairs={{0,252},{4,0},{8,4},{12,8},{16,12},{20,16},{24,20},{28,24},{32,28}... | collective-permute-start | bytes 98312 | tf_op jit(solution)/shard_map/ppermute | solution.py:181
  35.7 1.6 %collective-permute-done.12 = bf16[16,1024]{1,0:T(8,128)(2,1)S(1)} collective-permute-done((bf16[16,1024]{1,0:T(8,128)(2,1)S(1)}, bf16[16,1024]{1,0:T(8,128)(2,1)S(1)}, u32[]{:S(2)}, u32[]{:S(2)}) %collective-permute-start.12) | collective-permute-done | bytes 32800 | tf_op jit(solution)/shard_map/ppermute | solution.py:181
  37.3 1.7 %collective-permute-done.13 = bf16[16,1024]{1,0:T(8,128)(2,1)S(1)} collective-permute-done((bf16[16,1024]{1,0:T(8,128)(2,1)S(1)}, bf16[16,1024]{1,0:T(8,128)(2,1)S(1)}, u32[]{:S(2)}, u32[]{:S(2)}) %collective-permute-start.13) | collective-permute-done | bytes 32800 | tf_op jit(solution)/shard_map/ppermute | solution.py:181
  39.2 1.7 %collective-permute-start.4 = (bf16[16,1024]{1,0:T(8,128)(2,1)S(1)}, bf16[16,1024]{1,0:T(8,128)(2,1)S(1)}, u32[]{:S(2)}, u32[]{:S(2)}) collective-permute-start(bf16[16,1024]{1,0:T(8,128)(2,1)S(1)} %get-tuple-element.51.own_ref), channel_id=1, source_target_pairs={{0,252},{4,0},{8,4},{12,8},{16,12},{20,16},{24,20},{28,24},{32,28}... | collective-permute-start | bytes 98312 | tf_op jit(solution)/shard_map/ppermute | solution.py:181
  40.9 1.6 %collective-permute-done.3.u_ref = bf16[16,1024]{1,0:T(8,128)(2,1)S(1)} collective-permute-done((bf16[16,1024]{1,0:T(8,128)(2,1)S(1)}, bf16[16,1024]{1,0:T(8,128)(2,1)S(1)}, u32[]{:S(2)}, u32[]{:S(2)}) %collective-permute-start.3) | collective-permute-done | bytes 32800 | tf_op jit(solution)/shard_map/ppermute | solution.py:181
  42.7 10.2 %collective-permute-start.6 = (bf16[48,1024]{1,0:T(8,128)(2,1)S(1)}, bf16[48,1024]{1,0:T(8,128)(2,1)S(1)}, u32[]{:S(2)}, u32[]{:S(2)}) collective-permute-start(bf16[48,1024]{1,0:T(8,128)(2,1)S(1)} %pad_maximum_fusion), channel_id=1, source_target_pairs={{0,244},{4,248},{8,252},{12,0},{16,4},{20,8},{24,12},{28,16},{32,2... | collective-permute-start | bytes 294920 | tf_op jit(solution)/shard_map/ppermute | solution.py:181
  52.9 2.0 %collective-permute-done.5.p_ref = bf16[48,1024]{1,0:T(8,128)(2,1)S(1)} collective-permute-done((bf16[48,1024]{1,0:T(8,128)(2,1)S(1)}, bf16[48,1024]{1,0:T(8,128)(2,1)S(1)}, u32[]{:S(2)}, u32[]{:S(2)}) %collective-permute-start.5) | collective-permute-done | bytes 98336 | tf_op jit(solution)/shard_map/ppermute | solution.py:181
  55.1 6.4 %gather.1 = (bf16[48,1024]{1,0:T(8,128)(2,1)S(1)}, f32[48,432]{1,0:T(8,128)S(1)}) custom-call(s32[8,8]{1,0:T(8,128)S(1)} %bitcast.6, bf16[16,1024]{1,0:T(8,128)(2,1)S(1)} %get-tuple-element.51.own_ref, bf16[16,1024]{1,0:T(8,128)(2,1)S(1)} %collective-permute-done.3.u_ref, bf16[16,1024]{1,0:T(8,128)(2,1)S(1)} %collective-permute-done.4.v_ref, ...), custom_call_target="tpu_custom_call" | custom-call | flops 5000000000 | bytes 1048576 | tf_op jit(solution)/shard_map/gather/pallas_call | solution.py:240
  63.2 2.9 %collective-permute-start.8 = (bf16[48,1024]{1,0:T(8,128)(2,1)S(1)}, bf16[48,1024]{1,0:T(8,128)(2,1)S(1)}, u32[]{:S(2)}, u32[]{:S(2)}) collective-permute-start(bf16[48,1024]{1,0:T(8,128)(2,1)S(1)} %get-tuple-element.29.m0), channel_id=1, source_target_pairs={{0,2},{1,3},{2,0},{3,1},{4,6},{5,7},{6,4},{7,5},{8,10},{9,11},{10,... | collective-permute-start | bytes 294920 | tf_op jit(solution)/shard_map/ppermute | solution.py:181
  66.8 1.3 %collective-permute-start.14 = (bf16[16,1024]{1,0:T(8,128)(2,1)S(1)}, bf16[16,1024]{1,0:T(8,128)(2,1)S(1)}, u32[]{:S(2)}, u32[]{:S(2)}) collective-permute-start(bf16[16,1024]{1,0:T(8,128)(2,1)S(1)} %get-tuple-element.50.g0), channel_id=1, source_target_pairs={{0,1},{1,2},{2,3},{3,0},{4,5},{5,6},{6,7},{7,4},{8,9},{9,10},{10,1... | collective-permute-start | bytes 98312 | tf_op jit(solution)/shard_map/ppermute | solution.py:181
  68.7 2.3 %collective-permute-start.16 = (bf16[16,1024]{1,0:T(8,128)(2,1)S(1)}, bf16[16,1024]{1,0:T(8,128)(2,1)S(1)}, u32[]{:S(2)}, u32[]{:S(2)}) collective-permute-start(bf16[16,1024]{1,0:T(8,128)(2,1)S(1)} %get-tuple-element.50.g0), channel_id=1, source_target_pairs={{0,3},{1,0},{2,1},{3,2},{4,7},{5,4},{6,5},{7,6},{8,11},{9,8},{10,9... | collective-permute-start | bytes 98312 | tf_op jit(solution)/shard_map/ppermute | solution.py:181
  72.4 1.9 %output.1 = (bf16[48,1024]{1,0:T(8,128)(2,1)}, bf16[48,1024]{1,0:T(8,128)(2,1)}) custom-call(bf16[48,1024]{1,0:T(8,128)(2,1)} %copy-done.1, bf16[48,1024]{1,0:T(8,128)(2,1)} %copy-done.7, bf16[48,1024]{1,0:T(8,128)(2,1)} %copy-done.8, bf16[48,1024]{1,0:T(8,128)(2,1)} %copy-done.9, bf16[48,48]{1,0:T(8,128)(2,1)} %outf_ref.3), custom_call_target="tpu_custom_call" | custom-call | tf_op jit(solution)/shard_map/output/pallas_call | solution.py:256
  74.9 2.2 %gradient.1 = (bf16[48,1024]{1,0:T(8,128)(2,1)}, f32[48,640]{1,0:T(8,128)}) custom-call(s32[1]{0:T(128)} %bitcast.1.group_ref, bf16[16,1024]{1,0:T(8,128)(2,1)} %copy-done.5, bf16[16,1024]{1,0:T(8,128)(2,1)} %copy-done.10, bf16[16,1024]{1,0:T(8,128)(2,1)} %copy-done.11, bf16[16,1024]{1,0:T(8,128)(2,1)} %copy-done.12, bf16[48,48]{1,0:T(8,128)(2,1)} %in_ref.3, ...), custom_call_target="tpu_custom_call" | custom-call | tf_op jit(solution)/shard_map/gradient/pallas_call | solution.py:265
  77.1 1.5 %collective-permute-done.17 = f32[48,640]{1,0:T(8,128)S(1)} collective-permute-done((f32[48,640]{1,0:T(8,128)}, f32[48,640]{1,0:T(8,128)S(1)}, u32[]{:S(2)}, u32[]{:S(2)}) %collective-permute-start.17) | collective-permute-done | bytes 122912 | tf_op jit(solution)/shard_map/ppermute | solution.py:186
  79.5 1.4 %collective-permute-start.18 = (f32[48,640]{1,0:T(8,128)S(1)}, f32[48,640]{1,0:T(8,128)S(1)}, u32[]{:S(2)}, u32[]{:S(2)}) collective-permute-start(f32[48,640]{1,0:T(8,128)S(1)} %add.56), channel_id=1, source_target_pairs={{0,8},{4,12},{8,0},{12,4},{16,24},{20,28},{24,16},{28,20},{32,40},... | collective-permute-start | bytes 368648 | tf_op jit(solution)/shard_map/ppermute | solution.py:186
  80.9 4.1 %collective-permute-done.18 = f32[48,640]{1,0:T(8,128)S(1)} collective-permute-done((f32[48,640]{1,0:T(8,128)S(1)}, f32[48,640]{1,0:T(8,128)S(1)}, u32[]{:S(2)}, u32[]{:S(2)}) %collective-permute-start.18) | collective-permute-done | bytes 122912 | tf_op jit(solution)/shard_map/ppermute | solution.py:186
  85.1 6.4 %collective-permute-done.19 = f32[48,640]{1,0:T(8,128)S(1)} collective-permute-done((f32[48,640]{1,0:T(8,128)S(1)}, f32[48,640]{1,0:T(8,128)S(1)}, u32[]{:S(2)}, u32[]{:S(2)}) %collective-permute-start.19) | collective-permute-done | bytes 122912 | tf_op jit(solution)/shard_map/ppermute | solution.py:186
  91.6 4.9 %collective-permute-done.20 = f32[48,640]{1,0:T(8,128)S(1)} collective-permute-done((f32[48,640]{1,0:T(8,128)S(1)}, f32[48,640]{1,0:T(8,128)S(1)}, u32[]{:S(2)}, u32[]{:S(2)}) %collective-permute-start.20) | collective-permute-done | bytes 122912 | tf_op jit(solution)/shard_map/ppermute | solution.py:186
  96.6 6.6 %collective-permute-done.21 = f32[48,640]{1,0:T(8,128)S(1)} collective-permute-done((f32[48,640]{1,0:T(8,128)S(1)}, f32[48,640]{1,0:T(8,128)S(1)}, u32[]{:S(2)}, u32[]{:S(2)}) %collective-permute-start.21) | collective-permute-done | bytes 122912 | tf_op jit(solution)/shard_map/ppermute | solution.py:186
  103.2 2.0 %collective-permute-start.22 = (f32[48,640]{1,0:T(8,128)S(1)}, f32[48,640]{1,0:T(8,128)S(1)}, u32[]{:S(2)}, u32[]{:S(2)}) collective-permute-start(f32[48,640]{1,0:T(8,128)S(1)} %add.60), channel_id=1, source_target_pairs={{0,128},{4,132},{8,136},{12,140},{16,144},{20,148},{24,152},{28,15... | collective-permute-start | bytes 368648 | tf_op jit(solution)/shard_map/ppermute | solution.py:186
  105.2 7.6 %collective-permute-done.22 = f32[48,640]{1,0:T(8,128)S(1)} collective-permute-done((f32[48,640]{1,0:T(8,128)S(1)}, f32[48,640]{1,0:T(8,128)S(1)}, u32[]{:S(2)}, u32[]{:S(2)}) %collective-permute-start.22) | collective-permute-done | bytes 122912 | tf_op jit(solution)/shard_map/ppermute | solution.py:186
  113.5 1.7 %unpack.1 = (f32[48,48]{1,0:T(8,128)}, f32[27,12,48]{2,1,0:T(8,128)}, f32[48,48]{1,0:T(8,128)}) custom-call(f32[48,640]{1,0:T(8,128)} %add.61.refs_0_), custom_call_target="tpu_custom_call" | custom-call | tf_op jit(solution)/shard_map/unpack/pallas_call | solution.py:275
  115.3 1.7 %copy.14 = f32[27,12,48]{2,0,1:T(8,128)} copy(f32[27,12,48]{2,1,0:T(8,128)} %get-tuple-element.46) | data formatting | bytes 124416
  (62 shorter events, 8.2 us)
Async XLA Ops:
  0.6 8.0 %copy-start.6 = (bf16[27,12,48]{2,0,1:T(8,128)(2,1)S(1)}, bf16[27,12,48]{2,0,1:T(8,128)(2,1)}, u32[]{:S(2)}) copy-start(bf16[27,12,48]{2,0,1:T(8,128)(2,1)} %param.10) | copy-start | bytes 93316
  2.8 6.7 %collective-permute-start = (bf16[64,1024]{1,0:T(8,128)(2,1)}, bf16[64,1024]{1,0:T(8,128)(2,1)S(1)}, u32[]{:S(2)}, u32[]{:S(2)}) collective-permute-start(bf16[64,1024]{1,0:T(8,128)(2,1)} %get-tuple-element.25), channel_id=1, source_target_pairs={{0,1},{1,2},{2,3},{3,0},{4,5},{5,6},{6,7},{7,4},{8,9},{9,10},{10,1... | collective-permute-start | bytes 393224 | tf_op jit(solution)/shard_map/ppermute | solution.py:181
  4.3 9.1 %collective-permute-start.1 = (bf16[64,1024]{1,0:T(8,128)(2,1)}, bf16[64,1024]{1,0:T(8,128)(2,1)S(1)}, u32[]{:S(2)}, u32[]{:S(2)}) collective-permute-start(bf16[64,1024]{1,0:T(8,128)(2,1)} %get-tuple-element.26), channel_id=1, source_target_pairs={{0,2},{1,3},{2,0},{3,1},{4,6},{5,7},{6,4},{7,5},{8,10},{9,11},{10,... | collective-permute-start | bytes 393224 | tf_op jit(solution)/shard_map/ppermute | solution.py:181
  7.2 6.2 %collective-permute-start.2 = (bf16[64,1024]{1,0:T(8,128)(2,1)}, bf16[64,1024]{1,0:T(8,128)(2,1)S(1)}, u32[]{:S(2)}, u32[]{:S(2)}) collective-permute-start(bf16[64,1024]{1,0:T(8,128)(2,1)} %get-tuple-element.27), channel_id=1, source_target_pairs={{0,3},{1,0},{2,1},{3,2},{4,7},{5,4},{6,5},{7,6},{8,11},{9,8},{10,9... | collective-permute-start | bytes 393224 | tf_op jit(solution)/shard_map/ppermute | solution.py:181
  8.6 4.9 %copy-start.3 = (s32[27,1024]{1,0:T(8,128)S(1)}, s32[27,1024]{1,0:T(8,128)}, u32[]{:S(2)}) copy-start(s32[27,1024]{1,0:T(8,128)} %nbr_ref.3) | copy-start | bytes 331780
  8.6 4.8 %copy-start.2 = (bf16[64,1024]{1,0:T(8,128)(2,1)S(1)}, bf16[64,1024]{1,0:T(8,128)(2,1)}, u32[]{:S(2)}) copy-start(bf16[64,1024]{1,0:T(8,128)(2,1)} %get-tuple-element.24.p0) | copy-start | bytes 393220
  8.7 4.8 %copy-start.4 = (s32[1,8,8]{2,1,0:T(8,128)S(1)}, s32[1,8,8]{2,1,0:T(8,128)}, u32[]{:S(2)}) copy-start(s32[1,8,8]{2,1,0:T(8,128)} %param.13) | copy-start | bytes 772
  19.8 8.3 %collective-permute-start.10 = (bf16[48,1024]{1,0:T(8,128)(2,1)S(1)}, bf16[48,1024]{1,0:T(8,128)(2,1)S(1)}, u32[]{:S(2)}, u32[]{:S(2)}) collective-permute-start(bf16[48,1024]{1,0:T(8,128)(2,1)S(1)} %get-tuple-element.32), channel_id=1, source_target_pairs={{0,244},{4,248},{8,252},{12,0},{16,4},{20,8},{24,12},{28,16},{32,2... | collective-permute-start | bytes 294920 | tf_op jit(solution)/shard_map/ppermute | solution.py:181
  25.9 7.7 %collective-permute-start.11 = (bf16[48,1024]{1,0:T(8,128)(2,1)S(1)}, bf16[48,1024]{1,0:T(8,128)(2,1)S(1)}, u32[]{:S(2)}, u32[]{:S(2)}) collective-permute-start(bf16[48,1024]{1,0:T(8,128)(2,1)S(1)} %get-tuple-element.33), channel_id=1, source_target_pairs={{0,12},{4,16},{8,20},{12,24},{16,28},{20,32},{24,36},{28,40},{32,4... | collective-permute-start | bytes 294920 | tf_op jit(solution)/shard_map/ppermute | solution.py:181
  33.6 2.1 %copy-start.13 = (s32[1024]{0:T(1024)S(1)}, s32[1024]{0:T(1024)}, u32[]{:S(2)}) copy-start(s32[1024]{0:T(1024)} %param.14) | copy-start | bytes 12292
  33.7 3.6 %collective-permute-start.12 = (bf16[16,1024]{1,0:T(8,128)(2,1)S(1)}, bf16[16,1024]{1,0:T(8,128)(2,1)S(1)}, u32[]{:S(2)}, u32[]{:S(2)}) collective-permute-start(bf16[16,1024]{1,0:T(8,128)(2,1)S(1)} %get-tuple-element.48), channel_id=1, source_target_pairs={{0,252},{4,0},{8,4},{12,8},{16,12},{20,16},{24,20},{28,24},{32,28}... | collective-permute-start | bytes 98312 | tf_op jit(solution)/shard_map/ppermute | solution.py:181
  35.7 3.3 %collective-permute-start.13 = (bf16[16,1024]{1,0:T(8,128)(2,1)S(1)}, bf16[16,1024]{1,0:T(8,128)(2,1)S(1)}, u32[]{:S(2)}, u32[]{:S(2)}) collective-permute-start(bf16[16,1024]{1,0:T(8,128)(2,1)S(1)} %get-tuple-element.49), channel_id=1, source_target_pairs={{0,4},{4,8},{8,12},{12,16},{16,20},{20,24},{24,28},{28,32},{32,36}... | collective-permute-start | bytes 98312 | tf_op jit(solution)/shard_map/ppermute | solution.py:181
  39.1 29.6 %copy-start.5 = (bf16[16,1024]{1,0:T(8,128)(2,1)}, bf16[16,1024]{1,0:T(8,128)(2,1)S(1)}, u32[]{:S(2)}) copy-start(bf16[16,1024]{1,0:T(8,128)(2,1)S(1)} %get-tuple-element.50.g0) | copy-start | bytes 98308
  39.1 3.4 %collective-permute-start.3 = (bf16[16,1024]{1,0:T(8,128)(2,1)S(1)}, bf16[16,1024]{1,0:T(8,128)(2,1)S(1)}, u32[]{:S(2)}, u32[]{:S(2)}) collective-permute-start(bf16[16,1024]{1,0:T(8,128)(2,1)S(1)} %get-tuple-element.51.own_ref), channel_id=1, source_target_pairs={{0,4},{4,8},{8,12},{12,16},{16,20},{20,24},{24,28},{28,32},{32,36}... | collective-permute-start | bytes 98312 | tf_op jit(solution)/shard_map/ppermute | solution.py:181
  39.2 3.4 %collective-permute-start.4 = (bf16[16,1024]{1,0:T(8,128)(2,1)S(1)}, bf16[16,1024]{1,0:T(8,128)(2,1)S(1)}, u32[]{:S(2)}, u32[]{:S(2)}) collective-permute-start(bf16[16,1024]{1,0:T(8,128)(2,1)S(1)} %get-tuple-element.51.own_ref), channel_id=1, source_target_pairs={{0,252},{4,0},{8,4},{12,8},{16,12},{20,16},{24,20},{28,24},{32,28}... | collective-permute-start | bytes 98312 | tf_op jit(solution)/shard_map/ppermute | solution.py:181
  42.7 12.3 %collective-permute-start.5 = (bf16[48,1024]{1,0:T(8,128)(2,1)S(1)}, bf16[48,1024]{1,0:T(8,128)(2,1)S(1)}, u32[]{:S(2)}, u32[]{:S(2)}) collective-permute-start(bf16[48,1024]{1,0:T(8,128)(2,1)S(1)} %pad_maximum_fusion), channel_id=1, source_target_pairs={{0,12},{4,16},{8,20},{12,24},{16,28},{20,32},{24,36},{28,40},{32,4... | collective-permute-start | bytes 294920 | tf_op jit(solution)/shard_map/ppermute | solution.py:181
  42.7 12.4 %collective-permute-start.6 = (bf16[48,1024]{1,0:T(8,128)(2,1)S(1)}, bf16[48,1024]{1,0:T(8,128)(2,1)S(1)}, u32[]{:S(2)}, u32[]{:S(2)}) collective-permute-start(bf16[48,1024]{1,0:T(8,128)(2,1)S(1)} %pad_maximum_fusion), channel_id=1, source_target_pairs={{0,244},{4,248},{8,252},{12,0},{16,4},{20,8},{24,12},{28,16},{32,2... | collective-permute-start | bytes 294920 | tf_op jit(solution)/shard_map/ppermute | solution.py:181
  62.2 8.9 %copy-start.1 = (bf16[48,1024]{1,0:T(8,128)(2,1)}, bf16[48,1024]{1,0:T(8,128)(2,1)S(1)}, u32[]{:S(2)}) copy-start(bf16[48,1024]{1,0:T(8,128)(2,1)S(1)} %get-tuple-element.29.m0) | copy-start | bytes 294916
  62.2 6.5 %collective-permute-start.7 = (bf16[48,1024]{1,0:T(8,128)(2,1)S(1)}, bf16[48,1024]{1,0:T(8,128)(2,1)S(1)}, u32[]{:S(2)}, u32[]{:S(2)}) collective-permute-start(bf16[48,1024]{1,0:T(8,128)(2,1)S(1)} %get-tuple-element.29.m0), channel_id=1, source_target_pairs={{0,1},{1,2},{2,3},{3,0},{4,5},{5,6},{6,7},{7,4},{8,9},{9,10},{10,1... | collective-permute-start | bytes 294920 | tf_op jit(solution)/shard_map/ppermute | solution.py:181
  63.2 7.9 %collective-permute-start.8 = (bf16[48,1024]{1,0:T(8,128)(2,1)S(1)}, bf16[48,1024]{1,0:T(8,128)(2,1)S(1)}, u32[]{:S(2)}, u32[]{:S(2)}) collective-permute-start(bf16[48,1024]{1,0:T(8,128)(2,1)S(1)} %get-tuple-element.29.m0), channel_id=1, source_target_pairs={{0,2},{1,3},{2,0},{3,1},{4,6},{5,7},{6,4},{7,5},{8,10},{9,11},{10,... | collective-permute-start | bytes 294920 | tf_op jit(solution)/shard_map/ppermute | solution.py:181
  66.1 5.0 %collective-permute-start.9 = (bf16[48,1024]{1,0:T(8,128)(2,1)S(1)}, bf16[48,1024]{1,0:T(8,128)(2,1)S(1)}, u32[]{:S(2)}, u32[]{:S(2)}) collective-permute-start(bf16[48,1024]{1,0:T(8,128)(2,1)S(1)} %get-tuple-element.29.m0), channel_id=1, source_target_pairs={{0,3},{1,0},{2,1},{3,2},{4,7},{5,4},{6,5},{7,6},{8,11},{9,8},{10,9... | collective-permute-start | bytes 294920 | tf_op jit(solution)/shard_map/ppermute | solution.py:181
  66.8 7.4 %collective-permute-start.14 = (bf16[16,1024]{1,0:T(8,128)(2,1)S(1)}, bf16[16,1024]{1,0:T(8,128)(2,1)S(1)}, u32[]{:S(2)}, u32[]{:S(2)}) collective-permute-start(bf16[16,1024]{1,0:T(8,128)(2,1)S(1)} %get-tuple-element.50.g0), channel_id=1, source_target_pairs={{0,1},{1,2},{2,3},{3,0},{4,5},{5,6},{6,7},{7,4},{8,9},{9,10},{10,1... | collective-permute-start | bytes 98312 | tf_op jit(solution)/shard_map/ppermute | solution.py:181
  68.1 6.1 %collective-permute-start.15 = (bf16[16,1024]{1,0:T(8,128)(2,1)S(1)}, bf16[16,1024]{1,0:T(8,128)(2,1)S(1)}, u32[]{:S(2)}, u32[]{:S(2)}) collective-permute-start(bf16[16,1024]{1,0:T(8,128)(2,1)S(1)} %get-tuple-element.50.g0), channel_id=1, source_target_pairs={{0,2},{1,3},{2,0},{3,1},{4,6},{5,7},{6,4},{7,5},{8,10},{9,11},{10,... | collective-permute-start | bytes 98312 | tf_op jit(solution)/shard_map/ppermute | solution.py:181
  68.7 2.3 %copy-start.7 = (bf16[48,1024]{1,0:T(8,128)(2,1)}, bf16[48,1024]{1,0:T(8,128)(2,1)S(1)}, u32[]{:S(2)}) copy-start(bf16[48,1024]{1,0:T(8,128)(2,1)S(1)} %collective-permute-done.7.m1) | copy-start | bytes 294916
  68.7 5.5 %collective-permute-start.16 = (bf16[16,1024]{1,0:T(8,128)(2,1)S(1)}, bf16[16,1024]{1,0:T(8,128)(2,1)S(1)}, u32[]{:S(2)}, u32[]{:S(2)}) collective-permute-start(bf16[16,1024]{1,0:T(8,128)(2,1)S(1)} %get-tuple-element.50.g0), channel_id=1, source_target_pairs={{0,3},{1,0},{2,1},{3,2},{4,7},{5,4},{6,5},{7,6},{8,11},{9,8},{10,9... | collective-permute-start | bytes 98312 | tf_op jit(solution)/shard_map/ppermute | solution.py:181
  71.1 0.6 copy-start.8
  77.1 1.5 %collective-permute-start.17 = (f32[48,640]{1,0:T(8,128)}, f32[48,640]{1,0:T(8,128)S(1)}, u32[]{:S(2)}, u32[]{:S(2)}) collective-permute-start(f32[48,640]{1,0:T(8,128)} %get-tuple-element.39), channel_id=1, source_target_pairs={{0,4},{4,0},{8,12},{12,8},{16,20},{20,16},{24,28},{28,24},{32,36},... | collective-permute-start | bytes 368648 | tf_op jit(solution)/shard_map/ppermute | solution.py:186
  79.5 5.5 %collective-permute-start.18 = (f32[48,640]{1,0:T(8,128)S(1)}, f32[48,640]{1,0:T(8,128)S(1)}, u32[]{:S(2)}, u32[]{:S(2)}) collective-permute-start(f32[48,640]{1,0:T(8,128)S(1)} %add.56), channel_id=1, source_target_pairs={{0,8},{4,12},{8,0},{12,4},{16,24},{20,28},{24,16},{28,20},{32,40},... | collective-permute-start | bytes 368648 | tf_op jit(solution)/shard_map/ppermute | solution.py:186
  85.0 6.5 %collective-permute-start.19 = (f32[48,640]{1,0:T(8,128)S(1)}, f32[48,640]{1,0:T(8,128)S(1)}, u32[]{:S(2)}, u32[]{:S(2)}) collective-permute-start(f32[48,640]{1,0:T(8,128)S(1)} %add.57), channel_id=1, source_target_pairs={{0,16},{4,20},{8,24},{12,28},{16,0},{20,4},{24,8},{28,12},{32,48},... | collective-permute-start | bytes 368648 | tf_op jit(solution)/shard_map/ppermute | solution.py:186
  91.5 5.0 %collective-permute-start.20 = (f32[48,640]{1,0:T(8,128)S(1)}, f32[48,640]{1,0:T(8,128)S(1)}, u32[]{:S(2)}, u32[]{:S(2)}) collective-permute-start(f32[48,640]{1,0:T(8,128)S(1)} %add.58), channel_id=1, source_target_pairs={{0,32},{4,36},{8,40},{12,44},{16,48},{20,52},{24,56},{28,60},{32,0... | collective-permute-start | bytes 368648 | tf_op jit(solution)/shard_map/ppermute | solution.py:186
  96.5 6.7 %collective-permute-start.21 = (f32[48,640]{1,0:T(8,128)S(1)}, f32[48,640]{1,0:T(8,128)S(1)}, u32[]{:S(2)}, u32[]{:S(2)}) collective-permute-start(f32[48,640]{1,0:T(8,128)S(1)} %add.59), channel_id=1, source_target_pairs={{0,64},{4,68},{8,72},{12,76},{16,80},{20,84},{24,88},{28,92},{32,9... | collective-permute-start | bytes 368648 | tf_op jit(solution)/shard_map/ppermute | solution.py:186
  103.2 9.7 %collective-permute-start.22 = (f32[48,640]{1,0:T(8,128)S(1)}, f32[48,640]{1,0:T(8,128)S(1)}, u32[]{:S(2)}, u32[]{:S(2)}) collective-permute-start(f32[48,640]{1,0:T(8,128)S(1)} %add.60), channel_id=1, source_target_pairs={{0,128},{4,132},{8,136},{12,140},{16,144},{20,148},{24,152},{28,15... | collective-permute-start | bytes 368648 | tf_op jit(solution)/shard_map/ppermute | solution.py:186
  (5 other events, 3.1 us)

commit v2 on v1

v2 whole, which is shorter than its diff:
```python
import jax
import jax.numpy as jnp
from jax import lax
from jax.experimental import pallas as pl
from jax.experimental.pallas import tpu as pltpu
from jax.sharding import PartitionSpec as P

BF = jnp.bfloat16
F32 = jnp.float32
LOW = 256
SLAB = 16
VMEM = pl.BlockSpec(memory_space=pltpu.VMEM)
SMEM = pl.BlockSpec(memory_space=pltpu.SMEM)
ROOMY = pltpu.CompilerParams(vmem_limit_bytes=40 * 2**20)


def dot(a, b, contract=((1,), (0,))):
    return lax.dot_general(a, b, (contract, ((), ())), preferred_element_type=F32)


NT = ((1,), (1,))
TN = ((0,), (0,))


def rank_picker(shape, slab_dim, group, group_count, width, sign):
    padded = lax.broadcasted_iota(jnp.int32, shape, slab_dim)
    rank = lax.broadcasted_iota(jnp.int32, shape, 1 - slab_dim)
    step = padded // SLAB
    lane = padded % SLAB
    slab = lax.rem(group + sign * step + group_count, group_count)
    hit = (rank == slab * width + lane) & (lane < width)
    return jnp.where(hit, 1.0, 0.0).astype(BF)


def project_kernel(place_ref, feat_ref, in_ref, cot_ref, outf_ref, *payload_refs):
    group_count = len(payload_refs)
    rank = in_ref.shape[1]
    width = rank // group_count
    pick = rank_picker((group_count * SLAB, rank), 0, place_ref[0], group_count, width, 1)
    weights = dot(pick, in_ref[...], NT).astype(BF)
    reduced = dot(weights, feat_ref[...])
    grad_mixed = dot(outf_ref[...], cot_ref[...])
    for j in range(group_count):
        payload_refs[j][0:SLAB, :] = reduced[j * SLAB : (j + 1) * SLAB].astype(payload_refs[j].dtype)
        payload_refs[j][SLAB:, :] = grad_mixed.astype(payload_refs[j].dtype)


def low_onehot(low):
    shape = (LOW, low.shape[1])
    want = jnp.broadcast_to(low.astype(F32), shape).astype(BF)
    have = lax.broadcasted_iota(jnp.int32, shape, 0).astype(F32).astype(BF)
    return jnp.where(have == want, jnp.ones((), BF), jnp.zeros((), BF))


def first_octant(halo_ref, slot):
    return jnp.clip(halo_ref[slot, 0] & 15, 0, 8) * 64


def mirrored(core, view, near):
    return jnp.where(core == 0, view, near - 1 - view)


def scatter_kernel(place_ref, halo_ref, p0, p1, p2, p3, core_ref, nbr_ref, gm_ref, own_ref, kept_ref,
                   cross_ref, terms_ref, acc_ref):
    rows = nbr_ref.shape[1]
    tiles = acc_ref.shape[0] // SLAB
    total = (p0[SLAB:, :] + p1[SLAB:, :].astype(F32)) + (
        p2[SLAB:, :].astype(F32) + p3[SLAB:, :].astype(F32)
    )
    grad_mixed = total.astype(BF)
    gm_ref[...] = grad_mixed
    terms_ref[...] = dot(core_ref[...], grad_mixed).astype(BF)
    acc_ref[...] = jnp.zeros_like(acc_ref)

    def step(k, carry):
        index = nbr_ref[pl.ds(k, 1), :]
        onehot = low_onehot(index & (LOW - 1))
        high = jnp.broadcast_to((index >> 8).astype(F32), (SLAB, rows)).astype(BF)
        terms = terms_ref[pl.ds(pl.multiple_of(k * SLAB, SLAB), SLAB), :]
        spread = jnp.concatenate(
            [jnp.where(high == jnp.full((), t, BF), terms, jnp.zeros((), BF)) for t in range(tiles)], 0
        )
        acc_ref[...] += dot(spread, onehot, NT)
        return carry

    lax.fori_loop(0, nbr_ref.shape[0], step, 0, unroll=9)

    def tile(t):
        return acc_ref[pl.ds(pl.multiple_of(t * SLAB, SLAB), SLAB), :]

    own_tiles = rows // LOW
    own_ref[...] = jnp.concatenate([tile(t) for t in range(own_tiles)], 1)
    near = halo_ref.shape[0]
    per_peer = (tiles - own_tiles) // near
    blank = jnp.zeros((SLAB, rows - per_peer * LOW), F32)
    for view in range(near):
        slot = mirrored(place_ref[1], view, near)
        start = own_tiles + slot * per_peer
        window = jnp.concatenate([tile(start + i) for i in range(per_peer)] + [blank], 1)
        block = pltpu.roll(window, first_octant(halo_ref, slot), 1)
        if view < 4:
            kept_ref[view * SLAB : (view + 1) * SLAB, :] = block
        else:
            cross_ref[(view - 4) * SLAB : (view - 3) * SLAB, :] = block.astype(BF)


def gather_kernel(place_ref, halo_ref, own_ref, pair_ref, near_ref, far_ref, cross_ref, gm_ref, core_ref,
                  nbr_ref, mix_ref, gc_ref, table_ref, ga_ref):
    rows = nbr_ref.shape[1]
    tiles = table_ref.shape[0] // SLAB
    own_tiles = rows // LOW
    near = halo_ref.shape[0]
    per_peer = (tiles - own_tiles) // near
    for t in range(own_tiles):
        table_ref[t * SLAB : (t + 1) * SLAB, :] = own_ref[:, t * LOW : (t + 1) * LOW]
    views = (
        far_ref[0:SLAB, :],
        far_ref[SLAB:, :],
        near_ref[0:SLAB, :],
        near_ref[SLAB:, :],
        pair_ref[...],
        cross_ref[SLAB : 2 * SLAB, :],
        cross_ref[0:SLAB, :],
        cross_ref[3 * SLAB :, :],
    )
    for view in range(near):
        slot = mirrored(place_ref[1], view, near)
        window = pltpu.roll(views[view].astype(F32), rows - first_octant(halo_ref, slot), 1).astype(BF)
        for i in range(per_peer):
            t = own_tiles + slot * per_peer + i
            table_ref[pl.ds(pl.multiple_of(t * SLAB, SLAB), SLAB), :] = window[:, i * LOW : (i + 1) * LOW]

    def step(k, carry):
        index = nbr_ref[pl.ds(k, 1), :]
        onehot = low_onehot(index & (LOW - 1))
        high = jnp.broadcast_to(index >> 8, (SLAB, rows))
        picked = dot(table_ref[...], onehot)
        found = jnp.zeros((SLAB, rows), F32)
        for t in range(tiles):
            found = jnp.where(high == t, picked[t * SLAB : (t + 1) * SLAB], found)
        ga_ref[pl.ds(pl.multiple_of(k * SLAB, SLAB), SLAB), :] = found.astype(BF)
        return carry

    lax.fori_loop(0, nbr_ref.shape[0], step, 0, unroll=9)
    gathered = ga_ref[...]
    mix_ref[...] = dot(core_ref[...], gathered, TN)
    gc_ref[...] = dot(gm_ref[...], gathered, NT)


def finish_kernel(place_ref, mix_ref, e0, e1, e2, e3, in_ref, feat_ref, outf_ref, cot_ref, gc_ref,
                  gf_ref, out_ref, packed_ref):
    rank = in_ref.shape[1]
    rows = feat_ref.shape[1]
    pick = rank_picker((rank, 4 * SLAB), 1, place_ref[0], 4, rank // 4, -1)
    slabs = jnp.concatenate([e[0:SLAB, :] for e in (e0, e1, e2, e3)], 0)
    grad_rows = dot(pick, slabs).astype(BF)
    gf_ref[...] = dot(in_ref[...], grad_rows).astype(BF)
    total = (mix_ref[...] + e1[SLAB:, :].astype(F32)) + (e2[SLAB:, :].astype(F32) + e3[SLAB:, :].astype(F32))
    mixed = total.astype(BF)
    out_ref[...] = dot(outf_ref[...], mixed, TN).astype(BF)
    wide = gc_ref.shape[1]
    right = jnp.concatenate([cot_ref[...], jnp.zeros((80, rows), BF)], 0)
    left = jnp.concatenate([jnp.zeros((64, rows), BF), grad_rows, jnp.zeros((16, rows), BF)], 0)
    packed_ref[:, 0:128] = dot(mixed, right, NT) + dot(feat_ref[...], left, NT)
    packed_ref[:, 128 : 128 + wide] = gc_ref[...]
    packed_ref[:, 128 + wide :] = jnp.zeros_like(packed_ref[:, 128 + wide :])


def unpack_kernel(factor, packed_ref, left_ref, core_ref, right_ref, flat_ref):
    tail = packed_ref[:, 0:128] * factor
    right_ref[...] = tail[:, 0:48]
    left_ref[...] = tail[:, 64:112]
    flat_ref[...] = (packed_ref[:, 128:] * factor).T
    width, offsets, rank = core_ref.shape
    for c in range(width):
        core_ref[c] = flat_ref[pl.ds(c, offsets, stride=SLAB), :]


def shifted(block, axis, distance):
    count = lax.axis_size(axis)
    return lax.ppermute(block, axis, [(i, (i + distance) % count) for i in range(count)])


def crossed(block, mask):
    return lax.ppermute(block, "leaf", [(i, i ^ mask) for i in range(lax.axis_size("leaf"))])


def outward(block, chips):
    count = lax.axis_size("leaf")
    return lax.ppermute(
        block, "leaf", [(i, (i + (2 * chips if i % 2 == 0 else -2 * chips)) % count) for i in range(count)]
    )


def leaf_sum(total, core):
    half = total.shape[0] // 2
    low, high = total[:half], total[half:]
    mine = jnp.where(core == 0, low, high) + crossed(jnp.where(core == 0, high, low), 1)
    for masks in ((8,), (2, 4, 6), (16, 32, 48)):
        mine = mine + sum(crossed(mine, mask) for mask in masks)
    other = crossed(mine, 1)
    return jnp.concatenate([jnp.where(core == 0, mine, other), jnp.where(core == 0, other, mine)], 0)


def struct(shape, dtype):
    return jax.ShapeDtypeStruct(shape, dtype)


def body(features, in_factor, core, out_factor, neighbours, halo_blocks, row_mask, cotangent):
    channels, rows = features.shape
    offsets, width, rank = core.shape
    near, slots = halo_blocks.shape[1:]
    table_rows = (rows + near * slots * 64) // LOW * SLAB
    core_bit = lax.axis_index("leaf") % 2
    place = jnp.stack([lax.axis_index("chan"), core_bit]).astype(jnp.int32)
    keep = row_mask.astype(F32).reshape(1, rows)
    halo = halo_blocks[0]
    core_rows = jnp.pad(core, ((0, 0), (0, SLAB - width), (0, 0))).reshape(offsets * SLAB, rank)
    estimate = pl.CostEstimate(flops=5 * 10**9, bytes_accessed=2**20, transcendentals=0)

    payload = pl.pallas_call(
        project_kernel,
        out_shape=[struct((SLAB + rank, rows), F32)] + [struct((SLAB + rank, rows), BF)] * 3,
        in_specs=[SMEM] + [VMEM] * 4,
        out_specs=[VMEM] * 4,
        name="project",
    )(place, features, in_factor, cotangent, out_factor)
    parts = [payload[0]] + [shifted(payload[j], "chan", j) for j in (1, 2, 3)]
    reduced = sum(part[:SLAB].astype(F32) for part in parts) * keep
    reduced = reduced.astype(BF)

    pair = crossed(reduced, 1)
    both, parts = lax.optimization_barrier((jnp.concatenate([reduced, pair], 0), parts))
    near_pair = outward(both, 1)
    far_pair = outward(both, 2)

    grad_mixed, own, kept, cross = pl.pallas_call(
        scatter_kernel,
        out_shape=[
            struct((rank, rows), BF),
            struct((SLAB, rows), F32),
            struct((4 * SLAB, rows), F32),
            struct((4 * SLAB, rows), BF),
        ],
        in_specs=[SMEM] * 2 + [VMEM] * 6,
        out_specs=[VMEM] * 4,
        scratch_shapes=[pltpu.VMEM((offsets * SLAB, rows), BF), pltpu.VMEM((table_rows, LOW), F32)],
        compiler_params=ROOMY,
        cost_estimate=estimate,
        name="scatter",
    )(place, halo, *parts, core_rows, neighbours)

    beyond = crossed(jnp.concatenate([near_pair, far_pair], 0), 1)
    handed = crossed(cross, 1).astype(F32)
    own = own + handed[:SLAB]
    to_near = jnp.concatenate(
        [kept[2 * SLAB : 3 * SLAB] + handed[2 * SLAB : 3 * SLAB], kept[3 * SLAB :] + handed[SLAB : 2 * SLAB]], 0
    ).astype(BF)
    to_far = jnp.concatenate([kept[:SLAB], kept[SLAB : 2 * SLAB] + handed[3 * SLAB :]], 0).astype(BF)
    beyond, to_near, to_far = lax.optimization_barrier((beyond, to_near, to_far))
    from_near = outward(to_near, -1).astype(F32)
    from_far = outward(to_far, -2).astype(F32)

    mixed_part, grad_core = pl.pallas_call(
        gather_kernel,
        out_shape=[struct((rank, rows), F32), struct((rank, offsets * SLAB), F32)],
        in_specs=[SMEM] * 2 + [VMEM] * 8,
        out_specs=[VMEM] * 2,
        scratch_shapes=[pltpu.VMEM((table_rows, LOW), BF), pltpu.VMEM((offsets * SLAB, rows), BF)],
        compiler_params=ROOMY,
        cost_estimate=estimate,
        name="gather",
    )(place, halo, reduced, pair, near_pair, far_pair, beyond, grad_mixed, core_rows, neighbours)

    returned = from_near + from_far
    last = crossed(returned[SLAB:].astype(BF), 1).astype(F32)
    grad_slab = ((own + returned[:SLAB] + last) * keep).astype(BF)
    shared = jnp.concatenate([grad_slab, mixed_part.astype(BF)], 0)
    exchanged = [shared] + [shifted(shared, "chan", j) for j in (1, 2, 3)]

    packed_width = 128 + (offsets * SLAB + 127) // 128 * 128
    grad_features, output, packed = pl.pallas_call(
        finish_kernel,
        out_shape=[struct((channels, rows), BF)] * 2 + [struct((rank, packed_width), F32)],
        in_specs=[SMEM] + [VMEM] * 10,
        out_specs=[VMEM] * 3,
        name="finish",
    )(place, mixed_part, *exchanged, in_factor, features, out_factor, cotangent, grad_core)
    packed = leaf_sum(packed, core_bit)

    factor = float(rows * lax.axis_size("leaf")) ** (-0.5)
    grad_in, grad_core, grad_out = pl.pallas_call(
        lambda *refs: unpack_kernel(factor, *refs),
        out_shape=[struct((channels, rank), F32), struct((width, offsets, rank), F32), struct((rank, channels), F32)],
        in_specs=[VMEM],
        out_specs=[VMEM] * 3,
        scratch_shapes=[pltpu.VMEM((packed_width - 128, rank), F32)],
        name="unpack",
    )(packed)
    return (output, grad_features, grad_in, jnp.transpose(grad_core, (1, 0, 2)), grad_out)


def solution(mesh):
    placed = (
        P("chan", "leaf"),
        P("chan", None),
        P(None, "chan", None),
        P(None, "chan"),
        P(None, "leaf"),
        P("leaf", None, None),
        P("leaf"),
        P("chan", "leaf"),
    )
    return jax.shard_map(
        body,
        mesh=mesh,
        in_specs=placed,
        out_specs=(
            P("chan", "leaf"),
            P("chan", "leaf"),
            P("chan", None),
            P(None, "chan", None),
            P(None, "chan"),
        ),
        check_vma=False,
    )
```

time: 117 us -> 95 us (0.81)
  the two profiles are of different devices: /device:TPU:2 before, /device:TPU:1 now
where the time goes in v2:
time: 95 us; the launch traced here: 94.8 us
  starting transfers between devices  36.5 us (38%)
  waiting for transfers between devices  33.1 us (35%)
  Pallas kernels  19 us (20%)
  other arithmetic  3.27 us (3%)
  local copies, waits for them, and re-layouts  2.01 us (2%)
    ppermute x13, starting transfers between devices, crossed(): lax.ppermute(block, 'leaf', [(i, i ^ mask) for i in range(lax.axis_size('...  17.4 us
    ppermute x13, waiting for transfers between devices, crossed(): lax.ppermute(block, 'leaf', [(i, i ^ mask) for i in range(lax.axis_size('...  13.9 us
    ppermute x6, waiting for transfers between devices, shifted(): lax.ppermute(block, axis, [(i, (i + distance) % count) for i in range(cou...  13.1 us
    ppermute x4, starting transfers between devices, outward(): lax.ppermute(block, 'leaf', [(i, (i + (2 * chips if i % 2 == 0 else -2 *...  9.9 us
    ppermute x6, starting transfers between devices, shifted(): lax.ppermute(block, axis, [(i, (i + distance) % count) for i in range(cou...  9.22 us
    pallas_call x1, Pallas kernels, body(): pl.pallas_call(gather_kernel, out_shape=[struct((rank, rows), F32), struc...  6.42 us
    pallas_call x1, Pallas kernels, body(): pl.pallas_call(scatter_kernel, out_shape=[struct((rank, rows), BF), struc...  6.33 us
    ppermute x4, waiting for transfers between devices, outward(): lax.ppermute(block, 'leaf', [(i, (i + (2 * chips if i % 2 == 0 else -2 *...  6.1 us
  transfers between devices with their start and end apart: 23, of which 18 were waited for; matrix products, arithmetic and copies ran while one was open for 0% of the time, Pallas kernels for 13%

profile of v2, /device:TPU:1, one launch (start us, length us, event | category | flops | bytes accessed | tf_op | source)
XLA Modules:
  0.0 94.8 jit_solution(12592211809498666913)
XLA Ops:
  1.2 2.1 %project.1 = (f32[64,1024]{1,0:T(8,128)}, bf16[64,1024]{1,0:T(8,128)(2,1)}, bf16[64,1024]{1,0:T(8,128)(2,1)}, bf16[64,1024]{1,0:T(8,128)(2,1)}) custom-call(s32[2]{0:T(128)} %pad_add_fusion.place_ref, bf16[48,1024]{1,0:T(8,128)(2,1)} %feat_ref.3, bf16[48,48]{1,0:T(8,128)(2,1)} %in_ref.3, bf16[48,1024]{1,0:T(8,128)(2,1)} %cot_ref.3, bf16[48,48]{1,0:T(8,128)(2,1)} %outf_ref.3), custom_call_target="tpu_custom_call" | custom-call | tf_op jit(solution)/shard_map/project/pallas_call | solution.py:221
  3.4 2.1 %collective-permute-start = (bf16[64,1024]{1,0:T(8,128)(2,1)}, bf16[64,1024]{1,0:T(8,128)(2,1)S(1)}, u32[]{:S(2)}, u32[]{:S(2)}) collective-permute-start(bf16[64,1024]{1,0:T(8,128)(2,1)} %get-tuple-element.30), channel_id=1, source_target_pairs={{0,1},{1,2},{2,3},{3,0},{4,5},{5,6},{6,7},{7,4},{8,9},{9,10},{10,1... | collective-permute-start | bytes 393224 | tf_op jit(solution)/shard_map/ppermute | solution.py:181
  5.5 2.6 %collective-permute-start.1 = (bf16[64,1024]{1,0:T(8,128)(2,1)}, bf16[64,1024]{1,0:T(8,128)(2,1)S(1)}, u32[]{:S(2)}, u32[]{:S(2)}) collective-permute-start(bf16[64,1024]{1,0:T(8,128)(2,1)} %get-tuple-element.31), channel_id=1, source_target_pairs={{0,2},{1,3},{2,0},{3,1},{4,6},{5,7},{6,4},{7,5},{8,10},{9,11},{10,... | collective-permute-start | bytes 393224 | tf_op jit(solution)/shard_map/ppermute | solution.py:181
  8.1 1.1 %collective-permute-start.2 = (bf16[64,1024]{1,0:T(8,128)(2,1)}, bf16[64,1024]{1,0:T(8,128)(2,1)S(1)}, u32[]{:S(2)}, u32[]{:S(2)}) collective-permute-start(bf16[64,1024]{1,0:T(8,128)(2,1)} %get-tuple-element.32), channel_id=1, source_target_pairs={{0,3},{1,0},{2,1},{3,2},{4,7},{5,4},{6,5},{7,6},{8,11},{9,8},{10,9... | collective-permute-start | bytes 393224 | tf_op jit(solution)/shard_map/ppermute | solution.py:181
  9.5 4.5 %collective-permute-done.1.p2 = bf16[64,1024]{1,0:T(8,128)(2,1)S(1)} collective-permute-done((bf16[64,1024]{1,0:T(8,128)(2,1)}, bf16[64,1024]{1,0:T(8,128)(2,1)S(1)}, u32[]{:S(2)}, u32[]{:S(2)}) %collective-permute-start.1) | collective-permute-done | bytes 131104 | tf_op jit(solution)/shard_map/ppermute | solution.py:181
  14.0 0.9 multiply_convert_fusion.own_ref
  14.9 1.9 %collective-permute-start.3 = (bf16[16,1024]{1,0:T(8,128)(2,1)S(1)}, bf16[16,1024]{1,0:T(8,128)(2,1)S(1)}, u32[]{:S(2)}, u32[]{:S(2)}) collective-permute-start(bf16[16,1024]{1,0:T(8,128)(2,1)S(1)} %multiply_convert_fusion.own_ref), channel_id=1, source_target_pairs={{0,4},{4,0},{8,12},{12,8},{16,20},{20,16},{24,28},{28,24},{32,36},... | collective-permute-start | bytes 98312 | tf_op jit(solution)/shard_map/ppermute | solution.py:185
  17.7 7.8 %collective-permute-start.5 = (bf16[32,1024]{1,0:T(8,128)(2,1)S(1)}, bf16[32,1024]{1,0:T(8,128)(2,1)S(1)}, u32[]{:S(2)}, u32[]{:S(2)}) collective-permute-start(bf16[32,1024]{1,0:T(8,128)(2,1)S(1)} %pad_maximum_fusion.3), channel_id=1, source_target_pairs={{0,16},{4,244},{8,24},{12,252},{16,32},{20,4},{24,40},{28,12},{32,... | collective-permute-start | bytes 196616 | tf_op jit(solution)/shard_map/ppermute | solution.py:190
  27.0 6.3 %scatter.1 = (bf16[48,1024]{1,0:T(8,128)(2,1)S(1)}, f32[16,1024]{1,0:T(8,128)S(1)}, f32[64,1024]{1,0:T(8,128)S(1)}, bf16[64,1024]{1,0:T(8,128)(2,1)S(1)}) custom-call(s32[2]{0:T(128)S(1)} %copy-done.3, s32[8,8]{1,0:T(8,128)S(1)} %bitcast.7, f32[64,1024]{1,0:T(8,128)S(1)} %copy-done.2, bf16[64,1024]{1,0:T(8,128)(2,1)S(1)} %collective-permute-done.p1, ...), custom_call_target="tpu_custom_call" | custom-call | flops 5000000000 | bytes 1048576 | tf_op jit(solution)/shard_map/scatter/pallas_call | solution.py:237
  36.3 5.2 %collective-permute-done.8 = bf16[32,1024]{1,0:T(8,128)(2,1)S(1)} collective-permute-done((bf16[32,1024]{1,0:T(8,128)(2,1)S(1)}, bf16[32,1024]{1,0:T(8,128)(2,1)S(1)}, u32[]{:S(2)}, u32[]{:S(2)}) %collective-permute-start.8) | collective-permute-done | bytes 65568 | tf_op jit(solution)/shard_map/ppermute | solution.py:190
  41.5 0.9 collective-permute-done.9
  42.5 6.4 %gather.1 = (f32[48,1024]{1,0:T(8,128)S(1)}, f32[48,432]{1,0:T(8,128)S(1)}) custom-call(s32[2]{0:T(128)S(1)} %copy-done.3, s32[8,8]{1,0:T(8,128)S(1)} %bitcast.8, bf16[16,1024]{1,0:T(8,128)(2,1)S(1)} %multiply_convert_fusion.own_ref, bf16[16,1024]{1,0:T(8,128)(2,1)S(1)} %collective-permute-done.3.pair_ref, ...), custom_call_target="tpu_custom_call" | custom-call | flops 5000000000 | bytes 1048576 | tf_op jit(solution)/shard_map/gather/pallas_call | solution.py:264
  49.6 2.1 %collective-permute-start.13 = (bf16[64,1024]{1,0:T(8,128)(2,1)S(1)}, bf16[64,1024]{1,0:T(8,128)(2,1)S(1)}, u32[]{:S(2)}, u32[]{:S(2)}) collective-permute-start(bf16[64,1024]{1,0:T(8,128)(2,1)S(1)} %pad_maximum_fusion.1.e0), channel_id=1, source_target_pairs={{0,3},{1,0},{2,1},{3,2},{4,7},{5,4},{6,5},{7,6},{8,11},{9,8},{10,9... | collective-permute-start | bytes 393224 | tf_op jit(solution)/shard_map/ppermute | solution.py:181
  51.8 0.9 collective-permute-start.12
  53.0 1.4 %collective-permute-done.13.e3 = bf16[64,1024]{1,0:T(8,128)(2,1)S(1)} collective-permute-done((bf16[64,1024]{1,0:T(8,128)(2,1)S(1)}, bf16[64,1024]{1,0:T(8,128)(2,1)S(1)}, u32[]{:S(2)}, u32[]{:S(2)}) %collective-permute-start.13) | collective-permute-done | bytes 131104 | tf_op jit(solution)/shard_map/ppermute | solution.py:181
  54.5 3.0 %collective-permute-done.12.e2 = bf16[64,1024]{1,0:T(8,128)(2,1)S(1)} collective-permute-done((bf16[64,1024]{1,0:T(8,128)(2,1)S(1)}, bf16[64,1024]{1,0:T(8,128)(2,1)S(1)}, u32[]{:S(2)}, u32[]{:S(2)}) %collective-permute-start.12) | collective-permute-done | bytes 131104 | tf_op jit(solution)/shard_map/ppermute | solution.py:181
  57.5 3.8 %collective-permute-done.11.e1 = bf16[64,1024]{1,0:T(8,128)(2,1)S(1)} collective-permute-done((bf16[64,1024]{1,0:T(8,128)(2,1)S(1)}, bf16[64,1024]{1,0:T(8,128)(2,1)S(1)}, u32[]{:S(2)}, u32[]{:S(2)}) %collective-permute-start.11) | collective-permute-done | bytes 131104 | tf_op jit(solution)/shard_map/ppermute | solution.py:181
  62.0 2.4 %finish.1 = (bf16[48,1024]{1,0:T(8,128)(2,1)}, bf16[48,1024]{1,0:T(8,128)(2,1)}, f32[48,640]{1,0:T(8,128)}) custom-call(s32[2]{0:T(128)} %pad_add_fusion.place_ref, f32[48,1024]{1,0:T(8,128)} %copy-done, bf16[64,1024]{1,0:T(8,128)(2,1)} %copy-done.6, bf16[64,1024]{1,0:T(8,128)(2,1)} %copy-done.10, bf16[64,1024]{1,0:T(8,128)(2,1)} %copy-done.9, ...), custom_call_target="tpu_custom_call" | custom-call | tf_op jit(solution)/shard_map/finish/pallas_call | solution.py:282
  64.4 0.9 slice_select_fusion
  66.0 0.9 collective-permute-done.14
  67.1 3.1 %collective-permute-done.15 = f32[24,640]{1,0:T(8,128)S(1)} collective-permute-done((f32[24,640]{1,0:T(8,128)S(1)}, f32[24,640]{1,0:T(8,128)S(1)}, u32[]{:S(2)}, u32[]{:S(2)}) %collective-permute-start.15) | collective-permute-done | bytes 61472 | tf_op jit(solution)/shard_map/ppermute | solution.py:185
  70.1 1.6 %collective-permute-start.18 = (f32[24,640]{1,0:T(8,128)S(1)}, f32[24,640]{1,0:T(8,128)S(1)}, u32[]{:S(2)}, u32[]{:S(2)}) collective-permute-start(f32[24,640]{1,0:T(8,128)S(1)} %add.72), channel_id=1, source_target_pairs={{0,24},{4,28},{8,16},{12,20},{16,8},{20,12},{24,0},{28,4},{32,56},... | collective-permute-start | bytes 184328 | tf_op jit(solution)/shard_map/ppermute | solution.py:185
  71.7 1.5 %collective-permute-start.17 = (f32[24,640]{1,0:T(8,128)S(1)}, f32[24,640]{1,0:T(8,128)S(1)}, u32[]{:S(2)}, u32[]{:S(2)}) collective-permute-start(f32[24,640]{1,0:T(8,128)S(1)} %add.72), channel_id=1, source_target_pairs={{0,16},{4,20},{8,24},{12,28},{16,0},{20,4},{24,8},{28,12},{32,48},... | collective-permute-start | bytes 184328 | tf_op jit(solution)/shard_map/ppermute | solution.py:185
  73.5 1.0 %collective-permute-done.18 = f32[24,640]{1,0:T(8,128)S(1)} collective-permute-done((f32[24,640]{1,0:T(8,128)S(1)}, f32[24,640]{1,0:T(8,128)S(1)}, u32[]{:S(2)}, u32[]{:S(2)}) %collective-permute-start.18) | collective-permute-done | bytes 61472 | tf_op jit(solution)/shard_map/ppermute | solution.py:185
  74.5 1.8 %collective-permute-done.17 = f32[24,640]{1,0:T(8,128)S(1)} collective-permute-done((f32[24,640]{1,0:T(8,128)S(1)}, f32[24,640]{1,0:T(8,128)S(1)}, u32[]{:S(2)}, u32[]{:S(2)}) %collective-permute-start.17) | collective-permute-done | bytes 61472 | tf_op jit(solution)/shard_map/ppermute | solution.py:185
  76.6 2.3 %collective-permute-start.21 = (f32[24,640]{1,0:T(8,128)S(1)}, f32[24,640]{1,0:T(8,128)S(1)}, u32[]{:S(2)}, u32[]{:S(2)}) collective-permute-start(f32[24,640]{1,0:T(8,128)S(1)} %add_add_fusion.1), channel_id=1, source_target_pairs={{0,192},{4,196},{8,200},{12,204},{16,208},{20,212},{24,216},{28,22... | collective-permute-start | bytes 184328 | tf_op jit(solution)/shard_map/ppermute | solution.py:185
  78.9 3.9 %collective-permute-start.20 = (f32[24,640]{1,0:T(8,128)S(1)}, f32[24,640]{1,0:T(8,128)S(1)}, u32[]{:S(2)}, u32[]{:S(2)}) collective-permute-start(f32[24,640]{1,0:T(8,128)S(1)} %add_add_fusion.1), channel_id=1, source_target_pairs={{0,128},{4,132},{8,136},{12,140},{16,144},{20,148},{24,152},{28,15... | collective-permute-start | bytes 184328 | tf_op jit(solution)/shard_map/ppermute | solution.py:185
  82.8 3.3 %collective-permute-done.20 = f32[24,640]{1,0:T(8,128)S(1)} collective-permute-done((f32[24,640]{1,0:T(8,128)S(1)}, f32[24,640]{1,0:T(8,128)S(1)}, u32[]{:S(2)}, u32[]{:S(2)}) %collective-permute-start.20) | collective-permute-done | bytes 61472 | tf_op jit(solution)/shard_map/ppermute | solution.py:185
  86.0 1.0 %collective-permute-done.19 = f32[24,640]{1,0:T(8,128)S(1)} collective-permute-done((f32[24,640]{1,0:T(8,128)S(1)}, f32[24,640]{1,0:T(8,128)S(1)}, u32[]{:S(2)}, u32[]{:S(2)}) %collective-permute-start.19) | collective-permute-done | bytes 61472 | tf_op jit(solution)/shard_map/ppermute | solution.py:185
  87.0 4.4 %collective-permute-start.22 = (f32[24,640]{1,0:T(8,128)S(1)}, f32[24,640]{1,0:T(8,128)S(1)}, u32[]{:S(2)}, u32[]{:S(2)}) collective-permute-start(f32[24,640]{1,0:T(8,128)S(1)} %add_add_fusion), channel_id=1, source_target_pairs={{0,4},{4,0},{8,12},{12,8},{16,20},{20,16},{24,28},{28,24},{32,36},... | collective-permute-start | bytes 184328 | tf_op jit(solution)/shard_map/ppermute | solution.py:185
  91.4 0.9 collective-permute-done.22
  93.0 1.8 %unpack.1 = (f32[48,48]{1,0:T(8,128)}, f32[12,27,48]{2,1,0:T(8,128)}, f32[48,48]{1,0:T(8,128)}) custom-call(f32[48,640]{1,0:T(8,128)} %pad_maximum_fusion.2.refs_0_), custom_call_target="tpu_custom_call" | custom-call | tf_op jit(solution)/shard_map/unpack/pallas_call | solution.py:292
  (68 shorter events, 10.1 us)
Async XLA Ops:
  3.4 5.8 %copy-start.12 = (s32[1024]{0:T(1024)S(1)}, s32[1024]{0:T(1024)}, u32[]{:S(2)}) copy-start(s32[1024]{0:T(1024)} %param.14) | copy-start | bytes 12292
  3.4 6.1 %collective-permute-start = (bf16[64,1024]{1,0:T(8,128)(2,1)}, bf16[64,1024]{1,0:T(8,128)(2,1)S(1)}, u32[]{:S(2)}, u32[]{:S(2)}) collective-permute-start(bf16[64,1024]{1,0:T(8,128)(2,1)} %get-tuple-element.30), channel_id=1, source_target_pairs={{0,1},{1,2},{2,3},{3,0},{4,5},{5,6},{6,7},{7,4},{8,9},{9,10},{10,1... | collective-permute-start | bytes 393224 | tf_op jit(solution)/shard_map/ppermute | solution.py:181
  5.5 8.5 %collective-permute-start.1 = (bf16[64,1024]{1,0:T(8,128)(2,1)}, bf16[64,1024]{1,0:T(8,128)(2,1)S(1)}, u32[]{:S(2)}, u32[]{:S(2)}) collective-permute-start(bf16[64,1024]{1,0:T(8,128)(2,1)} %get-tuple-element.31), channel_id=1, source_target_pairs={{0,2},{1,3},{2,0},{3,1},{4,6},{5,7},{6,4},{7,5},{8,10},{9,11},{10,... | collective-permute-start | bytes 393224 | tf_op jit(solution)/shard_map/ppermute | solution.py:181
  8.1 5.9 %collective-permute-start.2 = (bf16[64,1024]{1,0:T(8,128)(2,1)}, bf16[64,1024]{1,0:T(8,128)(2,1)S(1)}, u32[]{:S(2)}, u32[]{:S(2)}) collective-permute-start(bf16[64,1024]{1,0:T(8,128)(2,1)} %get-tuple-element.32), channel_id=1, source_target_pairs={{0,3},{1,0},{2,1},{3,2},{4,7},{5,4},{6,5},{7,6},{8,11},{9,8},{10,9... | collective-permute-start | bytes 393224 | tf_op jit(solution)/shard_map/ppermute | solution.py:181
  14.0 2.8 %copy-start.11 = (bf16[27,12,48]{2,0,1:T(8,128)(2,1)S(1)}, bf16[27,12,48]{2,0,1:T(8,128)(2,1)}, u32[]{:S(2)}) copy-start(bf16[27,12,48]{2,0,1:T(8,128)(2,1)} %param.10) | copy-start | bytes 93316
  14.9 11.4 %copy-start.2 = (f32[64,1024]{1,0:T(8,128)S(1)}, f32[64,1024]{1,0:T(8,128)}, u32[]{:S(2)}) copy-start(f32[64,1024]{1,0:T(8,128)} %get-tuple-element.34.p0) | copy-start | bytes 786436
  14.9 2.7 %collective-permute-start.3 = (bf16[16,1024]{1,0:T(8,128)(2,1)S(1)}, bf16[16,1024]{1,0:T(8,128)(2,1)S(1)}, u32[]{:S(2)}, u32[]{:S(2)}) collective-permute-start(bf16[16,1024]{1,0:T(8,128)(2,1)S(1)} %multiply_convert_fusion.own_ref), channel_id=1, source_target_pairs={{0,4},{4,0},{8,12},{12,8},{16,20},{20,16},{24,28},{28,24},{32,36},... | collective-permute-start | bytes 98312 | tf_op jit(solution)/shard_map/ppermute | solution.py:185
  16.9 9.5 %copy-start.4 = (s32[27,1024]{1,0:T(8,128)S(1)}, s32[27,1024]{1,0:T(8,128)}, u32[]{:S(2)}) copy-start(s32[27,1024]{1,0:T(8,128)} %nbr_ref.3) | copy-start | bytes 331780
  16.9 9.4 %copy-start.5 = (s32[1,8,8]{2,1,0:T(8,128)S(1)}, s32[1,8,8]{2,1,0:T(8,128)}, u32[]{:S(2)}) copy-start(s32[1,8,8]{2,1,0:T(8,128)} %param.13) | copy-start | bytes 772
  17.7 15.7 %collective-permute-start.5 = (bf16[32,1024]{1,0:T(8,128)(2,1)S(1)}, bf16[32,1024]{1,0:T(8,128)(2,1)S(1)}, u32[]{:S(2)}, u32[]{:S(2)}) collective-permute-start(bf16[32,1024]{1,0:T(8,128)(2,1)S(1)} %pad_maximum_fusion.3), channel_id=1, source_target_pairs={{0,16},{4,244},{8,24},{12,252},{16,32},{20,4},{24,40},{28,12},{32,... | collective-permute-start | bytes 196616 | tf_op jit(solution)/shard_map/ppermute | solution.py:190
  25.5 7.9 %collective-permute-start.4 = (bf16[32,1024]{1,0:T(8,128)(2,1)S(1)}, bf16[32,1024]{1,0:T(8,128)(2,1)S(1)}, u32[]{:S(2)}, u32[]{:S(2)}) collective-permute-start(bf16[32,1024]{1,0:T(8,128)(2,1)S(1)} %pad_maximum_fusion.3), channel_id=1, source_target_pairs={{0,8},{4,252},{8,16},{12,4},{16,24},{20,12},{24,32},{28,20},{32,40... | collective-permute-start | bytes 196616 | tf_op jit(solution)/shard_map/ppermute | solution.py:190
  33.3 1.4 %collective-permute-start.7 = (bf16[64,1024]{1,0:T(8,128)(2,1)S(1)}, bf16[64,1024]{1,0:T(8,128)(2,1)S(1)}, u32[]{:S(2)}, u32[]{:S(2)}) collective-permute-start(bf16[64,1024]{1,0:T(8,128)(2,1)S(1)} %get-tuple-element.39), channel_id=1, source_target_pairs={{0,4},{4,0},{8,12},{12,8},{16,20},{20,16},{24,28},{28,24},{32,36},... | collective-permute-start | bytes 393224 | tf_op jit(solution)/shard_map/ppermute | solution.py:185
  33.5 1.6 %collective-permute-start.6 = (bf16[64,1024]{1,0:T(8,128)(2,1)S(1)}, bf16[64,1024]{1,0:T(8,128)(2,1)S(1)}, u32[]{:S(2)}, u32[]{:S(2)}) collective-permute-start(bf16[64,1024]{1,0:T(8,128)(2,1)S(1)} %pad_maximum_fusion), channel_id=1, source_target_pairs={{0,4},{4,0},{8,12},{12,8},{16,20},{20,16},{24,28},{28,24},{32,36},... | collective-permute-start | bytes 393224 | tf_op jit(solution)/shard_map/ppermute | solution.py:185
  35.0 6.4 %collective-permute-start.8 = (bf16[32,1024]{1,0:T(8,128)(2,1)S(1)}, bf16[32,1024]{1,0:T(8,128)(2,1)S(1)}, u32[]{:S(2)}, u32[]{:S(2)}) collective-permute-start(bf16[32,1024]{1,0:T(8,128)(2,1)S(1)} %get-tuple-element.44), channel_id=1, source_target_pairs={{0,248},{4,12},{8,0},{12,20},{16,8},{20,28},{24,16},{28,36},{32,24... | collective-permute-start | bytes 196616 | tf_op jit(solution)/shard_map/ppermute | solution.py:190
  35.6 6.7 %collective-permute-start.9 = (bf16[32,1024]{1,0:T(8,128)(2,1)S(1)}, bf16[32,1024]{1,0:T(8,128)(2,1)S(1)}, u32[]{:S(2)}, u32[]{:S(2)}) collective-permute-start(bf16[32,1024]{1,0:T(8,128)(2,1)S(1)} %get-tuple-element.45), channel_id=1, source_target_pairs={{0,240},{4,20},{8,248},{12,28},{16,0},{20,36},{24,8},{28,44},{32,1... | collective-permute-start | bytes 196616 | tf_op jit(solution)/shard_map/ppermute | solution.py:190
  42.4 7.2 %collective-permute-start.10 = (bf16[16,1024]{1,0:T(8,128)(2,1)S(1)}, bf16[16,1024]{1,0:T(8,128)(2,1)S(1)}, u32[]{:S(2)}, u32[]{:S(2)}) collective-permute-start(bf16[16,1024]{1,0:T(8,128)(2,1)S(1)} %slice.108), channel_id=1, source_target_pairs={{0,4},{4,0},{8,12},{12,8},{16,20},{20,16},{24,28},{28,24},{32,36},... | collective-permute-start | bytes 98312 | tf_op jit(solution)/shard_map/ppermute | solution.py:185
  49.6 11.7 %copy-start.6 = (bf16[64,1024]{1,0:T(8,128)(2,1)}, bf16[64,1024]{1,0:T(8,128)(2,1)S(1)}, u32[]{:S(2)}) copy-start(bf16[64,1024]{1,0:T(8,128)(2,1)S(1)} %pad_maximum_fusion.1.e0) | copy-start | bytes 393220
  49.6 4.8 %collective-permute-start.13 = (bf16[64,1024]{1,0:T(8,128)(2,1)S(1)}, bf16[64,1024]{1,0:T(8,128)(2,1)S(1)}, u32[]{:S(2)}, u32[]{:S(2)}) collective-permute-start(bf16[64,1024]{1,0:T(8,128)(2,1)S(1)} %pad_maximum_fusion.1.e0), channel_id=1, source_target_pairs={{0,3},{1,0},{2,1},{3,2},{4,7},{5,4},{6,5},{7,6},{8,11},{9,8},{10,9... | collective-permute-start | bytes 393224 | tf_op jit(solution)/shard_map/ppermute | solution.py:181
  51.8 5.8 %collective-permute-start.12 = (bf16[64,1024]{1,0:T(8,128)(2,1)S(1)}, bf16[64,1024]{1,0:T(8,128)(2,1)S(1)}, u32[]{:S(2)}, u32[]{:S(2)}) collective-permute-start(bf16[64,1024]{1,0:T(8,128)(2,1)S(1)} %pad_maximum_fusion.1.e0), channel_id=1, source_target_pairs={{0,2},{1,3},{2,0},{3,1},{4,6},{5,7},{6,4},{7,5},{8,10},{9,11},{10,... | collective-permute-start | bytes 393224 | tf_op jit(solution)/shard_map/ppermute | solution.py:181
  52.6 8.7 %collective-permute-start.11 = (bf16[64,1024]{1,0:T(8,128)(2,1)S(1)}, bf16[64,1024]{1,0:T(8,128)(2,1)S(1)}, u32[]{:S(2)}, u32[]{:S(2)}) collective-permute-start(bf16[64,1024]{1,0:T(8,128)(2,1)S(1)} %pad_maximum_fusion.1.e0), channel_id=1, source_target_pairs={{0,1},{1,2},{2,3},{3,0},{4,5},{5,6},{6,7},{7,4},{8,9},{9,10},{10,1... | collective-permute-start | bytes 393224 | tf_op jit(solution)/shard_map/ppermute | solution.py:181
  54.5 6.8 %copy-start.8 = (bf16[64,1024]{1,0:T(8,128)(2,1)}, bf16[64,1024]{1,0:T(8,128)(2,1)S(1)}, u32[]{:S(2)}) copy-start(bf16[64,1024]{1,0:T(8,128)(2,1)S(1)} %collective-permute-done.13.e3) | copy-start | bytes 393220
  57.5 3.8 %copy-start.9 = (bf16[64,1024]{1,0:T(8,128)(2,1)}, bf16[64,1024]{1,0:T(8,128)(2,1)S(1)}, u32[]{:S(2)}) copy-start(bf16[64,1024]{1,0:T(8,128)(2,1)S(1)} %collective-permute-done.12.e2) | copy-start | bytes 393220
  64.4 2.6 %copy-start.7 = (f32[48,640]{1,0:T(8,128)S(1)}, f32[48,640]{1,0:T(8,128)}, u32[]{:S(2)}) copy-start(f32[48,640]{1,0:T(8,128)} %get-tuple-element.49) | copy-start | bytes 368644
  65.3 1.7 %collective-permute-start.14 = (f32[24,640]{1,0:T(8,128)S(1)}, f32[24,640]{1,0:T(8,128)S(1)}, u32[]{:S(2)}, u32[]{:S(2)}) collective-permute-start(f32[24,640]{1,0:T(8,128)S(1)} %slice_select_fusion), channel_id=1, source_target_pairs={{0,4},{4,0},{8,12},{12,8},{16,20},{20,16},{24,28},{28,24},{32,36},... | collective-permute-start | bytes 184328 | tf_op jit(solution)/shard_map/ppermute | solution.py:185
  67.0 3.2 %collective-permute-start.15 = (f32[24,640]{1,0:T(8,128)S(1)}, f32[24,640]{1,0:T(8,128)S(1)}, u32[]{:S(2)}, u32[]{:S(2)}) collective-permute-start(f32[24,640]{1,0:T(8,128)S(1)} %select_add_fusion), channel_id=1, source_target_pairs={{0,32},{4,36},{8,40},{12,44},{16,48},{20,52},{24,56},{28,60},{32,0... | collective-permute-start | bytes 184328 | tf_op jit(solution)/shard_map/ppermute | solution.py:185
  70.1 4.4 %collective-permute-start.18 = (f32[24,640]{1,0:T(8,128)S(1)}, f32[24,640]{1,0:T(8,128)S(1)}, u32[]{:S(2)}, u32[]{:S(2)}) collective-permute-start(f32[24,640]{1,0:T(8,128)S(1)} %add.72), channel_id=1, source_target_pairs={{0,24},{4,28},{8,16},{12,20},{16,8},{20,12},{24,0},{28,4},{32,56},... | collective-permute-start | bytes 184328 | tf_op jit(solution)/shard_map/ppermute | solution.py:185
  71.7 4.6 %collective-permute-start.17 = (f32[24,640]{1,0:T(8,128)S(1)}, f32[24,640]{1,0:T(8,128)S(1)}, u32[]{:S(2)}, u32[]{:S(2)}) collective-permute-start(f32[24,640]{1,0:T(8,128)S(1)} %add.72), channel_id=1, source_target_pairs={{0,16},{4,20},{8,24},{12,28},{16,0},{20,4},{24,8},{28,12},{32,48},... | collective-permute-start | bytes 184328 | tf_op jit(solution)/shard_map/ppermute | solution.py:185
  73.2 3.4 %collective-permute-start.16 = (f32[24,640]{1,0:T(8,128)S(1)}, f32[24,640]{1,0:T(8,128)S(1)}, u32[]{:S(2)}, u32[]{:S(2)}) collective-permute-start(f32[24,640]{1,0:T(8,128)S(1)} %add.72), channel_id=1, source_target_pairs={{0,8},{4,12},{8,0},{12,4},{16,24},{20,28},{24,16},{28,20},{32,40},... | collective-permute-start | bytes 184328 | tf_op jit(solution)/shard_map/ppermute | solution.py:185
  76.6 6.2 %collective-permute-start.21 = (f32[24,640]{1,0:T(8,128)S(1)}, f32[24,640]{1,0:T(8,128)S(1)}, u32[]{:S(2)}, u32[]{:S(2)}) collective-permute-start(f32[24,640]{1,0:T(8,128)S(1)} %add_add_fusion.1), channel_id=1, source_target_pairs={{0,192},{4,196},{8,200},{12,204},{16,208},{20,212},{24,216},{28,22... | collective-permute-start | bytes 184328 | tf_op jit(solution)/shard_map/ppermute | solution.py:185
  78.9 7.1 %collective-permute-start.20 = (f32[24,640]{1,0:T(8,128)S(1)}, f32[24,640]{1,0:T(8,128)S(1)}, u32[]{:S(2)}, u32[]{:S(2)}) collective-permute-start(f32[24,640]{1,0:T(8,128)S(1)} %add_add_fusion.1), channel_id=1, source_target_pairs={{0,128},{4,132},{8,136},{12,140},{16,144},{20,148},{24,152},{28,15... | collective-permute-start | bytes 184328 | tf_op jit(solution)/shard_map/ppermute | solution.py:185
  82.8 4.2 %collective-permute-start.19 = (f32[24,640]{1,0:T(8,128)S(1)}, f32[24,640]{1,0:T(8,128)S(1)}, u32[]{:S(2)}, u32[]{:S(2)}) collective-permute-start(f32[24,640]{1,0:T(8,128)S(1)} %add_add_fusion.1), channel_id=1, source_target_pairs={{0,64},{4,68},{8,72},{12,76},{16,80},{20,84},{24,88},{28,92},{32,9... | collective-permute-start | bytes 184328 | tf_op jit(solution)/shard_map/ppermute | solution.py:185
  87.0 5.3 %collective-permute-start.22 = (f32[24,640]{1,0:T(8,128)S(1)}, f32[24,640]{1,0:T(8,128)S(1)}, u32[]{:S(2)}, u32[]{:S(2)}) collective-permute-start(f32[24,640]{1,0:T(8,128)S(1)} %add_add_fusion), channel_id=1, source_target_pairs={{0,4},{4,0},{8,12},{12,8},{16,20},{20,16},{24,28},{28,24},{32,36},... | collective-permute-start | bytes 184328 | tf_op jit(solution)/shard_map/ppermute | solution.py:185
  (4 other events, 2.6 us)

commit v3 on v2

--- a/solution.py
+++ b/solution.py
@@ -12,6 +12,7 @@
 VMEM = pl.BlockSpec(memory_space=pltpu.VMEM)
 SMEM = pl.BlockSpec(memory_space=pltpu.SMEM)
 ROOMY = pltpu.CompilerParams(vmem_limit_bytes=40 * 2**20)
+SNUG = pltpu.CompilerParams(vmem_limit_bytes=12 * 2**20)
 
 
 def dot(a, b, contract=((1,), (0,))):
@@ -32,11 +33,11 @@
     return jnp.where(hit, 1.0, 0.0).astype(BF)
 
 
-def project_kernel(place_ref, feat_ref, in_ref, cot_ref, outf_ref, *payload_refs):
+def project_kernel(feat_ref, in_ref, cot_ref, outf_ref, *payload_refs):
     group_count = len(payload_refs)
     rank = in_ref.shape[1]
     width = rank // group_count
-    pick = rank_picker((group_count * SLAB, rank), 0, place_ref[0], group_count, width, 1)
+    pick = rank_picker((group_count * SLAB, rank), 0, lax.axis_index("chan"), group_count, width, 1)
     weights = dot(pick, in_ref[...], NT).astype(BF)
     reduced = dot(weights, feat_ref[...])
     grad_mixed = dot(outf_ref[...], cot_ref[...])
@@ -52,6 +53,10 @@
     return jnp.where(have == want, jnp.ones((), BF), jnp.zeros((), BF))
 
 
+def core_bit():
+    return lax.axis_index("leaf") % 2
+
+
 def first_octant(halo_ref, slot):
     return jnp.clip(halo_ref[slot, 0] & 15, 0, 8) * 64
 
@@ -60,7 +65,7 @@
     return jnp.where(core == 0, view, near - 1 - view)
 
 
-def scatter_kernel(place_ref, halo_ref, p0, p1, p2, p3, core_ref, nbr_ref, gm_ref, own_ref, kept_ref,
+def scatter_kernel(halo_ref, p0, p1, p2, p3, core_ref, nbr_ref, gm_ref, own_ref, kept_ref,
                    cross_ref, terms_ref, acc_ref):
     rows = nbr_ref.shape[1]
     tiles = acc_ref.shape[0] // SLAB
@@ -94,7 +99,7 @@
     per_peer = (tiles - own_tiles) // near
     blank = jnp.zeros((SLAB, rows - per_peer * LOW), F32)
     for view in range(near):
-        slot = mirrored(place_ref[1], view, near)
+        slot = mirrored(core_bit(), view, near)
         start = own_tiles + slot * per_peer
         window = jnp.concatenate([tile(start + i) for i in range(per_peer)] + [blank], 1)
         block = pltpu.roll(window, first_octant(halo_ref, slot), 1)
@@ -104,7 +109,7 @@
             cross_ref[(view - 4) * SLAB : (view - 3) * SLAB, :] = block.astype(BF)
 
 
-def gather_kernel(place_ref, halo_ref, own_ref, pair_ref, near_ref, far_ref, cross_ref, gm_ref, core_ref,
+def gather_kernel(halo_ref, own_ref, pair_ref, near_ref, far_ref, cross_ref, gm_ref, core_ref,
                   nbr_ref, mix_ref, gc_ref, table_ref, ga_ref):
     rows = nbr_ref.shape[1]
     tiles = table_ref.shape[0] // SLAB
@@ -124,7 +129,7 @@
         cross_ref[3 * SLAB :, :],
     )
     for view in range(near):
-        slot = mirrored(place_ref[1], view, near)
+        slot = mirrored(core_bit(), view, near)
         window = pltpu.roll(views[view].astype(F32), rows - first_octant(halo_ref, slot), 1).astype(BF)
         for i in range(per_peer):
             t = own_tiles + slot * per_peer + i
@@ -142,38 +147,52 @@
         return carry
 
     lax.fori_loop(0, nbr_ref.shape[0], step, 0, unroll=9)
-    gathered = ga_ref[...]
-    mix_ref[...] = dot(core_ref[...], gathered, TN)
-    gc_ref[...] = dot(gm_ref[...], gathered, NT)
-
-
-def finish_kernel(place_ref, mix_ref, e0, e1, e2, e3, in_ref, feat_ref, outf_ref, cot_ref, gc_ref,
-                  gf_ref, out_ref, packed_ref):
+    used = core_ref.shape[0]
+    ga_ref[used:, :] = jnp.zeros_like(ga_ref[used:, :])
+    mix_ref[...] = dot(core_ref[...], ga_ref[:used, :], TN)
+    gc_ref[...] = dot(gm_ref[...], ga_ref[...], NT)
+
+
+def finish_kernel(mix_ref, e0, e1, e2, e3, in_ref, feat_ref, outf_ref, cot_ref, gc_ref,
+                  gf_ref, out_ref, keep_ref, give_ref):
     rank = in_ref.shape[1]
     rows = feat_ref.shape[1]
-    pick = rank_picker((rank, 4 * SLAB), 1, place_ref[0], 4, rank // 4, -1)
+    wide = gc_ref.shape[1]
+    group = lax.axis_index("chan")
+    pick = rank_picker((rank, 4 * SLAB), 1, group, 4, rank // 4, -1)
     slabs = jnp.concatenate([e[0:SLAB, :] for e in (e0, e1, e2, e3)], 0)
     grad_rows = dot(pick, slabs).astype(BF)
     gf_ref[...] = dot(in_ref[...], grad_rows).astype(BF)
     total = (mix_ref[...] + e1[SLAB:, :].astype(F32)) + (e2[SLAB:, :].astype(F32) + e3[SLAB:, :].astype(F32))
     mixed = total.astype(BF)
     out_ref[...] = dot(outf_ref[...], mixed, TN).astype(BF)
-    wide = gc_ref.shape[1]
-    right = jnp.concatenate([cot_ref[...], jnp.zeros((80, rows), BF)], 0)
-    left = jnp.concatenate([jnp.zeros((64, rows), BF), grad_rows, jnp.zeros((16, rows), BF)], 0)
-    packed_ref[:, 0:128] = dot(mixed, right, NT) + dot(feat_ref[...], left, NT)
-    packed_ref[:, 128 : 128 + wide] = gc_ref[...]
-    packed_ref[:, 128 + wide :] = jnp.zeros_like(packed_ref[:, 128 + wide :])
-
-
-def unpack_kernel(factor, packed_ref, left_ref, core_ref, right_ref, flat_ref):
-    tail = packed_ref[:, 0:128] * factor
-    right_ref[...] = tail[:, 0:48]
-    left_ref[...] = tail[:, 64:112]
-    flat_ref[...] = (packed_ref[:, 128:] * factor).T
+    column = lax.broadcasted_iota(jnp.int32, (wide, rank), 0)
+    wanted = lax.broadcasted_iota(jnp.int32, (wide, rank), 1)
+    free = column % SLAB - (SLAB - 4)
+    place = jnp.where((free >= 0) & (column // SLAB * 4 + free == wanted), 1.0, 0.0).astype(BF)
+    spread = dot(place, grad_rows).astype(BF)
+    right = jnp.concatenate([jnp.zeros((48, rows), BF), cot_ref[...], jnp.zeros((32, rows), BF)], 0)
+    tail = dot(mixed, right, NT)
+    packed = gc_ref[...] + dot(feat_ref[...], spread, NT)
+    packed = jnp.concatenate([packed[:, : wide - 128], packed[:, wide - 128 :] + tail], 1)
+    half = rank // 2
+    first = core_bit() == 0
+    keep_ref[...] = jnp.where(first, packed[:half], packed[half:])
+    give_ref[...] = jnp.where(first, packed[half:], packed[:half])
+
+
+def unpack_kernel(factor, mine_ref, other_ref, left_ref, core_ref, right_ref, flat_ref, turned_ref):
     width, offsets, rank = core_ref.shape
+    mine, other = mine_ref[...] * factor, other_ref[...] * factor
+    first = core_bit() == 0
+    packed = jnp.concatenate([jnp.where(first, mine, other), jnp.where(first, other, mine)], 0)
+    flat_ref[...] = packed.T
     for c in range(width):
         core_ref[c] = flat_ref[pl.ds(c, offsets, stride=SLAB), :]
+    for j in range(4):
+        turned_ref[pl.ds(j, rank // 4, stride=4), :] = flat_ref[pl.ds(width + j, rank // 4, stride=SLAB), :]
+    left_ref[...] = turned_ref[...].T
+    right_ref[...] = flat_ref[offsets * SLAB : offsets * SLAB + rank, :].T
 
 
 def shifted(block, axis, distance):
@@ -192,14 +211,11 @@
     )
 
 
-def leaf_sum(total, core):
-    half = total.shape[0] // 2
-    low, high = total[:half], total[half:]
-    mine = jnp.where(core == 0, low, high) + crossed(jnp.where(core == 0, high, low), 1)
+def leaf_sum(mine, give):
+    mine = mine + crossed(give, 1)
     for masks in ((8,), (2, 4, 6), (16, 32, 48)):
         mine = mine + sum(crossed(mine, mask) for mask in masks)
-    other = crossed(mine, 1)
-    return jnp.concatenate([jnp.where(core == 0, mine, other), jnp.where(core == 0, other, mine)], 0)
+    return mine, crossed(mine, 1)
 
 
 def struct(shape, dtype):
@@ -211,8 +227,7 @@
     offsets, width, rank = core.shape
     near, slots = halo_blocks.shape[1:]
     table_rows = (rows + near * slots * 64) // LOW * SLAB
-    core_bit = lax.axis_index("leaf") % 2
-    place = jnp.stack([lax.axis_index("chan"), core_bit]).astype(jnp.int32)
+    packed_width = (offsets * SLAB + 127) // 128 * 128
     keep = row_mask.astype(F32).reshape(1, rows)
     halo = halo_blocks[0]
     core_rows = jnp.pad(core, ((0, 0), (0, SLAB - width), (0, 0))).reshape(offsets * SLAB, rank)
@@ -221,10 +236,10 @@
     payload = pl.pallas_call(
         project_kernel,
         out_shape=[struct((SLAB + rank, rows), F32)] + [struct((SLAB + rank, rows), BF)] * 3,
-        in_specs=[SMEM] + [VMEM] * 4,
+        in_specs=[VMEM] * 4,
         out_specs=[VMEM] * 4,
         name="project",
-    )(place, features, in_factor, cotangent, out_factor)
+    )(features, in_factor, cotangent, out_factor)
     parts = [payload[0]] + [shifted(payload[j], "chan", j) for j in (1, 2, 3)]
     reduced = sum(part[:SLAB].astype(F32) for part in parts) * keep
     reduced = reduced.astype(BF)
@@ -242,13 +257,13 @@
             struct((4 * SLAB, rows), F32),
             struct((4 * SLAB, rows), BF),
         ],
-        in_specs=[SMEM] * 2 + [VMEM] * 6,
+        in_specs=[SMEM] + [VMEM] * 6,
         out_specs=[VMEM] * 4,
         scratch_shapes=[pltpu.VMEM((offsets * SLAB, rows), BF), pltpu.VMEM((table_rows, LOW), F32)],
         compiler_params=ROOMY,
         cost_estimate=estimate,
         name="scatter",
-    )(place, halo, *parts, core_rows, neighbours)
+    )(halo, *parts, core_rows, neighbours)
 
     beyond = crossed(jnp.concatenate([near_pair, far_pair], 0), 1)
     handed = crossed(cross, 1).astype(F32)
@@ -258,45 +273,48 @@
     ).astype(BF)
     to_far = jnp.concatenate([kept[:SLAB], kept[SLAB : 2 * SLAB] + handed[3 * SLAB :]], 0).astype(BF)
     beyond, to_near, to_far = lax.optimization_barrier((beyond, to_near, to_far))
-    from_near = outward(to_near, -1).astype(F32)
-    from_far = outward(to_far, -2).astype(F32)
+    from_near = outward(to_near, -1)
+    from_far = outward(to_far, -2)
 
     mixed_part, grad_core = pl.pallas_call(
         gather_kernel,
-        out_shape=[struct((rank, rows), F32), struct((rank, offsets * SLAB), F32)],
-        in_specs=[SMEM] * 2 + [VMEM] * 8,
+        out_shape=[struct((rank, rows), F32), struct((rank, packed_width), F32)],
+        in_specs=[SMEM] + [VMEM] * 8,
         out_specs=[VMEM] * 2,
-        scratch_shapes=[pltpu.VMEM((table_rows, LOW), BF), pltpu.VMEM((offsets * SLAB, rows), BF)],
+        scratch_shapes=[pltpu.VMEM((table_rows, LOW), BF), pltpu.VMEM((packed_width, rows), BF)],
         compiler_params=ROOMY,
         cost_estimate=estimate,
         name="gather",
-    )(place, halo, reduced, pair, near_pair, far_pair, beyond, grad_mixed, core_rows, neighbours)
-
-    returned = from_near + from_far
+    )(halo, reduced, pair, near_pair, far_pair, beyond, grad_mixed, core_rows, neighbours)
+
+    mixed_part, from_near, from_far = lax.optimization_barrier((mixed_part, from_near, from_far))
+    returned = from_near.astype(F32) + from_far.astype(F32)
     last = crossed(returned[SLAB:].astype(BF), 1).astype(F32)
     grad_slab = ((own + returned[:SLAB] + last) * keep).astype(BF)
     shared = jnp.concatenate([grad_slab, mixed_part.astype(BF)], 0)
     exchanged = [shared] + [shifted(shared, "chan", j) for j in (1, 2, 3)]
 
-    packed_width = 128 + (offsets * SLAB + 127) // 128 * 128
-    grad_features, output, packed = pl.pallas_call(
+    half = struct((rank // 2, packed_width), F32)
+    grad_features, output, mine, give = pl.pallas_call(
         finish_kernel,
-        out_shape=[struct((channels, rows), BF)] * 2 + [struct((rank, packed_width), F32)],
-        in_specs=[SMEM] + [VMEM] * 10,
-        out_specs=[VMEM] * 3,
+        out_shape=[struct((channels, rows), BF)] * 2 + [half] * 2,
+        in_specs=[VMEM] * 10,
+        out_specs=[VMEM] * 4,
+        compiler_params=SNUG,
         name="finish",
-    )(place, mixed_part, *exchanged, in_factor, features, out_factor, cotangent, grad_core)
-    packed = leaf_sum(packed, core_bit)
+    )(mixed_part, *exchanged, in_factor, features, out_factor, cotangent, grad_core)
+    mine, other = leaf_sum(mine, give)
 
     factor = float(rows * lax.axis_size("leaf")) ** (-0.5)
     grad_in, grad_core, grad_out = pl.pallas_call(
         lambda *refs: unpack_kernel(factor, *refs),
         out_shape=[struct((channels, rank), F32), struct((width, offsets, rank), F32), struct((rank, channels), F32)],
-        in_specs=[VMEM],
+        in_specs=[VMEM] * 2,
         out_specs=[VMEM] * 3,
-        scratch_shapes=[pltpu.VMEM((packed_width - 128, rank), F32)],
+        scratch_shapes=[pltpu.VMEM((packed_width, rank), F32), pltpu.VMEM((rank, channels), F32)],
+        compiler_params=SNUG,
         name="unpack",
-    )(packed)
+    )(mine, other)
     return (output, grad_features, grad_in, jnp.transpose(grad_core, (1, 0, 2)), grad_out)
 
 

time: 95 us -> 83.5 us (0.88)
  waiting for transfers between devices: 33.1 us -> 25.3 us
  starting transfers between devices: 36.5 us -> 38.8 us
  other arithmetic: 3.27 us -> 1.08 us
  local copies, waits for them, and re-layouts: 2.01 us -> 0.13 us
  Pallas kernels: 19 us -> 17.3 us
    ppermute x4, waiting for transfers between devices: 6.1 us -> 0.01 us  [outward(): lax.ppermute(block, 'leaf', [(i, (i + (2 * chips if i % 2 == 0 else -2 *...]
    ppermute x13, starting transfers between devices: 17.4 us -> 19.7 us  [crossed(): lax.ppermute(block, 'leaf', [(i, i ^ mask) for i in range(lax.axis_size('...]
    ppermute x13, waiting for transfers between devices: 13.9 us -> 12 us  [crossed(): lax.ppermute(block, 'leaf', [(i, i ^ mask) for i in range(lax.axis_size('...]
    unnamed x27 -> x19, local copies, waits for them, and re-layouts: 1.97 us -> 0.09 us
  transfers between devices with their start and end apart: 23 -> 23, of which waited for: 18 -> 15; matrix products, arithmetic and copies ran while one was open for 0% -> 0% of each run, Pallas kernels for 13% -> 15%
where the time goes in v3:
time: 83.5 us; the launch traced here: 83.4 us
  starting transfers between devices  38.8 us (46%)
  waiting for transfers between devices  25.3 us (30%)
  Pallas kernels  17.3 us (21%)
  other arithmetic  1.08 us (1%)
  between operations  0.87 us (1%)
    ppermute x13, starting transfers between devices, crossed(): lax.ppermute(block, 'leaf', [(i, i ^ mask) for i in range(lax.axis_size('...  19.7 us
    ppermute x6, waiting for transfers between devices, shifted(): lax.ppermute(block, axis, [(i, (i + distance) % count) for i in range(cou...  13.3 us
    ppermute x13, waiting for transfers between devices, crossed(): lax.ppermute(block, 'leaf', [(i, i ^ mask) for i in range(lax.axis_size('...  12 us
    ppermute x4, starting transfers between devices, outward(): lax.ppermute(block, 'leaf', [(i, (i + (2 * chips if i % 2 == 0 else -2 *...  9.9 us
    ppermute x6, starting transfers between devices, shifted(): lax.ppermute(block, axis, [(i, (i + distance) % count) for i in range(cou...  9.22 us
    pallas_call x1, Pallas kernels, body(): pl.pallas_call(gather_kernel, out_shape=[struct((rank, rows), F32), struc...  6.5 us
    pallas_call x1, Pallas kernels, body(): pl.pallas_call(scatter_kernel, out_shape=[struct((rank, rows), BF), struc...  6.33 us
    pallas_call x1, Pallas kernels, body(): pl.pallas_call(project_kernel, out_shape=[struct((SLAB + rank, rows), F32...  2.12 us
  transfers between devices with their start and end apart: 23, of which 15 were waited for; matrix products, arithmetic and copies ran while one was open for 0% of the time, Pallas kernels for 15%

profile of v3, /device:TPU:1, one launch (start us, length us, event | category | flops | bytes accessed | tf_op | source)
XLA Modules:
  0.0 83.4 jit_solution(18385637006200969173)
XLA Ops:
  0.6 2.1 %project.1 = (f32[64,1024]{1,0:T(8,128)}, bf16[64,1024]{1,0:T(8,128)(2,1)}, bf16[64,1024]{1,0:T(8,128)(2,1)}, bf16[64,1024]{1,0:T(8,128)(2,1)}) custom-call(bf16[48,1024]{1,0:T(8,128)(2,1)} %feat_ref.3, bf16[48,48]{1,0:T(8,128)(2,1)} %in_ref.3, bf16[48,1024]{1,0:T(8,128)(2,1)} %cot_ref.3, bf16[48,48]{1,0:T(8,128)(2,1)} %outf_ref.3), custom_call_target="tpu_custom_call" | custom-call | tf_op jit(solution)/shard_map/project/pallas_call | solution.py:236
  2.8 2.1 %collective-permute-start = (bf16[64,1024]{1,0:T(8,128)(2,1)}, bf16[64,1024]{1,0:T(8,128)(2,1)S(1)}, u32[]{:S(2)}, u32[]{:S(2)}) collective-permute-start(bf16[64,1024]{1,0:T(8,128)(2,1)} %get-tuple-element.34), channel_id=1, source_target_pairs={{0,1},{1,2},{2,3},{3,0},{4,5},{5,6},{6,7},{7,4},{8,9},{9,10},{10,1... | collective-permute-start | bytes 393224 | tf_op jit(solution)/shard_map/ppermute | solution.py:200
  4.9 2.6 %collective-permute-start.1 = (bf16[64,1024]{1,0:T(8,128)(2,1)}, bf16[64,1024]{1,0:T(8,128)(2,1)S(1)}, u32[]{:S(2)}, u32[]{:S(2)}) collective-permute-start(bf16[64,1024]{1,0:T(8,128)(2,1)} %get-tuple-element.35), channel_id=1, source_target_pairs={{0,2},{1,3},{2,0},{3,1},{4,6},{5,7},{6,4},{7,5},{8,10},{9,11},{10,... | collective-permute-start | bytes 393224 | tf_op jit(solution)/shard_map/ppermute | solution.py:200
  7.5 1.1 %collective-permute-start.2 = (bf16[64,1024]{1,0:T(8,128)(2,1)}, bf16[64,1024]{1,0:T(8,128)(2,1)S(1)}, u32[]{:S(2)}, u32[]{:S(2)}) collective-permute-start(bf16[64,1024]{1,0:T(8,128)(2,1)} %get-tuple-element.36), channel_id=1, source_target_pairs={{0,3},{1,0},{2,1},{3,2},{4,7},{5,4},{6,5},{7,6},{8,11},{9,8},{10,9... | collective-permute-start | bytes 393224 | tf_op jit(solution)/shard_map/ppermute | solution.py:200
  8.9 4.5 %collective-permute-done.1.p2 = bf16[64,1024]{1,0:T(8,128)(2,1)S(1)} collective-permute-done((bf16[64,1024]{1,0:T(8,128)(2,1)}, bf16[64,1024]{1,0:T(8,128)(2,1)S(1)}, u32[]{:S(2)}, u32[]{:S(2)}) %collective-permute-start.1) | collective-permute-done | bytes 131104 | tf_op jit(solution)/shard_map/ppermute | solution.py:200
  13.4 0.9 %multiply_convert_fusion.own_ref = bf16[16,1024]{1,0:T(8,128)(2,1)S(1)} fusion(f32[64,1024]{1,0:T(8,128)} %get-tuple-element.38.p0, bf16[64,1024]{1,0:T(8,128)(2,1)S(1)} %collective-permute-done.2.p3, bf16[64,1024]{1,0:T(8,128)(2,1)S(1)} %collective-permute-done.1.p2, bf16[64,1024]{1,0:T(8,128)(2,1)S(1)} %collective-permute-done.p1, ...), kind=kLoop, calls=%fused_computation.19 | loop fusion | flops 131072 | bytes 200704 | tf_op jit(solution)/shard_map/convert_element_type | solution.py:245
  14.3 1.9 %collective-permute-start.3 = (bf16[16,1024]{1,0:T(8,128)(2,1)S(1)}, bf16[16,1024]{1,0:T(8,128)(2,1)S(1)}, u32[]{:S(2)}, u32[]{:S(2)}) collective-permute-start(bf16[16,1024]{1,0:T(8,128)(2,1)S(1)} %multiply_convert_fusion.own_ref), channel_id=1, source_target_pairs={{0,4},{4,0},{8,12},{12,8},{16,20},{20,16},{24,28},{28,24},{32,36},... | collective-permute-start | bytes 98312 | tf_op jit(solution)/shard_map/ppermute | solution.py:204
  17.1 7.8 %collective-permute-start.5 = (bf16[32,1024]{1,0:T(8,128)(2,1)S(1)}, bf16[32,1024]{1,0:T(8,128)(2,1)S(1)}, u32[]{:S(2)}, u32[]{:S(2)}) collective-permute-start(bf16[32,1024]{1,0:T(8,128)(2,1)S(1)} %pad_maximum_fusion.2), channel_id=1, source_target_pairs={{0,16},{4,244},{8,24},{12,252},{16,32},{20,4},{24,40},{28,12},{32,... | collective-permute-start | bytes 196616 | tf_op jit(solution)/shard_map/ppermute | solution.py:209
  24.9 0.9 %collective-permute-start.4 = (bf16[32,1024]{1,0:T(8,128)(2,1)S(1)}, bf16[32,1024]{1,0:T(8,128)(2,1)S(1)}, u32[]{:S(2)}, u32[]{:S(2)}) collective-permute-start(bf16[32,1024]{1,0:T(8,128)(2,1)S(1)} %pad_maximum_fusion.2), channel_id=1, source_target_pairs={{0,8},{4,252},{8,16},{12,4},{16,24},{20,12},{24,32},{28,20},{32,40... | collective-permute-start | bytes 196616 | tf_op jit(solution)/shard_map/ppermute | solution.py:209
  25.7 6.3 %scatter.1 = (bf16[48,1024]{1,0:T(8,128)(2,1)S(1)}, f32[16,1024]{1,0:T(8,128)S(1)}, f32[64,1024]{1,0:T(8,128)S(1)}, bf16[64,1024]{1,0:T(8,128)(2,1)S(1)}) custom-call(s32[8,8]{1,0:T(8,128)S(1)} %bitcast.5, f32[64,1024]{1,0:T(8,128)S(1)} %copy-done.4, bf16[64,1024]{1,0:T(8,128)(2,1)S(1)} %collective-permute-done.p1, ...), custom_call_target="tpu_custom_call" | custom-call | flops 5000000000 | bytes 1048576 | tf_op jit(solution)/shard_map/scatter/pallas_call | solution.py:252
  35.0 6.5 %gather.1 = (f32[48,1024]{1,0:T(8,128)S(1)}, f32[48,512]{1,0:T(8,128)S(1)}) custom-call(s32[8,8]{1,0:T(8,128)S(1)} %bitcast.6, bf16[16,1024]{1,0:T(8,128)(2,1)S(1)} %multiply_convert_fusion.own_ref, bf16[16,1024]{1,0:T(8,128)(2,1)S(1)} %collective-permute-done.3.pair_ref, bf16[32,1024]{1,0:T(8,128)(2,1)S(1)} %collective-permute-done.4.near_ref, ...), custom_call_target="tpu_custom_call" | custom-call | flops 5000000000 | bytes 1048576 | tf_op jit(solution)/shard_map/gather/pallas_call | solution.py:279
  41.6 2.6 %collective-permute-start.10 = (bf16[16,1024]{1,0:T(8,128)(2,1)S(1)}, bf16[16,1024]{1,0:T(8,128)(2,1)S(1)}, u32[]{:S(2)}, u32[]{:S(2)}) collective-permute-start(bf16[16,1024]{1,0:T(8,128)(2,1)S(1)} %slice.96), channel_id=1, source_target_pairs={{0,4},{4,0},{8,12},{12,8},{16,20},{20,16},{24,28},{28,24},{32,36},... | collective-permute-start | bytes 98312 | tf_op jit(solution)/shard_map/ppermute | solution.py:204
  44.2 0.8 %collective-permute-done.10 = bf16[16,1024]{1,0:T(8,128)(2,1)S(1)} collective-permute-done((bf16[16,1024]{1,0:T(8,128)(2,1)S(1)}, bf16[16,1024]{1,0:T(8,128)(2,1)S(1)}, u32[]{:S(2)}, u32[]{:S(2)}) %collective-permute-start.10) | collective-permute-done | bytes 32800 | tf_op jit(solution)/shard_map/ppermute | solution.py:204
  45.1 2.1 %collective-permute-start.13 = (bf16[64,1024]{1,0:T(8,128)(2,1)S(1)}, bf16[64,1024]{1,0:T(8,128)(2,1)S(1)}, u32[]{:S(2)}, u32[]{:S(2)}) collective-permute-start(bf16[64,1024]{1,0:T(8,128)(2,1)S(1)} %pad_maximum_fusion.1.e0), channel_id=1, source_target_pairs={{0,3},{1,0},{2,1},{3,2},{4,7},{5,4},{6,5},{7,6},{8,11},{9,8},{10,9... | collective-permute-start | bytes 393224 | tf_op jit(solution)/shard_map/ppermute | solution.py:200
  47.3 0.9 %collective-permute-start.12 = (bf16[64,1024]{1,0:T(8,128)(2,1)S(1)}, bf16[64,1024]{1,0:T(8,128)(2,1)S(1)}, u32[]{:S(2)}, u32[]{:S(2)}) collective-permute-start(bf16[64,1024]{1,0:T(8,128)(2,1)S(1)} %pad_maximum_fusion.1.e0), channel_id=1, source_target_pairs={{0,2},{1,3},{2,0},{3,1},{4,6},{5,7},{6,4},{7,5},{8,10},{9,11},{10,... | collective-permute-start | bytes 393224 | tf_op jit(solution)/shard_map/ppermute | solution.py:200
  48.6 1.6 %collective-permute-done.13.e3 = bf16[64,1024]{1,0:T(8,128)(2,1)S(1)} collective-permute-done((bf16[64,1024]{1,0:T(8,128)(2,1)S(1)}, bf16[64,1024]{1,0:T(8,128)(2,1)S(1)}, u32[]{:S(2)}, u32[]{:S(2)}) %collective-permute-start.13) | collective-permute-done | bytes 131104 | tf_op jit(solution)/shard_map/ppermute | solution.py:200
  50.1 3.1 %collective-permute-done.12.e2 = bf16[64,1024]{1,0:T(8,128)(2,1)S(1)} collective-permute-done((bf16[64,1024]{1,0:T(8,128)(2,1)S(1)}, bf16[64,1024]{1,0:T(8,128)(2,1)S(1)}, u32[]{:S(2)}, u32[]{:S(2)}) %collective-permute-start.12) | collective-permute-done | bytes 131104 | tf_op jit(solution)/shard_map/ppermute | solution.py:200
  53.2 3.8 %collective-permute-done.11.e1 = bf16[64,1024]{1,0:T(8,128)(2,1)S(1)} collective-permute-done((bf16[64,1024]{1,0:T(8,128)(2,1)S(1)}, bf16[64,1024]{1,0:T(8,128)(2,1)S(1)}, u32[]{:S(2)}, u32[]{:S(2)}) %collective-permute-start.11) | collective-permute-done | bytes 131104 | tf_op jit(solution)/shard_map/ppermute | solution.py:200
  57.0 1.5 %finish.1 = (bf16[48,1024]{1,0:T(8,128)(2,1)}, bf16[48,1024]{1,0:T(8,128)(2,1)}, f32[24,512]{1,0:T(8,128)S(1)}, f32[24,512]{1,0:T(8,128)S(1)}) custom-call(f32[48,1024]{1,0:T(8,128)S(1)} %get-tuple-element.49.mix_ref, bf16[64,1024]{1,0:T(8,128)(2,1)S(1)} %pad_maximum_fusion.1.e0, bf16[64,1024]{1,0:T(8,128)(2,1)S(1)} %collective-permute-done.11.e1, ...), custom_call_target="tpu_custom_call" | custom-call | tf_op jit(solution)/shard_map/finish/pallas_call | solution.py:298
  59.0 0.9 %collective-permute-done.14 = f32[24,512]{1,0:T(8,128)S(1)} collective-permute-done((f32[24,512]{1,0:T(8,128)S(1)}, f32[24,512]{1,0:T(8,128)S(1)}, u32[]{:S(2)}, u32[]{:S(2)}) %collective-permute-start.14) | collective-permute-done | bytes 49184 | tf_op jit(solution)/shard_map/ppermute | solution.py:204
  60.7 2.2 %collective-permute-done.15 = f32[24,512]{1,0:T(8,128)S(1)} collective-permute-done((f32[24,512]{1,0:T(8,128)S(1)}, f32[24,512]{1,0:T(8,128)S(1)}, u32[]{:S(2)}, u32[]{:S(2)}) %collective-permute-start.15) | collective-permute-done | bytes 49184 | tf_op jit(solution)/shard_map/ppermute | solution.py:204
  62.9 1.1 %collective-permute-start.18 = (f32[24,512]{1,0:T(8,128)S(1)}, f32[24,512]{1,0:T(8,128)S(1)}, u32[]{:S(2)}, u32[]{:S(2)}) collective-permute-start(f32[24,512]{1,0:T(8,128)S(1)} %add.67), channel_id=1, source_target_pairs={{0,24},{4,28},{8,16},{12,20},{16,8},{20,12},{24,0},{28,4},{32,56},... | collective-permute-start | bytes 147464 | tf_op jit(solution)/shard_map/ppermute | solution.py:204
  64.5 1.7 %collective-permute-start.16 = (f32[24,512]{1,0:T(8,128)S(1)}, f32[24,512]{1,0:T(8,128)S(1)}, u32[]{:S(2)}, u32[]{:S(2)}) collective-permute-start(f32[24,512]{1,0:T(8,128)S(1)} %add.67), channel_id=1, source_target_pairs={{0,8},{4,12},{8,0},{12,4},{16,24},{20,28},{24,16},{28,20},{32,40},... | collective-permute-start | bytes 147464 | tf_op jit(solution)/shard_map/ppermute | solution.py:204
  66.2 0.9 %collective-permute-done.18 = f32[24,512]{1,0:T(8,128)S(1)} collective-permute-done((f32[24,512]{1,0:T(8,128)S(1)}, f32[24,512]{1,0:T(8,128)S(1)}, u32[]{:S(2)}, u32[]{:S(2)}) %collective-permute-start.18) | collective-permute-done | bytes 49184 | tf_op jit(solution)/shard_map/ppermute | solution.py:204
  67.1 1.3 %collective-permute-done.17 = f32[24,512]{1,0:T(8,128)S(1)} collective-permute-done((f32[24,512]{1,0:T(8,128)S(1)}, f32[24,512]{1,0:T(8,128)S(1)}, u32[]{:S(2)}, u32[]{:S(2)}) %collective-permute-start.17) | collective-permute-done | bytes 49184 | tf_op jit(solution)/shard_map/ppermute | solution.py:204
  68.5 2.1 %collective-permute-start.21 = (f32[24,512]{1,0:T(8,128)S(1)}, f32[24,512]{1,0:T(8,128)S(1)}, u32[]{:S(2)}, u32[]{:S(2)}) collective-permute-start(f32[24,512]{1,0:T(8,128)S(1)} %add_add_fusion.1), channel_id=1, source_target_pairs={{0,192},{4,196},{8,200},{12,204},{16,208},{20,212},{24,216},{28,22... | collective-permute-start | bytes 147464 | tf_op jit(solution)/shard_map/ppermute | solution.py:204
  70.6 2.6 %collective-permute-start.20 = (f32[24,512]{1,0:T(8,128)S(1)}, f32[24,512]{1,0:T(8,128)S(1)}, u32[]{:S(2)}, u32[]{:S(2)}) collective-permute-start(f32[24,512]{1,0:T(8,128)S(1)} %add_add_fusion.1), channel_id=1, source_target_pairs={{0,128},{4,132},{8,136},{12,140},{16,144},{20,148},{24,152},{28,15... | collective-permute-start | bytes 147464 | tf_op jit(solution)/shard_map/ppermute | solution.py:204
  73.2 1.1 %collective-permute-start.19 = (f32[24,512]{1,0:T(8,128)S(1)}, f32[24,512]{1,0:T(8,128)S(1)}, u32[]{:S(2)}, u32[]{:S(2)}) collective-permute-start(f32[24,512]{1,0:T(8,128)S(1)} %add_add_fusion.1), channel_id=1, source_target_pairs={{0,64},{4,68},{8,72},{12,76},{16,80},{20,84},{24,88},{28,92},{32,9... | collective-permute-start | bytes 147464 | tf_op jit(solution)/shard_map/ppermute | solution.py:204
  74.2 3.3 %collective-permute-done.20 = f32[24,512]{1,0:T(8,128)S(1)} collective-permute-done((f32[24,512]{1,0:T(8,128)S(1)}, f32[24,512]{1,0:T(8,128)S(1)}, u32[]{:S(2)}, u32[]{:S(2)}) %collective-permute-start.20) | collective-permute-done | bytes 49184 | tf_op jit(solution)/shard_map/ppermute | solution.py:204
  77.5 4.1 %collective-permute-start.22 = (f32[24,512]{1,0:T(8,128)S(1)}, f32[24,512]{1,0:T(8,128)S(1)}, u32[]{:S(2)}, u32[]{:S(2)}) collective-permute-start(f32[24,512]{1,0:T(8,128)S(1)} %add_add_fusion.refs_0_), channel_id=1, source_target_pairs={{0,4},{4,0},{8,12},{12,8},{16,20},{20,16},{24,28},{28,24},{32,36},... | collective-permute-start | bytes 147464 | tf_op jit(solution)/shard_map/ppermute | solution.py:204
  81.7 0.9 %collective-permute-done.22.refs_1_ = f32[24,512]{1,0:T(8,128)S(1)} collective-permute-done((f32[24,512]{1,0:T(8,128)S(1)}, f32[24,512]{1,0:T(8,128)S(1)}, u32[]{:S(2)}, u32[]{:S(2)}) %collective-permute-start.22) | collective-permute-done | bytes 49184 | tf_op jit(solution)/shard_map/ppermute | solution.py:204
  82.5 0.8 %unpack.1 = (f32[48,48]{1,0:T(8,128)}, f32[12,27,48]{2,1,0:T(8,128)}, f32[48,48]{1,0:T(8,128)}) custom-call(f32[24,512]{1,0:T(8,128)S(1)} %add_add_fusion.refs_0_, f32[24,512]{1,0:T(8,128)S(1)} %collective-permute-done.22.refs_1_), custom_call_target="tpu_custom_call" | custom-call | tf_op jit(solution)/shard_map/unpack/pallas_call | solution.py:309
  (56 shorter events, 6.4 us)
Async XLA Ops:
  2.8 5.8 %copy-start.8 = (s32[1024]{0:T(1024)S(1)}, s32[1024]{0:T(1024)}, u32[]{:S(2)}) copy-start(s32[1024]{0:T(1024)} %param.14) | copy-start | bytes 12292
  2.8 6.1 %collective-permute-start = (bf16[64,1024]{1,0:T(8,128)(2,1)}, bf16[64,1024]{1,0:T(8,128)(2,1)S(1)}, u32[]{:S(2)}, u32[]{:S(2)}) collective-permute-start(bf16[64,1024]{1,0:T(8,128)(2,1)} %get-tuple-element.34), channel_id=1, source_target_pairs={{0,1},{1,2},{2,3},{3,0},{4,5},{5,6},{6,7},{7,4},{8,9},{9,10},{10,1... | collective-permute-start | bytes 393224 | tf_op jit(solution)/shard_map/ppermute | solution.py:200
  4.9 8.5 %collective-permute-start.1 = (bf16[64,1024]{1,0:T(8,128)(2,1)}, bf16[64,1024]{1,0:T(8,128)(2,1)S(1)}, u32[]{:S(2)}, u32[]{:S(2)}) collective-permute-start(bf16[64,1024]{1,0:T(8,128)(2,1)} %get-tuple-element.35), channel_id=1, source_target_pairs={{0,2},{1,3},{2,0},{3,1},{4,6},{5,7},{6,4},{7,5},{8,10},{9,11},{10,... | collective-permute-start | bytes 393224 | tf_op jit(solution)/shard_map/ppermute | solution.py:200
  7.5 5.9 %collective-permute-start.2 = (bf16[64,1024]{1,0:T(8,128)(2,1)}, bf16[64,1024]{1,0:T(8,128)(2,1)S(1)}, u32[]{:S(2)}, u32[]{:S(2)}) collective-permute-start(bf16[64,1024]{1,0:T(8,128)(2,1)} %get-tuple-element.36), channel_id=1, source_target_pairs={{0,3},{1,0},{2,1},{3,2},{4,7},{5,4},{6,5},{7,6},{8,11},{9,8},{10,9... | collective-permute-start | bytes 393224 | tf_op jit(solution)/shard_map/ppermute | solution.py:200
  13.4 2.8 %copy-start.7 = (bf16[27,12,48]{2,0,1:T(8,128)(2,1)S(1)}, bf16[27,12,48]{2,0,1:T(8,128)(2,1)}, u32[]{:S(2)}) copy-start(bf16[27,12,48]{2,0,1:T(8,128)(2,1)} %param.10) | copy-start | bytes 93316
  14.3 11.4 %copy-start.4 = (f32[64,1024]{1,0:T(8,128)S(1)}, f32[64,1024]{1,0:T(8,128)}, u32[]{:S(2)}) copy-start(f32[64,1024]{1,0:T(8,128)} %get-tuple-element.38.p0) | copy-start | bytes 786436
  14.3 2.7 %collective-permute-start.3 = (bf16[16,1024]{1,0:T(8,128)(2,1)S(1)}, bf16[16,1024]{1,0:T(8,128)(2,1)S(1)}, u32[]{:S(2)}, u32[]{:S(2)}) collective-permute-start(bf16[16,1024]{1,0:T(8,128)(2,1)S(1)} %multiply_convert_fusion.own_ref), channel_id=1, source_target_pairs={{0,4},{4,0},{8,12},{12,8},{16,20},{20,16},{24,28},{28,24},{32,36},... | collective-permute-start | bytes 98312 | tf_op jit(solution)/shard_map/ppermute | solution.py:204
  16.2 9.5 %copy-start.5 = (s32[27,1024]{1,0:T(8,128)S(1)}, s32[27,1024]{1,0:T(8,128)}, u32[]{:S(2)}) copy-start(s32[27,1024]{1,0:T(8,128)} %nbr_ref.3) | copy-start | bytes 331780
  16.3 9.4 %copy-start.6 = (s32[1,8,8]{2,1,0:T(8,128)S(1)}, s32[1,8,8]{2,1,0:T(8,128)}, u32[]{:S(2)}) copy-start(s32[1,8,8]{2,1,0:T(8,128)} %param.13) | copy-start | bytes 772
  17.1 15.1 %collective-permute-start.5 = (bf16[32,1024]{1,0:T(8,128)(2,1)S(1)}, bf16[32,1024]{1,0:T(8,128)(2,1)S(1)}, u32[]{:S(2)}, u32[]{:S(2)}) collective-permute-start(bf16[32,1024]{1,0:T(8,128)(2,1)S(1)} %pad_maximum_fusion.2), channel_id=1, source_target_pairs={{0,16},{4,244},{8,24},{12,252},{16,32},{20,4},{24,40},{28,12},{32,... | collective-permute-start | bytes 196616 | tf_op jit(solution)/shard_map/ppermute | solution.py:209
  24.9 7.3 %collective-permute-start.4 = (bf16[32,1024]{1,0:T(8,128)(2,1)S(1)}, bf16[32,1024]{1,0:T(8,128)(2,1)S(1)}, u32[]{:S(2)}, u32[]{:S(2)}) collective-permute-start(bf16[32,1024]{1,0:T(8,128)(2,1)S(1)} %pad_maximum_fusion.2), channel_id=1, source_target_pairs={{0,8},{4,252},{8,16},{12,4},{16,24},{20,12},{24,32},{28,20},{32,40... | collective-permute-start | bytes 196616 | tf_op jit(solution)/shard_map/ppermute | solution.py:209
  32.1 1.4 %collective-permute-start.7 = (bf16[64,1024]{1,0:T(8,128)(2,1)S(1)}, bf16[64,1024]{1,0:T(8,128)(2,1)S(1)}, u32[]{:S(2)}, u32[]{:S(2)}) collective-permute-start(bf16[64,1024]{1,0:T(8,128)(2,1)S(1)} %get-tuple-element.43), channel_id=1, source_target_pairs={{0,4},{4,0},{8,12},{12,8},{16,20},{20,16},{24,28},{28,24},{32,36},... | collective-permute-start | bytes 393224 | tf_op jit(solution)/shard_map/ppermute | solution.py:204
  32.2 1.6 %collective-permute-start.6 = (bf16[64,1024]{1,0:T(8,128)(2,1)S(1)}, bf16[64,1024]{1,0:T(8,128)(2,1)S(1)}, u32[]{:S(2)}, u32[]{:S(2)}) collective-permute-start(bf16[64,1024]{1,0:T(8,128)(2,1)S(1)} %pad_maximum_fusion), channel_id=1, source_target_pairs={{0,4},{4,0},{8,12},{12,8},{16,20},{20,16},{24,28},{28,24},{32,36},... | collective-permute-start | bytes 393224 | tf_op jit(solution)/shard_map/ppermute | solution.py:204
  33.8 7.7 %collective-permute-start.8 = (bf16[32,1024]{1,0:T(8,128)(2,1)S(1)}, bf16[32,1024]{1,0:T(8,128)(2,1)S(1)}, u32[]{:S(2)}, u32[]{:S(2)}) collective-permute-start(bf16[32,1024]{1,0:T(8,128)(2,1)S(1)} %get-tuple-element.47), channel_id=1, source_target_pairs={{0,248},{4,12},{8,0},{12,20},{16,8},{20,28},{24,16},{28,36},{32,24... | collective-permute-start | bytes 196616 | tf_op jit(solution)/shard_map/ppermute | solution.py:209
  34.4 7.1 %collective-permute-start.9 = (bf16[32,1024]{1,0:T(8,128)(2,1)S(1)}, bf16[32,1024]{1,0:T(8,128)(2,1)S(1)}, u32[]{:S(2)}, u32[]{:S(2)}) collective-permute-start(bf16[32,1024]{1,0:T(8,128)(2,1)S(1)} %get-tuple-element.48), channel_id=1, source_target_pairs={{0,240},{4,20},{8,248},{12,28},{16,0},{20,36},{24,8},{28,44},{32,1... | collective-permute-start | bytes 196616 | tf_op jit(solution)/shard_map/ppermute | solution.py:209
  41.6 3.5 %collective-permute-start.10 = (bf16[16,1024]{1,0:T(8,128)(2,1)S(1)}, bf16[16,1024]{1,0:T(8,128)(2,1)S(1)}, u32[]{:S(2)}, u32[]{:S(2)}) collective-permute-start(bf16[16,1024]{1,0:T(8,128)(2,1)S(1)} %slice.96), channel_id=1, source_target_pairs={{0,4},{4,0},{8,12},{12,8},{16,20},{20,16},{24,28},{28,24},{32,36},... | collective-permute-start | bytes 98312 | tf_op jit(solution)/shard_map/ppermute | solution.py:204
  45.1 11.9 %copy-start = (bf16[48,1024]{1,0:T(8,128)(2,1)S(1)}, bf16[48,1024]{1,0:T(8,128)(2,1)}, u32[]{:S(2)}) copy-start(bf16[48,1024]{1,0:T(8,128)(2,1)} %feat_ref.3) | copy-start | bytes 294916
  45.1 11.9 %copy-start.1 = (bf16[48,1024]{1,0:T(8,128)(2,1)S(1)}, bf16[48,1024]{1,0:T(8,128)(2,1)}, u32[]{:S(2)}) copy-start(bf16[48,1024]{1,0:T(8,128)(2,1)} %cot_ref.3) | copy-start | bytes 294916
  45.1 11.9 %copy-start.2 = (bf16[48,48]{1,0:T(8,128)(2,1)S(1)}, bf16[48,48]{1,0:T(8,128)(2,1)}, u32[]{:S(2)}) copy-start(bf16[48,48]{1,0:T(8,128)(2,1)} %in_ref.3) | copy-start | bytes 13828
  45.1 11.9 %copy-start.3 = (bf16[48,48]{1,0:T(8,128)(2,1)S(1)}, bf16[48,48]{1,0:T(8,128)(2,1)}, u32[]{:S(2)}) copy-start(bf16[48,48]{1,0:T(8,128)(2,1)} %outf_ref.3) | copy-start | bytes 13828
  45.1 5.0 %collective-permute-start.13 = (bf16[64,1024]{1,0:T(8,128)(2,1)S(1)}, bf16[64,1024]{1,0:T(8,128)(2,1)S(1)}, u32[]{:S(2)}, u32[]{:S(2)}) collective-permute-start(bf16[64,1024]{1,0:T(8,128)(2,1)S(1)} %pad_maximum_fusion.1.e0), channel_id=1, source_target_pairs={{0,3},{1,0},{2,1},{3,2},{4,7},{5,4},{6,5},{7,6},{8,11},{9,8},{10,9... | collective-permute-start | bytes 393224 | tf_op jit(solution)/shard_map/ppermute | solution.py:200
  47.3 5.9 %collective-permute-start.12 = (bf16[64,1024]{1,0:T(8,128)(2,1)S(1)}, bf16[64,1024]{1,0:T(8,128)(2,1)S(1)}, u32[]{:S(2)}, u32[]{:S(2)}) collective-permute-start(bf16[64,1024]{1,0:T(8,128)(2,1)S(1)} %pad_maximum_fusion.1.e0), channel_id=1, source_target_pairs={{0,2},{1,3},{2,0},{3,1},{4,6},{5,7},{6,4},{7,5},{8,10},{9,11},{10,... | collective-permute-start | bytes 393224 | tf_op jit(solution)/shard_map/ppermute | solution.py:200
  48.1 8.9 %collective-permute-start.11 = (bf16[64,1024]{1,0:T(8,128)(2,1)S(1)}, bf16[64,1024]{1,0:T(8,128)(2,1)S(1)}, u32[]{:S(2)}, u32[]{:S(2)}) collective-permute-start(bf16[64,1024]{1,0:T(8,128)(2,1)S(1)} %pad_maximum_fusion.1.e0), channel_id=1, source_target_pairs={{0,1},{1,2},{2,3},{3,0},{4,5},{5,6},{6,7},{7,4},{8,9},{9,10},{10,1... | collective-permute-start | bytes 393224 | tf_op jit(solution)/shard_map/ppermute | solution.py:200
  58.5 1.4 %collective-permute-start.14 = (f32[24,512]{1,0:T(8,128)S(1)}, f32[24,512]{1,0:T(8,128)S(1)}, u32[]{:S(2)}, u32[]{:S(2)}) collective-permute-start(f32[24,512]{1,0:T(8,128)S(1)} %get-tuple-element.57), channel_id=1, source_target_pairs={{0,4},{4,0},{8,12},{12,8},{16,20},{20,16},{24,28},{28,24},{32,36},... | collective-permute-start | bytes 147464 | tf_op jit(solution)/shard_map/ppermute | solution.py:204
  59.9 3.0 %collective-permute-start.15 = (f32[24,512]{1,0:T(8,128)S(1)}, f32[24,512]{1,0:T(8,128)S(1)}, u32[]{:S(2)}, u32[]{:S(2)}) collective-permute-start(f32[24,512]{1,0:T(8,128)S(1)} %add.66), channel_id=1, source_target_pairs={{0,32},{4,36},{8,40},{12,44},{16,48},{20,52},{24,56},{28,60},{32,0... | collective-permute-start | bytes 147464 | tf_op jit(solution)/shard_map/ppermute | solution.py:204
  62.9 4.2 %collective-permute-start.18 = (f32[24,512]{1,0:T(8,128)S(1)}, f32[24,512]{1,0:T(8,128)S(1)}, u32[]{:S(2)}, u32[]{:S(2)}) collective-permute-start(f32[24,512]{1,0:T(8,128)S(1)} %add.67), channel_id=1, source_target_pairs={{0,24},{4,28},{8,16},{12,20},{16,8},{20,12},{24,0},{28,4},{32,56},... | collective-permute-start | bytes 147464 | tf_op jit(solution)/shard_map/ppermute | solution.py:204
  64.0 4.4 %collective-permute-start.17 = (f32[24,512]{1,0:T(8,128)S(1)}, f32[24,512]{1,0:T(8,128)S(1)}, u32[]{:S(2)}, u32[]{:S(2)}) collective-permute-start(f32[24,512]{1,0:T(8,128)S(1)} %add.67), channel_id=1, source_target_pairs={{0,16},{4,20},{8,24},{12,28},{16,0},{20,4},{24,8},{28,12},{32,48},... | collective-permute-start | bytes 147464 | tf_op jit(solution)/shard_map/ppermute | solution.py:204
  64.5 4.0 %collective-permute-start.16 = (f32[24,512]{1,0:T(8,128)S(1)}, f32[24,512]{1,0:T(8,128)S(1)}, u32[]{:S(2)}, u32[]{:S(2)}) collective-permute-start(f32[24,512]{1,0:T(8,128)S(1)} %add.67), channel_id=1, source_target_pairs={{0,8},{4,12},{8,0},{12,4},{16,24},{20,28},{24,16},{28,20},{32,40},... | collective-permute-start | bytes 147464 | tf_op jit(solution)/shard_map/ppermute | solution.py:204
  68.5 5.7 %collective-permute-start.21 = (f32[24,512]{1,0:T(8,128)S(1)}, f32[24,512]{1,0:T(8,128)S(1)}, u32[]{:S(2)}, u32[]{:S(2)}) collective-permute-start(f32[24,512]{1,0:T(8,128)S(1)} %add_add_fusion.1), channel_id=1, source_target_pairs={{0,192},{4,196},{8,200},{12,204},{16,208},{20,212},{24,216},{28,22... | collective-permute-start | bytes 147464 | tf_op jit(solution)/shard_map/ppermute | solution.py:204
  70.6 7.0 %collective-permute-start.20 = (f32[24,512]{1,0:T(8,128)S(1)}, f32[24,512]{1,0:T(8,128)S(1)}, u32[]{:S(2)}, u32[]{:S(2)}) collective-permute-start(f32[24,512]{1,0:T(8,128)S(1)} %add_add_fusion.1), channel_id=1, source_target_pairs={{0,128},{4,132},{8,136},{12,140},{16,144},{20,148},{24,152},{28,15... | collective-permute-start | bytes 147464 | tf_op jit(solution)/shard_map/ppermute | solution.py:204
  73.2 4.3 %collective-permute-start.19 = (f32[24,512]{1,0:T(8,128)S(1)}, f32[24,512]{1,0:T(8,128)S(1)}, u32[]{:S(2)}, u32[]{:S(2)}) collective-permute-start(f32[24,512]{1,0:T(8,128)S(1)} %add_add_fusion.1), channel_id=1, source_target_pairs={{0,64},{4,68},{8,72},{12,76},{16,80},{20,84},{24,88},{28,92},{32,9... | collective-permute-start | bytes 147464 | tf_op jit(solution)/shard_map/ppermute | solution.py:204
  77.5 5.0 %collective-permute-start.22 = (f32[24,512]{1,0:T(8,128)S(1)}, f32[24,512]{1,0:T(8,128)S(1)}, u32[]{:S(2)}, u32[]{:S(2)}) collective-permute-start(f32[24,512]{1,0:T(8,128)S(1)} %add_add_fusion.refs_0_), channel_id=1, source_target_pairs={{0,4},{4,0},{8,12},{12,8},{16,20},{20,16},{24,28},{28,24},{32,36},... | collective-permute-start | bytes 147464 | tf_op jit(solution)/shard_map/ppermute | solution.py:204

commit v4 on v3

--- a/solution.py
+++ b/solution.py
@@ -33,17 +33,19 @@
     return jnp.where(hit, 1.0, 0.0).astype(BF)
 
 
-def project_kernel(feat_ref, in_ref, cot_ref, outf_ref, *payload_refs):
-    group_count = len(payload_refs)
+def project_kernel(feat_ref, in_ref, cot_ref, outf_ref, own_reduced_ref, own_mixed_ref, *payload_refs):
+    group_count = 1 + len(payload_refs)
     rank = in_ref.shape[1]
     width = rank // group_count
     pick = rank_picker((group_count * SLAB, rank), 0, lax.axis_index("chan"), group_count, width, 1)
     weights = dot(pick, in_ref[...], NT).astype(BF)
     reduced = dot(weights, feat_ref[...])
     grad_mixed = dot(outf_ref[...], cot_ref[...])
-    for j in range(group_count):
-        payload_refs[j][0:SLAB, :] = reduced[j * SLAB : (j + 1) * SLAB].astype(payload_refs[j].dtype)
-        payload_refs[j][SLAB:, :] = grad_mixed.astype(payload_refs[j].dtype)
+    own_reduced_ref[...] = reduced[:SLAB]
+    own_mixed_ref[...] = grad_mixed
+    for j, payload_ref in enumerate(payload_refs):
+        payload_ref[0:SLAB, :] = reduced[(j + 1) * SLAB : (j + 2) * SLAB].astype(BF)
+        payload_ref[SLAB:, :] = grad_mixed.astype(BF)
 
 
 def low_onehot(low):
@@ -69,7 +71,7 @@
                    cross_ref, terms_ref, acc_ref):
     rows = nbr_ref.shape[1]
     tiles = acc_ref.shape[0] // SLAB
-    total = (p0[SLAB:, :] + p1[SLAB:, :].astype(F32)) + (
+    total = (p0[...] + p1[SLAB:, :].astype(F32)) + (
         p2[SLAB:, :].astype(F32) + p3[SLAB:, :].astype(F32)
     )
     grad_mixed = total.astype(BF)
@@ -153,7 +155,7 @@
     gc_ref[...] = dot(gm_ref[...], ga_ref[...], NT)
 
 
-def finish_kernel(mix_ref, e0, e1, e2, e3, in_ref, feat_ref, outf_ref, cot_ref, gc_ref,
+def finish_kernel(mix_ref, e0, e2, e1, e3, in_ref, feat_ref, outf_ref, cot_ref, gc_ref,
                   gf_ref, out_ref, keep_ref, give_ref):
     rank = in_ref.shape[1]
     rows = feat_ref.shape[1]
@@ -213,7 +215,7 @@
 
 def leaf_sum(mine, give):
     mine = mine + crossed(give, 1)
-    for masks in ((8,), (2, 4, 6), (16, 32, 48)):
+    for masks in ((8,), (4, 2, 6), (32, 16, 48)):
         mine = mine + sum(crossed(mine, mask) for mask in masks)
     return mine, crossed(mine, 1)
 
@@ -233,21 +235,22 @@
     core_rows = jnp.pad(core, ((0, 0), (0, SLAB - width), (0, 0))).reshape(offsets * SLAB, rank)
     estimate = pl.CostEstimate(flops=5 * 10**9, bytes_accessed=2**20, transcendentals=0)
 
-    payload = pl.pallas_call(
+    own_reduced, own_mixed, *payload = pl.pallas_call(
         project_kernel,
-        out_shape=[struct((SLAB + rank, rows), F32)] + [struct((SLAB + rank, rows), BF)] * 3,
+        out_shape=[struct((SLAB, rows), F32), struct((rank, rows), F32)] + [struct((SLAB + rank, rows), BF)] * 3,
         in_specs=[VMEM] * 4,
-        out_specs=[VMEM] * 4,
+        out_specs=[VMEM] * 5,
         name="project",
     )(features, in_factor, cotangent, out_factor)
-    parts = [payload[0]] + [shifted(payload[j], "chan", j) for j in (1, 2, 3)]
-    reduced = sum(part[:SLAB].astype(F32) for part in parts) * keep
-    reduced = reduced.astype(BF)
+    arrived = {j: shifted(payload[j - 1], "chan", j) for j in (1, 3, 2)}
+    parts = [arrived[1], arrived[3], arrived[2]]
+    reduced = own_reduced + sum(part[:SLAB].astype(F32) for part in parts)
+    reduced = (reduced * keep).astype(BF)
 
     pair = crossed(reduced, 1)
     both, parts = lax.optimization_barrier((jnp.concatenate([reduced, pair], 0), parts))
+    far_pair = outward(both, 2)
     near_pair = outward(both, 1)
-    far_pair = outward(both, 2)
 
     grad_mixed, own, kept, cross = pl.pallas_call(
         scatter_kernel,
@@ -263,10 +266,10 @@
         compiler_params=ROOMY,
         cost_estimate=estimate,
         name="scatter",
-    )(halo, *parts, core_rows, neighbours)
-
-    beyond = crossed(jnp.concatenate([near_pair, far_pair], 0), 1)
-    handed = crossed(cross, 1).astype(F32)
+    )(halo, own_mixed, *parts, core_rows, neighbours)
+
+    swapped = crossed(jnp.concatenate([cross, near_pair, far_pair], 0), 1)
+    handed, beyond = swapped[: 4 * SLAB].astype(F32), swapped[4 * SLAB :]
     own = own + handed[:SLAB]
     to_near = jnp.concatenate(
         [kept[2 * SLAB : 3 * SLAB] + handed[2 * SLAB : 3 * SLAB], kept[3 * SLAB :] + handed[SLAB : 2 * SLAB]], 0
@@ -292,7 +295,7 @@
     last = crossed(returned[SLAB:].astype(BF), 1).astype(F32)
     grad_slab = ((own + returned[:SLAB] + last) * keep).astype(BF)
     shared = jnp.concatenate([grad_slab, mixed_part.astype(BF)], 0)
-    exchanged = [shared] + [shifted(shared, "chan", j) for j in (1, 2, 3)]
+    exchanged = [shared] + [shifted(shared, "chan", j) for j in (2, 1, 3)]
 
     half = struct((rank // 2, packed_width), F32)
     grad_features, output, mine, give = pl.pallas_call(

time: 83.5 us -> 82.8 us (level)
  starting transfers between devices: 38.8 us -> 37.3 us
    ppermute x13 -> x12, waiting for transfers between devices: 12 us -> 14.9 us  [crossed(): lax.ppermute(block, 'leaf', [(i, i ^ mask) for i in range(lax.axis_size('...]
    ppermute x6, waiting for transfers between devices: 13.3 us -> 11.1 us  [shifted(): lax.ppermute(block, axis, [(i, (i + distance) % count) for i in range(cou...]
    ppermute x13 -> x12, starting transfers between devices: 19.7 us -> 18.4 us  [crossed(): lax.ppermute(block, 'leaf', [(i, i ^ mask) for i in range(lax.axis_size('...]
  transfers between devices with their start and end apart: 23 -> 22, of which waited for: 15 -> 15; matrix products, arithmetic and copies ran while one was open for 0% -> 0% of each run, Pallas kernels for 15% -> 16%
where the time goes in v4:
time: 82.8 us; the launch traced here: 82.6 us
  starting transfers between devices  37.3 us (45%)
  waiting for transfers between devices  26 us (31%)
  Pallas kernels  17.2 us (21%)
  other arithmetic  1.1 us (1%)
  between operations  0.86 us (1%)
    ppermute x12, starting transfers between devices, crossed(): lax.ppermute(block, 'leaf', [(i, i ^ mask) for i in range(lax.axis_size('...  18.4 us
    ppermute x12, waiting for transfers between devices, crossed(): lax.ppermute(block, 'leaf', [(i, i ^ mask) for i in range(lax.axis_size('...  14.9 us
    ppermute x6, waiting for transfers between devices, shifted(): lax.ppermute(block, axis, [(i, (i + distance) % count) for i in range(cou...  11.1 us
    ppermute x4, starting transfers between devices, outward(): lax.ppermute(block, 'leaf', [(i, (i + (2 * chips if i % 2 == 0 else -2 *...  9.98 us
    ppermute x6, starting transfers between devices, shifted(): lax.ppermute(block, axis, [(i, (i + distance) % count) for i in range(cou...  8.88 us
    pallas_call x1, Pallas kernels, body(): pl.pallas_call(gather_kernel, out_shape=[struct((rank, rows), F32), struc...  6.5 us
    pallas_call x1, Pallas kernels, body(): pl.pallas_call(scatter_kernel, out_shape=[struct((rank, rows), BF), struc...  6.34 us
    pallas_call x1, Pallas kernels, body(): pl.pallas_call(project_kernel, out_shape=[struct((SLAB, rows), F32), stru...  2.11 us
  transfers between devices with their start and end apart: 22, of which 15 were waited for; matrix products, arithmetic and copies ran while one was open for 0% of the time, Pallas kernels for 16%

profile of v4, /device:TPU:1, one launch (start us, length us, event | category | flops | bytes accessed | tf_op | source)
XLA Modules:
  0.0 82.6 jit_solution(1461341206302114778)
XLA Ops:
  0.6 2.1 %project.1 = (f32[16,1024]{1,0:T(8,128)}, f32[48,1024]{1,0:T(8,128)}, bf16[64,1024]{1,0:T(8,128)(2,1)}, bf16[64,1024]{1,0:T(8,128)(2,1)}, bf16[64,1024]{1,0:T(8,128)(2,1)}) custom-call(bf16[48,1024]{1,0:T(8,128)(2,1)} %feat_ref.3, bf16[48,48]{1,0:T(8,128)(2,1)} %in_ref.3, bf16[48,1024]{1,0:T(8,128)(2,1)} %cot_ref.3, bf16[48,48]{1,0:T(8,128)(2,1)} %outf_ref.3), custom_call_target="tpu_custom_call" | custom-call | tf_op jit(solution)/shard_map/project/pallas_call | solution.py:238
  2.7 2.1 %collective-permute-start = (bf16[64,1024]{1,0:T(8,128)(2,1)}, bf16[64,1024]{1,0:T(8,128)(2,1)S(1)}, u32[]{:S(2)}, u32[]{:S(2)}) collective-permute-start(bf16[64,1024]{1,0:T(8,128)(2,1)} %get-tuple-element.34), channel_id=1, source_target_pairs={{0,1},{1,2},{2,3},{3,0},{4,5},{5,6},{6,7},{7,4},{8,9},{9,10},{10,1... | collective-permute-start | bytes 393224 | tf_op jit(solution)/shard_map/ppermute | solution.py:202
  4.9 1.5 %collective-permute-start.1 = (bf16[64,1024]{1,0:T(8,128)(2,1)}, bf16[64,1024]{1,0:T(8,128)(2,1)S(1)}, u32[]{:S(2)}, u32[]{:S(2)}) collective-permute-start(bf16[64,1024]{1,0:T(8,128)(2,1)} %get-tuple-element.35), channel_id=1, source_target_pairs={{0,3},{1,0},{2,1},{3,2},{4,7},{5,4},{6,5},{7,6},{8,11},{9,8},{10,9... | collective-permute-start | bytes 393224 | tf_op jit(solution)/shard_map/ppermute | solution.py:202
  6.4 1.6 %collective-permute-start.2 = (bf16[64,1024]{1,0:T(8,128)(2,1)}, bf16[64,1024]{1,0:T(8,128)(2,1)S(1)}, u32[]{:S(2)}, u32[]{:S(2)}) collective-permute-start(bf16[64,1024]{1,0:T(8,128)(2,1)} %get-tuple-element.36), channel_id=1, source_target_pairs={{0,2},{1,3},{2,0},{3,1},{4,6},{5,7},{6,4},{7,5},{8,10},{9,11},{10,... | collective-permute-start | bytes 393224 | tf_op jit(solution)/shard_map/ppermute | solution.py:202
  8.0 0.9 %collective-permute-done.p1 = bf16[64,1024]{1,0:T(8,128)(2,1)S(1)} collective-permute-done((bf16[64,1024]{1,0:T(8,128)(2,1)}, bf16[64,1024]{1,0:T(8,128)(2,1)S(1)}, u32[]{:S(2)}, u32[]{:S(2)}) %collective-permute-start) | collective-permute-done | bytes 131104 | tf_op jit(solution)/shard_map/ppermute | solution.py:202
  8.9 4.0 %collective-permute-done.2.p3 = bf16[64,1024]{1,0:T(8,128)(2,1)S(1)} collective-permute-done((bf16[64,1024]{1,0:T(8,128)(2,1)}, bf16[64,1024]{1,0:T(8,128)(2,1)S(1)}, u32[]{:S(2)}, u32[]{:S(2)}) %collective-permute-start.2) | collective-permute-done | bytes 131104 | tf_op jit(solution)/shard_map/ppermute | solution.py:202
  12.9 0.9 %multiply_convert_fusion.own_ref = bf16[16,1024]{1,0:T(8,128)(2,1)S(1)} fusion(f32[16,1024]{1,0:T(8,128)} %get-tuple-element.33, bf16[64,1024]{1,0:T(8,128)(2,1)S(1)} %collective-permute-done.2.p3, bf16[64,1024]{1,0:T(8,128)(2,1)S(1)} %collective-permute-done.1.p2, bf16[64,1024]{1,0:T(8,128)(2,1)S(1)} %collective-permute-done.p1, ...), kind=kLoop, calls=%fused_computation.20 | loop fusion | flops 131072 | bytes 200704 | tf_op jit(solution)/shard_map/convert_element_type | solution.py:248
  13.8 3.1 %collective-permute-start.3 = (bf16[16,1024]{1,0:T(8,128)(2,1)S(1)}, bf16[16,1024]{1,0:T(8,128)(2,1)S(1)}, u32[]{:S(2)}, u32[]{:S(2)}) collective-permute-start(bf16[16,1024]{1,0:T(8,128)(2,1)S(1)} %multiply_convert_fusion.own_ref), channel_id=1, source_target_pairs={{0,4},{4,0},{8,12},{12,8},{16,20},{20,16},{24,28},{28,24},{32,36},... | collective-permute-start | bytes 98312 | tf_op jit(solution)/shard_map/ppermute | solution.py:206
  17.8 6.8 %collective-permute-start.4 = (bf16[32,1024]{1,0:T(8,128)(2,1)S(1)}, bf16[32,1024]{1,0:T(8,128)(2,1)S(1)}, u32[]{:S(2)}, u32[]{:S(2)}) collective-permute-start(bf16[32,1024]{1,0:T(8,128)(2,1)S(1)} %pad_maximum_fusion.2), channel_id=1, source_target_pairs={{0,8},{4,252},{8,16},{12,4},{16,24},{20,12},{24,32},{28,20},{32,40... | collective-permute-start | bytes 196616 | tf_op jit(solution)/shard_map/ppermute | solution.py:211
  25.1 6.3 %scatter.1 = (bf16[48,1024]{1,0:T(8,128)(2,1)S(1)}, f32[16,1024]{1,0:T(8,128)S(1)}, f32[64,1024]{1,0:T(8,128)S(1)}, bf16[64,1024]{1,0:T(8,128)(2,1)S(1)}) custom-call(s32[8,8]{1,0:T(8,128)S(1)} %bitcast.5, f32[48,1024]{1,0:T(8,128)S(1)} %copy-done.4, bf16[64,1024]{1,0:T(8,128)(2,1)S(1)} %collective-permute-done.p1, ...), custom_call_target="tpu_custom_call" | custom-call | flops 5000000000 | bytes 1048576 | tf_op jit(solution)/shard_map/scatter/pallas_call | solution.py:255
  31.6 1.5 %collective-permute-done.6 = bf16[128,1024]{1,0:T(8,128)(2,1)S(1)} collective-permute-done((bf16[128,1024]{1,0:T(8,128)(2,1)S(1)}, bf16[128,1024]{1,0:T(8,128)(2,1)S(1)}, u32[]{:S(2)}, u32[]{:S(2)}) %collective-permute-start.6) | collective-permute-done | bytes 262176 | tf_op jit(solution)/shard_map/ppermute | solution.py:206
  33.9 1.9 %collective-permute-start.8 = (bf16[32,1024]{1,0:T(8,128)(2,1)S(1)}, bf16[32,1024]{1,0:T(8,128)(2,1)S(1)}, u32[]{:S(2)}, u32[]{:S(2)}) collective-permute-start(bf16[32,1024]{1,0:T(8,128)(2,1)S(1)} %get-tuple-element.48), channel_id=1, source_target_pairs={{0,240},{4,20},{8,248},{12,28},{16,0},{20,36},{24,8},{28,44},{32,1... | collective-permute-start | bytes 196616 | tf_op jit(solution)/shard_map/ppermute | solution.py:211
  35.9 6.5 %gather.1 = (f32[48,1024]{1,0:T(8,128)S(1)}, f32[48,512]{1,0:T(8,128)S(1)}) custom-call(s32[8,8]{1,0:T(8,128)S(1)} %bitcast.6, bf16[16,1024]{1,0:T(8,128)(2,1)S(1)} %multiply_convert_fusion.own_ref, bf16[16,1024]{1,0:T(8,128)(2,1)S(1)} %collective-permute-done.3.pair_ref, bf16[32,1024]{1,0:T(8,128)(2,1)S(1)} %collective-permute-done.4.near_ref, ...), custom_call_target="tpu_custom_call" | custom-call | flops 5000000000 | bytes 1048576 | tf_op jit(solution)/shard_map/gather/pallas_call | solution.py:282
  42.4 1.1 %collective-permute-start.9 = (bf16[16,1024]{1,0:T(8,128)(2,1)S(1)}, bf16[16,1024]{1,0:T(8,128)(2,1)S(1)}, u32[]{:S(2)}, u32[]{:S(2)}) collective-permute-start(bf16[16,1024]{1,0:T(8,128)(2,1)S(1)} %slice.102), channel_id=1, source_target_pairs={{0,4},{4,0},{8,12},{12,8},{16,20},{20,16},{24,28},{28,24},{32,36},... | collective-permute-start | bytes 98312 | tf_op jit(solution)/shard_map/ppermute | solution.py:206
  44.5 1.0 %collective-permute-start.10 = (bf16[64,1024]{1,0:T(8,128)(2,1)S(1)}, bf16[64,1024]{1,0:T(8,128)(2,1)S(1)}, u32[]{:S(2)}, u32[]{:S(2)}) collective-permute-start(bf16[64,1024]{1,0:T(8,128)(2,1)S(1)} %pad_maximum_fusion.1.e0), channel_id=1, source_target_pairs={{0,2},{1,3},{2,0},{3,1},{4,6},{5,7},{6,4},{7,5},{8,10},{9,11},{10,... | collective-permute-start | bytes 393224 | tf_op jit(solution)/shard_map/ppermute | solution.py:202
  45.5 1.2 %collective-permute-start.11 = (bf16[64,1024]{1,0:T(8,128)(2,1)S(1)}, bf16[64,1024]{1,0:T(8,128)(2,1)S(1)}, u32[]{:S(2)}, u32[]{:S(2)}) collective-permute-start(bf16[64,1024]{1,0:T(8,128)(2,1)S(1)} %pad_maximum_fusion.1.e0), channel_id=1, source_target_pairs={{0,1},{1,2},{2,3},{3,0},{4,5},{5,6},{6,7},{7,4},{8,9},{9,10},{10,1... | collective-permute-start | bytes 393224 | tf_op jit(solution)/shard_map/ppermute | solution.py:202
  46.7 1.5 %collective-permute-start.12 = (bf16[64,1024]{1,0:T(8,128)(2,1)S(1)}, bf16[64,1024]{1,0:T(8,128)(2,1)S(1)}, u32[]{:S(2)}, u32[]{:S(2)}) collective-permute-start(bf16[64,1024]{1,0:T(8,128)(2,1)S(1)} %pad_maximum_fusion.1.e0), channel_id=1, source_target_pairs={{0,3},{1,0},{2,1},{3,2},{4,7},{5,4},{6,5},{7,6},{8,11},{9,8},{10,9... | collective-permute-start | bytes 393224 | tf_op jit(solution)/shard_map/ppermute | solution.py:202
  48.1 2.6 %collective-permute-done.10.e2 = bf16[64,1024]{1,0:T(8,128)(2,1)S(1)} collective-permute-done((bf16[64,1024]{1,0:T(8,128)(2,1)S(1)}, bf16[64,1024]{1,0:T(8,128)(2,1)S(1)}, u32[]{:S(2)}, u32[]{:S(2)}) %collective-permute-start.10) | collective-permute-done | bytes 131104 | tf_op jit(solution)/shard_map/ppermute | solution.py:202
  50.8 3.5 %collective-permute-done.11.e1 = bf16[64,1024]{1,0:T(8,128)(2,1)S(1)} collective-permute-done((bf16[64,1024]{1,0:T(8,128)(2,1)S(1)}, bf16[64,1024]{1,0:T(8,128)(2,1)S(1)}, u32[]{:S(2)}, u32[]{:S(2)}) %collective-permute-start.11) | collective-permute-done | bytes 131104 | tf_op jit(solution)/shard_map/ppermute | solution.py:202
  54.3 1.4 %finish.1 = (bf16[48,1024]{1,0:T(8,128)(2,1)}, bf16[48,1024]{1,0:T(8,128)(2,1)}, f32[24,512]{1,0:T(8,128)S(1)}, f32[24,512]{1,0:T(8,128)S(1)}) custom-call(f32[48,1024]{1,0:T(8,128)S(1)} %get-tuple-element.49.mix_ref, bf16[64,1024]{1,0:T(8,128)(2,1)S(1)} %pad_maximum_fusion.1.e0, bf16[64,1024]{1,0:T(8,128)(2,1)S(1)} %collective-permute-done.10.e2, ...), custom_call_target="tpu_custom_call" | custom-call | tf_op jit(solution)/shard_map/finish/pallas_call | solution.py:301
  56.3 0.9 %collective-permute-done.13 = f32[24,512]{1,0:T(8,128)S(1)} collective-permute-done((f32[24,512]{1,0:T(8,128)S(1)}, f32[24,512]{1,0:T(8,128)S(1)}, u32[]{:S(2)}, u32[]{:S(2)}) %collective-permute-start.13) | collective-permute-done | bytes 49184 | tf_op jit(solution)/shard_map/ppermute | solution.py:206
  58.0 2.2 %collective-permute-done.14 = f32[24,512]{1,0:T(8,128)S(1)} collective-permute-done((f32[24,512]{1,0:T(8,128)S(1)}, f32[24,512]{1,0:T(8,128)S(1)}, u32[]{:S(2)}, u32[]{:S(2)}) %collective-permute-start.14) | collective-permute-done | bytes 49184 | tf_op jit(solution)/shard_map/ppermute | solution.py:206
  60.2 1.1 %collective-permute-start.15 = (f32[24,512]{1,0:T(8,128)S(1)}, f32[24,512]{1,0:T(8,128)S(1)}, u32[]{:S(2)}, u32[]{:S(2)}) collective-permute-start(f32[24,512]{1,0:T(8,128)S(1)} %add.67), channel_id=1, source_target_pairs={{0,16},{4,20},{8,24},{12,28},{16,0},{20,4},{24,8},{28,12},{32,48},... | collective-permute-start | bytes 147464 | tf_op jit(solution)/shard_map/ppermute | solution.py:206
  61.9 1.7 %collective-permute-start.17 = (f32[24,512]{1,0:T(8,128)S(1)}, f32[24,512]{1,0:T(8,128)S(1)}, u32[]{:S(2)}, u32[]{:S(2)}) collective-permute-start(f32[24,512]{1,0:T(8,128)S(1)} %add.67), channel_id=1, source_target_pairs={{0,24},{4,28},{8,16},{12,20},{16,8},{20,12},{24,0},{28,4},{32,56},... | collective-permute-start | bytes 147464 | tf_op jit(solution)/shard_map/ppermute | solution.py:206
  63.6 1.1 %collective-permute-done.15 = f32[24,512]{1,0:T(8,128)S(1)} collective-permute-done((f32[24,512]{1,0:T(8,128)S(1)}, f32[24,512]{1,0:T(8,128)S(1)}, u32[]{:S(2)}, u32[]{:S(2)}) %collective-permute-start.15) | collective-permute-done | bytes 49184 | tf_op jit(solution)/shard_map/ppermute | solution.py:206
  64.7 1.3 %collective-permute-done.17 = f32[24,512]{1,0:T(8,128)S(1)} collective-permute-done((f32[24,512]{1,0:T(8,128)S(1)}, f32[24,512]{1,0:T(8,128)S(1)}, u32[]{:S(2)}, u32[]{:S(2)}) %collective-permute-start.17) | collective-permute-done | bytes 49184 | tf_op jit(solution)/shard_map/ppermute | solution.py:206
  66.0 5.0 %collective-permute-start.18 = (f32[24,512]{1,0:T(8,128)S(1)}, f32[24,512]{1,0:T(8,128)S(1)}, u32[]{:S(2)}, u32[]{:S(2)}) collective-permute-start(f32[24,512]{1,0:T(8,128)S(1)} %add_add_fusion.1), channel_id=1, source_target_pairs={{0,128},{4,132},{8,136},{12,140},{16,144},{20,148},{24,152},{28,15... | collective-permute-start | bytes 147464 | tf_op jit(solution)/shard_map/ppermute | solution.py:206
  71.8 1.3 %collective-permute-done.18 = f32[24,512]{1,0:T(8,128)S(1)} collective-permute-done((f32[24,512]{1,0:T(8,128)S(1)}, f32[24,512]{1,0:T(8,128)S(1)}, u32[]{:S(2)}, u32[]{:S(2)}) %collective-permute-start.18) | collective-permute-done | bytes 49184 | tf_op jit(solution)/shard_map/ppermute | solution.py:206
  73.1 2.0 %collective-permute-done.19 = f32[24,512]{1,0:T(8,128)S(1)} collective-permute-done((f32[24,512]{1,0:T(8,128)S(1)}, f32[24,512]{1,0:T(8,128)S(1)}, u32[]{:S(2)}, u32[]{:S(2)}) %collective-permute-start.19) | collective-permute-done | bytes 49184 | tf_op jit(solution)/shard_map/ppermute | solution.py:206
  75.1 2.0 %collective-permute-done.20 = f32[24,512]{1,0:T(8,128)S(1)} collective-permute-done((f32[24,512]{1,0:T(8,128)S(1)}, f32[24,512]{1,0:T(8,128)S(1)}, u32[]{:S(2)}, u32[]{:S(2)}) %collective-permute-start.20) | collective-permute-done | bytes 49184 | tf_op jit(solution)/shard_map/ppermute | solution.py:206
  77.2 3.7 %collective-permute-start.21 = (f32[24,512]{1,0:T(8,128)S(1)}, f32[24,512]{1,0:T(8,128)S(1)}, u32[]{:S(2)}, u32[]{:S(2)}) collective-permute-start(f32[24,512]{1,0:T(8,128)S(1)} %add_add_fusion.refs_0_), channel_id=1, source_target_pairs={{0,4},{4,0},{8,12},{12,8},{16,20},{20,16},{24,28},{28,24},{32,36},... | collective-permute-start | bytes 147464 | tf_op jit(solution)/shard_map/ppermute | solution.py:206
  80.9 0.9 %collective-permute-done.21.refs_1_ = f32[24,512]{1,0:T(8,128)S(1)} collective-permute-done((f32[24,512]{1,0:T(8,128)S(1)}, f32[24,512]{1,0:T(8,128)S(1)}, u32[]{:S(2)}, u32[]{:S(2)}) %collective-permute-start.21) | collective-permute-done | bytes 49184 | tf_op jit(solution)/shard_map/ppermute | solution.py:206
  (54 shorter events, 6.8 us)
Async XLA Ops:
  2.7 5.2 %copy-start.8 = (s32[1024]{0:T(1024)S(1)}, s32[1024]{0:T(1024)}, u32[]{:S(2)}) copy-start(s32[1024]{0:T(1024)} %param.14) | copy-start | bytes 12292
  2.7 6.1 %collective-permute-start = (bf16[64,1024]{1,0:T(8,128)(2,1)}, bf16[64,1024]{1,0:T(8,128)(2,1)S(1)}, u32[]{:S(2)}, u32[]{:S(2)}) collective-permute-start(bf16[64,1024]{1,0:T(8,128)(2,1)} %get-tuple-element.34), channel_id=1, source_target_pairs={{0,1},{1,2},{2,3},{3,0},{4,5},{5,6},{6,7},{7,4},{8,9},{9,10},{10,1... | collective-permute-start | bytes 393224 | tf_op jit(solution)/shard_map/ppermute | solution.py:202
  4.9 4.0 %collective-permute-start.1 = (bf16[64,1024]{1,0:T(8,128)(2,1)}, bf16[64,1024]{1,0:T(8,128)(2,1)S(1)}, u32[]{:S(2)}, u32[]{:S(2)}) collective-permute-start(bf16[64,1024]{1,0:T(8,128)(2,1)} %get-tuple-element.35), channel_id=1, source_target_pairs={{0,3},{1,0},{2,1},{3,2},{4,7},{5,4},{6,5},{7,6},{8,11},{9,8},{10,9... | collective-permute-start | bytes 393224 | tf_op jit(solution)/shard_map/ppermute | solution.py:202
  6.4 6.5 %collective-permute-start.2 = (bf16[64,1024]{1,0:T(8,128)(2,1)}, bf16[64,1024]{1,0:T(8,128)(2,1)S(1)}, u32[]{:S(2)}, u32[]{:S(2)}) collective-permute-start(bf16[64,1024]{1,0:T(8,128)(2,1)} %get-tuple-element.36), channel_id=1, source_target_pairs={{0,2},{1,3},{2,0},{3,1},{4,6},{5,7},{6,4},{7,5},{8,10},{9,11},{10,... | collective-permute-start | bytes 393224 | tf_op jit(solution)/shard_map/ppermute | solution.py:202
  12.9 4.0 %copy-start.7 = (bf16[27,12,48]{2,0,1:T(8,128)(2,1)S(1)}, bf16[27,12,48]{2,0,1:T(8,128)(2,1)}, u32[]{:S(2)}) copy-start(bf16[27,12,48]{2,0,1:T(8,128)(2,1)} %param.10) | copy-start | bytes 93316
  13.8 3.9 %collective-permute-start.3 = (bf16[16,1024]{1,0:T(8,128)(2,1)S(1)}, bf16[16,1024]{1,0:T(8,128)(2,1)S(1)}, u32[]{:S(2)}, u32[]{:S(2)}) collective-permute-start(bf16[16,1024]{1,0:T(8,128)(2,1)S(1)} %multiply_convert_fusion.own_ref), channel_id=1, source_target_pairs={{0,4},{4,0},{8,12},{12,8},{16,20},{20,16},{24,28},{28,24},{32,36},... | collective-permute-start | bytes 98312 | tf_op jit(solution)/shard_map/ppermute | solution.py:206
  16.9 8.2 %copy-start.4 = (f32[48,1024]{1,0:T(8,128)S(1)}, f32[48,1024]{1,0:T(8,128)}, u32[]{:S(2)}) copy-start(f32[48,1024]{1,0:T(8,128)} %get-tuple-element.38.p0) | copy-start | bytes 589828
  16.9 8.2 %copy-start.5 = (s32[27,1024]{1,0:T(8,128)S(1)}, s32[27,1024]{1,0:T(8,128)}, u32[]{:S(2)}) copy-start(s32[27,1024]{1,0:T(8,128)} %nbr_ref.3) | copy-start | bytes 331780
  17.8 7.4 %copy-start.6 = (s32[1,8,8]{2,1,0:T(8,128)S(1)}, s32[1,8,8]{2,1,0:T(8,128)}, u32[]{:S(2)}) copy-start(s32[1,8,8]{2,1,0:T(8,128)} %param.13) | copy-start | bytes 772
  17.8 13.7 %collective-permute-start.4 = (bf16[32,1024]{1,0:T(8,128)(2,1)S(1)}, bf16[32,1024]{1,0:T(8,128)(2,1)S(1)}, u32[]{:S(2)}, u32[]{:S(2)}) collective-permute-start(bf16[32,1024]{1,0:T(8,128)(2,1)S(1)} %pad_maximum_fusion.2), channel_id=1, source_target_pairs={{0,8},{4,252},{8,16},{12,4},{16,24},{20,12},{24,32},{28,20},{32,40... | collective-permute-start | bytes 196616 | tf_op jit(solution)/shard_map/ppermute | solution.py:211
  24.6 6.9 %collective-permute-start.5 = (bf16[32,1024]{1,0:T(8,128)(2,1)S(1)}, bf16[32,1024]{1,0:T(8,128)(2,1)S(1)}, u32[]{:S(2)}, u32[]{:S(2)}) collective-permute-start(bf16[32,1024]{1,0:T(8,128)(2,1)S(1)} %pad_maximum_fusion.2), channel_id=1, source_target_pairs={{0,16},{4,244},{8,24},{12,252},{16,32},{20,4},{24,40},{28,12},{32,... | collective-permute-start | bytes 196616 | tf_op jit(solution)/shard_map/ppermute | solution.py:211
  31.5 1.6 %collective-permute-start.6 = (bf16[128,1024]{1,0:T(8,128)(2,1)S(1)}, bf16[128,1024]{1,0:T(8,128)(2,1)S(1)}, u32[]{:S(2)}, u32[]{:S(2)}) collective-permute-start(bf16[128,1024]{1,0:T(8,128)(2,1)S(1)} %pad_maximum_fusion), channel_id=1, source_target_pairs={{0,4},{4,0},{8,12},{12,8},{16,20},{20,16},{24,28},{28,24},{32,36},... | collective-permute-start | bytes 786440 | tf_op jit(solution)/shard_map/ppermute | solution.py:206
  33.2 9.1 %collective-permute-start.7 = (bf16[32,1024]{1,0:T(8,128)(2,1)S(1)}, bf16[32,1024]{1,0:T(8,128)(2,1)S(1)}, u32[]{:S(2)}, u32[]{:S(2)}) collective-permute-start(bf16[32,1024]{1,0:T(8,128)(2,1)S(1)} %get-tuple-element.47), channel_id=1, source_target_pairs={{0,248},{4,12},{8,0},{12,20},{16,8},{20,28},{24,16},{28,36},{32,24... | collective-permute-start | bytes 196616 | tf_op jit(solution)/shard_map/ppermute | solution.py:211
  33.9 8.4 %collective-permute-start.8 = (bf16[32,1024]{1,0:T(8,128)(2,1)S(1)}, bf16[32,1024]{1,0:T(8,128)(2,1)S(1)}, u32[]{:S(2)}, u32[]{:S(2)}) collective-permute-start(bf16[32,1024]{1,0:T(8,128)(2,1)S(1)} %get-tuple-element.48), channel_id=1, source_target_pairs={{0,240},{4,20},{8,248},{12,28},{16,0},{20,36},{24,8},{28,44},{32,1... | collective-permute-start | bytes 196616 | tf_op jit(solution)/shard_map/ppermute | solution.py:211
  42.4 1.9 %collective-permute-start.9 = (bf16[16,1024]{1,0:T(8,128)(2,1)S(1)}, bf16[16,1024]{1,0:T(8,128)(2,1)S(1)}, u32[]{:S(2)}, u32[]{:S(2)}) collective-permute-start(bf16[16,1024]{1,0:T(8,128)(2,1)S(1)} %slice.102), channel_id=1, source_target_pairs={{0,4},{4,0},{8,12},{12,8},{16,20},{20,16},{24,28},{28,24},{32,36},... | collective-permute-start | bytes 98312 | tf_op jit(solution)/shard_map/ppermute | solution.py:206
  44.4 9.9 %copy-start = (bf16[48,1024]{1,0:T(8,128)(2,1)S(1)}, bf16[48,1024]{1,0:T(8,128)(2,1)}, u32[]{:S(2)}) copy-start(bf16[48,1024]{1,0:T(8,128)(2,1)} %feat_ref.3) | copy-start | bytes 294916
  44.4 9.9 %copy-start.1 = (bf16[48,1024]{1,0:T(8,128)(2,1)S(1)}, bf16[48,1024]{1,0:T(8,128)(2,1)}, u32[]{:S(2)}) copy-start(bf16[48,1024]{1,0:T(8,128)(2,1)} %cot_ref.3) | copy-start | bytes 294916
  44.4 9.9 %copy-start.2 = (bf16[48,48]{1,0:T(8,128)(2,1)S(1)}, bf16[48,48]{1,0:T(8,128)(2,1)}, u32[]{:S(2)}) copy-start(bf16[48,48]{1,0:T(8,128)(2,1)} %in_ref.3) | copy-start | bytes 13828
  44.4 9.9 %copy-start.3 = (bf16[48,48]{1,0:T(8,128)(2,1)S(1)}, bf16[48,48]{1,0:T(8,128)(2,1)}, u32[]{:S(2)}) copy-start(bf16[48,48]{1,0:T(8,128)(2,1)} %outf_ref.3) | copy-start | bytes 13828
  44.5 6.3 %collective-permute-start.10 = (bf16[64,1024]{1,0:T(8,128)(2,1)S(1)}, bf16[64,1024]{1,0:T(8,128)(2,1)S(1)}, u32[]{:S(2)}, u32[]{:S(2)}) collective-permute-start(bf16[64,1024]{1,0:T(8,128)(2,1)S(1)} %pad_maximum_fusion.1.e0), channel_id=1, source_target_pairs={{0,2},{1,3},{2,0},{3,1},{4,6},{5,7},{6,4},{7,5},{8,10},{9,11},{10,... | collective-permute-start | bytes 393224 | tf_op jit(solution)/shard_map/ppermute | solution.py:202
  45.5 8.8 %collective-permute-start.11 = (bf16[64,1024]{1,0:T(8,128)(2,1)S(1)}, bf16[64,1024]{1,0:T(8,128)(2,1)S(1)}, u32[]{:S(2)}, u32[]{:S(2)}) collective-permute-start(bf16[64,1024]{1,0:T(8,128)(2,1)S(1)} %pad_maximum_fusion.1.e0), channel_id=1, source_target_pairs={{0,1},{1,2},{2,3},{3,0},{4,5},{5,6},{6,7},{7,4},{8,9},{9,10},{10,1... | collective-permute-start | bytes 393224 | tf_op jit(solution)/shard_map/ppermute | solution.py:202
  46.7 7.6 %collective-permute-start.12 = (bf16[64,1024]{1,0:T(8,128)(2,1)S(1)}, bf16[64,1024]{1,0:T(8,128)(2,1)S(1)}, u32[]{:S(2)}, u32[]{:S(2)}) collective-permute-start(bf16[64,1024]{1,0:T(8,128)(2,1)S(1)} %pad_maximum_fusion.1.e0), channel_id=1, source_target_pairs={{0,3},{1,0},{2,1},{3,2},{4,7},{5,4},{6,5},{7,6},{8,11},{9,8},{10,9... | collective-permute-start | bytes 393224 | tf_op jit(solution)/shard_map/ppermute | solution.py:202
  55.8 1.4 %collective-permute-start.13 = (f32[24,512]{1,0:T(8,128)S(1)}, f32[24,512]{1,0:T(8,128)S(1)}, u32[]{:S(2)}, u32[]{:S(2)}) collective-permute-start(f32[24,512]{1,0:T(8,128)S(1)} %get-tuple-element.57), channel_id=1, source_target_pairs={{0,4},{4,0},{8,12},{12,8},{16,20},{20,16},{24,28},{28,24},{32,36},... | collective-permute-start | bytes 147464 | tf_op jit(solution)/shard_map/ppermute | solution.py:206
  57.2 3.0 %collective-permute-start.14 = (f32[24,512]{1,0:T(8,128)S(1)}, f32[24,512]{1,0:T(8,128)S(1)}, u32[]{:S(2)}, u32[]{:S(2)}) collective-permute-start(f32[24,512]{1,0:T(8,128)S(1)} %add.66), channel_id=1, source_target_pairs={{0,32},{4,36},{8,40},{12,44},{16,48},{20,52},{24,56},{28,60},{32,0... | collective-permute-start | bytes 147464 | tf_op jit(solution)/shard_map/ppermute | solution.py:206
  60.2 4.5 %collective-permute-start.15 = (f32[24,512]{1,0:T(8,128)S(1)}, f32[24,512]{1,0:T(8,128)S(1)}, u32[]{:S(2)}, u32[]{:S(2)}) collective-permute-start(f32[24,512]{1,0:T(8,128)S(1)} %add.67), channel_id=1, source_target_pairs={{0,16},{4,20},{8,24},{12,28},{16,0},{20,4},{24,8},{28,12},{32,48},... | collective-permute-start | bytes 147464 | tf_op jit(solution)/shard_map/ppermute | solution.py:206
  61.3 3.5 %collective-permute-start.16 = (f32[24,512]{1,0:T(8,128)S(1)}, f32[24,512]{1,0:T(8,128)S(1)}, u32[]{:S(2)}, u32[]{:S(2)}) collective-permute-start(f32[24,512]{1,0:T(8,128)S(1)} %add.67), channel_id=1, source_target_pairs={{0,8},{4,12},{8,0},{12,4},{16,24},{20,28},{24,16},{28,20},{32,40},... | collective-permute-start | bytes 147464 | tf_op jit(solution)/shard_map/ppermute | solution.py:206
  61.9 4.2 %collective-permute-start.17 = (f32[24,512]{1,0:T(8,128)S(1)}, f32[24,512]{1,0:T(8,128)S(1)}, u32[]{:S(2)}, u32[]{:S(2)}) collective-permute-start(f32[24,512]{1,0:T(8,128)S(1)} %add.67), channel_id=1, source_target_pairs={{0,24},{4,28},{8,16},{12,20},{16,8},{20,12},{24,0},{28,4},{32,56},... | collective-permute-start | bytes 147464 | tf_op jit(solution)/shard_map/ppermute | solution.py:206
  66.0 7.0 %collective-permute-start.18 = (f32[24,512]{1,0:T(8,128)S(1)}, f32[24,512]{1,0:T(8,128)S(1)}, u32[]{:S(2)}, u32[]{:S(2)}) collective-permute-start(f32[24,512]{1,0:T(8,128)S(1)} %add_add_fusion.1), channel_id=1, source_target_pairs={{0,128},{4,132},{8,136},{12,140},{16,144},{20,148},{24,152},{28,15... | collective-permute-start | bytes 147464 | tf_op jit(solution)/shard_map/ppermute | solution.py:206
  71.1 4.1 %collective-permute-start.19 = (f32[24,512]{1,0:T(8,128)S(1)}, f32[24,512]{1,0:T(8,128)S(1)}, u32[]{:S(2)}, u32[]{:S(2)}) collective-permute-start(f32[24,512]{1,0:T(8,128)S(1)} %add_add_fusion.1), channel_id=1, source_target_pairs={{0,64},{4,68},{8,72},{12,76},{16,80},{20,84},{24,88},{28,92},{32,9... | collective-permute-start | bytes 147464 | tf_op jit(solution)/shard_map/ppermute | solution.py:206
  71.1 6.1 %collective-permute-start.20 = (f32[24,512]{1,0:T(8,128)S(1)}, f32[24,512]{1,0:T(8,128)S(1)}, u32[]{:S(2)}, u32[]{:S(2)}) collective-permute-start(f32[24,512]{1,0:T(8,128)S(1)} %add_add_fusion.1), channel_id=1, source_target_pairs={{0,192},{4,196},{8,200},{12,204},{16,208},{20,212},{24,216},{28,22... | collective-permute-start | bytes 147464 | tf_op jit(solution)/shard_map/ppermute | solution.py:206
  77.2 4.6 %collective-permute-start.21 = (f32[24,512]{1,0:T(8,128)S(1)}, f32[24,512]{1,0:T(8,128)S(1)}, u32[]{:S(2)}, u32[]{:S(2)}) collective-permute-start(f32[24,512]{1,0:T(8,128)S(1)} %add_add_fusion.refs_0_), channel_id=1, source_target_pairs={{0,4},{4,0},{8,12},{12,8},{16,20},{20,16},{24,28},{28,24},{32,36},... | collective-permute-start | bytes 147464 | tf_op jit(solution)/shard_map/ppermute | solution.py:206

commit v5 on v4

--- a/solution.py
+++ b/solution.py
@@ -33,7 +33,8 @@
     return jnp.where(hit, 1.0, 0.0).astype(BF)
 
 
-def project_kernel(feat_ref, in_ref, cot_ref, outf_ref, own_reduced_ref, own_mixed_ref, *payload_refs):
+def project_kernel(feat_ref, in_ref, cot_ref, outf_ref, own_reduced_ref, own_mixed_ref, mixed_ref,
+                   *payload_refs):
     group_count = 1 + len(payload_refs)
     rank = in_ref.shape[1]
     width = rank // group_count
@@ -44,8 +45,8 @@
     own_reduced_ref[...] = reduced[:SLAB]
     own_mixed_ref[...] = grad_mixed
     for j, payload_ref in enumerate(payload_refs):
-        payload_ref[0:SLAB, :] = reduced[(j + 1) * SLAB : (j + 2) * SLAB].astype(BF)
-        payload_ref[SLAB:, :] = grad_mixed.astype(BF)
+        payload_ref[...] = reduced[(j + 1) * SLAB : (j + 2) * SLAB].astype(BF)
+    mixed_ref[...] = grad_mixed.astype(BF)
 
 
 def low_onehot(low):
@@ -71,9 +72,7 @@
                    cross_ref, terms_ref, acc_ref):
     rows = nbr_ref.shape[1]
     tiles = acc_ref.shape[0] // SLAB
-    total = (p0[...] + p1[SLAB:, :].astype(F32)) + (
-        p2[SLAB:, :].astype(F32) + p3[SLAB:, :].astype(F32)
-    )
+    total = (p0[...] + p1[...].astype(F32)) + (p2[...].astype(F32) + p3[...].astype(F32))
     grad_mixed = total.astype(BF)
     gm_ref[...] = grad_mixed
     terms_ref[...] = dot(core_ref[...], grad_mixed).astype(BF)
@@ -90,13 +89,16 @@
         acc_ref[...] += dot(spread, onehot, NT)
         return carry
 
-    lax.fori_loop(0, nbr_ref.shape[0], step, 0, unroll=9)
+    offsets = nbr_ref.shape[0]
+    middle = offsets // 2
+    lax.fori_loop(0, offsets - 1, lambda i, carry: step(i + (i >= middle), carry), 0, unroll=13)
 
     def tile(t):
         return acc_ref[pl.ds(pl.multiple_of(t * SLAB, SLAB), SLAB), :]
 
     own_tiles = rows // LOW
-    own_ref[...] = jnp.concatenate([tile(t) for t in range(own_tiles)], 1)
+    itself = terms_ref[middle * SLAB : (middle + 1) * SLAB, :].astype(F32)
+    own_ref[...] = jnp.concatenate([tile(t) for t in range(own_tiles)], 1) + itself
     near = halo_ref.shape[0]
     per_peer = (tiles - own_tiles) // near
     blank = jnp.zeros((SLAB, rows - per_peer * LOW), F32)
@@ -148,14 +150,17 @@
         ga_ref[pl.ds(pl.multiple_of(k * SLAB, SLAB), SLAB), :] = found.astype(BF)
         return carry
 
-    lax.fori_loop(0, nbr_ref.shape[0], step, 0, unroll=9)
+    offsets = nbr_ref.shape[0]
+    middle = offsets // 2
+    lax.fori_loop(0, offsets - 1, lambda i, carry: step(i + (i >= middle), carry), 0, unroll=13)
+    ga_ref[middle * SLAB : (middle + 1) * SLAB, :] = own_ref[...]
     used = core_ref.shape[0]
     ga_ref[used:, :] = jnp.zeros_like(ga_ref[used:, :])
     mix_ref[...] = dot(core_ref[...], ga_ref[:used, :], TN)
     gc_ref[...] = dot(gm_ref[...], ga_ref[...], NT)
 
 
-def finish_kernel(mix_ref, e0, e2, e1, e3, in_ref, feat_ref, outf_ref, cot_ref, gc_ref,
+def finish_kernel(mix_ref, e0, e1, e3, e2, in_ref, feat_ref, outf_ref, cot_ref, gc_ref,
                   gf_ref, out_ref, keep_ref, give_ref):
     rank = in_ref.shape[1]
     rows = feat_ref.shape[1]
@@ -215,7 +220,7 @@
 
 def leaf_sum(mine, give):
     mine = mine + crossed(give, 1)
-    for masks in ((8,), (4, 2, 6), (32, 16, 48)):
+    for masks in ((8,), (2, 6, 4), (16, 48, 32)):
         mine = mine + sum(crossed(mine, mask) for mask in masks)
     return mine, crossed(mine, 1)
 
@@ -235,20 +240,21 @@
     core_rows = jnp.pad(core, ((0, 0), (0, SLAB - width), (0, 0))).reshape(offsets * SLAB, rank)
     estimate = pl.CostEstimate(flops=5 * 10**9, bytes_accessed=2**20, transcendentals=0)
 
-    own_reduced, own_mixed, *payload = pl.pallas_call(
+    slab = struct((SLAB, rows), BF)
+    own_reduced, own_mixed, sent_mixed, *payload = pl.pallas_call(
         project_kernel,
-        out_shape=[struct((SLAB, rows), F32), struct((rank, rows), F32)] + [struct((SLAB + rank, rows), BF)] * 3,
+        out_shape=[struct((SLAB, rows), F32), struct((rank, rows), F32), struct((rank, rows), BF)] + [slab] * 3,
         in_specs=[VMEM] * 4,
-        out_specs=[VMEM] * 5,
+        out_specs=[VMEM] * 6,
         name="project",
     )(features, in_factor, cotangent, out_factor)
-    arrived = {j: shifted(payload[j - 1], "chan", j) for j in (1, 3, 2)}
-    parts = [arrived[1], arrived[3], arrived[2]]
-    reduced = own_reduced + sum(part[:SLAB].astype(F32) for part in parts)
+    reduced = own_reduced + sum(shifted(payload[j - 1], "chan", j).astype(F32) for j in (1, 3, 2))
+    parts = [shifted(sent_mixed, "chan", j) for j in (1, 3, 2)]
     reduced = (reduced * keep).astype(BF)
 
     pair = crossed(reduced, 1)
-    both, parts = lax.optimization_barrier((jnp.concatenate([reduced, pair], 0), parts))
+    both = jnp.concatenate([reduced, pair], 0)
+    parts, unused = lax.optimization_barrier((parts, pair))
     far_pair = outward(both, 2)
     near_pair = outward(both, 1)
 
@@ -295,7 +301,7 @@
     last = crossed(returned[SLAB:].astype(BF), 1).astype(F32)
     grad_slab = ((own + returned[:SLAB] + last) * keep).astype(BF)
     shared = jnp.concatenate([grad_slab, mixed_part.astype(BF)], 0)
-    exchanged = [shared] + [shifted(shared, "chan", j) for j in (2, 1, 3)]
+    exchanged = [shared] + [shifted(shared, "chan", j) for j in (1, 3, 2)]
 
     half = struct((rank // 2, packed_width), F32)
     grad_features, output, mine, give = pl.pallas_call(

time: 82.8 us -> 86 us (1.039)
  starting transfers between devices: 37.3 us -> 44.3 us
  waiting for transfers between devices: 26 us -> 22.9 us
    ppermute x12, starting transfers between devices: 18.4 us -> 23.4 us  [crossed(): lax.ppermute(block, 'leaf', [(i, i ^ mask) for i in range(lax.axis_size('...]
    ppermute x6 -> x9, waiting for transfers between devices: 11.1 us -> 8.59 us  [shifted(): lax.ppermute(block, axis, [(i, (i + distance) % count) for i in range(cou...]
    ppermute x6 -> x9, starting transfers between devices: 8.88 us -> 11 us  [shifted(): lax.ppermute(block, axis, [(i, (i + distance) % count) for i in range(cou...]
  transfers between devices with their start and end apart: 22 -> 25, of which waited for: 15 -> 11; matrix products, arithmetic and copies ran while one was open for 0% -> 0% of each run, Pallas kernels for 16% -> 14%
where the time goes in v5:
time: 86 us; the launch traced here: 85.9 us
  starting transfers between devices  44.3 us (52%)
  waiting for transfers between devices  22.9 us (27%)
  Pallas kernels  16.4 us (19%)
  other arithmetic  1.1 us (1%)
  between operations  0.94 us (1%)
    ppermute x12, starting transfers between devices, crossed(): lax.ppermute(block, 'leaf', [(i, i ^ mask) for i in range(lax.axis_size('...  23.4 us
    ppermute x12, waiting for transfers between devices, crossed(): lax.ppermute(block, 'leaf', [(i, i ^ mask) for i in range(lax.axis_size('...  14.3 us
    ppermute x9, starting transfers between devices, shifted(): lax.ppermute(block, axis, [(i, (i + distance) % count) for i in range(cou...  11 us
    ppermute x4, starting transfers between devices, outward(): lax.ppermute(block, 'leaf', [(i, (i + (2 * chips if i % 2 == 0 else -2 *...  9.92 us
    ppermute x9, waiting for transfers between devices, shifted(): lax.ppermute(block, axis, [(i, (i + distance) % count) for i in range(cou...  8.59 us
    pallas_call x1, Pallas kernels, body(): pl.pallas_call(gather_kernel, out_shape=[struct((rank, rows), F32), struc...  6.15 us
    pallas_call x1, Pallas kernels, body(): pl.pallas_call(scatter_kernel, out_shape=[struct((rank, rows), BF), struc...  5.97 us
    pallas_call x1, Pallas kernels, body(): pl.pallas_call(project_kernel, out_shape=[struct((SLAB, rows), F32), stru...  2 us
  transfers between devices with their start and end apart: 25, of which 11 were waited for; matrix products, arithmetic and copies ran while one was open for 0% of the time, Pallas kernels for 14%

profile of v5, /device:TPU:1, one launch (start us, length us, event | category | flops | bytes accessed | tf_op | source)
XLA Modules:
  0.0 85.9 jit_solution(11290863951969989965)
XLA Ops:
  0.6 2.0 %project.1 = (f32[16,1024]{1,0:T(8,128)}, f32[48,1024]{1,0:T(8,128)}, bf16[48,1024]{1,0:T(8,128)(2,1)}, bf16[16,1024]{1,0:T(8,128)(2,1)}, bf16[16,1024]{1,0:T(8,128)(2,1)}, /*index=5*/bf16[16,1024]{1,0:T(8,128)(2,1)}) custom-call(bf16[48,1024]{1,0:T(8,128)(2,1)} %feat_ref.3, bf16[48,48]{1,0:T(8,128)(2,1)} %in_ref.3, bf16[48,1024]{1,0:T(8,128)(2,1)} %cot_ref.3, ...), custom_call_target="tpu_custom_call" | custom-call | tf_op jit(solution)/shard_map/project/pallas_call | solution.py:244
  2.6 2.2 %collective-permute-start = (bf16[16,1024]{1,0:T(8,128)(2,1)}, bf16[16,1024]{1,0:T(8,128)(2,1)S(1)}, u32[]{:S(2)}, u32[]{:S(2)}) collective-permute-start(bf16[16,1024]{1,0:T(8,128)(2,1)} %get-tuple-element.34), channel_id=1, source_target_pairs={{0,1},{1,2},{2,3},{3,0},{4,5},{5,6},{6,7},{7,4},{8,9},{9,10},{10,1... | collective-permute-start | bytes 98312 | tf_op jit(solution)/shard_map/ppermute | solution.py:207
  4.8 1.5 %collective-permute-start.1 = (bf16[16,1024]{1,0:T(8,128)(2,1)}, bf16[16,1024]{1,0:T(8,128)(2,1)S(1)}, u32[]{:S(2)}, u32[]{:S(2)}) collective-permute-start(bf16[16,1024]{1,0:T(8,128)(2,1)} %get-tuple-element.35), channel_id=1, source_target_pairs={{0,3},{1,0},{2,1},{3,2},{4,7},{5,4},{6,5},{7,6},{8,11},{9,8},{10,9... | collective-permute-start | bytes 98312 | tf_op jit(solution)/shard_map/ppermute | solution.py:207
  6.3 1.6 %collective-permute-start.2 = (bf16[16,1024]{1,0:T(8,128)(2,1)}, bf16[16,1024]{1,0:T(8,128)(2,1)S(1)}, u32[]{:S(2)}, u32[]{:S(2)}) collective-permute-start(bf16[16,1024]{1,0:T(8,128)(2,1)} %get-tuple-element.36), channel_id=1, source_target_pairs={{0,2},{1,3},{2,0},{3,1},{4,6},{5,7},{6,4},{7,5},{8,10},{9,11},{10,... | collective-permute-start | bytes 98312 | tf_op jit(solution)/shard_map/ppermute | solution.py:207
  7.9 3.0 %collective-permute-done.2 = bf16[16,1024]{1,0:T(8,128)(2,1)S(1)} collective-permute-done((bf16[16,1024]{1,0:T(8,128)(2,1)}, bf16[16,1024]{1,0:T(8,128)(2,1)S(1)}, u32[]{:S(2)}, u32[]{:S(2)}) %collective-permute-start.2) | collective-permute-done | bytes 32800 | tf_op jit(solution)/shard_map/ppermute | solution.py:207
  10.9 0.9 %multiply_convert_fusion.own_ref = bf16[16,1024]{1,0:T(8,128)(2,1)S(1)} fusion(f32[16,1024]{1,0:T(8,128)} %get-tuple-element.33, bf16[16,1024]{1,0:T(8,128)(2,1)S(1)} %collective-permute-done.2, bf16[16,1024]{1,0:T(8,128)(2,1)S(1)} %collective-permute-done.1, bf16[16,1024]{1,0:T(8,128)(2,1)S(1)} %collective-permute-done, f32[1024]{0:T(1024)S(1)} %convert_element_type.41), kind=kLoop, calls=%fused_computation.20 | loop fusion | flops 131072 | bytes 200704 | tf_op jit(solution)/shard_map/convert_element_type | solution.py:253
  11.8 4.0 %collective-permute-start.3 = (bf16[16,1024]{1,0:T(8,128)(2,1)S(1)}, bf16[16,1024]{1,0:T(8,128)(2,1)S(1)}, u32[]{:S(2)}, u32[]{:S(2)}) collective-permute-start(bf16[16,1024]{1,0:T(8,128)(2,1)S(1)} %multiply_convert_fusion.own_ref), channel_id=1, source_target_pairs={{0,4},{4,0},{8,12},{12,8},{16,20},{20,16},{24,28},{28,24},{32,36},... | collective-permute-start | bytes 98312 | tf_op jit(solution)/shard_map/ppermute | solution.py:211
  15.8 2.7 %collective-permute-start.7 = (bf16[48,1024]{1,0:T(8,128)(2,1)S(1)}, bf16[48,1024]{1,0:T(8,128)(2,1)S(1)}, u32[]{:S(2)}, u32[]{:S(2)}) collective-permute-start(bf16[48,1024]{1,0:T(8,128)(2,1)S(1)} %copy-done.9), channel_id=1, source_target_pairs={{0,3},{1,0},{2,1},{3,2},{4,7},{5,4},{6,5},{7,6},{8,11},{9,8},{10,9... | collective-permute-start | bytes 294920 | tf_op jit(solution)/shard_map/ppermute | solution.py:207
  18.6 6.6 %collective-permute-start.4 = (bf16[32,1024]{1,0:T(8,128)(2,1)S(1)}, bf16[32,1024]{1,0:T(8,128)(2,1)S(1)}, u32[]{:S(2)}, u32[]{:S(2)}) collective-permute-start(bf16[32,1024]{1,0:T(8,128)(2,1)S(1)} %pad_maximum_fusion.2), channel_id=1, source_target_pairs={{0,8},{4,252},{8,16},{12,4},{16,24},{20,12},{24,32},{28,20},{32,40... | collective-permute-start | bytes 196616 | tf_op jit(solution)/shard_map/ppermute | solution.py:216
  25.8 6.0 %scatter.1 = (bf16[48,1024]{1,0:T(8,128)(2,1)S(1)}, f32[16,1024]{1,0:T(8,128)S(1)}, f32[64,1024]{1,0:T(8,128)S(1)}, bf16[64,1024]{1,0:T(8,128)(2,1)S(1)}) custom-call(s32[8,8]{1,0:T(8,128)S(1)} %bitcast.5, f32[48,1024]{1,0:T(8,128)S(1)} %copy-done.4, bf16[48,1024]{1,0:T(8,128)(2,1)S(1)} %collective-permute-done.6.p1, ...), custom_call_target="tpu_custom_call" | custom-call | flops 5000000000 | bytes 1048576 | tf_op jit(solution)/shard_map/scatter/pallas_call | solution.py:261
  31.9 1.5 %collective-permute-done.9 = bf16[128,1024]{1,0:T(8,128)(2,1)S(1)} collective-permute-done((bf16[128,1024]{1,0:T(8,128)(2,1)S(1)}, bf16[128,1024]{1,0:T(8,128)(2,1)S(1)}, u32[]{:S(2)}, u32[]{:S(2)}) %collective-permute-start.9) | collective-permute-done | bytes 262176 | tf_op jit(solution)/shard_map/ppermute | solution.py:211
  34.2 2.1 %collective-permute-start.11 = (bf16[32,1024]{1,0:T(8,128)(2,1)S(1)}, bf16[32,1024]{1,0:T(8,128)(2,1)S(1)}, u32[]{:S(2)}, u32[]{:S(2)}) collective-permute-start(bf16[32,1024]{1,0:T(8,128)(2,1)S(1)} %get-tuple-element.48), channel_id=1, source_target_pairs={{0,240},{4,20},{8,248},{12,28},{16,0},{20,36},{24,8},{28,44},{32,1... | collective-permute-start | bytes 196616 | tf_op jit(solution)/shard_map/ppermute | solution.py:216
  36.3 6.2 %gather.1 = (f32[48,1024]{1,0:T(8,128)S(1)}, f32[48,512]{1,0:T(8,128)S(1)}) custom-call(s32[8,8]{1,0:T(8,128)S(1)} %bitcast.6, bf16[16,1024]{1,0:T(8,128)(2,1)S(1)} %multiply_convert_fusion.own_ref, bf16[16,1024]{1,0:T(8,128)(2,1)S(1)} %collective-permute-done.3.pair_ref, bf16[32,1024]{1,0:T(8,128)(2,1)S(1)} %collective-permute-done.4.near_ref, ...), custom_call_target="tpu_custom_call" | custom-call | flops 5000000000 | bytes 1048576 | tf_op jit(solution)/shard_map/gather/pallas_call | solution.py:288
  42.5 3.9 %collective-permute-start.12 = (bf16[16,1024]{1,0:T(8,128)(2,1)S(1)}, bf16[16,1024]{1,0:T(8,128)(2,1)S(1)}, u32[]{:S(2)}, u32[]{:S(2)}) collective-permute-start(bf16[16,1024]{1,0:T(8,128)(2,1)S(1)} %slice.84), channel_id=1, source_target_pairs={{0,4},{4,0},{8,12},{12,8},{16,20},{20,16},{24,28},{28,24},{32,36},... | collective-permute-start | bytes 98312 | tf_op jit(solution)/shard_map/ppermute | solution.py:211
  46.5 0.8 collective-permute-done.12
  47.5 2.7 %collective-permute-start.14 = (bf16[64,1024]{1,0:T(8,128)(2,1)S(1)}, bf16[64,1024]{1,0:T(8,128)(2,1)S(1)}, u32[]{:S(2)}, u32[]{:S(2)}) collective-permute-start(bf16[64,1024]{1,0:T(8,128)(2,1)S(1)} %pad_maximum_fusion.1.e0), channel_id=1, source_target_pairs={{0,3},{1,0},{2,1},{3,2},{4,7},{5,4},{6,5},{7,6},{8,11},{9,8},{10,9... | collective-permute-start | bytes 393224 | tf_op jit(solution)/shard_map/ppermute | solution.py:207
  50.5 3.0 %collective-permute-done.13.e1 = bf16[64,1024]{1,0:T(8,128)(2,1)S(1)} collective-permute-done((bf16[64,1024]{1,0:T(8,128)(2,1)S(1)}, bf16[64,1024]{1,0:T(8,128)(2,1)S(1)}, u32[]{:S(2)}, u32[]{:S(2)}) %collective-permute-start.13) | collective-permute-done | bytes 131104 | tf_op jit(solution)/shard_map/ppermute | solution.py:207
  53.5 2.6 %collective-permute-done.15.e2 = bf16[64,1024]{1,0:T(8,128)(2,1)S(1)} collective-permute-done((bf16[64,1024]{1,0:T(8,128)(2,1)S(1)}, bf16[64,1024]{1,0:T(8,128)(2,1)S(1)}, u32[]{:S(2)}, u32[]{:S(2)}) %collective-permute-start.15) | collective-permute-done | bytes 131104 | tf_op jit(solution)/shard_map/ppermute | solution.py:207
  56.1 1.5 %finish.1 = (bf16[48,1024]{1,0:T(8,128)(2,1)}, bf16[48,1024]{1,0:T(8,128)(2,1)}, f32[24,512]{1,0:T(8,128)S(1)}, f32[24,512]{1,0:T(8,128)S(1)}) custom-call(f32[48,1024]{1,0:T(8,128)S(1)} %get-tuple-element.49.mix_ref, bf16[64,1024]{1,0:T(8,128)(2,1)S(1)} %pad_maximum_fusion.1.e0, bf16[64,1024]{1,0:T(8,128)(2,1)S(1)} %collective-permute-done.13.e1, ...), custom_call_target="tpu_custom_call" | custom-call | tf_op jit(solution)/shard_map/finish/pallas_call | solution.py:307
  57.5 1.7 %collective-permute-start.16 = (f32[24,512]{1,0:T(8,128)S(1)}, f32[24,512]{1,0:T(8,128)S(1)}, u32[]{:S(2)}, u32[]{:S(2)}) collective-permute-start(f32[24,512]{1,0:T(8,128)S(1)} %get-tuple-element.57), channel_id=1, source_target_pairs={{0,4},{4,0},{8,12},{12,8},{16,20},{20,16},{24,28},{28,24},{32,36},... | collective-permute-start | bytes 147464 | tf_op jit(solution)/shard_map/ppermute | solution.py:211
  59.2 0.9 %collective-permute-done.16 = f32[24,512]{1,0:T(8,128)S(1)} collective-permute-done((f32[24,512]{1,0:T(8,128)S(1)}, f32[24,512]{1,0:T(8,128)S(1)}, u32[]{:S(2)}, u32[]{:S(2)}) %collective-permute-start.16) | collective-permute-done | bytes 49184 | tf_op jit(solution)/shard_map/ppermute | solution.py:211
  60.2 2.9 %collective-permute-done.17 = f32[24,512]{1,0:T(8,128)S(1)} collective-permute-done((f32[24,512]{1,0:T(8,128)S(1)}, f32[24,512]{1,0:T(8,128)S(1)}, u32[]{:S(2)}, u32[]{:S(2)}) %collective-permute-start.17) | collective-permute-done | bytes 49184 | tf_op jit(solution)/shard_map/ppermute | solution.py:211
  63.1 0.7 collective-permute-start.18
  63.8 2.1 %collective-permute-start.19 = (f32[24,512]{1,0:T(8,128)S(1)}, f32[24,512]{1,0:T(8,128)S(1)}, u32[]{:S(2)}, u32[]{:S(2)}) collective-permute-start(f32[24,512]{1,0:T(8,128)S(1)} %add.67), channel_id=1, source_target_pairs={{0,24},{4,28},{8,16},{12,20},{16,8},{20,12},{24,0},{28,4},{32,56},... | collective-permute-start | bytes 147464 | tf_op jit(solution)/shard_map/ppermute | solution.py:211
  66.5 1.5 %collective-permute-done.19 = f32[24,512]{1,0:T(8,128)S(1)} collective-permute-done((f32[24,512]{1,0:T(8,128)S(1)}, f32[24,512]{1,0:T(8,128)S(1)}, u32[]{:S(2)}, u32[]{:S(2)}) %collective-permute-start.19) | collective-permute-done | bytes 49184 | tf_op jit(solution)/shard_map/ppermute | solution.py:211
  68.0 2.5 %collective-permute-done.20 = f32[24,512]{1,0:T(8,128)S(1)} collective-permute-done((f32[24,512]{1,0:T(8,128)S(1)}, f32[24,512]{1,0:T(8,128)S(1)}, u32[]{:S(2)}, u32[]{:S(2)}) %collective-permute-start.20) | collective-permute-done | bytes 49184 | tf_op jit(solution)/shard_map/ppermute | solution.py:211
  70.6 1.7 %collective-permute-start.22 = (f32[24,512]{1,0:T(8,128)S(1)}, f32[24,512]{1,0:T(8,128)S(1)}, u32[]{:S(2)}, u32[]{:S(2)}) collective-permute-start(f32[24,512]{1,0:T(8,128)S(1)} %add_add_fusion.1), channel_id=1, source_target_pairs={{0,192},{4,196},{8,200},{12,204},{16,208},{20,212},{24,216},{28,22... | collective-permute-start | bytes 147464 | tf_op jit(solution)/shard_map/ppermute | solution.py:211
  72.3 4.0 %collective-permute-start.23 = (f32[24,512]{1,0:T(8,128)S(1)}, f32[24,512]{1,0:T(8,128)S(1)}, u32[]{:S(2)}, u32[]{:S(2)}) collective-permute-start(f32[24,512]{1,0:T(8,128)S(1)} %add_add_fusion.1), channel_id=1, source_target_pairs={{0,128},{4,132},{8,136},{12,140},{16,144},{20,148},{24,152},{28,15... | collective-permute-start | bytes 147464 | tf_op jit(solution)/shard_map/ppermute | solution.py:211
  76.3 3.3 %collective-permute-done.23 = f32[24,512]{1,0:T(8,128)S(1)} collective-permute-done((f32[24,512]{1,0:T(8,128)S(1)}, f32[24,512]{1,0:T(8,128)S(1)}, u32[]{:S(2)}, u32[]{:S(2)}) %collective-permute-start.23) | collective-permute-done | bytes 49184 | tf_op jit(solution)/shard_map/ppermute | solution.py:211
  79.6 4.6 %collective-permute-start.24 = (f32[24,512]{1,0:T(8,128)S(1)}, f32[24,512]{1,0:T(8,128)S(1)}, u32[]{:S(2)}, u32[]{:S(2)}) collective-permute-start(f32[24,512]{1,0:T(8,128)S(1)} %add_add_fusion.refs_0_), channel_id=1, source_target_pairs={{0,4},{4,0},{8,12},{12,8},{16,20},{20,16},{24,28},{28,24},{32,36},... | collective-permute-start | bytes 147464 | tf_op jit(solution)/shard_map/ppermute | solution.py:211
  84.2 0.9 %collective-permute-done.24.refs_1_ = f32[24,512]{1,0:T(8,128)S(1)} collective-permute-done((f32[24,512]{1,0:T(8,128)S(1)}, f32[24,512]{1,0:T(8,128)S(1)}, u32[]{:S(2)}, u32[]{:S(2)}) %collective-permute-start.24) | collective-permute-done | bytes 49184 | tf_op jit(solution)/shard_map/ppermute | solution.py:211
  85.1 0.8 unpack.1
  (62 shorter events, 2.8 us)
Async XLA Ops:
  2.6 5.3 %collective-permute-start = (bf16[16,1024]{1,0:T(8,128)(2,1)}, bf16[16,1024]{1,0:T(8,128)(2,1)S(1)}, u32[]{:S(2)}, u32[]{:S(2)}) collective-permute-start(bf16[16,1024]{1,0:T(8,128)(2,1)} %get-tuple-element.34), channel_id=1, source_target_pairs={{0,1},{1,2},{2,3},{3,0},{4,5},{5,6},{6,7},{7,4},{8,9},{9,10},{10,1... | collective-permute-start | bytes 98312 | tf_op jit(solution)/shard_map/ppermute | solution.py:207
  4.8 3.1 %collective-permute-start.1 = (bf16[16,1024]{1,0:T(8,128)(2,1)}, bf16[16,1024]{1,0:T(8,128)(2,1)S(1)}, u32[]{:S(2)}, u32[]{:S(2)}) collective-permute-start(bf16[16,1024]{1,0:T(8,128)(2,1)} %get-tuple-element.35), channel_id=1, source_target_pairs={{0,3},{1,0},{2,1},{3,2},{4,7},{5,4},{6,5},{7,6},{8,11},{9,8},{10,9... | collective-permute-start | bytes 98312 | tf_op jit(solution)/shard_map/ppermute | solution.py:207
  6.3 4.6 %collective-permute-start.2 = (bf16[16,1024]{1,0:T(8,128)(2,1)}, bf16[16,1024]{1,0:T(8,128)(2,1)S(1)}, u32[]{:S(2)}, u32[]{:S(2)}) collective-permute-start(bf16[16,1024]{1,0:T(8,128)(2,1)} %get-tuple-element.36), channel_id=1, source_target_pairs={{0,2},{1,3},{2,0},{3,1},{4,6},{5,7},{6,4},{7,5},{8,10},{9,11},{10,... | collective-permute-start | bytes 98312 | tf_op jit(solution)/shard_map/ppermute | solution.py:207
  10.9 7.6 %copy-start.7 = (bf16[27,12,48]{2,0,1:T(8,128)(2,1)S(1)}, bf16[27,12,48]{2,0,1:T(8,128)(2,1)}, u32[]{:S(2)}) copy-start(bf16[27,12,48]{2,0,1:T(8,128)(2,1)} %param.10) | copy-start | bytes 93316
  11.8 6.8 %collective-permute-start.3 = (bf16[16,1024]{1,0:T(8,128)(2,1)S(1)}, bf16[16,1024]{1,0:T(8,128)(2,1)S(1)}, u32[]{:S(2)}, u32[]{:S(2)}) collective-permute-start(bf16[16,1024]{1,0:T(8,128)(2,1)S(1)} %multiply_convert_fusion.own_ref), channel_id=1, source_target_pairs={{0,4},{4,0},{8,12},{12,8},{16,20},{20,16},{24,28},{28,24},{32,36},... | collective-permute-start | bytes 98312 | tf_op jit(solution)/shard_map/ppermute | solution.py:211
  15.8 10.0 %collective-permute-start.6 = (bf16[48,1024]{1,0:T(8,128)(2,1)S(1)}, bf16[48,1024]{1,0:T(8,128)(2,1)S(1)}, u32[]{:S(2)}, u32[]{:S(2)}) collective-permute-start(bf16[48,1024]{1,0:T(8,128)(2,1)S(1)} %copy-done.9), channel_id=1, source_target_pairs={{0,1},{1,2},{2,3},{3,0},{4,5},{5,6},{6,7},{7,4},{8,9},{9,10},{10,1... | collective-permute-start | bytes 294920 | tf_op jit(solution)/shard_map/ppermute | solution.py:207
  15.8 10.0 %collective-permute-start.7 = (bf16[48,1024]{1,0:T(8,128)(2,1)S(1)}, bf16[48,1024]{1,0:T(8,128)(2,1)S(1)}, u32[]{:S(2)}, u32[]{:S(2)}) collective-permute-start(bf16[48,1024]{1,0:T(8,128)(2,1)S(1)} %copy-done.9), channel_id=1, source_target_pairs={{0,3},{1,0},{2,1},{3,2},{4,7},{5,4},{6,5},{7,6},{8,11},{9,8},{10,9... | collective-permute-start | bytes 294920 | tf_op jit(solution)/shard_map/ppermute | solution.py:207
  18.5 7.3 %collective-permute-start.8 = (bf16[48,1024]{1,0:T(8,128)(2,1)S(1)}, bf16[48,1024]{1,0:T(8,128)(2,1)S(1)}, u32[]{:S(2)}, u32[]{:S(2)}) collective-permute-start(bf16[48,1024]{1,0:T(8,128)(2,1)S(1)} %copy-done.9), channel_id=1, source_target_pairs={{0,2},{1,3},{2,0},{3,1},{4,6},{5,7},{6,4},{7,5},{8,10},{9,11},{10,... | collective-permute-start | bytes 294920 | tf_op jit(solution)/shard_map/ppermute | solution.py:207
  18.5 7.2 %copy-start.4 = (f32[48,1024]{1,0:T(8,128)S(1)}, f32[48,1024]{1,0:T(8,128)}, u32[]{:S(2)}) copy-start(f32[48,1024]{1,0:T(8,128)} %get-tuple-element.37.p0) | copy-start | bytes 589828
  18.5 7.2 %copy-start.5 = (s32[27,1024]{1,0:T(8,128)S(1)}, s32[27,1024]{1,0:T(8,128)}, u32[]{:S(2)}) copy-start(s32[27,1024]{1,0:T(8,128)} %nbr_ref.3) | copy-start | bytes 331780
  18.6 13.1 %collective-permute-start.4 = (bf16[32,1024]{1,0:T(8,128)(2,1)S(1)}, bf16[32,1024]{1,0:T(8,128)(2,1)S(1)}, u32[]{:S(2)}, u32[]{:S(2)}) collective-permute-start(bf16[32,1024]{1,0:T(8,128)(2,1)S(1)} %pad_maximum_fusion.2), channel_id=1, source_target_pairs={{0,8},{4,252},{8,16},{12,4},{16,24},{20,12},{24,32},{28,20},{32,40... | collective-permute-start | bytes 196616 | tf_op jit(solution)/shard_map/ppermute | solution.py:216
  25.2 6.6 %collective-permute-start.5 = (bf16[32,1024]{1,0:T(8,128)(2,1)S(1)}, bf16[32,1024]{1,0:T(8,128)(2,1)S(1)}, u32[]{:S(2)}, u32[]{:S(2)}) collective-permute-start(bf16[32,1024]{1,0:T(8,128)(2,1)S(1)} %pad_maximum_fusion.2), channel_id=1, source_target_pairs={{0,16},{4,244},{8,24},{12,252},{16,32},{20,4},{24,40},{28,12},{32,... | collective-permute-start | bytes 196616 | tf_op jit(solution)/shard_map/ppermute | solution.py:216
  31.8 1.6 %collective-permute-start.9 = (bf16[128,1024]{1,0:T(8,128)(2,1)S(1)}, bf16[128,1024]{1,0:T(8,128)(2,1)S(1)}, u32[]{:S(2)}, u32[]{:S(2)}) collective-permute-start(bf16[128,1024]{1,0:T(8,128)(2,1)S(1)} %pad_maximum_fusion), channel_id=1, source_target_pairs={{0,4},{4,0},{8,12},{12,8},{16,20},{20,16},{24,28},{28,24},{32,36},... | collective-permute-start | bytes 786440 | tf_op jit(solution)/shard_map/ppermute | solution.py:211
  33.5 9.0 %collective-permute-start.10 = (bf16[32,1024]{1,0:T(8,128)(2,1)S(1)}, bf16[32,1024]{1,0:T(8,128)(2,1)S(1)}, u32[]{:S(2)}, u32[]{:S(2)}) collective-permute-start(bf16[32,1024]{1,0:T(8,128)(2,1)S(1)} %get-tuple-element.47), channel_id=1, source_target_pairs={{0,248},{4,12},{8,0},{12,20},{16,8},{20,28},{24,16},{28,36},{32,24... | collective-permute-start | bytes 196616 | tf_op jit(solution)/shard_map/ppermute | solution.py:216
  34.2 8.3 %collective-permute-start.11 = (bf16[32,1024]{1,0:T(8,128)(2,1)S(1)}, bf16[32,1024]{1,0:T(8,128)(2,1)S(1)}, u32[]{:S(2)}, u32[]{:S(2)}) collective-permute-start(bf16[32,1024]{1,0:T(8,128)(2,1)S(1)} %get-tuple-element.48), channel_id=1, source_target_pairs={{0,240},{4,20},{8,248},{12,28},{16,0},{20,36},{24,8},{28,44},{32,1... | collective-permute-start | bytes 196616 | tf_op jit(solution)/shard_map/ppermute | solution.py:216
  42.5 4.8 %collective-permute-start.12 = (bf16[16,1024]{1,0:T(8,128)(2,1)S(1)}, bf16[16,1024]{1,0:T(8,128)(2,1)S(1)}, u32[]{:S(2)}, u32[]{:S(2)}) collective-permute-start(bf16[16,1024]{1,0:T(8,128)(2,1)S(1)} %slice.84), channel_id=1, source_target_pairs={{0,4},{4,0},{8,12},{12,8},{16,20},{20,16},{24,28},{28,24},{32,36},... | collective-permute-start | bytes 98312 | tf_op jit(solution)/shard_map/ppermute | solution.py:211
  47.4 8.7 %copy-start = (bf16[48,1024]{1,0:T(8,128)(2,1)S(1)}, bf16[48,1024]{1,0:T(8,128)(2,1)}, u32[]{:S(2)}) copy-start(bf16[48,1024]{1,0:T(8,128)(2,1)} %feat_ref.3) | copy-start | bytes 294916
  47.4 8.7 %copy-start.1 = (bf16[48,1024]{1,0:T(8,128)(2,1)S(1)}, bf16[48,1024]{1,0:T(8,128)(2,1)}, u32[]{:S(2)}) copy-start(bf16[48,1024]{1,0:T(8,128)(2,1)} %cot_ref.3) | copy-start | bytes 294916
  47.4 8.7 %copy-start.2 = (bf16[48,48]{1,0:T(8,128)(2,1)S(1)}, bf16[48,48]{1,0:T(8,128)(2,1)}, u32[]{:S(2)}) copy-start(bf16[48,48]{1,0:T(8,128)(2,1)} %in_ref.3) | copy-start | bytes 13828
  47.4 8.7 %copy-start.3 = (bf16[48,48]{1,0:T(8,128)(2,1)S(1)}, bf16[48,48]{1,0:T(8,128)(2,1)}, u32[]{:S(2)}) copy-start(bf16[48,48]{1,0:T(8,128)(2,1)} %outf_ref.3) | copy-start | bytes 13828
  47.4 6.0 %collective-permute-start.13 = (bf16[64,1024]{1,0:T(8,128)(2,1)S(1)}, bf16[64,1024]{1,0:T(8,128)(2,1)S(1)}, u32[]{:S(2)}, u32[]{:S(2)}) collective-permute-start(bf16[64,1024]{1,0:T(8,128)(2,1)S(1)} %pad_maximum_fusion.1.e0), channel_id=1, source_target_pairs={{0,1},{1,2},{2,3},{3,0},{4,5},{5,6},{6,7},{7,4},{8,9},{9,10},{10,1... | collective-permute-start | bytes 393224 | tf_op jit(solution)/shard_map/ppermute | solution.py:207
  47.5 5.9 %collective-permute-start.14 = (bf16[64,1024]{1,0:T(8,128)(2,1)S(1)}, bf16[64,1024]{1,0:T(8,128)(2,1)S(1)}, u32[]{:S(2)}, u32[]{:S(2)}) collective-permute-start(bf16[64,1024]{1,0:T(8,128)(2,1)S(1)} %pad_maximum_fusion.1.e0), channel_id=1, source_target_pairs={{0,3},{1,0},{2,1},{3,2},{4,7},{5,4},{6,5},{7,6},{8,11},{9,8},{10,9... | collective-permute-start | bytes 393224 | tf_op jit(solution)/shard_map/ppermute | solution.py:207
  50.2 5.9 %collective-permute-start.15 = (bf16[64,1024]{1,0:T(8,128)(2,1)S(1)}, bf16[64,1024]{1,0:T(8,128)(2,1)S(1)}, u32[]{:S(2)}, u32[]{:S(2)}) collective-permute-start(bf16[64,1024]{1,0:T(8,128)(2,1)S(1)} %pad_maximum_fusion.1.e0), channel_id=1, source_target_pairs={{0,2},{1,3},{2,0},{3,1},{4,6},{5,7},{6,4},{7,5},{8,10},{9,11},{10,... | collective-permute-start | bytes 393224 | tf_op jit(solution)/shard_map/ppermute | solution.py:207
  57.5 2.6 %collective-permute-start.16 = (f32[24,512]{1,0:T(8,128)S(1)}, f32[24,512]{1,0:T(8,128)S(1)}, u32[]{:S(2)}, u32[]{:S(2)}) collective-permute-start(f32[24,512]{1,0:T(8,128)S(1)} %get-tuple-element.57), channel_id=1, source_target_pairs={{0,4},{4,0},{8,12},{12,8},{16,20},{20,16},{24,28},{28,24},{32,36},... | collective-permute-start | bytes 147464 | tf_op jit(solution)/shard_map/ppermute | solution.py:211
  60.1 3.0 %collective-permute-start.17 = (f32[24,512]{1,0:T(8,128)S(1)}, f32[24,512]{1,0:T(8,128)S(1)}, u32[]{:S(2)}, u32[]{:S(2)}) collective-permute-start(f32[24,512]{1,0:T(8,128)S(1)} %add.66), channel_id=1, source_target_pairs={{0,32},{4,36},{8,40},{12,44},{16,48},{20,52},{24,56},{28,60},{32,0... | collective-permute-start | bytes 147464 | tf_op jit(solution)/shard_map/ppermute | solution.py:211
  63.1 3.3 %collective-permute-start.18 = (f32[24,512]{1,0:T(8,128)S(1)}, f32[24,512]{1,0:T(8,128)S(1)}, u32[]{:S(2)}, u32[]{:S(2)}) collective-permute-start(f32[24,512]{1,0:T(8,128)S(1)} %add.67), channel_id=1, source_target_pairs={{0,8},{4,12},{8,0},{12,4},{16,24},{20,28},{24,16},{28,20},{32,40},... | collective-permute-start | bytes 147464 | tf_op jit(solution)/shard_map/ppermute | solution.py:211
  63.8 4.2 %collective-permute-start.19 = (f32[24,512]{1,0:T(8,128)S(1)}, f32[24,512]{1,0:T(8,128)S(1)}, u32[]{:S(2)}, u32[]{:S(2)}) collective-permute-start(f32[24,512]{1,0:T(8,128)S(1)} %add.67), channel_id=1, source_target_pairs={{0,24},{4,28},{8,16},{12,20},{16,8},{20,12},{24,0},{28,4},{32,56},... | collective-permute-start | bytes 147464 | tf_op jit(solution)/shard_map/ppermute | solution.py:211
  65.9 4.6 %collective-permute-start.20 = (f32[24,512]{1,0:T(8,128)S(1)}, f32[24,512]{1,0:T(8,128)S(1)}, u32[]{:S(2)}, u32[]{:S(2)}) collective-permute-start(f32[24,512]{1,0:T(8,128)S(1)} %add.67), channel_id=1, source_target_pairs={{0,16},{4,20},{8,24},{12,28},{16,0},{20,4},{24,8},{28,12},{32,48},... | collective-permute-start | bytes 147464 | tf_op jit(solution)/shard_map/ppermute | solution.py:211
  70.5 5.7 %collective-permute-start.21 = (f32[24,512]{1,0:T(8,128)S(1)}, f32[24,512]{1,0:T(8,128)S(1)}, u32[]{:S(2)}, u32[]{:S(2)}) collective-permute-start(f32[24,512]{1,0:T(8,128)S(1)} %add_add_fusion.1), channel_id=1, source_target_pairs={{0,64},{4,68},{8,72},{12,76},{16,80},{20,84},{24,88},{28,92},{32,9... | collective-permute-start | bytes 147464 | tf_op jit(solution)/shard_map/ppermute | solution.py:211
  70.6 5.7 %collective-permute-start.22 = (f32[24,512]{1,0:T(8,128)S(1)}, f32[24,512]{1,0:T(8,128)S(1)}, u32[]{:S(2)}, u32[]{:S(2)}) collective-permute-start(f32[24,512]{1,0:T(8,128)S(1)} %add_add_fusion.1), channel_id=1, source_target_pairs={{0,192},{4,196},{8,200},{12,204},{16,208},{20,212},{24,216},{28,22... | collective-permute-start | bytes 147464 | tf_op jit(solution)/shard_map/ppermute | solution.py:211
  72.3 7.3 %collective-permute-start.23 = (f32[24,512]{1,0:T(8,128)S(1)}, f32[24,512]{1,0:T(8,128)S(1)}, u32[]{:S(2)}, u32[]{:S(2)}) collective-permute-start(f32[24,512]{1,0:T(8,128)S(1)} %add_add_fusion.1), channel_id=1, source_target_pairs={{0,128},{4,132},{8,136},{12,140},{16,144},{20,148},{24,152},{28,15... | collective-permute-start | bytes 147464 | tf_op jit(solution)/shard_map/ppermute | solution.py:211
  79.6 5.5 %collective-permute-start.24 = (f32[24,512]{1,0:T(8,128)S(1)}, f32[24,512]{1,0:T(8,128)S(1)}, u32[]{:S(2)}, u32[]{:S(2)}) collective-permute-start(f32[24,512]{1,0:T(8,128)S(1)} %add_add_fusion.refs_0_), channel_id=1, source_target_pairs={{0,4},{4,0},{8,12},{12,8},{16,20},{20,16},{24,28},{28,24},{32,36},... | collective-permute-start | bytes 147464 | tf_op jit(solution)/shard_map/ppermute | solution.py:211
  (3 other events, 17.3 us)

commit v6 on v4

--- a/solution.py
+++ b/solution.py
@@ -67,7 +67,7 @@
     return jnp.where(core == 0, view, near - 1 - view)
 
 
-def scatter_kernel(halo_ref, p0, p1, p2, p3, core_ref, nbr_ref, gm_ref, own_ref, kept_ref,
+def scatter_kernel(halo_ref, r0, p0, p1, p2, p3, mask_ref, core_ref, nbr_ref, gm_ref, own_ref, kept_ref,
                    cross_ref, terms_ref, acc_ref):
     rows = nbr_ref.shape[1]
     tiles = acc_ref.shape[0] // SLAB
@@ -76,6 +76,8 @@
     )
     grad_mixed = total.astype(BF)
     gm_ref[...] = grad_mixed
+    reduced = (r0[...] + p1[:SLAB, :].astype(F32)) + (p2[:SLAB, :].astype(F32) + p3[:SLAB, :].astype(F32))
+    cross_ref[0:SLAB, :] = (reduced * mask_ref[...].astype(F32)).astype(BF)
     terms_ref[...] = dot(core_ref[...], grad_mixed).astype(BF)
     acc_ref[...] = jnp.zeros_like(acc_ref)
 
@@ -90,13 +92,16 @@
         acc_ref[...] += dot(spread, onehot, NT)
         return carry
 
-    lax.fori_loop(0, nbr_ref.shape[0], step, 0, unroll=9)
+    offsets = nbr_ref.shape[0]
+    middle = offsets // 2
+    lax.fori_loop(0, offsets - 1, lambda i, carry: step(i + (i >= middle), carry), 0, unroll=13)
 
     def tile(t):
         return acc_ref[pl.ds(pl.multiple_of(t * SLAB, SLAB), SLAB), :]
 
     own_tiles = rows // LOW
-    own_ref[...] = jnp.concatenate([tile(t) for t in range(own_tiles)], 1)
+    itself = terms_ref[middle * SLAB : (middle + 1) * SLAB, :].astype(F32)
+    own_ref[...] = jnp.concatenate([tile(t) for t in range(own_tiles)], 1) + itself
     near = halo_ref.shape[0]
     per_peer = (tiles - own_tiles) // near
     blank = jnp.zeros((SLAB, rows - per_peer * LOW), F32)
@@ -105,10 +110,10 @@
         start = own_tiles + slot * per_peer
         window = jnp.concatenate([tile(start + i) for i in range(per_peer)] + [blank], 1)
         block = pltpu.roll(window, first_octant(halo_ref, slot), 1)
-        if view < 4:
-            kept_ref[view * SLAB : (view + 1) * SLAB, :] = block
+        if view < 5:
+            cross_ref[(view + 1) * SLAB : (view + 2) * SLAB, :] = block.astype(BF)
         else:
-            cross_ref[(view - 4) * SLAB : (view - 3) * SLAB, :] = block.astype(BF)
+            kept_ref[(view - 5) * SLAB : (view - 4) * SLAB, :] = block
 
 
 def gather_kernel(halo_ref, own_ref, pair_ref, near_ref, far_ref, cross_ref, gm_ref, core_ref,
@@ -128,7 +133,7 @@
         pair_ref[...],
         cross_ref[SLAB : 2 * SLAB, :],
         cross_ref[0:SLAB, :],
-        cross_ref[3 * SLAB :, :],
+        cross_ref[3 * SLAB : 4 * SLAB, :],
     )
     for view in range(near):
         slot = mirrored(core_bit(), view, near)
@@ -148,14 +153,17 @@
         ga_ref[pl.ds(pl.multiple_of(k * SLAB, SLAB), SLAB), :] = found.astype(BF)
         return carry
 
-    lax.fori_loop(0, nbr_ref.shape[0], step, 0, unroll=9)
+    offsets = nbr_ref.shape[0]
+    middle = offsets // 2
+    lax.fori_loop(0, offsets - 1, lambda i, carry: step(i + (i >= middle), carry), 0, unroll=13)
+    ga_ref[middle * SLAB : (middle + 1) * SLAB, :] = own_ref[...]
     used = core_ref.shape[0]
     ga_ref[used:, :] = jnp.zeros_like(ga_ref[used:, :])
     mix_ref[...] = dot(core_ref[...], ga_ref[:used, :], TN)
     gc_ref[...] = dot(gm_ref[...], ga_ref[...], NT)
 
 
-def finish_kernel(mix_ref, e0, e2, e1, e3, in_ref, feat_ref, outf_ref, cot_ref, gc_ref,
+def finish_kernel(mix_ref, e0, e1, e3, e2, in_ref, feat_ref, outf_ref, cot_ref, gc_ref,
                   gf_ref, out_ref, keep_ref, give_ref):
     rank = in_ref.shape[1]
     rows = feat_ref.shape[1]
@@ -215,7 +223,7 @@
 
 def leaf_sum(mine, give):
     mine = mine + crossed(give, 1)
-    for masks in ((8,), (4, 2, 6), (32, 16, 48)):
+    for masks in ((8,), (2, 6, 4), (16, 48, 32)):
         mine = mine + sum(crossed(mine, mask) for mask in masks)
     return mine, crossed(mine, 1)
 
@@ -230,7 +238,7 @@
     near, slots = halo_blocks.shape[1:]
     table_rows = (rows + near * slots * 64) // LOW * SLAB
     packed_width = (offsets * SLAB + 127) // 128 * 128
-    keep = row_mask.astype(F32).reshape(1, rows)
+    keep = row_mask.reshape(1, rows)
     halo = halo_blocks[0]
     core_rows = jnp.pad(core, ((0, 0), (0, SLAB - width), (0, 0))).reshape(offsets * SLAB, rank)
     estimate = pl.CostEstimate(flops=5 * 10**9, bytes_accessed=2**20, transcendentals=0)
@@ -243,41 +251,37 @@
         name="project",
     )(features, in_factor, cotangent, out_factor)
     arrived = {j: shifted(payload[j - 1], "chan", j) for j in (1, 3, 2)}
-    parts = [arrived[1], arrived[3], arrived[2]]
-    reduced = own_reduced + sum(part[:SLAB].astype(F32) for part in parts)
-    reduced = (reduced * keep).astype(BF)
-
-    pair = crossed(reduced, 1)
-    both, parts = lax.optimization_barrier((jnp.concatenate([reduced, pair], 0), parts))
-    far_pair = outward(both, 2)
-    near_pair = outward(both, 1)
-
+
+    triple = struct((3 * SLAB, rows), F32)
     grad_mixed, own, kept, cross = pl.pallas_call(
         scatter_kernel,
-        out_shape=[
-            struct((rank, rows), BF),
-            struct((SLAB, rows), F32),
-            struct((4 * SLAB, rows), F32),
-            struct((4 * SLAB, rows), BF),
-        ],
-        in_specs=[SMEM] + [VMEM] * 6,
+        out_shape=[struct((rank, rows), BF), struct((SLAB, rows), F32), triple, struct((6 * SLAB, rows), BF)],
+        in_specs=[SMEM] + [VMEM] * 8,
         out_specs=[VMEM] * 4,
         scratch_shapes=[pltpu.VMEM((offsets * SLAB, rows), BF), pltpu.VMEM((table_rows, LOW), F32)],
         compiler_params=ROOMY,
         cost_estimate=estimate,
         name="scatter",
-    )(halo, own_mixed, *parts, core_rows, neighbours)
-
-    swapped = crossed(jnp.concatenate([cross, near_pair, far_pair], 0), 1)
-    handed, beyond = swapped[: 4 * SLAB].astype(F32), swapped[4 * SLAB :]
-    own = own + handed[:SLAB]
-    to_near = jnp.concatenate(
-        [kept[2 * SLAB : 3 * SLAB] + handed[2 * SLAB : 3 * SLAB], kept[3 * SLAB :] + handed[SLAB : 2 * SLAB]], 0
-    ).astype(BF)
-    to_far = jnp.concatenate([kept[:SLAB], kept[SLAB : 2 * SLAB] + handed[3 * SLAB :]], 0).astype(BF)
-    beyond, to_near, to_far = lax.optimization_barrier((beyond, to_near, to_far))
-    from_near = outward(to_near, -1)
-    from_far = outward(to_far, -2)
+    )(halo, own_reduced, own_mixed, arrived[1], arrived[3], arrived[2], keep, core_rows, neighbours)
+
+    def slabs_of(block, first, last):
+        return block[first * SLAB : last * SLAB]
+
+    reduced = slabs_of(cross, 0, 1)
+    handed = crossed(cross, 1)
+    pair = slabs_of(handed, 0, 1)
+    far_other, far_same, near_other, near_same, mine = (
+        slabs_of(handed, i, i + 1).astype(F32) for i in range(1, 6)
+    )
+    to_near = [slabs_of(kept, 0, 1) + near_same, slabs_of(kept, 1, 2) + near_other]
+    to_far = [slabs_of(kept, 2, 3) + far_same, far_other]
+    near = outward(jnp.concatenate([reduced, pair] + [x.astype(BF) for x in to_near], 0), 1)
+    far = outward(jnp.concatenate([reduced, pair] + [x.astype(BF) for x in to_far], 0), 2)
+    near_pair, far_pair = slabs_of(near, 0, 2), slabs_of(far, 0, 2)
+    passed = slabs_of(near, 3, 4).astype(F32) + slabs_of(far, 3, 4).astype(F32)
+    beyond = crossed(jnp.concatenate([near_pair, far_pair, passed.astype(BF)], 0), 1)
+    returned = (slabs_of(near, 2, 3).astype(F32) + slabs_of(far, 2, 3).astype(F32)) + slabs_of(beyond, 4, 5).astype(F32)
+    grad_slab = (((own + mine) + returned) * keep.astype(F32)).astype(BF)
 
     mixed_part, grad_core = pl.pallas_call(
         gather_kernel,
@@ -290,12 +294,8 @@
         name="gather",
     )(halo, reduced, pair, near_pair, far_pair, beyond, grad_mixed, core_rows, neighbours)
 
-    mixed_part, from_near, from_far = lax.optimization_barrier((mixed_part, from_near, from_far))
-    returned = from_near.astype(F32) + from_far.astype(F32)
-    last = crossed(returned[SLAB:].astype(BF), 1).astype(F32)
-    grad_slab = ((own + returned[:SLAB] + last) * keep).astype(BF)
     shared = jnp.concatenate([grad_slab, mixed_part.astype(BF)], 0)
-    exchanged = [shared] + [shifted(shared, "chan", j) for j in (2, 1, 3)]
+    exchanged = [shared] + [shifted(shared, "chan", j) for j in (1, 3, 2)]
 
     half = struct((rank // 2, packed_width), F32)
     grad_features, output, mine, give = pl.pallas_call(

time: 82.8 us -> 84.1 us (1.016)
  waiting for transfers between devices: 26 us -> 30.4 us
  starting transfers between devices: 37.3 us -> 35 us
  other arithmetic: 1.1 us -> 0.18 us
    ppermute x4 -> x2, waiting for transfers between devices: 0.01 us -> 5.25 us  [outward(): lax.ppermute(block, 'leaf', [(i, (i + (2 * chips if i % 2 == 0 else -2 *...]
    ppermute x4 -> x2, starting transfers between devices: 9.98 us -> 7.42 us  [outward(): lax.ppermute(block, 'leaf', [(i, (i + (2 * chips if i % 2 == 0 else -2 *...]
    ppermute x12 -> x11, starting transfers between devices: 18.4 us -> 19.6 us  [crossed(): lax.ppermute(block, 'leaf', [(i, i ^ mask) for i in range(lax.axis_size('...]
    convert_element_type x4, other arithmetic: 0.95 us -> 0.07 us  [the longest x2 0.03 us: body(): grad_slab = ((own + mine + returned) * keep.astype(F32)).astype(BF)]
    ppermute x6, starting transfers between devices: 8.88 us -> 8.03 us  [shifted(): lax.ppermute(block, axis, [(i, (i + distance) % count) for i in range(cou...]
    ppermute x12 -> x11, waiting for transfers between devices: 14.9 us -> 14.6 us  [crossed(): lax.ppermute(block, 'leaf', [(i, i ^ mask) for i in range(lax.axis_size('...]
  transfers between devices with their start and end apart: 22 -> 19, of which waited for: 15 -> 15; matrix products, arithmetic and copies ran while one was open for 0% -> 0% of each run, Pallas kernels for 16% -> 0%
where the time goes in v6:
time: 84.1 us; the launch traced here: 83.9 us
  starting transfers between devices  35 us (42%)
  waiting for transfers between devices  30.4 us (36%)
  Pallas kernels  16.6 us (20%)
  between operations  0.86 us (1%)
    ppermute x11, starting transfers between devices, crossed(): lax.ppermute(block, 'leaf', [(i, i ^ mask) for i in range(lax.axis_size('...  19.6 us
    ppermute x11, waiting for transfers between devices, crossed(): lax.ppermute(block, 'leaf', [(i, i ^ mask) for i in range(lax.axis_size('...  14.6 us
    ppermute x6, waiting for transfers between devices, shifted(): lax.ppermute(block, axis, [(i, (i + distance) % count) for i in range(cou...  10.6 us
    ppermute x6, starting transfers between devices, shifted(): lax.ppermute(block, axis, [(i, (i + distance) % count) for i in range(cou...  8.03 us
    ppermute x2, starting transfers between devices, outward(): lax.ppermute(block, 'leaf', [(i, (i + (2 * chips if i % 2 == 0 else -2 *...  7.42 us
    pallas_call x1, Pallas kernels, body(): pl.pallas_call(gather_kernel, out_shape=[struct((rank, rows), F32), struc...  6.15 us
    pallas_call x1, Pallas kernels, body(): pl.pallas_call(scatter_kernel, out_shape=[struct((rank, rows), BF), struc...  5.99 us
    ppermute x2, waiting for transfers between devices, outward(): lax.ppermute(block, 'leaf', [(i, (i + (2 * chips if i % 2 == 0 else -2 *...  5.25 us
  transfers between devices with their start and end apart: 19, of which 15 were waited for; matrix products, arithmetic and copies ran while one was open for 0% of the time, Pallas kernels for 0%

profile of v6, /device:TPU:1, one launch (start us, length us, event | category | flops | bytes accessed | tf_op | source)
XLA Modules:
  0.0 83.9 jit_solution(6727714938926818611)
XLA Ops:
  0.6 2.1 %project.1 = (f32[16,1024]{1,0:T(8,128)}, f32[48,1024]{1,0:T(8,128)}, bf16[64,1024]{1,0:T(8,128)(2,1)}, bf16[64,1024]{1,0:T(8,128)(2,1)}, bf16[64,1024]{1,0:T(8,128)(2,1)}) custom-call(bf16[48,1024]{1,0:T(8,128)(2,1)} %feat_ref.3, bf16[48,48]{1,0:T(8,128)(2,1)} %in_ref.3, bf16[48,1024]{1,0:T(8,128)(2,1)} %cot_ref.3, bf16[48,48]{1,0:T(8,128)(2,1)} %outf_ref.3), custom_call_target="tpu_custom_call" | custom-call | tf_op jit(solution)/shard_map/project/pallas_call | solution.py:246
  2.8 2.1 %collective-permute-start = (bf16[64,1024]{1,0:T(8,128)(2,1)}, bf16[64,1024]{1,0:T(8,128)(2,1)S(1)}, u32[]{:S(2)}, u32[]{:S(2)}) collective-permute-start(bf16[64,1024]{1,0:T(8,128)(2,1)} %get-tuple-element.25), channel_id=1, source_target_pairs={{0,1},{1,2},{2,3},{3,0},{4,5},{5,6},{6,7},{7,4},{8,9},{9,10},{10,1... | collective-permute-start | bytes 393224 | tf_op jit(solution)/shard_map/ppermute | solution.py:210
  4.9 1.4 %collective-permute-start.1 = (bf16[64,1024]{1,0:T(8,128)(2,1)}, bf16[64,1024]{1,0:T(8,128)(2,1)S(1)}, u32[]{:S(2)}, u32[]{:S(2)}) collective-permute-start(bf16[64,1024]{1,0:T(8,128)(2,1)} %get-tuple-element.26), channel_id=1, source_target_pairs={{0,3},{1,0},{2,1},{3,2},{4,7},{5,4},{6,5},{7,6},{8,11},{9,8},{10,9... | collective-permute-start | bytes 393224 | tf_op jit(solution)/shard_map/ppermute | solution.py:210
  6.3 1.6 %collective-permute-start.2 = (bf16[64,1024]{1,0:T(8,128)(2,1)}, bf16[64,1024]{1,0:T(8,128)(2,1)S(1)}, u32[]{:S(2)}, u32[]{:S(2)}) collective-permute-start(bf16[64,1024]{1,0:T(8,128)(2,1)} %get-tuple-element.27), channel_id=1, source_target_pairs={{0,2},{1,3},{2,0},{3,1},{4,6},{5,7},{6,4},{7,5},{8,10},{9,11},{10,... | collective-permute-start | bytes 393224 | tf_op jit(solution)/shard_map/ppermute | solution.py:210
  8.1 0.8 collective-permute-done.p1
  8.9 4.0 %collective-permute-done.2.p3 = bf16[64,1024]{1,0:T(8,128)(2,1)S(1)} collective-permute-done((bf16[64,1024]{1,0:T(8,128)(2,1)}, bf16[64,1024]{1,0:T(8,128)(2,1)S(1)}, u32[]{:S(2)}, u32[]{:S(2)}) %collective-permute-start.2) | collective-permute-done | bytes 131104 | tf_op jit(solution)/shard_map/ppermute | solution.py:210
  13.6 6.0 %scatter.1 = (bf16[48,1024]{1,0:T(8,128)(2,1)S(1)}, f32[16,1024]{1,0:T(8,128)S(1)}, f32[48,1024]{1,0:T(8,128)S(1)}, bf16[96,1024]{1,0:T(8,128)(2,1)S(1)}) custom-call(s32[8,8]{1,0:T(8,128)S(1)} %bitcast.7, f32[16,1024]{1,0:T(8,128)S(1)} %copy-done.7, f32[48,1024]{1,0:T(8,128)S(1)} %copy-done.5, bf16[64,1024]{1,0:T(8,128)(2,1)S(1)} %collective-permute-done.p1, ...), custom_call_target="tpu_custom_call" | custom-call | flops 5000000000 | bytes 1048576 | tf_op jit(solution)/shard_map/scatter/pallas_call | solution.py:256
  19.6 3.1 %collective-permute-start.3 = (bf16[96,1024]{1,0:T(8,128)(2,1)S(1)}, bf16[96,1024]{1,0:T(8,128)(2,1)S(1)}, u32[]{:S(2)}, u32[]{:S(2)}) collective-permute-start(bf16[96,1024]{1,0:T(8,128)(2,1)S(1)} %get-tuple-element.28), channel_id=1, source_target_pairs={{0,4},{4,0},{8,12},{12,8},{16,20},{20,16},{24,28},{28,24},{32,36},... | collective-permute-start | bytes 589832 | tf_op jit(solution)/shard_map/ppermute | solution.py:214
  22.7 1.1 %collective-permute-done.3 = bf16[96,1024]{1,0:T(8,128)(2,1)S(1)} collective-permute-done((bf16[96,1024]{1,0:T(8,128)(2,1)S(1)}, bf16[96,1024]{1,0:T(8,128)(2,1)S(1)}, u32[]{:S(2)}, u32[]{:S(2)}) %collective-permute-start.3) | collective-permute-done | bytes 196640 | tf_op jit(solution)/shard_map/ppermute | solution.py:214
  23.9 6.9 %collective-permute-start.4 = (bf16[64,1024]{1,0:T(8,128)(2,1)S(1)}, bf16[64,1024]{1,0:T(8,128)(2,1)S(1)}, u32[]{:S(2)}, u32[]{:S(2)}) collective-permute-start(bf16[64,1024]{1,0:T(8,128)(2,1)S(1)} %get-tuple-element.47), channel_id=1, source_target_pairs={{0,8},{4,252},{8,16},{12,4},{16,24},{20,12},{24,32},{28,20},{32,40... | collective-permute-start | bytes 393224 | tf_op jit(solution)/shard_map/ppermute | solution.py:219
  31.3 1.4 %collective-permute-done.4 = bf16[64,1024]{1,0:T(8,128)(2,1)S(1)} collective-permute-done((bf16[64,1024]{1,0:T(8,128)(2,1)S(1)}, bf16[64,1024]{1,0:T(8,128)(2,1)S(1)}, u32[]{:S(2)}, u32[]{:S(2)}) %collective-permute-start.4) | collective-permute-done | bytes 131104 | tf_op jit(solution)/shard_map/ppermute | solution.py:219
  32.7 3.8 %collective-permute-done.5 = bf16[64,1024]{1,0:T(8,128)(2,1)S(1)} collective-permute-done((bf16[64,1024]{1,0:T(8,128)(2,1)S(1)}, bf16[64,1024]{1,0:T(8,128)(2,1)S(1)}, u32[]{:S(2)}, u32[]{:S(2)}) %collective-permute-start.5) | collective-permute-done | bytes 131104 | tf_op jit(solution)/shard_map/ppermute | solution.py:219
  36.7 1.4 %collective-permute-done.6.cross_ref = bf16[80,1024]{1,0:T(8,128)(2,1)S(1)} collective-permute-done((bf16[80,1024]{1,0:T(8,128)(2,1)S(1)}, bf16[80,1024]{1,0:T(8,128)(2,1)S(1)}, u32[]{:S(2)}, u32[]{:S(2)}) %collective-permute-start.6) | collective-permute-done | bytes 163872 | tf_op jit(solution)/shard_map/ppermute | solution.py:214
  38.1 6.2 %gather.1 = (f32[48,1024]{1,0:T(8,128)S(1)}, f32[48,512]{1,0:T(8,128)S(1)}) custom-call(s32[8,8]{1,0:T(8,128)S(1)} %bitcast.8, bf16[16,1024]{1,0:T(8,128)(2,1)S(1)} %slice.51.own_ref, bf16[16,1024]{1,0:T(8,128)(2,1)S(1)} %get-tuple-element.45.pair_ref, bf16[32,1024]{1,0:T(8,128)(2,1)S(1)} %slice.71.near_ref, bf16[32,1024]{1,0:T(8,128)(2,1)S(1)} %slice.74.far_ref, ...), custom_call_target="tpu_custom_call" | custom-call | flops 5000000000 | bytes 1048576 | tf_op jit(solution)/shard_map/gather/pallas_call | solution.py:286
  44.3 0.9 %collective-permute-start.7 = (bf16[64,1024]{1,0:T(8,128)(2,1)S(1)}, bf16[64,1024]{1,0:T(8,128)(2,1)S(1)}, u32[]{:S(2)}, u32[]{:S(2)}) collective-permute-start(bf16[64,1024]{1,0:T(8,128)(2,1)S(1)} %pad_maximum_fusion.4.e0), channel_id=1, source_target_pairs={{0,1},{1,2},{2,3},{3,0},{4,5},{5,6},{6,7},{7,4},{8,9},{9,10},{10,1... | collective-permute-start | bytes 393224 | tf_op jit(solution)/shard_map/ppermute | solution.py:210
  45.3 1.8 %collective-permute-start.8 = (bf16[64,1024]{1,0:T(8,128)(2,1)S(1)}, bf16[64,1024]{1,0:T(8,128)(2,1)S(1)}, u32[]{:S(2)}, u32[]{:S(2)}) collective-permute-start(bf16[64,1024]{1,0:T(8,128)(2,1)S(1)} %pad_maximum_fusion.4.e0), channel_id=1, source_target_pairs={{0,3},{1,0},{2,1},{3,2},{4,7},{5,4},{6,5},{7,6},{8,11},{9,8},{10,9... | collective-permute-start | bytes 393224 | tf_op jit(solution)/shard_map/ppermute | solution.py:210
  47.2 3.4 %collective-permute-done.7.e1 = bf16[64,1024]{1,0:T(8,128)(2,1)S(1)} collective-permute-done((bf16[64,1024]{1,0:T(8,128)(2,1)S(1)}, bf16[64,1024]{1,0:T(8,128)(2,1)S(1)}, u32[]{:S(2)}, u32[]{:S(2)}) %collective-permute-start.7) | collective-permute-done | bytes 131104 | tf_op jit(solution)/shard_map/ppermute | solution.py:210
  50.6 2.3 %collective-permute-done.9.e2 = bf16[64,1024]{1,0:T(8,128)(2,1)S(1)} collective-permute-done((bf16[64,1024]{1,0:T(8,128)(2,1)S(1)}, bf16[64,1024]{1,0:T(8,128)(2,1)S(1)}, u32[]{:S(2)}, u32[]{:S(2)}) %collective-permute-start.9) | collective-permute-done | bytes 131104 | tf_op jit(solution)/shard_map/ppermute | solution.py:210
  52.9 1.5 %finish.1 = (bf16[48,1024]{1,0:T(8,128)(2,1)}, bf16[48,1024]{1,0:T(8,128)(2,1)}, f32[24,512]{1,0:T(8,128)S(1)}, f32[24,512]{1,0:T(8,128)S(1)}) custom-call(f32[48,1024]{1,0:T(8,128)S(1)} %get-tuple-element.31.mix_ref, bf16[64,1024]{1,0:T(8,128)(2,1)S(1)} %pad_maximum_fusion.4.e0, bf16[64,1024]{1,0:T(8,128)(2,1)S(1)} %collective-permute-done.7.e1, ...), custom_call_target="tpu_custom_call" | custom-call | tf_op jit(solution)/shard_map/finish/pallas_call | solution.py:301
  54.4 1.6 %collective-permute-start.10 = (f32[24,512]{1,0:T(8,128)S(1)}, f32[24,512]{1,0:T(8,128)S(1)}, u32[]{:S(2)}, u32[]{:S(2)}) collective-permute-start(f32[24,512]{1,0:T(8,128)S(1)} %get-tuple-element.37), channel_id=1, source_target_pairs={{0,4},{4,0},{8,12},{12,8},{16,20},{20,16},{24,28},{28,24},{32,36},... | collective-permute-start | bytes 147464 | tf_op jit(solution)/shard_map/ppermute | solution.py:214
  56.0 0.9 %collective-permute-done.10 = f32[24,512]{1,0:T(8,128)S(1)} collective-permute-done((f32[24,512]{1,0:T(8,128)S(1)}, f32[24,512]{1,0:T(8,128)S(1)}, u32[]{:S(2)}, u32[]{:S(2)}) %collective-permute-start.10) | collective-permute-done | bytes 49184 | tf_op jit(solution)/shard_map/ppermute | solution.py:214
  57.0 2.9 %collective-permute-done.11 = f32[24,512]{1,0:T(8,128)S(1)} collective-permute-done((f32[24,512]{1,0:T(8,128)S(1)}, f32[24,512]{1,0:T(8,128)S(1)}, u32[]{:S(2)}, u32[]{:S(2)}) %collective-permute-start.11) | collective-permute-done | bytes 49184 | tf_op jit(solution)/shard_map/ppermute | solution.py:214
  60.1 3.1 %collective-permute-start.14 = (f32[24,512]{1,0:T(8,128)S(1)}, f32[24,512]{1,0:T(8,128)S(1)}, u32[]{:S(2)}, u32[]{:S(2)}) collective-permute-start(f32[24,512]{1,0:T(8,128)S(1)} %add.59), channel_id=1, source_target_pairs={{0,16},{4,20},{8,24},{12,28},{16,0},{20,4},{24,8},{28,12},{32,48},... | collective-permute-start | bytes 147464 | tf_op jit(solution)/shard_map/ppermute | solution.py:214
  63.3 1.0 %collective-permute-done.13 = f32[24,512]{1,0:T(8,128)S(1)} collective-permute-done((f32[24,512]{1,0:T(8,128)S(1)}, f32[24,512]{1,0:T(8,128)S(1)}, u32[]{:S(2)}, u32[]{:S(2)}) %collective-permute-start.13) | collective-permute-done | bytes 49184 | tf_op jit(solution)/shard_map/ppermute | solution.py:214
  64.8 2.5 %collective-permute-start.15 = (f32[24,512]{1,0:T(8,128)S(1)}, f32[24,512]{1,0:T(8,128)S(1)}, u32[]{:S(2)}, u32[]{:S(2)}) collective-permute-start(f32[24,512]{1,0:T(8,128)S(1)} %add_add_fusion.1), channel_id=1, source_target_pairs={{0,64},{4,68},{8,72},{12,76},{16,80},{20,84},{24,88},{28,92},{32,9... | collective-permute-start | bytes 147464 | tf_op jit(solution)/shard_map/ppermute | solution.py:214
  67.3 3.1 %collective-permute-start.16 = (f32[24,512]{1,0:T(8,128)S(1)}, f32[24,512]{1,0:T(8,128)S(1)}, u32[]{:S(2)}, u32[]{:S(2)}) collective-permute-start(f32[24,512]{1,0:T(8,128)S(1)} %add_add_fusion.1), channel_id=1, source_target_pairs={{0,192},{4,196},{8,200},{12,204},{16,208},{20,212},{24,216},{28,22... | collective-permute-start | bytes 147464 | tf_op jit(solution)/shard_map/ppermute | solution.py:214
  70.4 0.9 %collective-permute-start.17 = (f32[24,512]{1,0:T(8,128)S(1)}, f32[24,512]{1,0:T(8,128)S(1)}, u32[]{:S(2)}, u32[]{:S(2)}) collective-permute-start(f32[24,512]{1,0:T(8,128)S(1)} %add_add_fusion.1), channel_id=1, source_target_pairs={{0,128},{4,132},{8,136},{12,140},{16,144},{20,148},{24,152},{28,15... | collective-permute-start | bytes 147464 | tf_op jit(solution)/shard_map/ppermute | solution.py:214
  71.4 1.6 %collective-permute-done.16 = f32[24,512]{1,0:T(8,128)S(1)} collective-permute-done((f32[24,512]{1,0:T(8,128)S(1)}, f32[24,512]{1,0:T(8,128)S(1)}, u32[]{:S(2)}, u32[]{:S(2)}) %collective-permute-start.16) | collective-permute-done | bytes 49184 | tf_op jit(solution)/shard_map/ppermute | solution.py:214
  73.0 4.3 %collective-permute-done.17 = f32[24,512]{1,0:T(8,128)S(1)} collective-permute-done((f32[24,512]{1,0:T(8,128)S(1)}, f32[24,512]{1,0:T(8,128)S(1)}, u32[]{:S(2)}, u32[]{:S(2)}) %collective-permute-start.17) | collective-permute-done | bytes 49184 | tf_op jit(solution)/shard_map/ppermute | solution.py:214
  77.3 4.8 %collective-permute-start.18 = (f32[24,512]{1,0:T(8,128)S(1)}, f32[24,512]{1,0:T(8,128)S(1)}, u32[]{:S(2)}, u32[]{:S(2)}) collective-permute-start(f32[24,512]{1,0:T(8,128)S(1)} %add_add_fusion.refs_0_), channel_id=1, source_target_pairs={{0,4},{4,0},{8,12},{12,8},{16,20},{20,16},{24,28},{28,24},{32,36},... | collective-permute-start | bytes 147464 | tf_op jit(solution)/shard_map/ppermute | solution.py:214
  82.2 0.9 %collective-permute-done.18.refs_1_ = f32[24,512]{1,0:T(8,128)S(1)} collective-permute-done((f32[24,512]{1,0:T(8,128)S(1)}, f32[24,512]{1,0:T(8,128)S(1)}, u32[]{:S(2)}, u32[]{:S(2)}) %collective-permute-start.18) | collective-permute-done | bytes 49184 | tf_op jit(solution)/shard_map/ppermute | solution.py:214
  83.1 0.8 %unpack.1 = (f32[48,48]{1,0:T(8,128)}, f32[12,27,48]{2,1,0:T(8,128)}, f32[48,48]{1,0:T(8,128)}) custom-call(f32[24,512]{1,0:T(8,128)S(1)} %add_add_fusion.refs_0_, f32[24,512]{1,0:T(8,128)S(1)} %collective-permute-done.18.refs_1_), custom_call_target="tpu_custom_call" | custom-call | tf_op jit(solution)/shard_map/unpack/pallas_call | solution.py:312
  (49 shorter events, 2.5 us)
Async XLA Ops:
  0.6 7.4 %copy-start.9 = (bf16[27,12,48]{2,0,1:T(8,128)(2,1)S(1)}, bf16[27,12,48]{2,0,1:T(8,128)(2,1)}, u32[]{:S(2)}) copy-start(bf16[27,12,48]{2,0,1:T(8,128)(2,1)} %param.10) | copy-start | bytes 93316
  2.8 6.1 %collective-permute-start = (bf16[64,1024]{1,0:T(8,128)(2,1)}, bf16[64,1024]{1,0:T(8,128)(2,1)S(1)}, u32[]{:S(2)}, u32[]{:S(2)}) collective-permute-start(bf16[64,1024]{1,0:T(8,128)(2,1)} %get-tuple-element.25), channel_id=1, source_target_pairs={{0,1},{1,2},{2,3},{3,0},{4,5},{5,6},{6,7},{7,4},{8,9},{9,10},{10,1... | collective-permute-start | bytes 393224 | tf_op jit(solution)/shard_map/ppermute | solution.py:210
  4.9 4.0 %collective-permute-start.1 = (bf16[64,1024]{1,0:T(8,128)(2,1)}, bf16[64,1024]{1,0:T(8,128)(2,1)S(1)}, u32[]{:S(2)}, u32[]{:S(2)}) collective-permute-start(bf16[64,1024]{1,0:T(8,128)(2,1)} %get-tuple-element.26), channel_id=1, source_target_pairs={{0,3},{1,0},{2,1},{3,2},{4,7},{5,4},{6,5},{7,6},{8,11},{9,8},{10,9... | collective-permute-start | bytes 393224 | tf_op jit(solution)/shard_map/ppermute | solution.py:210
  6.3 6.6 %copy-start.5 = (f32[48,1024]{1,0:T(8,128)S(1)}, f32[48,1024]{1,0:T(8,128)}, u32[]{:S(2)}) copy-start(f32[48,1024]{1,0:T(8,128)} %get-tuple-element.24.p0) | copy-start | bytes 589828
  6.3 6.6 %collective-permute-start.2 = (bf16[64,1024]{1,0:T(8,128)(2,1)}, bf16[64,1024]{1,0:T(8,128)(2,1)S(1)}, u32[]{:S(2)}, u32[]{:S(2)}) collective-permute-start(bf16[64,1024]{1,0:T(8,128)(2,1)} %get-tuple-element.27), channel_id=1, source_target_pairs={{0,2},{1,3},{2,0},{3,1},{4,6},{5,7},{6,4},{7,5},{8,10},{9,11},{10,... | collective-permute-start | bytes 393224 | tf_op jit(solution)/shard_map/ppermute | solution.py:210
  8.0 4.9 %copy-start.6 = (s32[27,1024]{1,0:T(8,128)S(1)}, s32[27,1024]{1,0:T(8,128)}, u32[]{:S(2)}) copy-start(s32[27,1024]{1,0:T(8,128)} %nbr_ref.3) | copy-start | bytes 331780
  8.0 4.9 %copy-start.7 = (f32[16,1024]{1,0:T(8,128)S(1)}, f32[16,1024]{1,0:T(8,128)}, u32[]{:S(2)}) copy-start(f32[16,1024]{1,0:T(8,128)} %get-tuple-element.23.r0) | copy-start | bytes 196612
  12.9 0.7 copy-start.8
  12.9 0.7 copy-start.4
  19.6 4.2 %collective-permute-start.3 = (bf16[96,1024]{1,0:T(8,128)(2,1)S(1)}, bf16[96,1024]{1,0:T(8,128)(2,1)S(1)}, u32[]{:S(2)}, u32[]{:S(2)}) collective-permute-start(bf16[96,1024]{1,0:T(8,128)(2,1)S(1)} %get-tuple-element.28), channel_id=1, source_target_pairs={{0,4},{4,0},{8,12},{12,8},{16,20},{20,16},{24,28},{28,24},{32,36},... | collective-permute-start | bytes 589832 | tf_op jit(solution)/shard_map/ppermute | solution.py:214
  23.9 8.8 %collective-permute-start.4 = (bf16[64,1024]{1,0:T(8,128)(2,1)S(1)}, bf16[64,1024]{1,0:T(8,128)(2,1)S(1)}, u32[]{:S(2)}, u32[]{:S(2)}) collective-permute-start(bf16[64,1024]{1,0:T(8,128)(2,1)S(1)} %get-tuple-element.47), channel_id=1, source_target_pairs={{0,8},{4,252},{8,16},{12,4},{16,24},{20,12},{24,32},{28,20},{32,40... | collective-permute-start | bytes 393224 | tf_op jit(solution)/shard_map/ppermute | solution.py:219
  30.8 5.8 %collective-permute-start.5 = (bf16[64,1024]{1,0:T(8,128)(2,1)S(1)}, bf16[64,1024]{1,0:T(8,128)(2,1)S(1)}, u32[]{:S(2)}, u32[]{:S(2)}) collective-permute-start(bf16[64,1024]{1,0:T(8,128)(2,1)S(1)} %get-tuple-element.46), channel_id=1, source_target_pairs={{0,16},{4,244},{8,24},{12,252},{16,32},{20,4},{24,40},{28,12},{32,... | collective-permute-start | bytes 393224 | tf_op jit(solution)/shard_map/ppermute | solution.py:219
  36.6 1.5 %collective-permute-start.6 = (bf16[80,1024]{1,0:T(8,128)(2,1)S(1)}, bf16[80,1024]{1,0:T(8,128)(2,1)S(1)}, u32[]{:S(2)}, u32[]{:S(2)}) collective-permute-start(bf16[80,1024]{1,0:T(8,128)(2,1)S(1)} %pad_maximum_fusion), channel_id=1, source_target_pairs={{0,4},{4,0},{8,12},{12,8},{16,20},{20,16},{24,28},{28,24},{32,36},... | collective-permute-start | bytes 491528 | tf_op jit(solution)/shard_map/ppermute | solution.py:214
  44.3 8.6 %copy-start = (bf16[48,1024]{1,0:T(8,128)(2,1)S(1)}, bf16[48,1024]{1,0:T(8,128)(2,1)}, u32[]{:S(2)}) copy-start(bf16[48,1024]{1,0:T(8,128)(2,1)} %feat_ref.3) | copy-start | bytes 294916
  44.3 8.6 %copy-start.1 = (bf16[48,1024]{1,0:T(8,128)(2,1)S(1)}, bf16[48,1024]{1,0:T(8,128)(2,1)}, u32[]{:S(2)}) copy-start(bf16[48,1024]{1,0:T(8,128)(2,1)} %cot_ref.3) | copy-start | bytes 294916
  44.3 8.6 %copy-start.2 = (bf16[48,48]{1,0:T(8,128)(2,1)S(1)}, bf16[48,48]{1,0:T(8,128)(2,1)}, u32[]{:S(2)}) copy-start(bf16[48,48]{1,0:T(8,128)(2,1)} %in_ref.3) | copy-start | bytes 13828
  44.3 8.6 %copy-start.3 = (bf16[48,48]{1,0:T(8,128)(2,1)S(1)}, bf16[48,48]{1,0:T(8,128)(2,1)}, u32[]{:S(2)}) copy-start(bf16[48,48]{1,0:T(8,128)(2,1)} %outf_ref.3) | copy-start | bytes 13828
  44.3 6.2 %collective-permute-start.7 = (bf16[64,1024]{1,0:T(8,128)(2,1)S(1)}, bf16[64,1024]{1,0:T(8,128)(2,1)S(1)}, u32[]{:S(2)}, u32[]{:S(2)}) collective-permute-start(bf16[64,1024]{1,0:T(8,128)(2,1)S(1)} %pad_maximum_fusion.4.e0), channel_id=1, source_target_pairs={{0,1},{1,2},{2,3},{3,0},{4,5},{5,6},{6,7},{7,4},{8,9},{9,10},{10,1... | collective-permute-start | bytes 393224 | tf_op jit(solution)/shard_map/ppermute | solution.py:210
  45.3 5.3 %collective-permute-start.8 = (bf16[64,1024]{1,0:T(8,128)(2,1)S(1)}, bf16[64,1024]{1,0:T(8,128)(2,1)S(1)}, u32[]{:S(2)}, u32[]{:S(2)}) collective-permute-start(bf16[64,1024]{1,0:T(8,128)(2,1)S(1)} %pad_maximum_fusion.4.e0), channel_id=1, source_target_pairs={{0,3},{1,0},{2,1},{3,2},{4,7},{5,4},{6,5},{7,6},{8,11},{9,8},{10,9... | collective-permute-start | bytes 393224 | tf_op jit(solution)/shard_map/ppermute | solution.py:210
  47.1 5.8 %collective-permute-start.9 = (bf16[64,1024]{1,0:T(8,128)(2,1)S(1)}, bf16[64,1024]{1,0:T(8,128)(2,1)S(1)}, u32[]{:S(2)}, u32[]{:S(2)}) collective-permute-start(bf16[64,1024]{1,0:T(8,128)(2,1)S(1)} %pad_maximum_fusion.4.e0), channel_id=1, source_target_pairs={{0,2},{1,3},{2,0},{3,1},{4,6},{5,7},{6,4},{7,5},{8,10},{9,11},{10,... | collective-permute-start | bytes 393224 | tf_op jit(solution)/shard_map/ppermute | solution.py:210
  54.4 2.5 %collective-permute-start.10 = (f32[24,512]{1,0:T(8,128)S(1)}, f32[24,512]{1,0:T(8,128)S(1)}, u32[]{:S(2)}, u32[]{:S(2)}) collective-permute-start(f32[24,512]{1,0:T(8,128)S(1)} %get-tuple-element.37), channel_id=1, source_target_pairs={{0,4},{4,0},{8,12},{12,8},{16,20},{20,16},{24,28},{28,24},{32,36},... | collective-permute-start | bytes 147464 | tf_op jit(solution)/shard_map/ppermute | solution.py:214
  56.9 3.0 %collective-permute-start.11 = (f32[24,512]{1,0:T(8,128)S(1)}, f32[24,512]{1,0:T(8,128)S(1)}, u32[]{:S(2)}, u32[]{:S(2)}) collective-permute-start(f32[24,512]{1,0:T(8,128)S(1)} %add.58), channel_id=1, source_target_pairs={{0,32},{4,36},{8,40},{12,44},{16,48},{20,52},{24,56},{28,60},{32,0... | collective-permute-start | bytes 147464 | tf_op jit(solution)/shard_map/ppermute | solution.py:214
  59.9 3.3 %collective-permute-start.12 = (f32[24,512]{1,0:T(8,128)S(1)}, f32[24,512]{1,0:T(8,128)S(1)}, u32[]{:S(2)}, u32[]{:S(2)}) collective-permute-start(f32[24,512]{1,0:T(8,128)S(1)} %add.59), channel_id=1, source_target_pairs={{0,8},{4,12},{8,0},{12,4},{16,24},{20,28},{24,16},{28,20},{32,40},... | collective-permute-start | bytes 147464 | tf_op jit(solution)/shard_map/ppermute | solution.py:214
  60.0 4.2 %collective-permute-start.13 = (f32[24,512]{1,0:T(8,128)S(1)}, f32[24,512]{1,0:T(8,128)S(1)}, u32[]{:S(2)}, u32[]{:S(2)}) collective-permute-start(f32[24,512]{1,0:T(8,128)S(1)} %add.59), channel_id=1, source_target_pairs={{0,24},{4,28},{8,16},{12,20},{16,8},{20,12},{24,0},{28,4},{32,56},... | collective-permute-start | bytes 147464 | tf_op jit(solution)/shard_map/ppermute | solution.py:214
  60.1 4.7 %collective-permute-start.14 = (f32[24,512]{1,0:T(8,128)S(1)}, f32[24,512]{1,0:T(8,128)S(1)}, u32[]{:S(2)}, u32[]{:S(2)}) collective-permute-start(f32[24,512]{1,0:T(8,128)S(1)} %add.59), channel_id=1, source_target_pairs={{0,16},{4,20},{8,24},{12,28},{16,0},{20,4},{24,8},{28,12},{32,48},... | collective-permute-start | bytes 147464 | tf_op jit(solution)/shard_map/ppermute | solution.py:214
  64.8 6.6 %collective-permute-start.15 = (f32[24,512]{1,0:T(8,128)S(1)}, f32[24,512]{1,0:T(8,128)S(1)}, u32[]{:S(2)}, u32[]{:S(2)}) collective-permute-start(f32[24,512]{1,0:T(8,128)S(1)} %add_add_fusion.1), channel_id=1, source_target_pairs={{0,64},{4,68},{8,72},{12,76},{16,80},{20,84},{24,88},{28,92},{32,9... | collective-permute-start | bytes 147464 | tf_op jit(solution)/shard_map/ppermute | solution.py:214
  67.3 5.7 %collective-permute-start.16 = (f32[24,512]{1,0:T(8,128)S(1)}, f32[24,512]{1,0:T(8,128)S(1)}, u32[]{:S(2)}, u32[]{:S(2)}) collective-permute-start(f32[24,512]{1,0:T(8,128)S(1)} %add_add_fusion.1), channel_id=1, source_target_pairs={{0,192},{4,196},{8,200},{12,204},{16,208},{20,212},{24,216},{28,22... | collective-permute-start | bytes 147464 | tf_op jit(solution)/shard_map/ppermute | solution.py:214
  70.4 6.9 %collective-permute-start.17 = (f32[24,512]{1,0:T(8,128)S(1)}, f32[24,512]{1,0:T(8,128)S(1)}, u32[]{:S(2)}, u32[]{:S(2)}) collective-permute-start(f32[24,512]{1,0:T(8,128)S(1)} %add_add_fusion.1), channel_id=1, source_target_pairs={{0,128},{4,132},{8,136},{12,140},{16,144},{20,148},{24,152},{28,15... | collective-permute-start | bytes 147464 | tf_op jit(solution)/shard_map/ppermute | solution.py:214
  77.3 5.7 %collective-permute-start.18 = (f32[24,512]{1,0:T(8,128)S(1)}, f32[24,512]{1,0:T(8,128)S(1)}, u32[]{:S(2)}, u32[]{:S(2)}) collective-permute-start(f32[24,512]{1,0:T(8,128)S(1)} %add_add_fusion.refs_0_), channel_id=1, source_target_pairs={{0,4},{4,0},{8,12},{12,8},{16,20},{20,16},{24,28},{28,24},{32,36},... | collective-permute-start | bytes 147464 | tf_op jit(solution)/shard_map/ppermute | solution.py:214

commit v7 on v6

--- a/solution.py
+++ b/solution.py
@@ -116,50 +116,86 @@
             kept_ref[(view - 5) * SLAB : (view - 4) * SLAB, :] = block
 
 
-def gather_kernel(halo_ref, own_ref, pair_ref, near_ref, far_ref, cross_ref, gm_ref, core_ref,
-                  nbr_ref, mix_ref, gc_ref, table_ref, ga_ref):
+def pick_rows(table_ref, nbr_ref, highs, start_of, store):
     rows = nbr_ref.shape[1]
-    tiles = table_ref.shape[0] // SLAB
-    own_tiles = rows // LOW
-    near = halo_ref.shape[0]
-    per_peer = (tiles - own_tiles) // near
-    for t in range(own_tiles):
-        table_ref[t * SLAB : (t + 1) * SLAB, :] = own_ref[:, t * LOW : (t + 1) * LOW]
-    views = (
-        far_ref[0:SLAB, :],
-        far_ref[SLAB:, :],
-        near_ref[0:SLAB, :],
-        near_ref[SLAB:, :],
-        pair_ref[...],
-        cross_ref[SLAB : 2 * SLAB, :],
-        cross_ref[0:SLAB, :],
-        cross_ref[3 * SLAB : 4 * SLAB, :],
-    )
-    for view in range(near):
-        slot = mirrored(core_bit(), view, near)
-        window = pltpu.roll(views[view].astype(F32), rows - first_octant(halo_ref, slot), 1).astype(BF)
-        for i in range(per_peer):
-            t = own_tiles + slot * per_peer + i
-            table_ref[pl.ds(pl.multiple_of(t * SLAB, SLAB), SLAB), :] = window[:, i * LOW : (i + 1) * LOW]
-
-    def step(k, carry):
+    offsets = nbr_ref.shape[0]
+    middle = offsets // 2
+
+    def step(i, carry):
+        k = i + (i >= middle)
         index = nbr_ref[pl.ds(k, 1), :]
         onehot = low_onehot(index & (LOW - 1))
         high = jnp.broadcast_to(index >> 8, (SLAB, rows))
         picked = dot(table_ref[...], onehot)
-        found = jnp.zeros((SLAB, rows), F32)
-        for t in range(tiles):
-            found = jnp.where(high == t, picked[t * SLAB : (t + 1) * SLAB], found)
-        ga_ref[pl.ds(pl.multiple_of(k * SLAB, SLAB), SLAB), :] = found.astype(BF)
+        place = pl.ds(pl.multiple_of(k * SLAB, SLAB), SLAB)
+        found = start_of(place)
+        for t, value in enumerate(highs):
+            found = jnp.where(high == value, picked[t * SLAB : (t + 1) * SLAB], found)
+        store(place, found.astype(BF))
         return carry
 
-    offsets = nbr_ref.shape[0]
-    middle = offsets // 2
-    lax.fori_loop(0, offsets - 1, lambda i, carry: step(i + (i >= middle), carry), 0, unroll=13)
+    lax.fori_loop(0, offsets - 1, step, 0, unroll=13)
+
+
+def fill_window(table_ref, at, block, halo_ref, slot, per_peer):
+    rows = block.shape[1]
+    window = pltpu.roll(block.astype(F32), rows - first_octant(halo_ref, slot), 1).astype(BF)
+    for i in range(per_peer):
+        table_ref[at + i * SLAB : at + (i + 1) * SLAB, :] = window[:, i * LOW : (i + 1) * LOW]
+
+
+def near_gather_kernel(halo_ref, own_ref, pair_ref, nbr_ref, ga_ref, table_ref):
+    rows = nbr_ref.shape[1]
+    own_tiles = rows // LOW
+    per_peer = table_ref.shape[0] // SLAB - own_tiles
+    for t in range(own_tiles):
+        table_ref[t * SLAB : (t + 1) * SLAB, :] = own_ref[:, t * LOW : (t + 1) * LOW]
+    slot = mirrored(core_bit(), 4, halo_ref.shape[0])
+    fill_window(table_ref, own_tiles * SLAB, pair_ref[...], halo_ref, slot, per_peer)
+    highs = list(range(own_tiles)) + [own_tiles + slot * per_peer + i for i in range(per_peer)]
+    middle = nbr_ref.shape[0] // 2
+
+    def store(place, found):
+        ga_ref[place, :] = found
+
+    pick_rows(table_ref, nbr_ref, highs, lambda place: jnp.zeros((SLAB, rows), F32), store)
     ga_ref[middle * SLAB : (middle + 1) * SLAB, :] = own_ref[...]
+
+
+def far_gather_kernel(halo_ref, base_ref, near_ref, far_ref, cross_ref, core_ref, nbr_ref, mix_ref, ga_ref,
+                      table_ref):
+    rows = nbr_ref.shape[1]
+    own_tiles = rows // LOW
+    near = halo_ref.shape[0]
+    views = {
+        0: far_ref[0:SLAB, :],
+        1: far_ref[SLAB:, :],
+        2: near_ref[0:SLAB, :],
+        3: near_ref[SLAB:, :],
+        5: cross_ref[SLAB : 2 * SLAB, :],
+        6: cross_ref[0:SLAB, :],
+        7: cross_ref[3 * SLAB : 4 * SLAB, :],
+    }
+    per_peer = table_ref.shape[0] // SLAB // len(views)
+    highs = []
+    for n, (view, block) in enumerate(views.items()):
+        slot = mirrored(core_bit(), view, near)
+        fill_window(table_ref, n * per_peer * SLAB, block, halo_ref, slot, per_peer)
+        highs += [own_tiles + slot * per_peer + i for i in range(per_peer)]
     used = core_ref.shape[0]
+    middle = nbr_ref.shape[0] // 2
+    itself = slice(middle * SLAB, (middle + 1) * SLAB)
+
+    def store(place, found):
+        ga_ref[place, :] = found
+
+    pick_rows(table_ref, nbr_ref, highs, lambda place: base_ref[place, :].astype(F32), store)
+    ga_ref[itself, :] = base_ref[itself, :]
     ga_ref[used:, :] = jnp.zeros_like(ga_ref[used:, :])
     mix_ref[...] = dot(core_ref[...], ga_ref[:used, :], TN)
+
+
+def core_gradient_kernel(gm_ref, ga_ref, gc_ref):
     gc_ref[...] = dot(gm_ref[...], ga_ref[...], NT)
 
 
@@ -277,22 +313,44 @@
     to_far = [slabs_of(kept, 2, 3) + far_same, far_other]
     near = outward(jnp.concatenate([reduced, pair] + [x.astype(BF) for x in to_near], 0), 1)
     far = outward(jnp.concatenate([reduced, pair] + [x.astype(BF) for x in to_far], 0), 2)
+    per_peer = slots * 64 // LOW
+    near_tiles = rows // LOW + per_peer
+    found = pl.pallas_call(
+        near_gather_kernel,
+        out_shape=struct((offsets * SLAB, rows), BF),
+        in_specs=[SMEM] + [VMEM] * 3,
+        out_specs=VMEM,
+        scratch_shapes=[pltpu.VMEM((near_tiles * SLAB, LOW), BF)],
+        compiler_params=ROOMY,
+        cost_estimate=estimate,
+        name="near_gather",
+    )(halo, reduced, pair, neighbours)
+    near, far, found = lax.optimization_barrier((near, far, found))
     near_pair, far_pair = slabs_of(near, 0, 2), slabs_of(far, 0, 2)
     passed = slabs_of(near, 3, 4).astype(F32) + slabs_of(far, 3, 4).astype(F32)
     beyond = crossed(jnp.concatenate([near_pair, far_pair, passed.astype(BF)], 0), 1)
     returned = (slabs_of(near, 2, 3).astype(F32) + slabs_of(far, 2, 3).astype(F32)) + slabs_of(beyond, 4, 5).astype(F32)
     grad_slab = (((own + mine) + returned) * keep.astype(F32)).astype(BF)
 
-    mixed_part, grad_core = pl.pallas_call(
-        gather_kernel,
-        out_shape=[struct((rank, rows), F32), struct((rank, packed_width), F32)],
-        in_specs=[SMEM] + [VMEM] * 8,
+    mixed_part, gathered = pl.pallas_call(
+        far_gather_kernel,
+        out_shape=[struct((rank, rows), F32), struct((packed_width, rows), BF)],
+        in_specs=[SMEM] + [VMEM] * 6,
         out_specs=[VMEM] * 2,
-        scratch_shapes=[pltpu.VMEM((table_rows, LOW), BF), pltpu.VMEM((packed_width, rows), BF)],
+        scratch_shapes=[pltpu.VMEM((table_rows - near_tiles * SLAB, LOW), BF)],
         compiler_params=ROOMY,
         cost_estimate=estimate,
-        name="gather",
-    )(halo, reduced, pair, near_pair, far_pair, beyond, grad_mixed, core_rows, neighbours)
+        name="far_gather",
+    )(halo, found, near_pair, far_pair, beyond, core_rows, neighbours)
+    grad_core = pl.pallas_call(
+        core_gradient_kernel,
+        out_shape=struct((rank, packed_width), F32),
+        in_specs=[VMEM] * 2,
+        out_specs=VMEM,
+        compiler_params=SNUG,
+        cost_estimate=pl.CostEstimate(flops=5 * 10**8, bytes_accessed=2**20, transcendentals=0),
+        name="core_gradient",
+    )(grad_mixed, gathered)
 
     shared = jnp.concatenate([grad_slab, mixed_part.astype(BF)], 0)
     exchanged = [shared] + [shifted(shared, "chan", j) for j in (1, 3, 2)]

time: 84.1 us -> 80.1 us (0.952)
  waiting for transfers between devices: 30.4 us -> 24 us
  Pallas kernels: 16.6 us -> 18.5 us
    ppermute x2, waiting for transfers between devices: 5.25 us -> 0.08 us  [outward(): lax.ppermute(block, 'leaf', [(i, (i + (2 * chips if i % 2 == 0 else -2 *...]
    pallas_call x1 -> x3, Pallas kernels: 6.15 us -> 8.09 us  [the longest x1 4.5 us: body(): pl.pallas_call(far_gather_kernel, out_shape=[struct((rank, rows), F32), s...]
    ppermute x11, waiting for transfers between devices: 14.6 us -> 13.6 us  [crossed(): lax.ppermute(block, 'leaf', [(i, i ^ mask) for i in range(lax.axis_size('...]
  transfers between devices with their start and end apart: 19 -> 19, of which waited for: 15 -> 16; matrix products, arithmetic and copies ran while one was open for 0% -> 0% of each run, Pallas kernels for 0% -> 4%
where the time goes in v7:
time: 80.1 us; the launch traced here: 79.9 us
  starting transfers between devices  35.6 us (44%)
  waiting for transfers between devices  24 us (30%)
  Pallas kernels  18.5 us (23%)
  between operations  0.82 us (1%)
  local copies, waits for them, and re-layouts  0.81 us (1%)
    ppermute x11, starting transfers between devices, crossed(): lax.ppermute(block, 'leaf', [(i, i ^ mask) for i in range(lax.axis_size('...  19 us
    ppermute x11, waiting for transfers between devices, crossed(): lax.ppermute(block, 'leaf', [(i, i ^ mask) for i in range(lax.axis_size('...  13.6 us
    ppermute x6, waiting for transfers between devices, shifted(): lax.ppermute(block, axis, [(i, (i + distance) % count) for i in range(cou...  10.3 us
    ppermute x6, starting transfers between devices, shifted(): lax.ppermute(block, axis, [(i, (i + distance) % count) for i in range(cou...  8.56 us
    ppermute x2, starting transfers between devices, outward(): lax.ppermute(block, 'leaf', [(i, (i + (2 * chips if i % 2 == 0 else -2 *...  8.02 us
    pallas_call x1, Pallas kernels, body(): pl.pallas_call(scatter_kernel, out_shape=[struct((rank, rows), BF), struc...  5.98 us
    pallas_call x1, Pallas kernels, body(): pl.pallas_call(far_gather_kernel, out_shape=[struct((rank, rows), F32), s...  4.5 us
    pallas_call x1, Pallas kernels, body(): pl.pallas_call(near_gather_kernel, out_shape=struct((offsets * SLAB, rows...  3.16 us
  transfers between devices with their start and end apart: 19, of which 16 were waited for; matrix products, arithmetic and copies ran while one was open for 0% of the time, Pallas kernels for 4%

profile of v7, /device:TPU:1, one launch (start us, length us, event | category | flops | bytes accessed | tf_op | source)
XLA Modules:
  0.0 79.9 jit_solution(1645469052366177437)
XLA Ops:
  0.6 2.1 %project.1 = (f32[16,1024]{1,0:T(8,128)}, f32[48,1024]{1,0:T(8,128)}, bf16[64,1024]{1,0:T(8,128)(2,1)}, bf16[64,1024]{1,0:T(8,128)(2,1)}, bf16[64,1024]{1,0:T(8,128)(2,1)}) custom-call(bf16[48,1024]{1,0:T(8,128)(2,1)} %feat_ref.3, bf16[48,48]{1,0:T(8,128)(2,1)} %in_ref.3, bf16[48,1024]{1,0:T(8,128)(2,1)} %cot_ref.3, bf16[48,48]{1,0:T(8,128)(2,1)} %outf_ref.3), custom_call_target="tpu_custom_call" | custom-call | tf_op jit(solution)/shard_map/project/pallas_call | solution.py:282
  2.8 2.1 %collective-permute-start = (bf16[64,1024]{1,0:T(8,128)(2,1)}, bf16[64,1024]{1,0:T(8,128)(2,1)S(1)}, u32[]{:S(2)}, u32[]{:S(2)}) collective-permute-start(bf16[64,1024]{1,0:T(8,128)(2,1)} %get-tuple-element.28), channel_id=1, source_target_pairs={{0,1},{1,2},{2,3},{3,0},{4,5},{5,6},{6,7},{7,4},{8,9},{9,10},{10,1... | collective-permute-start | bytes 393224 | tf_op jit(solution)/shard_map/ppermute | solution.py:246
  4.9 1.4 %collective-permute-start.1 = (bf16[64,1024]{1,0:T(8,128)(2,1)}, bf16[64,1024]{1,0:T(8,128)(2,1)S(1)}, u32[]{:S(2)}, u32[]{:S(2)}) collective-permute-start(bf16[64,1024]{1,0:T(8,128)(2,1)} %get-tuple-element.29), channel_id=1, source_target_pairs={{0,3},{1,0},{2,1},{3,2},{4,7},{5,4},{6,5},{7,6},{8,11},{9,8},{10,9... | collective-permute-start | bytes 393224 | tf_op jit(solution)/shard_map/ppermute | solution.py:246
  6.3 1.6 %collective-permute-start.2 = (bf16[64,1024]{1,0:T(8,128)(2,1)}, bf16[64,1024]{1,0:T(8,128)(2,1)S(1)}, u32[]{:S(2)}, u32[]{:S(2)}) collective-permute-start(bf16[64,1024]{1,0:T(8,128)(2,1)} %get-tuple-element.30), channel_id=1, source_target_pairs={{0,2},{1,3},{2,0},{3,1},{4,6},{5,7},{6,4},{7,5},{8,10},{9,11},{10,... | collective-permute-start | bytes 393224 | tf_op jit(solution)/shard_map/ppermute | solution.py:246
  8.1 0.8 %collective-permute-done.p1 = bf16[64,1024]{1,0:T(8,128)(2,1)S(1)} collective-permute-done((bf16[64,1024]{1,0:T(8,128)(2,1)}, bf16[64,1024]{1,0:T(8,128)(2,1)S(1)}, u32[]{:S(2)}, u32[]{:S(2)}) %collective-permute-start) | collective-permute-done | bytes 131104 | tf_op jit(solution)/shard_map/ppermute | solution.py:246
  8.9 4.0 %collective-permute-done.2.p3 = bf16[64,1024]{1,0:T(8,128)(2,1)S(1)} collective-permute-done((bf16[64,1024]{1,0:T(8,128)(2,1)}, bf16[64,1024]{1,0:T(8,128)(2,1)S(1)}, u32[]{:S(2)}, u32[]{:S(2)}) %collective-permute-start.2) | collective-permute-done | bytes 131104 | tf_op jit(solution)/shard_map/ppermute | solution.py:246
  13.6 6.0 %scatter.1 = (bf16[48,1024]{1,0:T(8,128)(2,1)S(1)}, f32[16,1024]{1,0:T(8,128)S(1)}, f32[48,1024]{1,0:T(8,128)S(1)}, bf16[96,1024]{1,0:T(8,128)(2,1)S(1)}) custom-call(s32[8,8]{1,0:T(8,128)S(1)} %bitcast.7, f32[16,1024]{1,0:T(8,128)S(1)} %copy-done.7, f32[48,1024]{1,0:T(8,128)S(1)} %copy-done.5, bf16[64,1024]{1,0:T(8,128)(2,1)S(1)} %collective-permute-done.p1, ...), custom_call_target="tpu_custom_call" | custom-call | flops 5000000000 | bytes 1048576 | tf_op jit(solution)/shard_map/scatter/pallas_call | solution.py:292
  19.6 3.1 %collective-permute-start.3 = (bf16[96,1024]{1,0:T(8,128)(2,1)S(1)}, bf16[96,1024]{1,0:T(8,128)(2,1)S(1)}, u32[]{:S(2)}, u32[]{:S(2)}) collective-permute-start(bf16[96,1024]{1,0:T(8,128)(2,1)S(1)} %get-tuple-element.31), channel_id=1, source_target_pairs={{0,4},{4,0},{8,12},{12,8},{16,20},{20,16},{24,28},{28,24},{32,36},... | collective-permute-start | bytes 589832 | tf_op jit(solution)/shard_map/ppermute | solution.py:250
  22.7 1.1 %collective-permute-done.3 = bf16[96,1024]{1,0:T(8,128)(2,1)S(1)} collective-permute-done((bf16[96,1024]{1,0:T(8,128)(2,1)S(1)}, bf16[96,1024]{1,0:T(8,128)(2,1)S(1)}, u32[]{:S(2)}, u32[]{:S(2)}) %collective-permute-start.3) | collective-permute-done | bytes 196640 | tf_op jit(solution)/shard_map/ppermute | solution.py:250
  23.9 7.2 %collective-permute-start.5 = (bf16[64,1024]{1,0:T(8,128)(2,1)S(1)}, bf16[64,1024]{1,0:T(8,128)(2,1)S(1)}, u32[]{:S(2)}, u32[]{:S(2)}) collective-permute-start(bf16[64,1024]{1,0:T(8,128)(2,1)S(1)} %get-tuple-element.52), channel_id=1, source_target_pairs={{0,16},{4,244},{8,24},{12,252},{16,32},{20,4},{24,40},{28,12},{32,... | collective-permute-start | bytes 393224 | tf_op jit(solution)/shard_map/ppermute | solution.py:255
  31.0 0.9 %collective-permute-start.4 = (bf16[64,1024]{1,0:T(8,128)(2,1)S(1)}, bf16[64,1024]{1,0:T(8,128)(2,1)S(1)}, u32[]{:S(2)}, u32[]{:S(2)}) collective-permute-start(bf16[64,1024]{1,0:T(8,128)(2,1)S(1)} %get-tuple-element.53), channel_id=1, source_target_pairs={{0,8},{4,252},{8,16},{12,4},{16,24},{20,12},{24,32},{28,20},{32,40... | collective-permute-start | bytes 393224 | tf_op jit(solution)/shard_map/ppermute | solution.py:255
  31.9 3.2 %near_gather.1.base_ref = bf16[432,1024]{1,0:T(8,128)(2,1)S(1)} custom-call(s32[8,8]{1,0:T(8,128)S(1)} %bitcast.8, bf16[16,1024]{1,0:T(8,128)(2,1)S(1)} %slice.51.own_ref, bf16[16,1024]{1,0:T(8,128)(2,1)S(1)} %get-tuple-element.51.pair_ref, s32[27,1024]{1,0:T(8,128)S(1)} %copy-done.6), custom_call_target="tpu_custom_call" | custom-call | flops 5000000000 | bytes 1048576 | tf_op jit(solution)/shard_map/near_gather/pallas_call | solution.py:318
  35.2 1.0 %collective-permute-start.6 = (bf16[80,1024]{1,0:T(8,128)(2,1)S(1)}, bf16[80,1024]{1,0:T(8,128)(2,1)S(1)}, u32[]{:S(2)}, u32[]{:S(2)}) collective-permute-start(bf16[80,1024]{1,0:T(8,128)(2,1)S(1)} %pad_maximum_fusion), channel_id=1, source_target_pairs={{0,4},{4,0},{8,12},{12,8},{16,20},{20,16},{24,28},{28,24},{32,36},... | collective-permute-start | bytes 491528 | tf_op jit(solution)/shard_map/ppermute | solution.py:250
  36.2 1.0 %collective-permute-done.6.cross_ref = bf16[80,1024]{1,0:T(8,128)(2,1)S(1)} collective-permute-done((bf16[80,1024]{1,0:T(8,128)(2,1)S(1)}, bf16[80,1024]{1,0:T(8,128)(2,1)S(1)}, u32[]{:S(2)}, u32[]{:S(2)}) %collective-permute-start.6) | collective-permute-done | bytes 163872 | tf_op jit(solution)/shard_map/ppermute | solution.py:250
  37.3 4.5 %far_gather.1 = (f32[48,1024]{1,0:T(8,128)S(1)}, bf16[512,1024]{1,0:T(8,128)(2,1)S(1)}) custom-call(s32[8,8]{1,0:T(8,128)S(1)} %bitcast.9, bf16[432,1024]{1,0:T(8,128)(2,1)S(1)} %near_gather.1.base_ref, bf16[32,1024]{1,0:T(8,128)(2,1)S(1)} %slice.60.near_ref, bf16[32,1024]{1,0:T(8,128)(2,1)S(1)} %slice.61.far_ref, ...), custom_call_target="tpu_custom_call" | custom-call | flops 5000000000 | bytes 1048576 | tf_op jit(solution)/shard_map/far_gather/pallas_call | solution.py:335
  41.8 1.0 %collective-permute-start.9 = (bf16[64,1024]{1,0:T(8,128)(2,1)S(1)}, bf16[64,1024]{1,0:T(8,128)(2,1)S(1)}, u32[]{:S(2)}, u32[]{:S(2)}) collective-permute-start(bf16[64,1024]{1,0:T(8,128)(2,1)S(1)} %pad_maximum_fusion.4.e0), channel_id=1, source_target_pairs={{0,2},{1,3},{2,0},{3,1},{4,6},{5,7},{6,4},{7,5},{8,10},{9,11},{10,... | collective-permute-start | bytes 393224 | tf_op jit(solution)/shard_map/ppermute | solution.py:246
  42.8 2.3 %collective-permute-start.8 = (bf16[64,1024]{1,0:T(8,128)(2,1)S(1)}, bf16[64,1024]{1,0:T(8,128)(2,1)S(1)}, u32[]{:S(2)}, u32[]{:S(2)}) collective-permute-start(bf16[64,1024]{1,0:T(8,128)(2,1)S(1)} %pad_maximum_fusion.4.e0), channel_id=1, source_target_pairs={{0,3},{1,0},{2,1},{3,2},{4,7},{5,4},{6,5},{7,6},{8,11},{9,8},{10,9... | collective-permute-start | bytes 393224 | tf_op jit(solution)/shard_map/ppermute | solution.py:246
  45.6 2.5 %collective-permute-done.9.e2 = bf16[64,1024]{1,0:T(8,128)(2,1)S(1)} collective-permute-done((bf16[64,1024]{1,0:T(8,128)(2,1)S(1)}, bf16[64,1024]{1,0:T(8,128)(2,1)S(1)}, u32[]{:S(2)}, u32[]{:S(2)}) %collective-permute-start.9) | collective-permute-done | bytes 131104 | tf_op jit(solution)/shard_map/ppermute | solution.py:246
  48.1 1.9 %collective-permute-done.8.e3 = bf16[64,1024]{1,0:T(8,128)(2,1)S(1)} collective-permute-done((bf16[64,1024]{1,0:T(8,128)(2,1)S(1)}, bf16[64,1024]{1,0:T(8,128)(2,1)S(1)}, u32[]{:S(2)}, u32[]{:S(2)}) %collective-permute-start.8) | collective-permute-done | bytes 131104 | tf_op jit(solution)/shard_map/ppermute | solution.py:246
  50.1 1.0 %collective-permute-done.7.e1 = bf16[64,1024]{1,0:T(8,128)(2,1)S(1)} collective-permute-done((bf16[64,1024]{1,0:T(8,128)(2,1)S(1)}, bf16[64,1024]{1,0:T(8,128)(2,1)S(1)}, u32[]{:S(2)}, u32[]{:S(2)}) %collective-permute-start.7) | collective-permute-done | bytes 131104 | tf_op jit(solution)/shard_map/ppermute | solution.py:246
  51.1 1.5 %finish.1 = (bf16[48,1024]{1,0:T(8,128)(2,1)}, bf16[48,1024]{1,0:T(8,128)(2,1)}, f32[24,512]{1,0:T(8,128)S(1)}, f32[24,512]{1,0:T(8,128)S(1)}) custom-call(f32[48,1024]{1,0:T(8,128)S(1)} %get-tuple-element.36.mix_ref, bf16[64,1024]{1,0:T(8,128)(2,1)S(1)} %pad_maximum_fusion.4.e0, bf16[64,1024]{1,0:T(8,128)(2,1)S(1)} %collective-permute-done.7.e1, ...), custom_call_target="tpu_custom_call" | custom-call | tf_op jit(solution)/shard_map/finish/pallas_call | solution.py:359
  52.6 1.5 %collective-permute-start.10 = (f32[24,512]{1,0:T(8,128)S(1)}, f32[24,512]{1,0:T(8,128)S(1)}, u32[]{:S(2)}, u32[]{:S(2)}) collective-permute-start(f32[24,512]{1,0:T(8,128)S(1)} %get-tuple-element.43), channel_id=1, source_target_pairs={{0,4},{4,0},{8,12},{12,8},{16,20},{20,16},{24,28},{28,24},{32,36},... | collective-permute-start | bytes 147464 | tf_op jit(solution)/shard_map/ppermute | solution.py:250
  54.1 0.9 %collective-permute-done.10 = f32[24,512]{1,0:T(8,128)S(1)} collective-permute-done((f32[24,512]{1,0:T(8,128)S(1)}, f32[24,512]{1,0:T(8,128)S(1)}, u32[]{:S(2)}, u32[]{:S(2)}) %collective-permute-start.10) | collective-permute-done | bytes 49184 | tf_op jit(solution)/shard_map/ppermute | solution.py:250
  55.1 2.9 %collective-permute-done.11 = f32[24,512]{1,0:T(8,128)S(1)} collective-permute-done((f32[24,512]{1,0:T(8,128)S(1)}, f32[24,512]{1,0:T(8,128)S(1)}, u32[]{:S(2)}, u32[]{:S(2)}) %collective-permute-start.11) | collective-permute-done | bytes 49184 | tf_op jit(solution)/shard_map/ppermute | solution.py:250
  58.6 1.7 %collective-permute-start.13 = (f32[24,512]{1,0:T(8,128)S(1)}, f32[24,512]{1,0:T(8,128)S(1)}, u32[]{:S(2)}, u32[]{:S(2)}) collective-permute-start(f32[24,512]{1,0:T(8,128)S(1)} %add.59), channel_id=1, source_target_pairs={{0,24},{4,28},{8,16},{12,20},{16,8},{20,12},{24,0},{28,4},{32,56},... | collective-permute-start | bytes 147464 | tf_op jit(solution)/shard_map/ppermute | solution.py:250
  60.7 1.8 %collective-permute-done.14 = f32[24,512]{1,0:T(8,128)S(1)} collective-permute-done((f32[24,512]{1,0:T(8,128)S(1)}, f32[24,512]{1,0:T(8,128)S(1)}, u32[]{:S(2)}, u32[]{:S(2)}) %collective-permute-start.14) | collective-permute-done | bytes 49184 | tf_op jit(solution)/shard_map/ppermute | solution.py:250
  63.3 5.5 %collective-permute-start.17 = (f32[24,512]{1,0:T(8,128)S(1)}, f32[24,512]{1,0:T(8,128)S(1)}, u32[]{:S(2)}, u32[]{:S(2)}) collective-permute-start(f32[24,512]{1,0:T(8,128)S(1)} %add_add_fusion.1), channel_id=1, source_target_pairs={{0,128},{4,132},{8,136},{12,140},{16,144},{20,148},{24,152},{28,15... | collective-permute-start | bytes 147464 | tf_op jit(solution)/shard_map/ppermute | solution.py:250
  68.8 1.4 %collective-permute-start.15 = (f32[24,512]{1,0:T(8,128)S(1)}, f32[24,512]{1,0:T(8,128)S(1)}, u32[]{:S(2)}, u32[]{:S(2)}) collective-permute-start(f32[24,512]{1,0:T(8,128)S(1)} %add_add_fusion.1), channel_id=1, source_target_pairs={{0,64},{4,68},{8,72},{12,76},{16,80},{20,84},{24,88},{28,92},{32,9... | collective-permute-start | bytes 147464 | tf_op jit(solution)/shard_map/ppermute | solution.py:250
  70.4 4.1 %collective-permute-done.16 = f32[24,512]{1,0:T(8,128)S(1)} collective-permute-done((f32[24,512]{1,0:T(8,128)S(1)}, f32[24,512]{1,0:T(8,128)S(1)}, u32[]{:S(2)}, u32[]{:S(2)}) %collective-permute-start.16) | collective-permute-done | bytes 49184 | tf_op jit(solution)/shard_map/ppermute | solution.py:250
  74.5 3.7 %collective-permute-start.18 = (f32[24,512]{1,0:T(8,128)S(1)}, f32[24,512]{1,0:T(8,128)S(1)}, u32[]{:S(2)}, u32[]{:S(2)}) collective-permute-start(f32[24,512]{1,0:T(8,128)S(1)} %add_add_fusion.refs_0_), channel_id=1, source_target_pairs={{0,4},{4,0},{8,12},{12,8},{16,20},{20,16},{24,28},{28,24},{32,36},... | collective-permute-start | bytes 147464 | tf_op jit(solution)/shard_map/ppermute | solution.py:250
  78.2 0.9 %collective-permute-done.18.refs_1_ = f32[24,512]{1,0:T(8,128)S(1)} collective-permute-done((f32[24,512]{1,0:T(8,128)S(1)}, f32[24,512]{1,0:T(8,128)S(1)}, u32[]{:S(2)}, u32[]{:S(2)}) %collective-permute-start.18) | collective-permute-done | bytes 49184 | tf_op jit(solution)/shard_map/ppermute | solution.py:250
  79.1 0.8 %unpack.1 = (f32[48,48]{1,0:T(8,128)}, f32[12,27,48]{2,1,0:T(8,128)}, f32[48,48]{1,0:T(8,128)}) custom-call(f32[24,512]{1,0:T(8,128)S(1)} %add_add_fusion.refs_0_, f32[24,512]{1,0:T(8,128)S(1)} %collective-permute-done.18.refs_1_), custom_call_target="tpu_custom_call" | custom-call | tf_op jit(solution)/shard_map/unpack/pallas_call | solution.py:370
  (51 shorter events, 3.5 us)
Async XLA Ops:
  0.6 7.4 %copy-start.9 = (bf16[27,12,48]{2,0,1:T(8,128)(2,1)S(1)}, bf16[27,12,48]{2,0,1:T(8,128)(2,1)}, u32[]{:S(2)}) copy-start(bf16[27,12,48]{2,0,1:T(8,128)(2,1)} %param.10) | copy-start | bytes 93316
  2.8 6.1 %collective-permute-start = (bf16[64,1024]{1,0:T(8,128)(2,1)}, bf16[64,1024]{1,0:T(8,128)(2,1)S(1)}, u32[]{:S(2)}, u32[]{:S(2)}) collective-permute-start(bf16[64,1024]{1,0:T(8,128)(2,1)} %get-tuple-element.28), channel_id=1, source_target_pairs={{0,1},{1,2},{2,3},{3,0},{4,5},{5,6},{6,7},{7,4},{8,9},{9,10},{10,1... | collective-permute-start | bytes 393224 | tf_op jit(solution)/shard_map/ppermute | solution.py:246
  4.9 4.0 %collective-permute-start.1 = (bf16[64,1024]{1,0:T(8,128)(2,1)}, bf16[64,1024]{1,0:T(8,128)(2,1)S(1)}, u32[]{:S(2)}, u32[]{:S(2)}) collective-permute-start(bf16[64,1024]{1,0:T(8,128)(2,1)} %get-tuple-element.29), channel_id=1, source_target_pairs={{0,3},{1,0},{2,1},{3,2},{4,7},{5,4},{6,5},{7,6},{8,11},{9,8},{10,9... | collective-permute-start | bytes 393224 | tf_op jit(solution)/shard_map/ppermute | solution.py:246
  6.3 6.6 %copy-start.5 = (f32[48,1024]{1,0:T(8,128)S(1)}, f32[48,1024]{1,0:T(8,128)}, u32[]{:S(2)}) copy-start(f32[48,1024]{1,0:T(8,128)} %get-tuple-element.27.p0) | copy-start | bytes 589828
  6.3 6.6 %collective-permute-start.2 = (bf16[64,1024]{1,0:T(8,128)(2,1)}, bf16[64,1024]{1,0:T(8,128)(2,1)S(1)}, u32[]{:S(2)}, u32[]{:S(2)}) collective-permute-start(bf16[64,1024]{1,0:T(8,128)(2,1)} %get-tuple-element.30), channel_id=1, source_target_pairs={{0,2},{1,3},{2,0},{3,1},{4,6},{5,7},{6,4},{7,5},{8,10},{9,11},{10,... | collective-permute-start | bytes 393224 | tf_op jit(solution)/shard_map/ppermute | solution.py:246
  8.0 4.9 %copy-start.6 = (s32[27,1024]{1,0:T(8,128)S(1)}, s32[27,1024]{1,0:T(8,128)}, u32[]{:S(2)}) copy-start(s32[27,1024]{1,0:T(8,128)} %nbr_ref.5) | copy-start | bytes 331780
  8.0 4.9 %copy-start.7 = (f32[16,1024]{1,0:T(8,128)S(1)}, f32[16,1024]{1,0:T(8,128)}, u32[]{:S(2)}) copy-start(f32[16,1024]{1,0:T(8,128)} %get-tuple-element.26.r0) | copy-start | bytes 196612
  12.9 0.7 copy-start.8
  12.9 0.7 copy-start.4
  19.6 4.2 %collective-permute-start.3 = (bf16[96,1024]{1,0:T(8,128)(2,1)S(1)}, bf16[96,1024]{1,0:T(8,128)(2,1)S(1)}, u32[]{:S(2)}, u32[]{:S(2)}) collective-permute-start(bf16[96,1024]{1,0:T(8,128)(2,1)S(1)} %get-tuple-element.31), channel_id=1, source_target_pairs={{0,4},{4,0},{8,12},{12,8},{16,20},{20,16},{24,28},{28,24},{32,36},... | collective-permute-start | bytes 589832 | tf_op jit(solution)/shard_map/ppermute | solution.py:250
  23.9 11.2 %collective-permute-start.5 = (bf16[64,1024]{1,0:T(8,128)(2,1)S(1)}, bf16[64,1024]{1,0:T(8,128)(2,1)S(1)}, u32[]{:S(2)}, u32[]{:S(2)}) collective-permute-start(bf16[64,1024]{1,0:T(8,128)(2,1)S(1)} %get-tuple-element.52), channel_id=1, source_target_pairs={{0,16},{4,244},{8,24},{12,252},{16,32},{20,4},{24,40},{28,12},{32,... | collective-permute-start | bytes 393224 | tf_op jit(solution)/shard_map/ppermute | solution.py:255
  31.0 4.1 %collective-permute-start.4 = (bf16[64,1024]{1,0:T(8,128)(2,1)S(1)}, bf16[64,1024]{1,0:T(8,128)(2,1)S(1)}, u32[]{:S(2)}, u32[]{:S(2)}) collective-permute-start(bf16[64,1024]{1,0:T(8,128)(2,1)S(1)} %get-tuple-element.53), channel_id=1, source_target_pairs={{0,8},{4,252},{8,16},{12,4},{16,24},{20,12},{24,32},{28,20},{32,40... | collective-permute-start | bytes 393224 | tf_op jit(solution)/shard_map/ppermute | solution.py:255
  35.2 2.1 %collective-permute-start.6 = (bf16[80,1024]{1,0:T(8,128)(2,1)S(1)}, bf16[80,1024]{1,0:T(8,128)(2,1)S(1)}, u32[]{:S(2)}, u32[]{:S(2)}) collective-permute-start(bf16[80,1024]{1,0:T(8,128)(2,1)S(1)} %pad_maximum_fusion), channel_id=1, source_target_pairs={{0,4},{4,0},{8,12},{12,8},{16,20},{20,16},{24,28},{28,24},{32,36},... | collective-permute-start | bytes 491528 | tf_op jit(solution)/shard_map/ppermute | solution.py:250
  41.8 6.3 %collective-permute-start.9 = (bf16[64,1024]{1,0:T(8,128)(2,1)S(1)}, bf16[64,1024]{1,0:T(8,128)(2,1)S(1)}, u32[]{:S(2)}, u32[]{:S(2)}) collective-permute-start(bf16[64,1024]{1,0:T(8,128)(2,1)S(1)} %pad_maximum_fusion.4.e0), channel_id=1, source_target_pairs={{0,2},{1,3},{2,0},{3,1},{4,6},{5,7},{6,4},{7,5},{8,10},{9,11},{10,... | collective-permute-start | bytes 393224 | tf_op jit(solution)/shard_map/ppermute | solution.py:246
  42.8 7.2 %collective-permute-start.8 = (bf16[64,1024]{1,0:T(8,128)(2,1)S(1)}, bf16[64,1024]{1,0:T(8,128)(2,1)S(1)}, u32[]{:S(2)}, u32[]{:S(2)}) collective-permute-start(bf16[64,1024]{1,0:T(8,128)(2,1)S(1)} %pad_maximum_fusion.4.e0), channel_id=1, source_target_pairs={{0,3},{1,0},{2,1},{3,2},{4,7},{5,4},{6,5},{7,6},{8,11},{9,8},{10,9... | collective-permute-start | bytes 393224 | tf_op jit(solution)/shard_map/ppermute | solution.py:246
  45.2 5.9 %collective-permute-start.7 = (bf16[64,1024]{1,0:T(8,128)(2,1)S(1)}, bf16[64,1024]{1,0:T(8,128)(2,1)S(1)}, u32[]{:S(2)}, u32[]{:S(2)}) collective-permute-start(bf16[64,1024]{1,0:T(8,128)(2,1)S(1)} %pad_maximum_fusion.4.e0), channel_id=1, source_target_pairs={{0,1},{1,2},{2,3},{3,0},{4,5},{5,6},{6,7},{7,4},{8,9},{9,10},{10,1... | collective-permute-start | bytes 393224 | tf_op jit(solution)/shard_map/ppermute | solution.py:246
  45.2 5.9 %copy-start = (bf16[48,1024]{1,0:T(8,128)(2,1)S(1)}, bf16[48,1024]{1,0:T(8,128)(2,1)}, u32[]{:S(2)}) copy-start(bf16[48,1024]{1,0:T(8,128)(2,1)} %feat_ref.3) | copy-start | bytes 294916
  45.2 5.9 %copy-start.1 = (bf16[48,1024]{1,0:T(8,128)(2,1)S(1)}, bf16[48,1024]{1,0:T(8,128)(2,1)}, u32[]{:S(2)}) copy-start(bf16[48,1024]{1,0:T(8,128)(2,1)} %cot_ref.3) | copy-start | bytes 294916
  45.2 5.9 %copy-start.2 = (bf16[48,48]{1,0:T(8,128)(2,1)S(1)}, bf16[48,48]{1,0:T(8,128)(2,1)}, u32[]{:S(2)}) copy-start(bf16[48,48]{1,0:T(8,128)(2,1)} %in_ref.3) | copy-start | bytes 13828
  45.2 5.9 %copy-start.3 = (bf16[48,48]{1,0:T(8,128)(2,1)S(1)}, bf16[48,48]{1,0:T(8,128)(2,1)}, u32[]{:S(2)}) copy-start(bf16[48,48]{1,0:T(8,128)(2,1)} %outf_ref.3) | copy-start | bytes 13828
  52.6 2.4 %collective-permute-start.10 = (f32[24,512]{1,0:T(8,128)S(1)}, f32[24,512]{1,0:T(8,128)S(1)}, u32[]{:S(2)}, u32[]{:S(2)}) collective-permute-start(f32[24,512]{1,0:T(8,128)S(1)} %get-tuple-element.43), channel_id=1, source_target_pairs={{0,4},{4,0},{8,12},{12,8},{16,20},{20,16},{24,28},{28,24},{32,36},... | collective-permute-start | bytes 147464 | tf_op jit(solution)/shard_map/ppermute | solution.py:250
  55.0 3.0 %collective-permute-start.11 = (f32[24,512]{1,0:T(8,128)S(1)}, f32[24,512]{1,0:T(8,128)S(1)}, u32[]{:S(2)}, u32[]{:S(2)}) collective-permute-start(f32[24,512]{1,0:T(8,128)S(1)} %add.58), channel_id=1, source_target_pairs={{0,32},{4,36},{8,40},{12,44},{16,48},{20,52},{24,56},{28,60},{32,0... | collective-permute-start | bytes 147464 | tf_op jit(solution)/shard_map/ppermute | solution.py:250
  58.0 4.6 %collective-permute-start.14 = (f32[24,512]{1,0:T(8,128)S(1)}, f32[24,512]{1,0:T(8,128)S(1)}, u32[]{:S(2)}, u32[]{:S(2)}) collective-permute-start(f32[24,512]{1,0:T(8,128)S(1)} %add.59), channel_id=1, source_target_pairs={{0,16},{4,20},{8,24},{12,28},{16,0},{20,4},{24,8},{28,12},{32,48},... | collective-permute-start | bytes 147464 | tf_op jit(solution)/shard_map/ppermute | solution.py:250
  58.6 4.5 %collective-permute-start.13 = (f32[24,512]{1,0:T(8,128)S(1)}, f32[24,512]{1,0:T(8,128)S(1)}, u32[]{:S(2)}, u32[]{:S(2)}) collective-permute-start(f32[24,512]{1,0:T(8,128)S(1)} %add.59), channel_id=1, source_target_pairs={{0,24},{4,28},{8,16},{12,20},{16,8},{20,12},{24,0},{28,4},{32,56},... | collective-permute-start | bytes 147464 | tf_op jit(solution)/shard_map/ppermute | solution.py:250
  60.3 2.9 %collective-permute-start.12 = (f32[24,512]{1,0:T(8,128)S(1)}, f32[24,512]{1,0:T(8,128)S(1)}, u32[]{:S(2)}, u32[]{:S(2)}) collective-permute-start(f32[24,512]{1,0:T(8,128)S(1)} %add.59), channel_id=1, source_target_pairs={{0,8},{4,12},{8,0},{12,4},{16,24},{20,28},{24,16},{28,20},{32,40},... | collective-permute-start | bytes 147464 | tf_op jit(solution)/shard_map/ppermute | solution.py:250
  63.3 7.1 %collective-permute-start.17 = (f32[24,512]{1,0:T(8,128)S(1)}, f32[24,512]{1,0:T(8,128)S(1)}, u32[]{:S(2)}, u32[]{:S(2)}) collective-permute-start(f32[24,512]{1,0:T(8,128)S(1)} %add_add_fusion.1), channel_id=1, source_target_pairs={{0,128},{4,132},{8,136},{12,140},{16,144},{20,148},{24,152},{28,15... | collective-permute-start | bytes 147464 | tf_op jit(solution)/shard_map/ppermute | solution.py:250
  68.8 5.7 %collective-permute-start.16 = (f32[24,512]{1,0:T(8,128)S(1)}, f32[24,512]{1,0:T(8,128)S(1)}, u32[]{:S(2)}, u32[]{:S(2)}) collective-permute-start(f32[24,512]{1,0:T(8,128)S(1)} %add_add_fusion.1), channel_id=1, source_target_pairs={{0,192},{4,196},{8,200},{12,204},{16,208},{20,212},{24,216},{28,22... | collective-permute-start | bytes 147464 | tf_op jit(solution)/shard_map/ppermute | solution.py:250
  68.8 5.7 %collective-permute-start.15 = (f32[24,512]{1,0:T(8,128)S(1)}, f32[24,512]{1,0:T(8,128)S(1)}, u32[]{:S(2)}, u32[]{:S(2)}) collective-permute-start(f32[24,512]{1,0:T(8,128)S(1)} %add_add_fusion.1), channel_id=1, source_target_pairs={{0,64},{4,68},{8,72},{12,76},{16,80},{20,84},{24,88},{28,92},{32,9... | collective-permute-start | bytes 147464 | tf_op jit(solution)/shard_map/ppermute | solution.py:250
  74.5 4.6 %collective-permute-start.18 = (f32[24,512]{1,0:T(8,128)S(1)}, f32[24,512]{1,0:T(8,128)S(1)}, u32[]{:S(2)}, u32[]{:S(2)}) collective-permute-start(f32[24,512]{1,0:T(8,128)S(1)} %add_add_fusion.refs_0_), channel_id=1, source_target_pairs={{0,4},{4,0},{8,12},{12,8},{16,20},{20,16},{24,28},{28,24},{32,36},... | collective-permute-start | bytes 147464 | tf_op jit(solution)/shard_map/ppermute | solution.py:250

commit v8 on v7

--- a/solution.py
+++ b/solution.py
@@ -33,16 +33,16 @@
     return jnp.where(hit, 1.0, 0.0).astype(BF)
 
 
-def project_kernel(feat_ref, in_ref, cot_ref, outf_ref, own_reduced_ref, own_mixed_ref, *payload_refs):
+def project_kernel(feat_ref, in_ref, cot_ref, outf_ref, mask_ref, own_ref, *payload_refs):
     group_count = 1 + len(payload_refs)
     rank = in_ref.shape[1]
     width = rank // group_count
     pick = rank_picker((group_count * SLAB, rank), 0, lax.axis_index("chan"), group_count, width, 1)
     weights = dot(pick, in_ref[...], NT).astype(BF)
-    reduced = dot(weights, feat_ref[...])
+    reduced = dot(weights, feat_ref[...]) * mask_ref[...].astype(F32)
     grad_mixed = dot(outf_ref[...], cot_ref[...])
-    own_reduced_ref[...] = reduced[:SLAB]
-    own_mixed_ref[...] = grad_mixed
+    own_ref[0:SLAB, :] = reduced[:SLAB]
+    own_ref[SLAB:, :] = grad_mixed
     for j, payload_ref in enumerate(payload_refs):
         payload_ref[0:SLAB, :] = reduced[(j + 1) * SLAB : (j + 2) * SLAB].astype(BF)
         payload_ref[SLAB:, :] = grad_mixed.astype(BF)
@@ -67,17 +67,14 @@
     return jnp.where(core == 0, view, near - 1 - view)
 
 
-def scatter_kernel(halo_ref, r0, p0, p1, p2, p3, mask_ref, core_ref, nbr_ref, gm_ref, own_ref, kept_ref,
+def scatter_kernel(halo_ref, p0, p1, p2, p3, core_ref, nbr_ref, gm_ref, own_ref, kept_ref,
                    cross_ref, terms_ref, acc_ref):
     rows = nbr_ref.shape[1]
     tiles = acc_ref.shape[0] // SLAB
-    total = (p0[...] + p1[SLAB:, :].astype(F32)) + (
-        p2[SLAB:, :].astype(F32) + p3[SLAB:, :].astype(F32)
-    )
-    grad_mixed = total.astype(BF)
+    total = (p0[...] + p1[...].astype(F32)) + (p2[...].astype(F32) + p3[...].astype(F32))
+    cross_ref[0:SLAB, :] = total[:SLAB].astype(BF)
+    grad_mixed = total[SLAB:].astype(BF)
     gm_ref[...] = grad_mixed
-    reduced = (r0[...] + p1[:SLAB, :].astype(F32)) + (p2[:SLAB, :].astype(F32) + p3[:SLAB, :].astype(F32))
-    cross_ref[0:SLAB, :] = (reduced * mask_ref[...].astype(F32)).astype(BF)
     terms_ref[...] = dot(core_ref[...], grad_mixed).astype(BF)
     acc_ref[...] = jnp.zeros_like(acc_ref)
 
@@ -199,32 +196,39 @@
     gc_ref[...] = dot(gm_ref[...], ga_ref[...], NT)
 
 
-def finish_kernel(mix_ref, e0, e1, e3, e2, in_ref, feat_ref, outf_ref, cot_ref, gc_ref,
-                  gf_ref, out_ref, keep_ref, give_ref):
-    rank = in_ref.shape[1]
-    rows = feat_ref.shape[1]
+def sums_kernel(mix_ref, e0, e2, e3, e1, feat_ref, cot_ref, gc_ref, keep_ref, give_ref, rows_ref, mixed_ref):
+    rank, rows = mix_ref.shape
     wide = gc_ref.shape[1]
     group = lax.axis_index("chan")
     pick = rank_picker((rank, 4 * SLAB), 1, group, 4, rank // 4, -1)
     slabs = jnp.concatenate([e[0:SLAB, :] for e in (e0, e1, e2, e3)], 0)
     grad_rows = dot(pick, slabs).astype(BF)
-    gf_ref[...] = dot(in_ref[...], grad_rows).astype(BF)
+    rows_ref[...] = grad_rows
     total = (mix_ref[...] + e1[SLAB:, :].astype(F32)) + (e2[SLAB:, :].astype(F32) + e3[SLAB:, :].astype(F32))
     mixed = total.astype(BF)
-    out_ref[...] = dot(outf_ref[...], mixed, TN).astype(BF)
+    mixed_ref[...] = mixed
     column = lax.broadcasted_iota(jnp.int32, (wide, rank), 0)
     wanted = lax.broadcasted_iota(jnp.int32, (wide, rank), 1)
     free = column % SLAB - (SLAB - 4)
     place = jnp.where((free >= 0) & (column // SLAB * 4 + free == wanted), 1.0, 0.0).astype(BF)
-    spread = dot(place, grad_rows).astype(BF)
+    left = dot(feat_ref[...], grad_rows, NT)
+    high = left.astype(BF)
+    rest = left - high.astype(F32)
+    middle = rest.astype(BF)
+    low = (rest - middle.astype(F32)).astype(BF)
     right = jnp.concatenate([jnp.zeros((48, rows), BF), cot_ref[...], jnp.zeros((32, rows), BF)], 0)
     tail = dot(mixed, right, NT)
-    packed = gc_ref[...] + dot(feat_ref[...], spread, NT)
+    packed = gc_ref[...] + (dot(high, place, NT) + dot(middle, place, NT) + dot(low, place, NT))
     packed = jnp.concatenate([packed[:, : wide - 128], packed[:, wide - 128 :] + tail], 1)
     half = rank // 2
     first = core_bit() == 0
     keep_ref[...] = jnp.where(first, packed[:half], packed[half:])
     give_ref[...] = jnp.where(first, packed[half:], packed[:half])
+
+
+def outputs_kernel(rows_ref, mixed_ref, in_ref, outf_ref, gf_ref, out_ref):
+    gf_ref[...] = dot(in_ref[...], rows_ref[...]).astype(BF)
+    out_ref[...] = dot(outf_ref[...], mixed_ref[...], TN).astype(BF)
 
 
 def unpack_kernel(factor, mine_ref, other_ref, left_ref, core_ref, right_ref, flat_ref, turned_ref):
@@ -279,26 +283,26 @@
     core_rows = jnp.pad(core, ((0, 0), (0, SLAB - width), (0, 0))).reshape(offsets * SLAB, rank)
     estimate = pl.CostEstimate(flops=5 * 10**9, bytes_accessed=2**20, transcendentals=0)
 
-    own_reduced, own_mixed, *payload = pl.pallas_call(
+    own_payload, *payload = pl.pallas_call(
         project_kernel,
-        out_shape=[struct((SLAB, rows), F32), struct((rank, rows), F32)] + [struct((SLAB + rank, rows), BF)] * 3,
-        in_specs=[VMEM] * 4,
-        out_specs=[VMEM] * 5,
+        out_shape=[struct((SLAB + rank, rows), F32)] + [struct((SLAB + rank, rows), BF)] * 3,
+        in_specs=[VMEM] * 5,
+        out_specs=[VMEM] * 4,
         name="project",
-    )(features, in_factor, cotangent, out_factor)
+    )(features, in_factor, cotangent, out_factor, keep)
     arrived = {j: shifted(payload[j - 1], "chan", j) for j in (1, 3, 2)}
 
     triple = struct((3 * SLAB, rows), F32)
     grad_mixed, own, kept, cross = pl.pallas_call(
         scatter_kernel,
         out_shape=[struct((rank, rows), BF), struct((SLAB, rows), F32), triple, struct((6 * SLAB, rows), BF)],
-        in_specs=[SMEM] + [VMEM] * 8,
+        in_specs=[SMEM] + [VMEM] * 6,
         out_specs=[VMEM] * 4,
         scratch_shapes=[pltpu.VMEM((offsets * SLAB, rows), BF), pltpu.VMEM((table_rows, LOW), F32)],
         compiler_params=ROOMY,
         cost_estimate=estimate,
         name="scatter",
-    )(halo, own_reduced, own_mixed, arrived[1], arrived[3], arrived[2], keep, core_rows, neighbours)
+    )(halo, own_payload, arrived[1], arrived[3], arrived[2], core_rows, neighbours)
 
     def slabs_of(block, first, last):
         return block[first * SLAB : last * SLAB]
@@ -353,17 +357,26 @@
     )(grad_mixed, gathered)
 
     shared = jnp.concatenate([grad_slab, mixed_part.astype(BF)], 0)
-    exchanged = [shared] + [shifted(shared, "chan", j) for j in (1, 3, 2)]
-
-    half = struct((rank // 2, packed_width), F32)
-    grad_features, output, mine, give = pl.pallas_call(
-        finish_kernel,
-        out_shape=[struct((channels, rows), BF)] * 2 + [half] * 2,
-        in_specs=[VMEM] * 10,
+    exchanged = [shared] + [shifted(shared, "chan", j) for j in (2, 3, 1)]
+
+    sums, full = struct((rank // 2, packed_width), F32), struct((rank, rows), BF)
+    mine, give, grad_rows, mixed = pl.pallas_call(
+        sums_kernel,
+        out_shape=[sums, sums, full, full],
+        in_specs=[VMEM] * 8,
         out_specs=[VMEM] * 4,
         compiler_params=SNUG,
-        name="finish",
-    )(mixed_part, *exchanged, in_factor, features, out_factor, cotangent, grad_core)
+        name="sums",
+    )(mixed_part, *exchanged, features, cotangent, grad_core)
+    grad_features, output = pl.pallas_call(
+        outputs_kernel,
+        out_shape=[struct((channels, rows), BF)] * 2,
+        in_specs=[VMEM] * 4,
+        out_specs=[VMEM] * 2,
+        compiler_params=SNUG,
+        cost_estimate=pl.CostEstimate(flops=5 * 10**8, bytes_accessed=2**20, transcendentals=0),
+        name="outputs",
+    )(grad_rows, mixed, in_factor, out_factor)
     mine, other = leaf_sum(mine, give)
 
     factor = float(rows * lax.axis_size("leaf")) ** (-0.5)

time: 80.1 us -> 78 us (0.974)
  waiting for transfers between devices: 24 us -> 22.4 us
    ppermute x6, waiting for transfers between devices: 10.3 us -> 9.49 us  [shifted(): lax.ppermute(block, axis, [(i, (i + distance) % count) for i in range(cou...]
    pallas_call x2 -> x3, Pallas kernels: 3.59 us -> 3.57 us  [the longest x1 2.18 us: body(): pl.pallas_call(project_kernel, out_shape=[struct((SLAB + rank, rows), F32...]
  transfers between devices with their start and end apart: 19 -> 19, of which waited for: 16 -> 14; matrix products, arithmetic and copies ran while one was open for 0% -> 0% of each run, Pallas kernels for 4% -> 6%
where the time goes in v8:
time: 78 us; the launch traced here: 77.9 us
  starting transfers between devices  35.9 us (46%)
  waiting for transfers between devices  22.4 us (29%)
  Pallas kernels  18.5 us (24%)
  between operations  0.82 us (1%)
    ppermute x11, starting transfers between devices, crossed(): lax.ppermute(block, 'leaf', [(i, i ^ mask) for i in range(lax.axis_size('...  19.6 us
    ppermute x11, waiting for transfers between devices, crossed(): lax.ppermute(block, 'leaf', [(i, i ^ mask) for i in range(lax.axis_size('...  12.8 us
    ppermute x6, waiting for transfers between devices, shifted(): lax.ppermute(block, axis, [(i, (i + distance) % count) for i in range(cou...  9.49 us
    ppermute x6, starting transfers between devices, shifted(): lax.ppermute(block, axis, [(i, (i + distance) % count) for i in range(cou...  8.21 us
    ppermute x2, starting transfers between devices, outward(): lax.ppermute(block, 'leaf', [(i, (i + (2 * chips if i % 2 == 0 else -2 *...  8.03 us
    pallas_call x1, Pallas kernels, body(): pl.pallas_call(scatter_kernel, out_shape=[struct((rank, rows), BF), struc...  5.98 us
    pallas_call x1, Pallas kernels, body(): pl.pallas_call(far_gather_kernel, out_shape=[struct((rank, rows), F32), s...  4.5 us
    pallas_call x1, Pallas kernels, body(): pl.pallas_call(near_gather_kernel, out_shape=struct((offsets * SLAB, rows...  3.16 us
  transfers between devices with their start and end apart: 19, of which 14 were waited for; matrix products, arithmetic and copies ran while one was open for 0% of the time, Pallas kernels for 6%

profile of v8, /device:TPU:1, one launch (start us, length us, event | category | flops | bytes accessed | tf_op | source)
XLA Modules:
  0.0 77.9 jit_solution(11707716831397605688)
XLA Ops:
  0.6 2.2 %project.1 = (f32[64,1024]{1,0:T(8,128)}, bf16[64,1024]{1,0:T(8,128)(2,1)}, bf16[64,1024]{1,0:T(8,128)(2,1)}, bf16[64,1024]{1,0:T(8,128)(2,1)}) custom-call(bf16[48,1024]{1,0:T(8,128)(2,1)} %feat_ref.3, bf16[48,48]{1,0:T(8,128)(2,1)} %in_ref.3, bf16[48,1024]{1,0:T(8,128)(2,1)} %cot_ref.3, bf16[48,48]{1,0:T(8,128)(2,1)} %outf_ref.3, s32[1,1024]{1,0:T(1,128)} %bitcast.9), custom_call_target="tpu_custom_call" | custom-call | tf_op jit(solution)/shard_map/project/pallas_call | solution.py:286
  2.8 2.1 %collective-permute-start = (bf16[64,1024]{1,0:T(8,128)(2,1)}, bf16[64,1024]{1,0:T(8,128)(2,1)S(1)}, u32[]{:S(2)}, u32[]{:S(2)}) collective-permute-start(bf16[64,1024]{1,0:T(8,128)(2,1)} %get-tuple-element.28), channel_id=1, source_target_pairs={{0,1},{1,2},{2,3},{3,0},{4,5},{5,6},{6,7},{7,4},{8,9},{9,10},{10,1... | collective-permute-start | bytes 393224 | tf_op jit(solution)/shard_map/ppermute | solution.py:250
  5.0 1.5 %collective-permute-start.1 = (bf16[64,1024]{1,0:T(8,128)(2,1)}, bf16[64,1024]{1,0:T(8,128)(2,1)S(1)}, u32[]{:S(2)}, u32[]{:S(2)}) collective-permute-start(bf16[64,1024]{1,0:T(8,128)(2,1)} %get-tuple-element.29), channel_id=1, source_target_pairs={{0,3},{1,0},{2,1},{3,2},{4,7},{5,4},{6,5},{7,6},{8,11},{9,8},{10,9... | collective-permute-start | bytes 393224 | tf_op jit(solution)/shard_map/ppermute | solution.py:250
  6.5 1.6 %collective-permute-start.2 = (bf16[64,1024]{1,0:T(8,128)(2,1)}, bf16[64,1024]{1,0:T(8,128)(2,1)S(1)}, u32[]{:S(2)}, u32[]{:S(2)}) collective-permute-start(bf16[64,1024]{1,0:T(8,128)(2,1)} %get-tuple-element.30), channel_id=1, source_target_pairs={{0,2},{1,3},{2,0},{3,1},{4,6},{5,7},{6,4},{7,5},{8,10},{9,11},{10,... | collective-permute-start | bytes 393224 | tf_op jit(solution)/shard_map/ppermute | solution.py:250
  8.1 0.8 %collective-permute-done.p1 = bf16[64,1024]{1,0:T(8,128)(2,1)S(1)} collective-permute-done((bf16[64,1024]{1,0:T(8,128)(2,1)}, bf16[64,1024]{1,0:T(8,128)(2,1)S(1)}, u32[]{:S(2)}, u32[]{:S(2)}) %collective-permute-start) | collective-permute-done | bytes 131104 | tf_op jit(solution)/shard_map/ppermute | solution.py:250
  9.0 4.0 %collective-permute-done.2.p3 = bf16[64,1024]{1,0:T(8,128)(2,1)S(1)} collective-permute-done((bf16[64,1024]{1,0:T(8,128)(2,1)}, bf16[64,1024]{1,0:T(8,128)(2,1)S(1)}, u32[]{:S(2)}, u32[]{:S(2)}) %collective-permute-start.2) | collective-permute-done | bytes 131104 | tf_op jit(solution)/shard_map/ppermute | solution.py:250
  13.0 6.0 %scatter.1 = (bf16[48,1024]{1,0:T(8,128)(2,1)S(1)}, f32[16,1024]{1,0:T(8,128)S(1)}, f32[48,1024]{1,0:T(8,128)S(1)}, bf16[96,1024]{1,0:T(8,128)(2,1)S(1)}) custom-call(s32[8,8]{1,0:T(8,128)S(1)} %bitcast.6, f32[64,1024]{1,0:T(8,128)S(1)} %copy-done.4, bf16[64,1024]{1,0:T(8,128)(2,1)S(1)} %collective-permute-done.p1, ...), custom_call_target="tpu_custom_call" | custom-call | flops 5000000000 | bytes 1048576 | tf_op jit(solution)/shard_map/scatter/pallas_call | solution.py:296
  19.0 3.1 %collective-permute-start.3 = (bf16[96,1024]{1,0:T(8,128)(2,1)S(1)}, bf16[96,1024]{1,0:T(8,128)(2,1)S(1)}, u32[]{:S(2)}, u32[]{:S(2)}) collective-permute-start(bf16[96,1024]{1,0:T(8,128)(2,1)S(1)} %get-tuple-element.31), channel_id=1, source_target_pairs={{0,4},{4,0},{8,12},{12,8},{16,20},{20,16},{24,28},{28,24},{32,36},... | collective-permute-start | bytes 589832 | tf_op jit(solution)/shard_map/ppermute | solution.py:254
  22.1 1.1 %collective-permute-done.3 = bf16[96,1024]{1,0:T(8,128)(2,1)S(1)} collective-permute-done((bf16[96,1024]{1,0:T(8,128)(2,1)S(1)}, bf16[96,1024]{1,0:T(8,128)(2,1)S(1)}, u32[]{:S(2)}, u32[]{:S(2)}) %collective-permute-start.3) | collective-permute-done | bytes 196640 | tf_op jit(solution)/shard_map/ppermute | solution.py:254
  23.2 7.2 %collective-permute-start.5 = (bf16[64,1024]{1,0:T(8,128)(2,1)S(1)}, bf16[64,1024]{1,0:T(8,128)(2,1)S(1)}, u32[]{:S(2)}, u32[]{:S(2)}) collective-permute-start(bf16[64,1024]{1,0:T(8,128)(2,1)S(1)} %get-tuple-element.54), channel_id=1, source_target_pairs={{0,16},{4,244},{8,24},{12,252},{16,32},{20,4},{24,40},{28,12},{32,... | collective-permute-start | bytes 393224 | tf_op jit(solution)/shard_map/ppermute | solution.py:259
  30.4 0.9 %collective-permute-start.4 = (bf16[64,1024]{1,0:T(8,128)(2,1)S(1)}, bf16[64,1024]{1,0:T(8,128)(2,1)S(1)}, u32[]{:S(2)}, u32[]{:S(2)}) collective-permute-start(bf16[64,1024]{1,0:T(8,128)(2,1)S(1)} %get-tuple-element.55), channel_id=1, source_target_pairs={{0,8},{4,252},{8,16},{12,4},{16,24},{20,12},{24,32},{28,20},{32,40... | collective-permute-start | bytes 393224 | tf_op jit(solution)/shard_map/ppermute | solution.py:259
  31.2 3.2 %near_gather.1.base_ref = bf16[432,1024]{1,0:T(8,128)(2,1)S(1)} custom-call(s32[8,8]{1,0:T(8,128)S(1)} %bitcast.7, bf16[16,1024]{1,0:T(8,128)(2,1)S(1)} %slice.51.own_ref, bf16[16,1024]{1,0:T(8,128)(2,1)S(1)} %get-tuple-element.53.pair_ref, s32[27,1024]{1,0:T(8,128)S(1)} %copy-done.5), custom_call_target="tpu_custom_call" | custom-call | flops 5000000000 | bytes 1048576 | tf_op jit(solution)/shard_map/near_gather/pallas_call | solution.py:322
  34.5 1.0 %collective-permute-start.6 = (bf16[80,1024]{1,0:T(8,128)(2,1)S(1)}, bf16[80,1024]{1,0:T(8,128)(2,1)S(1)}, u32[]{:S(2)}, u32[]{:S(2)}) collective-permute-start(bf16[80,1024]{1,0:T(8,128)(2,1)S(1)} %pad_maximum_fusion), channel_id=1, source_target_pairs={{0,4},{4,0},{8,12},{12,8},{16,20},{20,16},{24,28},{28,24},{32,36},... | collective-permute-start | bytes 491528 | tf_op jit(solution)/shard_map/ppermute | solution.py:254
  35.6 1.0 %collective-permute-done.6.cross_ref = bf16[80,1024]{1,0:T(8,128)(2,1)S(1)} collective-permute-done((bf16[80,1024]{1,0:T(8,128)(2,1)S(1)}, bf16[80,1024]{1,0:T(8,128)(2,1)S(1)}, u32[]{:S(2)}, u32[]{:S(2)}) %collective-permute-start.6) | collective-permute-done | bytes 163872 | tf_op jit(solution)/shard_map/ppermute | solution.py:254
  36.6 4.5 %far_gather.1 = (f32[48,1024]{1,0:T(8,128)S(1)}, bf16[512,1024]{1,0:T(8,128)(2,1)S(1)}) custom-call(s32[8,8]{1,0:T(8,128)S(1)} %bitcast.8, bf16[432,1024]{1,0:T(8,128)(2,1)S(1)} %near_gather.1.base_ref, bf16[32,1024]{1,0:T(8,128)(2,1)S(1)} %slice.60.near_ref, bf16[32,1024]{1,0:T(8,128)(2,1)S(1)} %slice.61.far_ref, ...), custom_call_target="tpu_custom_call" | custom-call | flops 5000000000 | bytes 1048576 | tf_op jit(solution)/shard_map/far_gather/pallas_call | solution.py:339
  41.2 0.9 %collective-permute-start.9 = (bf16[64,1024]{1,0:T(8,128)(2,1)S(1)}, bf16[64,1024]{1,0:T(8,128)(2,1)S(1)}, u32[]{:S(2)}, u32[]{:S(2)}) collective-permute-start(bf16[64,1024]{1,0:T(8,128)(2,1)S(1)} %pad_maximum_fusion.4.e0), channel_id=1, source_target_pairs={{0,1},{1,2},{2,3},{3,0},{4,5},{5,6},{6,7},{7,4},{8,9},{9,10},{10,1... | collective-permute-start | bytes 393224 | tf_op jit(solution)/shard_map/ppermute | solution.py:250
  42.1 1.8 %collective-permute-start.8 = (bf16[64,1024]{1,0:T(8,128)(2,1)S(1)}, bf16[64,1024]{1,0:T(8,128)(2,1)S(1)}, u32[]{:S(2)}, u32[]{:S(2)}) collective-permute-start(bf16[64,1024]{1,0:T(8,128)(2,1)S(1)} %pad_maximum_fusion.4.e0), channel_id=1, source_target_pairs={{0,3},{1,0},{2,1},{3,2},{4,7},{5,4},{6,5},{7,6},{8,11},{9,8},{10,9... | collective-permute-start | bytes 393224 | tf_op jit(solution)/shard_map/ppermute | solution.py:250
  44.6 2.6 %collective-permute-done.9.e1 = bf16[64,1024]{1,0:T(8,128)(2,1)S(1)} collective-permute-done((bf16[64,1024]{1,0:T(8,128)(2,1)S(1)}, bf16[64,1024]{1,0:T(8,128)(2,1)S(1)}, u32[]{:S(2)}, u32[]{:S(2)}) %collective-permute-start.9) | collective-permute-done | bytes 131104 | tf_op jit(solution)/shard_map/ppermute | solution.py:250
  47.2 2.1 %collective-permute-done.7.e2 = bf16[64,1024]{1,0:T(8,128)(2,1)S(1)} collective-permute-done((bf16[64,1024]{1,0:T(8,128)(2,1)S(1)}, bf16[64,1024]{1,0:T(8,128)(2,1)S(1)}, u32[]{:S(2)}, u32[]{:S(2)}) %collective-permute-start.7) | collective-permute-done | bytes 131104 | tf_op jit(solution)/shard_map/ppermute | solution.py:250
  49.3 0.6 sums.1
  49.8 2.2 %collective-permute-start.10 = (f32[24,512]{1,0:T(8,128)S(1)}, f32[24,512]{1,0:T(8,128)S(1)}, u32[]{:S(2)}, u32[]{:S(2)}) collective-permute-start(f32[24,512]{1,0:T(8,128)S(1)} %get-tuple-element.45), channel_id=1, source_target_pairs={{0,4},{4,0},{8,12},{12,8},{16,20},{20,16},{24,28},{28,24},{32,36},... | collective-permute-start | bytes 147464 | tf_op jit(solution)/shard_map/ppermute | solution.py:254
  52.0 0.9 %collective-permute-done.10 = f32[24,512]{1,0:T(8,128)S(1)} collective-permute-done((f32[24,512]{1,0:T(8,128)S(1)}, f32[24,512]{1,0:T(8,128)S(1)}, u32[]{:S(2)}, u32[]{:S(2)}) %collective-permute-start.10) | collective-permute-done | bytes 49184 | tf_op jit(solution)/shard_map/ppermute | solution.py:254
  53.0 2.9 %collective-permute-done.11 = f32[24,512]{1,0:T(8,128)S(1)} collective-permute-done((f32[24,512]{1,0:T(8,128)S(1)}, f32[24,512]{1,0:T(8,128)S(1)}, u32[]{:S(2)}, u32[]{:S(2)}) %collective-permute-start.11) | collective-permute-done | bytes 49184 | tf_op jit(solution)/shard_map/ppermute | solution.py:254
  56.0 0.7 collective-permute-start.14
  56.6 1.8 %collective-permute-start.13 = (f32[24,512]{1,0:T(8,128)S(1)}, f32[24,512]{1,0:T(8,128)S(1)}, u32[]{:S(2)}, u32[]{:S(2)}) collective-permute-start(f32[24,512]{1,0:T(8,128)S(1)} %add.59), channel_id=1, source_target_pairs={{0,24},{4,28},{8,16},{12,20},{16,8},{20,12},{24,0},{28,4},{32,56},... | collective-permute-start | bytes 147464 | tf_op jit(solution)/shard_map/ppermute | solution.py:254
  58.7 1.8 %collective-permute-done.14 = f32[24,512]{1,0:T(8,128)S(1)} collective-permute-done((f32[24,512]{1,0:T(8,128)S(1)}, f32[24,512]{1,0:T(8,128)S(1)}, u32[]{:S(2)}, u32[]{:S(2)}) %collective-permute-start.14) | collective-permute-done | bytes 49184 | tf_op jit(solution)/shard_map/ppermute | solution.py:254
  61.4 5.4 %collective-permute-start.17 = (f32[24,512]{1,0:T(8,128)S(1)}, f32[24,512]{1,0:T(8,128)S(1)}, u32[]{:S(2)}, u32[]{:S(2)}) collective-permute-start(f32[24,512]{1,0:T(8,128)S(1)} %add_add_fusion.1), channel_id=1, source_target_pairs={{0,128},{4,132},{8,136},{12,140},{16,144},{20,148},{24,152},{28,15... | collective-permute-start | bytes 147464 | tf_op jit(solution)/shard_map/ppermute | solution.py:254
  66.8 1.4 %collective-permute-start.15 = (f32[24,512]{1,0:T(8,128)S(1)}, f32[24,512]{1,0:T(8,128)S(1)}, u32[]{:S(2)}, u32[]{:S(2)}) collective-permute-start(f32[24,512]{1,0:T(8,128)S(1)} %add_add_fusion.1), channel_id=1, source_target_pairs={{0,64},{4,68},{8,72},{12,76},{16,80},{20,84},{24,88},{28,92},{32,9... | collective-permute-start | bytes 147464 | tf_op jit(solution)/shard_map/ppermute | solution.py:254
  68.4 4.0 %collective-permute-done.16 = f32[24,512]{1,0:T(8,128)S(1)} collective-permute-done((f32[24,512]{1,0:T(8,128)S(1)}, f32[24,512]{1,0:T(8,128)S(1)}, u32[]{:S(2)}, u32[]{:S(2)}) %collective-permute-start.16) | collective-permute-done | bytes 49184 | tf_op jit(solution)/shard_map/ppermute | solution.py:254
  72.4 3.7 %collective-permute-start.18 = (f32[24,512]{1,0:T(8,128)S(1)}, f32[24,512]{1,0:T(8,128)S(1)}, u32[]{:S(2)}, u32[]{:S(2)}) collective-permute-start(f32[24,512]{1,0:T(8,128)S(1)} %add_add_fusion.refs_0_), channel_id=1, source_target_pairs={{0,4},{4,0},{8,12},{12,8},{16,20},{20,16},{24,28},{28,24},{32,36},... | collective-permute-start | bytes 147464 | tf_op jit(solution)/shard_map/ppermute | solution.py:254
  76.1 0.8 %outputs.1 = (bf16[48,1024]{1,0:T(8,128)(2,1)}, bf16[48,1024]{1,0:T(8,128)(2,1)}) custom-call(bf16[48,1024]{1,0:T(8,128)(2,1)S(1)} %get-tuple-element.40.rows_ref, bf16[48,1024]{1,0:T(8,128)(2,1)S(1)} %get-tuple-element.41.mixed_ref, bf16[48,48]{1,0:T(8,128)(2,1)S(1)} %copy-done.2, bf16[48,48]{1,0:T(8,128)(2,1)S(1)} %copy-done.3), custom_call_target="tpu_custom_call" | custom-call | flops 500000000 | bytes 1048576 | tf_op jit(solution)/shard_map/outputs/pallas_call | solution.py:371
  77.0 0.8 %unpack.1 = (f32[48,48]{1,0:T(8,128)}, f32[12,27,48]{2,1,0:T(8,128)}, f32[48,48]{1,0:T(8,128)}) custom-call(f32[24,512]{1,0:T(8,128)S(1)} %add_add_fusion.refs_0_, f32[24,512]{1,0:T(8,128)S(1)} %collective-permute-done.18.refs_1_), custom_call_target="tpu_custom_call" | custom-call | tf_op jit(solution)/shard_map/unpack/pallas_call | solution.py:383
  (50 shorter events, 2.6 us)
Async XLA Ops:
  0.6 7.4 %copy-start.7 = (bf16[27,12,48]{2,0,1:T(8,128)(2,1)S(1)}, bf16[27,12,48]{2,0,1:T(8,128)(2,1)}, u32[]{:S(2)}) copy-start(bf16[27,12,48]{2,0,1:T(8,128)(2,1)} %param.10) | copy-start | bytes 93316
  2.8 10.2 %copy-start.4 = (f32[64,1024]{1,0:T(8,128)S(1)}, f32[64,1024]{1,0:T(8,128)}, u32[]{:S(2)}) copy-start(f32[64,1024]{1,0:T(8,128)} %get-tuple-element.27.p0) | copy-start | bytes 786436
  2.8 6.1 %collective-permute-start = (bf16[64,1024]{1,0:T(8,128)(2,1)}, bf16[64,1024]{1,0:T(8,128)(2,1)S(1)}, u32[]{:S(2)}, u32[]{:S(2)}) collective-permute-start(bf16[64,1024]{1,0:T(8,128)(2,1)} %get-tuple-element.28), channel_id=1, source_target_pairs={{0,1},{1,2},{2,3},{3,0},{4,5},{5,6},{6,7},{7,4},{8,9},{9,10},{10,1... | collective-permute-start | bytes 393224 | tf_op jit(solution)/shard_map/ppermute | solution.py:250
  5.0 4.0 %collective-permute-start.1 = (bf16[64,1024]{1,0:T(8,128)(2,1)}, bf16[64,1024]{1,0:T(8,128)(2,1)S(1)}, u32[]{:S(2)}, u32[]{:S(2)}) collective-permute-start(bf16[64,1024]{1,0:T(8,128)(2,1)} %get-tuple-element.29), channel_id=1, source_target_pairs={{0,3},{1,0},{2,1},{3,2},{4,7},{5,4},{6,5},{7,6},{8,11},{9,8},{10,9... | collective-permute-start | bytes 393224 | tf_op jit(solution)/shard_map/ppermute | solution.py:250
  6.5 6.5 %collective-permute-start.2 = (bf16[64,1024]{1,0:T(8,128)(2,1)}, bf16[64,1024]{1,0:T(8,128)(2,1)S(1)}, u32[]{:S(2)}, u32[]{:S(2)}) collective-permute-start(bf16[64,1024]{1,0:T(8,128)(2,1)} %get-tuple-element.30), channel_id=1, source_target_pairs={{0,2},{1,3},{2,0},{3,1},{4,6},{5,7},{6,4},{7,5},{8,10},{9,11},{10,... | collective-permute-start | bytes 393224 | tf_op jit(solution)/shard_map/ppermute | solution.py:250
  8.1 4.9 %copy-start.5 = (s32[27,1024]{1,0:T(8,128)S(1)}, s32[27,1024]{1,0:T(8,128)}, u32[]{:S(2)}) copy-start(s32[27,1024]{1,0:T(8,128)} %nbr_ref.5) | copy-start | bytes 331780
  8.1 4.9 %copy-start.6 = (s32[1,8,8]{2,1,0:T(8,128)S(1)}, s32[1,8,8]{2,1,0:T(8,128)}, u32[]{:S(2)}) copy-start(s32[1,8,8]{2,1,0:T(8,128)} %param.13) | copy-start | bytes 772
  19.0 4.1 %collective-permute-start.3 = (bf16[96,1024]{1,0:T(8,128)(2,1)S(1)}, bf16[96,1024]{1,0:T(8,128)(2,1)S(1)}, u32[]{:S(2)}, u32[]{:S(2)}) collective-permute-start(bf16[96,1024]{1,0:T(8,128)(2,1)S(1)} %get-tuple-element.31), channel_id=1, source_target_pairs={{0,4},{4,0},{8,12},{12,8},{16,20},{20,16},{24,28},{28,24},{32,36},... | collective-permute-start | bytes 589832 | tf_op jit(solution)/shard_map/ppermute | solution.py:254
  23.2 11.2 %collective-permute-start.5 = (bf16[64,1024]{1,0:T(8,128)(2,1)S(1)}, bf16[64,1024]{1,0:T(8,128)(2,1)S(1)}, u32[]{:S(2)}, u32[]{:S(2)}) collective-permute-start(bf16[64,1024]{1,0:T(8,128)(2,1)S(1)} %get-tuple-element.54), channel_id=1, source_target_pairs={{0,16},{4,244},{8,24},{12,252},{16,32},{20,4},{24,40},{28,12},{32,... | collective-permute-start | bytes 393224 | tf_op jit(solution)/shard_map/ppermute | solution.py:259
  30.4 4.1 %collective-permute-start.4 = (bf16[64,1024]{1,0:T(8,128)(2,1)S(1)}, bf16[64,1024]{1,0:T(8,128)(2,1)S(1)}, u32[]{:S(2)}, u32[]{:S(2)}) collective-permute-start(bf16[64,1024]{1,0:T(8,128)(2,1)S(1)} %get-tuple-element.55), channel_id=1, source_target_pairs={{0,8},{4,252},{8,16},{12,4},{16,24},{20,12},{24,32},{28,20},{32,40... | collective-permute-start | bytes 393224 | tf_op jit(solution)/shard_map/ppermute | solution.py:259
  34.5 1.1 %copy-start.8 = (s32[1024]{0:T(1024)S(1)}, s32[1024]{0:T(1024)}, u32[]{:S(2)}) copy-start(s32[1024]{0:T(1024)} %param.14) | copy-start | bytes 12292
  34.5 2.1 %collective-permute-start.6 = (bf16[80,1024]{1,0:T(8,128)(2,1)S(1)}, bf16[80,1024]{1,0:T(8,128)(2,1)S(1)}, u32[]{:S(2)}, u32[]{:S(2)}) collective-permute-start(bf16[80,1024]{1,0:T(8,128)(2,1)S(1)} %pad_maximum_fusion), channel_id=1, source_target_pairs={{0,4},{4,0},{8,12},{12,8},{16,20},{20,16},{24,28},{28,24},{32,36},... | collective-permute-start | bytes 491528 | tf_op jit(solution)/shard_map/ppermute | solution.py:254
  41.2 6.0 %collective-permute-start.9 = (bf16[64,1024]{1,0:T(8,128)(2,1)S(1)}, bf16[64,1024]{1,0:T(8,128)(2,1)S(1)}, u32[]{:S(2)}, u32[]{:S(2)}) collective-permute-start(bf16[64,1024]{1,0:T(8,128)(2,1)S(1)} %pad_maximum_fusion.4.e0), channel_id=1, source_target_pairs={{0,1},{1,2},{2,3},{3,0},{4,5},{5,6},{6,7},{7,4},{8,9},{9,10},{10,1... | collective-permute-start | bytes 393224 | tf_op jit(solution)/shard_map/ppermute | solution.py:250
  42.1 5.1 %collective-permute-start.8 = (bf16[64,1024]{1,0:T(8,128)(2,1)S(1)}, bf16[64,1024]{1,0:T(8,128)(2,1)S(1)}, u32[]{:S(2)}, u32[]{:S(2)}) collective-permute-start(bf16[64,1024]{1,0:T(8,128)(2,1)S(1)} %pad_maximum_fusion.4.e0), channel_id=1, source_target_pairs={{0,3},{1,0},{2,1},{3,2},{4,7},{5,4},{6,5},{7,6},{8,11},{9,8},{10,9... | collective-permute-start | bytes 393224 | tf_op jit(solution)/shard_map/ppermute | solution.py:250
  44.0 5.3 %collective-permute-start.7 = (bf16[64,1024]{1,0:T(8,128)(2,1)S(1)}, bf16[64,1024]{1,0:T(8,128)(2,1)S(1)}, u32[]{:S(2)}, u32[]{:S(2)}) collective-permute-start(bf16[64,1024]{1,0:T(8,128)(2,1)S(1)} %pad_maximum_fusion.4.e0), channel_id=1, source_target_pairs={{0,2},{1,3},{2,0},{3,1},{4,6},{5,7},{6,4},{7,5},{8,10},{9,11},{10,... | collective-permute-start | bytes 393224 | tf_op jit(solution)/shard_map/ppermute | solution.py:250
  44.2 5.1 %copy-start = (bf16[48,1024]{1,0:T(8,128)(2,1)S(1)}, bf16[48,1024]{1,0:T(8,128)(2,1)}, u32[]{:S(2)}) copy-start(bf16[48,1024]{1,0:T(8,128)(2,1)} %feat_ref.3) | copy-start | bytes 294916
  44.2 5.1 %copy-start.1 = (bf16[48,1024]{1,0:T(8,128)(2,1)S(1)}, bf16[48,1024]{1,0:T(8,128)(2,1)}, u32[]{:S(2)}) copy-start(bf16[48,1024]{1,0:T(8,128)(2,1)} %cot_ref.3) | copy-start | bytes 294916
  49.8 3.1 %collective-permute-start.10 = (f32[24,512]{1,0:T(8,128)S(1)}, f32[24,512]{1,0:T(8,128)S(1)}, u32[]{:S(2)}, u32[]{:S(2)}) collective-permute-start(f32[24,512]{1,0:T(8,128)S(1)} %get-tuple-element.45), channel_id=1, source_target_pairs={{0,4},{4,0},{8,12},{12,8},{16,20},{20,16},{24,28},{28,24},{32,36},... | collective-permute-start | bytes 147464 | tf_op jit(solution)/shard_map/ppermute | solution.py:254
  52.9 3.0 %collective-permute-start.11 = (f32[24,512]{1,0:T(8,128)S(1)}, f32[24,512]{1,0:T(8,128)S(1)}, u32[]{:S(2)}, u32[]{:S(2)}) collective-permute-start(f32[24,512]{1,0:T(8,128)S(1)} %add.58), channel_id=1, source_target_pairs={{0,32},{4,36},{8,40},{12,44},{16,48},{20,52},{24,56},{28,60},{32,0... | collective-permute-start | bytes 147464 | tf_op jit(solution)/shard_map/ppermute | solution.py:254
  56.0 4.6 %collective-permute-start.14 = (f32[24,512]{1,0:T(8,128)S(1)}, f32[24,512]{1,0:T(8,128)S(1)}, u32[]{:S(2)}, u32[]{:S(2)}) collective-permute-start(f32[24,512]{1,0:T(8,128)S(1)} %add.59), channel_id=1, source_target_pairs={{0,16},{4,20},{8,24},{12,28},{16,0},{20,4},{24,8},{28,12},{32,48},... | collective-permute-start | bytes 147464 | tf_op jit(solution)/shard_map/ppermute | solution.py:254
  56.6 4.4 %collective-permute-start.13 = (f32[24,512]{1,0:T(8,128)S(1)}, f32[24,512]{1,0:T(8,128)S(1)}, u32[]{:S(2)}, u32[]{:S(2)}) collective-permute-start(f32[24,512]{1,0:T(8,128)S(1)} %add.59), channel_id=1, source_target_pairs={{0,24},{4,28},{8,16},{12,20},{16,8},{20,12},{24,0},{28,4},{32,56},... | collective-permute-start | bytes 147464 | tf_op jit(solution)/shard_map/ppermute | solution.py:254
  58.4 2.9 %collective-permute-start.12 = (f32[24,512]{1,0:T(8,128)S(1)}, f32[24,512]{1,0:T(8,128)S(1)}, u32[]{:S(2)}, u32[]{:S(2)}) collective-permute-start(f32[24,512]{1,0:T(8,128)S(1)} %add.59), channel_id=1, source_target_pairs={{0,8},{4,12},{8,0},{12,4},{16,24},{20,28},{24,16},{28,20},{32,40},... | collective-permute-start | bytes 147464 | tf_op jit(solution)/shard_map/ppermute | solution.py:254
  61.4 14.8 %copy-start.2 = (bf16[48,48]{1,0:T(8,128)(2,1)S(1)}, bf16[48,48]{1,0:T(8,128)(2,1)}, u32[]{:S(2)}) copy-start(bf16[48,48]{1,0:T(8,128)(2,1)} %in_ref.3) | copy-start | bytes 13828
  61.4 14.8 %copy-start.3 = (bf16[48,48]{1,0:T(8,128)(2,1)S(1)}, bf16[48,48]{1,0:T(8,128)(2,1)}, u32[]{:S(2)}) copy-start(bf16[48,48]{1,0:T(8,128)(2,1)} %outf_ref.3) | copy-start | bytes 13828
  61.4 7.0 %collective-permute-start.17 = (f32[24,512]{1,0:T(8,128)S(1)}, f32[24,512]{1,0:T(8,128)S(1)}, u32[]{:S(2)}, u32[]{:S(2)}) collective-permute-start(f32[24,512]{1,0:T(8,128)S(1)} %add_add_fusion.1), channel_id=1, source_target_pairs={{0,128},{4,132},{8,136},{12,140},{16,144},{20,148},{24,152},{28,15... | collective-permute-start | bytes 147464 | tf_op jit(solution)/shard_map/ppermute | solution.py:254
  66.8 5.6 %collective-permute-start.16 = (f32[24,512]{1,0:T(8,128)S(1)}, f32[24,512]{1,0:T(8,128)S(1)}, u32[]{:S(2)}, u32[]{:S(2)}) collective-permute-start(f32[24,512]{1,0:T(8,128)S(1)} %add_add_fusion.1), channel_id=1, source_target_pairs={{0,192},{4,196},{8,200},{12,204},{16,208},{20,212},{24,216},{28,22... | collective-permute-start | bytes 147464 | tf_op jit(solution)/shard_map/ppermute | solution.py:254
  66.8 5.6 %collective-permute-start.15 = (f32[24,512]{1,0:T(8,128)S(1)}, f32[24,512]{1,0:T(8,128)S(1)}, u32[]{:S(2)}, u32[]{:S(2)}) collective-permute-start(f32[24,512]{1,0:T(8,128)S(1)} %add_add_fusion.1), channel_id=1, source_target_pairs={{0,64},{4,68},{8,72},{12,76},{16,80},{20,84},{24,88},{28,92},{32,9... | collective-permute-start | bytes 147464 | tf_op jit(solution)/shard_map/ppermute | solution.py:254
  72.4 4.6 %collective-permute-start.18 = (f32[24,512]{1,0:T(8,128)S(1)}, f32[24,512]{1,0:T(8,128)S(1)}, u32[]{:S(2)}, u32[]{:S(2)}) collective-permute-start(f32[24,512]{1,0:T(8,128)S(1)} %add_add_fusion.refs_0_), channel_id=1, source_target_pairs={{0,4},{4,0},{8,12},{12,8},{16,20},{20,16},{24,28},{28,24},{32,36},... | collective-permute-start | bytes 147464 | tf_op jit(solution)/shard_map/ppermute | solution.py:254

commit v9 on v8

--- a/solution.py
+++ b/solution.py
@@ -113,55 +113,48 @@
             kept_ref[(view - 5) * SLAB : (view - 4) * SLAB, :] = block
 
 
-def pick_rows(table_ref, nbr_ref, highs, start_of, store):
-    rows = nbr_ref.shape[1]
-    offsets = nbr_ref.shape[0]
-    middle = offsets // 2
-
-    def step(i, carry):
-        k = i + (i >= middle)
-        index = nbr_ref[pl.ds(k, 1), :]
-        onehot = low_onehot(index & (LOW - 1))
-        high = jnp.broadcast_to(index >> 8, (SLAB, rows))
-        picked = dot(table_ref[...], onehot)
-        place = pl.ds(pl.multiple_of(k * SLAB, SLAB), SLAB)
-        found = start_of(place)
-        for t, value in enumerate(highs):
-            found = jnp.where(high == value, picked[t * SLAB : (t + 1) * SLAB], found)
-        store(place, found.astype(BF))
-        return carry
-
-    lax.fori_loop(0, offsets - 1, step, 0, unroll=13)
-
-
-def fill_window(table_ref, at, block, halo_ref, slot, per_peer):
-    rows = block.shape[1]
-    window = pltpu.roll(block.astype(F32), rows - first_octant(halo_ref, slot), 1).astype(BF)
-    for i in range(per_peer):
-        table_ref[at + i * SLAB : at + (i + 1) * SLAB, :] = window[:, i * LOW : (i + 1) * LOW]
+def offset_index(nbr_ref, i):
+    middle = nbr_ref.shape[0] // 2
+    k = i + (i >= middle)
+    index = nbr_ref[pl.ds(k, 1), :]
+    return pl.ds(pl.multiple_of(k * SLAB, SLAB), SLAB), low_onehot(index & (LOW - 1)), index >> 8
+
+
+def window_of(block, halo_ref, slot):
+    return pltpu.roll(block.astype(F32), block.shape[1] - first_octant(halo_ref, slot), 1)
 
 
 def near_gather_kernel(halo_ref, own_ref, pair_ref, nbr_ref, ga_ref, table_ref):
-    rows = nbr_ref.shape[1]
+    offsets, rows = nbr_ref.shape
     own_tiles = rows // LOW
     per_peer = table_ref.shape[0] // SLAB - own_tiles
     for t in range(own_tiles):
         table_ref[t * SLAB : (t + 1) * SLAB, :] = own_ref[:, t * LOW : (t + 1) * LOW]
     slot = mirrored(core_bit(), 4, halo_ref.shape[0])
-    fill_window(table_ref, own_tiles * SLAB, pair_ref[...], halo_ref, slot, per_peer)
+    window = window_of(pair_ref[...], halo_ref, slot).astype(BF)
+    for i in range(per_peer):
+        t = own_tiles + i
+        table_ref[t * SLAB : (t + 1) * SLAB, :] = window[:, i * LOW : (i + 1) * LOW]
     highs = list(range(own_tiles)) + [own_tiles + slot * per_peer + i for i in range(per_peer)]
-    middle = nbr_ref.shape[0] // 2
-
-    def store(place, found):
-        ga_ref[place, :] = found
-
-    pick_rows(table_ref, nbr_ref, highs, lambda place: jnp.zeros((SLAB, rows), F32), store)
+
+    def step(i, carry):
+        place, onehot, high = offset_index(nbr_ref, i)
+        high = jnp.broadcast_to(high, (SLAB, rows))
+        picked = dot(table_ref[...], onehot)
+        found = jnp.zeros((SLAB, rows), F32)
+        for t, value in enumerate(highs):
+            found = jnp.where(high == value, picked[t * SLAB : (t + 1) * SLAB], found)
+        ga_ref[place, :] = found.astype(BF)
+        return carry
+
+    lax.fori_loop(0, offsets - 1, step, 0, unroll=13)
+    middle = offsets // 2
     ga_ref[middle * SLAB : (middle + 1) * SLAB, :] = own_ref[...]
 
 
 def far_gather_kernel(halo_ref, base_ref, near_ref, far_ref, cross_ref, core_ref, nbr_ref, mix_ref, ga_ref,
-                      table_ref):
-    rows = nbr_ref.shape[1]
+                      wide_ref, table_ref):
+    offsets, rows = nbr_ref.shape
     own_tiles = rows // LOW
     near = halo_ref.shape[0]
     views = {
@@ -173,20 +166,33 @@
         6: cross_ref[0:SLAB, :],
         7: cross_ref[3 * SLAB : 4 * SLAB, :],
     }
-    per_peer = table_ref.shape[0] // SLAB // len(views)
+    both = table_ref.shape[0] // len(views)
+    width = both // 2
     highs = []
     for n, (view, block) in enumerate(views.items()):
         slot = mirrored(core_bit(), view, near)
-        fill_window(table_ref, n * per_peer * SLAB, block, halo_ref, slot, per_peer)
-        highs += [own_tiles + slot * per_peer + i for i in range(per_peer)]
+        window = window_of(block, halo_ref, slot)
+        wide_ref[n * both : n * both + width, :] = window[:width, :LOW]
+        wide_ref[n * both + width : (n + 1) * both, :] = window[:width, LOW : 2 * LOW]
+        highs.append(own_tiles + 2 * slot)
+    table_ref[...] = wide_ref[...].astype(BF)
+    second = (lax.broadcasted_iota(jnp.int32, (both, rows), 0) >= width).astype(jnp.int32)
+
+    def step(i, carry):
+        place, onehot, high = offset_index(nbr_ref, i)
+        high = jnp.broadcast_to(high, (both, rows)) - second
+        picked = dot(table_ref[...], onehot)
+        found = jnp.zeros((both, rows), F32)
+        for n, value in enumerate(highs):
+            found = jnp.where(high == value, picked[n * both : (n + 1) * both], found)
+        found = jnp.concatenate([found[:width] + found[width:], jnp.zeros((SLAB - width, rows), F32)], 0)
+        ga_ref[place, :] = (base_ref[place, :].astype(F32) + found).astype(BF)
+        return carry
+
+    lax.fori_loop(0, offsets - 1, step, 0, unroll=13)
     used = core_ref.shape[0]
-    middle = nbr_ref.shape[0] // 2
+    middle = offsets // 2
     itself = slice(middle * SLAB, (middle + 1) * SLAB)
-
-    def store(place, found):
-        ga_ref[place, :] = found
-
-    pick_rows(table_ref, nbr_ref, highs, lambda place: base_ref[place, :].astype(F32), store)
     ga_ref[itself, :] = base_ref[itself, :]
     ga_ref[used:, :] = jnp.zeros_like(ga_ref[used:, :])
     mix_ref[...] = dot(core_ref[...], ga_ref[:used, :], TN)
@@ -315,8 +321,8 @@
     )
     to_near = [slabs_of(kept, 0, 1) + near_same, slabs_of(kept, 1, 2) + near_other]
     to_far = [slabs_of(kept, 2, 3) + far_same, far_other]
+    far = outward(jnp.concatenate([reduced, pair] + [x.astype(BF) for x in to_far], 0), 2)
     near = outward(jnp.concatenate([reduced, pair] + [x.astype(BF) for x in to_near], 0), 1)
-    far = outward(jnp.concatenate([reduced, pair] + [x.astype(BF) for x in to_far], 0), 2)
     per_peer = slots * 64 // LOW
     near_tiles = rows // LOW + per_peer
     found = pl.pallas_call(
@@ -329,7 +335,7 @@
         cost_estimate=estimate,
         name="near_gather",
     )(halo, reduced, pair, neighbours)
-    near, far, found = lax.optimization_barrier((near, far, found))
+    far, near, found = lax.optimization_barrier((far, near, found))
     near_pair, far_pair = slabs_of(near, 0, 2), slabs_of(far, 0, 2)
     passed = slabs_of(near, 3, 4).astype(F32) + slabs_of(far, 3, 4).astype(F32)
     beyond = crossed(jnp.concatenate([near_pair, far_pair, passed.astype(BF)], 0), 1)
@@ -341,7 +347,7 @@
         out_shape=[struct((rank, rows), F32), struct((packed_width, rows), BF)],
         in_specs=[SMEM] + [VMEM] * 6,
         out_specs=[VMEM] * 2,
-        scratch_shapes=[pltpu.VMEM((table_rows - near_tiles * SLAB, LOW), BF)],
+        scratch_shapes=[pltpu.VMEM((14 * width, LOW), F32), pltpu.VMEM((14 * width, LOW), BF)],
         compiler_params=ROOMY,
         cost_estimate=estimate,
         name="far_gather",

time: 78 us -> 78.2 us (level)
  waiting for transfers between devices: 22.4 us -> 24.6 us
  starting transfers between devices: 35.9 us -> 33.8 us
    ppermute x2, waiting for transfers between devices: 0.08 us -> 2.09 us  [outward(): lax.ppermute(block, 'leaf', [(i, (i + (2 * chips if i % 2 == 0 else -2 *...]
    ppermute x11, starting transfers between devices: 19.6 us -> 18.3 us  [crossed(): lax.ppermute(block, 'leaf', [(i, i ^ mask) for i in range(lax.axis_size('...]
  transfers between devices with their start and end apart: 19 -> 19, of which waited for: 14 -> 13; matrix products, arithmetic and copies ran while one was open for 0% -> 0% of each run, Pallas kernels for 6% -> 6%
where the time goes in v9:
time: 78.2 us; the launch traced here: 78.1 us
  starting transfers between devices  33.8 us (43%)
  waiting for transfers between devices  24.6 us (31%)
  Pallas kernels  18.1 us (23%)
  between operations  0.83 us (1%)
    ppermute x11, starting transfers between devices, crossed(): lax.ppermute(block, 'leaf', [(i, i ^ mask) for i in range(lax.axis_size('...  18.3 us
    ppermute x11, waiting for transfers between devices, crossed(): lax.ppermute(block, 'leaf', [(i, i ^ mask) for i in range(lax.axis_size('...  12.3 us
    ppermute x6, waiting for transfers between devices, shifted(): lax.ppermute(block, axis, [(i, (i + distance) % count) for i in range(cou...  10.1 us
    ppermute x6, starting transfers between devices, shifted(): lax.ppermute(block, axis, [(i, (i + distance) % count) for i in range(cou...  8.06 us
    ppermute x2, starting transfers between devices, outward(): lax.ppermute(block, 'leaf', [(i, (i + (2 * chips if i % 2 == 0 else -2 *...  7.42 us
    pallas_call x1, Pallas kernels, body(): pl.pallas_call(scatter_kernel, out_shape=[struct((rank, rows), BF), struc...  5.98 us
    pallas_call x1, Pallas kernels, body(): pl.pallas_call(far_gather_kernel, out_shape=[struct((rank, rows), F32), s...  4.08 us
    pallas_call x1, Pallas kernels, body(): pl.pallas_call(near_gather_kernel, out_shape=struct((offsets * SLAB, rows...  3.16 us
  transfers between devices with their start and end apart: 19, of which 13 were waited for; matrix products, arithmetic and copies ran while one was open for 0% of the time, Pallas kernels for 6%

profile of v9, /device:TPU:1, one launch (start us, length us, event | category | flops | bytes accessed | tf_op | source)
XLA Modules:
  0.0 78.1 jit_solution(6692085769990821709)
XLA Ops:
  0.6 2.2 %project.1 = (f32[64,1024]{1,0:T(8,128)}, bf16[64,1024]{1,0:T(8,128)(2,1)}, bf16[64,1024]{1,0:T(8,128)(2,1)}, bf16[64,1024]{1,0:T(8,128)(2,1)}) custom-call(bf16[48,1024]{1,0:T(8,128)(2,1)} %feat_ref.3, bf16[48,48]{1,0:T(8,128)(2,1)} %in_ref.3, bf16[48,1024]{1,0:T(8,128)(2,1)} %cot_ref.3, bf16[48,48]{1,0:T(8,128)(2,1)} %outf_ref.3, s32[1,1024]{1,0:T(1,128)} %bitcast.9), custom_call_target="tpu_custom_call" | custom-call | tf_op jit(solution)/shard_map/project/pallas_call | solution.py:292
  2.8 2.1 %collective-permute-start = (bf16[64,1024]{1,0:T(8,128)(2,1)}, bf16[64,1024]{1,0:T(8,128)(2,1)S(1)}, u32[]{:S(2)}, u32[]{:S(2)}) collective-permute-start(bf16[64,1024]{1,0:T(8,128)(2,1)} %get-tuple-element.28), channel_id=1, source_target_pairs={{0,1},{1,2},{2,3},{3,0},{4,5},{5,6},{6,7},{7,4},{8,9},{9,10},{10,1... | collective-permute-start | bytes 393224 | tf_op jit(solution)/shard_map/ppermute | solution.py:256
  5.0 1.5 %collective-permute-start.1 = (bf16[64,1024]{1,0:T(8,128)(2,1)}, bf16[64,1024]{1,0:T(8,128)(2,1)S(1)}, u32[]{:S(2)}, u32[]{:S(2)}) collective-permute-start(bf16[64,1024]{1,0:T(8,128)(2,1)} %get-tuple-element.29), channel_id=1, source_target_pairs={{0,3},{1,0},{2,1},{3,2},{4,7},{5,4},{6,5},{7,6},{8,11},{9,8},{10,9... | collective-permute-start | bytes 393224 | tf_op jit(solution)/shard_map/ppermute | solution.py:256
  6.5 1.6 %collective-permute-start.2 = (bf16[64,1024]{1,0:T(8,128)(2,1)}, bf16[64,1024]{1,0:T(8,128)(2,1)S(1)}, u32[]{:S(2)}, u32[]{:S(2)}) collective-permute-start(bf16[64,1024]{1,0:T(8,128)(2,1)} %get-tuple-element.30), channel_id=1, source_target_pairs={{0,2},{1,3},{2,0},{3,1},{4,6},{5,7},{6,4},{7,5},{8,10},{9,11},{10,... | collective-permute-start | bytes 393224 | tf_op jit(solution)/shard_map/ppermute | solution.py:256
  8.1 0.8 %collective-permute-done.p1 = bf16[64,1024]{1,0:T(8,128)(2,1)S(1)} collective-permute-done((bf16[64,1024]{1,0:T(8,128)(2,1)}, bf16[64,1024]{1,0:T(8,128)(2,1)S(1)}, u32[]{:S(2)}, u32[]{:S(2)}) %collective-permute-start) | collective-permute-done | bytes 131104 | tf_op jit(solution)/shard_map/ppermute | solution.py:256
  9.0 4.0 %collective-permute-done.2.p3 = bf16[64,1024]{1,0:T(8,128)(2,1)S(1)} collective-permute-done((bf16[64,1024]{1,0:T(8,128)(2,1)}, bf16[64,1024]{1,0:T(8,128)(2,1)S(1)}, u32[]{:S(2)}, u32[]{:S(2)}) %collective-permute-start.2) | collective-permute-done | bytes 131104 | tf_op jit(solution)/shard_map/ppermute | solution.py:256
  13.0 6.0 %scatter.1 = (bf16[48,1024]{1,0:T(8,128)(2,1)S(1)}, f32[16,1024]{1,0:T(8,128)S(1)}, f32[48,1024]{1,0:T(8,128)S(1)}, bf16[96,1024]{1,0:T(8,128)(2,1)S(1)}) custom-call(s32[8,8]{1,0:T(8,128)S(1)} %bitcast.6, f32[64,1024]{1,0:T(8,128)S(1)} %copy-done.4, bf16[64,1024]{1,0:T(8,128)(2,1)S(1)} %collective-permute-done.p1, ...), custom_call_target="tpu_custom_call" | custom-call | flops 5000000000 | bytes 1048576 | tf_op jit(solution)/shard_map/scatter/pallas_call | solution.py:302
  19.0 3.1 %collective-permute-start.3 = (bf16[96,1024]{1,0:T(8,128)(2,1)S(1)}, bf16[96,1024]{1,0:T(8,128)(2,1)S(1)}, u32[]{:S(2)}, u32[]{:S(2)}) collective-permute-start(bf16[96,1024]{1,0:T(8,128)(2,1)S(1)} %get-tuple-element.31), channel_id=1, source_target_pairs={{0,4},{4,0},{8,12},{12,8},{16,20},{20,16},{24,28},{28,24},{32,36},... | collective-permute-start | bytes 589832 | tf_op jit(solution)/shard_map/ppermute | solution.py:260
  22.1 1.1 %collective-permute-done.3 = bf16[96,1024]{1,0:T(8,128)(2,1)S(1)} collective-permute-done((bf16[96,1024]{1,0:T(8,128)(2,1)S(1)}, bf16[96,1024]{1,0:T(8,128)(2,1)S(1)}, u32[]{:S(2)}, u32[]{:S(2)}) %collective-permute-start.3) | collective-permute-done | bytes 196640 | tf_op jit(solution)/shard_map/ppermute | solution.py:260
  23.2 6.9 %collective-permute-start.5 = (bf16[64,1024]{1,0:T(8,128)(2,1)S(1)}, bf16[64,1024]{1,0:T(8,128)(2,1)S(1)}, u32[]{:S(2)}, u32[]{:S(2)}) collective-permute-start(bf16[64,1024]{1,0:T(8,128)(2,1)S(1)} %get-tuple-element.54), channel_id=1, source_target_pairs={{0,8},{4,252},{8,16},{12,4},{16,24},{20,12},{24,32},{28,20},{32,40... | collective-permute-start | bytes 393224 | tf_op jit(solution)/shard_map/ppermute | solution.py:265
  30.6 3.2 %near_gather.1.base_ref = bf16[432,1024]{1,0:T(8,128)(2,1)S(1)} custom-call(s32[8,8]{1,0:T(8,128)S(1)} %bitcast.7, bf16[16,1024]{1,0:T(8,128)(2,1)S(1)} %slice.51.own_ref, bf16[16,1024]{1,0:T(8,128)(2,1)S(1)} %get-tuple-element.52.pair_ref, s32[27,1024]{1,0:T(8,128)S(1)} %copy-done.5), custom_call_target="tpu_custom_call" | custom-call | flops 5000000000 | bytes 1048576 | tf_op jit(solution)/shard_map/near_gather/pallas_call | solution.py:328
  33.8 2.1 %collective-permute-done.4 = bf16[64,1024]{1,0:T(8,128)(2,1)S(1)} collective-permute-done((bf16[64,1024]{1,0:T(8,128)(2,1)S(1)}, bf16[64,1024]{1,0:T(8,128)(2,1)S(1)}, u32[]{:S(2)}, u32[]{:S(2)}) %collective-permute-start.4) | collective-permute-done | bytes 131104 | tf_op jit(solution)/shard_map/ppermute | solution.py:265
  36.6 0.8 %collective-permute-done.6.cross_ref = bf16[80,1024]{1,0:T(8,128)(2,1)S(1)} collective-permute-done((bf16[80,1024]{1,0:T(8,128)(2,1)S(1)}, bf16[80,1024]{1,0:T(8,128)(2,1)S(1)}, u32[]{:S(2)}, u32[]{:S(2)}) %collective-permute-start.6) | collective-permute-done | bytes 163872 | tf_op jit(solution)/shard_map/ppermute | solution.py:260
  37.4 4.1 %far_gather.1 = (f32[48,1024]{1,0:T(8,128)S(1)}, bf16[512,1024]{1,0:T(8,128)(2,1)S(1)}) custom-call(s32[8,8]{1,0:T(8,128)S(1)} %bitcast.8, bf16[432,1024]{1,0:T(8,128)(2,1)S(1)} %near_gather.1.base_ref, bf16[32,1024]{1,0:T(8,128)(2,1)S(1)} %slice.60.near_ref, bf16[32,1024]{1,0:T(8,128)(2,1)S(1)} %slice.61.far_ref, ...), custom_call_target="tpu_custom_call" | custom-call | flops 5000000000 | bytes 1048576 | tf_op jit(solution)/shard_map/far_gather/pallas_call | solution.py:345
  41.6 0.9 %collective-permute-start.9 = (bf16[64,1024]{1,0:T(8,128)(2,1)S(1)}, bf16[64,1024]{1,0:T(8,128)(2,1)S(1)}, u32[]{:S(2)}, u32[]{:S(2)}) collective-permute-start(bf16[64,1024]{1,0:T(8,128)(2,1)S(1)} %pad_maximum_fusion.4.e0), channel_id=1, source_target_pairs={{0,1},{1,2},{2,3},{3,0},{4,5},{5,6},{6,7},{7,4},{8,9},{9,10},{10,1... | collective-permute-start | bytes 393224 | tf_op jit(solution)/shard_map/ppermute | solution.py:256
  42.5 1.8 %collective-permute-start.8 = (bf16[64,1024]{1,0:T(8,128)(2,1)S(1)}, bf16[64,1024]{1,0:T(8,128)(2,1)S(1)}, u32[]{:S(2)}, u32[]{:S(2)}) collective-permute-start(bf16[64,1024]{1,0:T(8,128)(2,1)S(1)} %pad_maximum_fusion.4.e0), channel_id=1, source_target_pairs={{0,3},{1,0},{2,1},{3,2},{4,7},{5,4},{6,5},{7,6},{8,11},{9,8},{10,9... | collective-permute-start | bytes 393224 | tf_op jit(solution)/shard_map/ppermute | solution.py:256
  44.9 3.0 %collective-permute-done.9.e1 = bf16[64,1024]{1,0:T(8,128)(2,1)S(1)} collective-permute-done((bf16[64,1024]{1,0:T(8,128)(2,1)S(1)}, bf16[64,1024]{1,0:T(8,128)(2,1)S(1)}, u32[]{:S(2)}, u32[]{:S(2)}) %collective-permute-start.9) | collective-permute-done | bytes 131104 | tf_op jit(solution)/shard_map/ppermute | solution.py:256
  47.8 2.3 %collective-permute-done.7.e2 = bf16[64,1024]{1,0:T(8,128)(2,1)S(1)} collective-permute-done((bf16[64,1024]{1,0:T(8,128)(2,1)S(1)}, bf16[64,1024]{1,0:T(8,128)(2,1)S(1)}, u32[]{:S(2)}, u32[]{:S(2)}) %collective-permute-start.7) | collective-permute-done | bytes 131104 | tf_op jit(solution)/shard_map/ppermute | solution.py:256
  50.2 0.6 sums.1
  50.7 1.7 %collective-permute-start.10 = (f32[24,512]{1,0:T(8,128)S(1)}, f32[24,512]{1,0:T(8,128)S(1)}, u32[]{:S(2)}, u32[]{:S(2)}) collective-permute-start(f32[24,512]{1,0:T(8,128)S(1)} %get-tuple-element.45), channel_id=1, source_target_pairs={{0,4},{4,0},{8,12},{12,8},{16,20},{20,16},{24,28},{28,24},{32,36},... | collective-permute-start | bytes 147464 | tf_op jit(solution)/shard_map/ppermute | solution.py:260
  52.4 0.9 %collective-permute-done.10 = f32[24,512]{1,0:T(8,128)S(1)} collective-permute-done((f32[24,512]{1,0:T(8,128)S(1)}, f32[24,512]{1,0:T(8,128)S(1)}, u32[]{:S(2)}, u32[]{:S(2)}) %collective-permute-start.10) | collective-permute-done | bytes 49184 | tf_op jit(solution)/shard_map/ppermute | solution.py:260
  53.4 2.9 %collective-permute-done.11 = f32[24,512]{1,0:T(8,128)S(1)} collective-permute-done((f32[24,512]{1,0:T(8,128)S(1)}, f32[24,512]{1,0:T(8,128)S(1)}, u32[]{:S(2)}, u32[]{:S(2)}) %collective-permute-start.11) | collective-permute-done | bytes 49184 | tf_op jit(solution)/shard_map/ppermute | solution.py:260
  56.8 1.4 %collective-permute-start.13 = (f32[24,512]{1,0:T(8,128)S(1)}, f32[24,512]{1,0:T(8,128)S(1)}, u32[]{:S(2)}, u32[]{:S(2)}) collective-permute-start(f32[24,512]{1,0:T(8,128)S(1)} %add.59), channel_id=1, source_target_pairs={{0,24},{4,28},{8,16},{12,20},{16,8},{20,12},{24,0},{28,4},{32,56},... | collective-permute-start | bytes 147464 | tf_op jit(solution)/shard_map/ppermute | solution.py:260
  58.3 0.8 %collective-permute-start.12 = (f32[24,512]{1,0:T(8,128)S(1)}, f32[24,512]{1,0:T(8,128)S(1)}, u32[]{:S(2)}, u32[]{:S(2)}) collective-permute-start(f32[24,512]{1,0:T(8,128)S(1)} %add.59), channel_id=1, source_target_pairs={{0,8},{4,12},{8,0},{12,4},{16,24},{20,28},{24,16},{28,20},{32,40},... | collective-permute-start | bytes 147464 | tf_op jit(solution)/shard_map/ppermute | solution.py:260
  59.1 1.8 %collective-permute-done.14 = f32[24,512]{1,0:T(8,128)S(1)} collective-permute-done((f32[24,512]{1,0:T(8,128)S(1)}, f32[24,512]{1,0:T(8,128)S(1)}, u32[]{:S(2)}, u32[]{:S(2)}) %collective-permute-start.14) | collective-permute-done | bytes 49184 | tf_op jit(solution)/shard_map/ppermute | solution.py:260
  61.4 5.1 %collective-permute-start.17 = (f32[24,512]{1,0:T(8,128)S(1)}, f32[24,512]{1,0:T(8,128)S(1)}, u32[]{:S(2)}, u32[]{:S(2)}) collective-permute-start(f32[24,512]{1,0:T(8,128)S(1)} %add_add_fusion.1), channel_id=1, source_target_pairs={{0,128},{4,132},{8,136},{12,140},{16,144},{20,148},{24,152},{28,15... | collective-permute-start | bytes 147464 | tf_op jit(solution)/shard_map/ppermute | solution.py:260
  66.6 1.1 %collective-permute-start.15 = (f32[24,512]{1,0:T(8,128)S(1)}, f32[24,512]{1,0:T(8,128)S(1)}, u32[]{:S(2)}, u32[]{:S(2)}) collective-permute-start(f32[24,512]{1,0:T(8,128)S(1)} %add_add_fusion.1), channel_id=1, source_target_pairs={{0,64},{4,68},{8,72},{12,76},{16,80},{20,84},{24,88},{28,92},{32,9... | collective-permute-start | bytes 147464 | tf_op jit(solution)/shard_map/ppermute | solution.py:260
  67.6 0.7 collective-permute-done.17
  68.4 3.5 %collective-permute-done.16 = f32[24,512]{1,0:T(8,128)S(1)} collective-permute-done((f32[24,512]{1,0:T(8,128)S(1)}, f32[24,512]{1,0:T(8,128)S(1)}, u32[]{:S(2)}, u32[]{:S(2)}) %collective-permute-start.16) | collective-permute-done | bytes 49184 | tf_op jit(solution)/shard_map/ppermute | solution.py:260
  71.9 4.4 %collective-permute-start.18 = (f32[24,512]{1,0:T(8,128)S(1)}, f32[24,512]{1,0:T(8,128)S(1)}, u32[]{:S(2)}, u32[]{:S(2)}) collective-permute-start(f32[24,512]{1,0:T(8,128)S(1)} %add_add_fusion.refs_0_), channel_id=1, source_target_pairs={{0,4},{4,0},{8,12},{12,8},{16,20},{20,16},{24,28},{28,24},{32,36},... | collective-permute-start | bytes 147464 | tf_op jit(solution)/shard_map/ppermute | solution.py:260
  76.4 0.8 %outputs.1 = (bf16[48,1024]{1,0:T(8,128)(2,1)}, bf16[48,1024]{1,0:T(8,128)(2,1)}) custom-call(bf16[48,1024]{1,0:T(8,128)(2,1)S(1)} %get-tuple-element.40.rows_ref, bf16[48,1024]{1,0:T(8,128)(2,1)S(1)} %get-tuple-element.41.mixed_ref, bf16[48,48]{1,0:T(8,128)(2,1)S(1)} %copy-done.2, bf16[48,48]{1,0:T(8,128)(2,1)S(1)} %copy-done.3), custom_call_target="tpu_custom_call" | custom-call | flops 500000000 | bytes 1048576 | tf_op jit(solution)/shard_map/outputs/pallas_call | solution.py:377
  77.2 0.8 %unpack.1 = (f32[48,48]{1,0:T(8,128)}, f32[12,27,48]{2,1,0:T(8,128)}, f32[48,48]{1,0:T(8,128)}) custom-call(f32[24,512]{1,0:T(8,128)S(1)} %add_add_fusion.refs_0_, f32[24,512]{1,0:T(8,128)S(1)} %collective-permute-done.18.refs_1_), custom_call_target="tpu_custom_call" | custom-call | tf_op jit(solution)/shard_map/unpack/pallas_call | solution.py:389
  (50 shorter events, 3.1 us)
Async XLA Ops:
  0.6 7.4 %copy-start.7 = (bf16[27,12,48]{2,0,1:T(8,128)(2,1)S(1)}, bf16[27,12,48]{2,0,1:T(8,128)(2,1)}, u32[]{:S(2)}) copy-start(bf16[27,12,48]{2,0,1:T(8,128)(2,1)} %param.10) | copy-start | bytes 93316
  2.8 10.2 %copy-start.4 = (f32[64,1024]{1,0:T(8,128)S(1)}, f32[64,1024]{1,0:T(8,128)}, u32[]{:S(2)}) copy-start(f32[64,1024]{1,0:T(8,128)} %get-tuple-element.27.p0) | copy-start | bytes 786436
  2.8 6.1 %collective-permute-start = (bf16[64,1024]{1,0:T(8,128)(2,1)}, bf16[64,1024]{1,0:T(8,128)(2,1)S(1)}, u32[]{:S(2)}, u32[]{:S(2)}) collective-permute-start(bf16[64,1024]{1,0:T(8,128)(2,1)} %get-tuple-element.28), channel_id=1, source_target_pairs={{0,1},{1,2},{2,3},{3,0},{4,5},{5,6},{6,7},{7,4},{8,9},{9,10},{10,1... | collective-permute-start | bytes 393224 | tf_op jit(solution)/shard_map/ppermute | solution.py:256
  5.0 4.0 %collective-permute-start.1 = (bf16[64,1024]{1,0:T(8,128)(2,1)}, bf16[64,1024]{1,0:T(8,128)(2,1)S(1)}, u32[]{:S(2)}, u32[]{:S(2)}) collective-permute-start(bf16[64,1024]{1,0:T(8,128)(2,1)} %get-tuple-element.29), channel_id=1, source_target_pairs={{0,3},{1,0},{2,1},{3,2},{4,7},{5,4},{6,5},{7,6},{8,11},{9,8},{10,9... | collective-permute-start | bytes 393224 | tf_op jit(solution)/shard_map/ppermute | solution.py:256
  6.5 6.5 %collective-permute-start.2 = (bf16[64,1024]{1,0:T(8,128)(2,1)}, bf16[64,1024]{1,0:T(8,128)(2,1)S(1)}, u32[]{:S(2)}, u32[]{:S(2)}) collective-permute-start(bf16[64,1024]{1,0:T(8,128)(2,1)} %get-tuple-element.30), channel_id=1, source_target_pairs={{0,2},{1,3},{2,0},{3,1},{4,6},{5,7},{6,4},{7,5},{8,10},{9,11},{10,... | collective-permute-start | bytes 393224 | tf_op jit(solution)/shard_map/ppermute | solution.py:256
  8.1 4.9 %copy-start.5 = (s32[27,1024]{1,0:T(8,128)S(1)}, s32[27,1024]{1,0:T(8,128)}, u32[]{:S(2)}) copy-start(s32[27,1024]{1,0:T(8,128)} %nbr_ref.5) | copy-start | bytes 331780
  8.1 4.9 %copy-start.6 = (s32[1,8,8]{2,1,0:T(8,128)S(1)}, s32[1,8,8]{2,1,0:T(8,128)}, u32[]{:S(2)}) copy-start(s32[1,8,8]{2,1,0:T(8,128)} %param.13) | copy-start | bytes 772
  19.0 4.1 %collective-permute-start.3 = (bf16[96,1024]{1,0:T(8,128)(2,1)S(1)}, bf16[96,1024]{1,0:T(8,128)(2,1)S(1)}, u32[]{:S(2)}, u32[]{:S(2)}) collective-permute-start(bf16[96,1024]{1,0:T(8,128)(2,1)S(1)} %get-tuple-element.31), channel_id=1, source_target_pairs={{0,4},{4,0},{8,12},{12,8},{16,20},{20,16},{24,28},{28,24},{32,36},... | collective-permute-start | bytes 589832 | tf_op jit(solution)/shard_map/ppermute | solution.py:260
  23.2 10.6 %collective-permute-start.5 = (bf16[64,1024]{1,0:T(8,128)(2,1)S(1)}, bf16[64,1024]{1,0:T(8,128)(2,1)S(1)}, u32[]{:S(2)}, u32[]{:S(2)}) collective-permute-start(bf16[64,1024]{1,0:T(8,128)(2,1)S(1)} %get-tuple-element.54), channel_id=1, source_target_pairs={{0,8},{4,252},{8,16},{12,4},{16,24},{20,12},{24,32},{28,20},{32,40... | collective-permute-start | bytes 393224 | tf_op jit(solution)/shard_map/ppermute | solution.py:265
  30.1 5.8 %collective-permute-start.4 = (bf16[64,1024]{1,0:T(8,128)(2,1)S(1)}, bf16[64,1024]{1,0:T(8,128)(2,1)S(1)}, u32[]{:S(2)}, u32[]{:S(2)}) collective-permute-start(bf16[64,1024]{1,0:T(8,128)(2,1)S(1)} %get-tuple-element.55), channel_id=1, source_target_pairs={{0,16},{4,244},{8,24},{12,252},{16,32},{20,4},{24,40},{28,12},{32,... | collective-permute-start | bytes 393224 | tf_op jit(solution)/shard_map/ppermute | solution.py:265
  35.9 0.7 copy-start.8
  35.9 1.5 %collective-permute-start.6 = (bf16[80,1024]{1,0:T(8,128)(2,1)S(1)}, bf16[80,1024]{1,0:T(8,128)(2,1)S(1)}, u32[]{:S(2)}, u32[]{:S(2)}) collective-permute-start(bf16[80,1024]{1,0:T(8,128)(2,1)S(1)} %pad_maximum_fusion), channel_id=1, source_target_pairs={{0,4},{4,0},{8,12},{12,8},{16,20},{20,16},{24,28},{28,24},{32,36},... | collective-permute-start | bytes 491528 | tf_op jit(solution)/shard_map/ppermute | solution.py:260
  41.6 6.2 %collective-permute-start.9 = (bf16[64,1024]{1,0:T(8,128)(2,1)S(1)}, bf16[64,1024]{1,0:T(8,128)(2,1)S(1)}, u32[]{:S(2)}, u32[]{:S(2)}) collective-permute-start(bf16[64,1024]{1,0:T(8,128)(2,1)S(1)} %pad_maximum_fusion.4.e0), channel_id=1, source_target_pairs={{0,1},{1,2},{2,3},{3,0},{4,5},{5,6},{6,7},{7,4},{8,9},{9,10},{10,1... | collective-permute-start | bytes 393224 | tf_op jit(solution)/shard_map/ppermute | solution.py:256
  42.5 5.3 %collective-permute-start.8 = (bf16[64,1024]{1,0:T(8,128)(2,1)S(1)}, bf16[64,1024]{1,0:T(8,128)(2,1)S(1)}, u32[]{:S(2)}, u32[]{:S(2)}) collective-permute-start(bf16[64,1024]{1,0:T(8,128)(2,1)S(1)} %pad_maximum_fusion.4.e0), channel_id=1, source_target_pairs={{0,3},{1,0},{2,1},{3,2},{4,7},{5,4},{6,5},{7,6},{8,11},{9,8},{10,9... | collective-permute-start | bytes 393224 | tf_op jit(solution)/shard_map/ppermute | solution.py:256
  44.3 5.8 %collective-permute-start.7 = (bf16[64,1024]{1,0:T(8,128)(2,1)S(1)}, bf16[64,1024]{1,0:T(8,128)(2,1)S(1)}, u32[]{:S(2)}, u32[]{:S(2)}) collective-permute-start(bf16[64,1024]{1,0:T(8,128)(2,1)S(1)} %pad_maximum_fusion.4.e0), channel_id=1, source_target_pairs={{0,2},{1,3},{2,0},{3,1},{4,6},{5,7},{6,4},{7,5},{8,10},{9,11},{10,... | collective-permute-start | bytes 393224 | tf_op jit(solution)/shard_map/ppermute | solution.py:256
  44.4 5.7 %copy-start = (bf16[48,1024]{1,0:T(8,128)(2,1)S(1)}, bf16[48,1024]{1,0:T(8,128)(2,1)}, u32[]{:S(2)}) copy-start(bf16[48,1024]{1,0:T(8,128)(2,1)} %feat_ref.3) | copy-start | bytes 294916
  44.4 5.7 %copy-start.1 = (bf16[48,1024]{1,0:T(8,128)(2,1)S(1)}, bf16[48,1024]{1,0:T(8,128)(2,1)}, u32[]{:S(2)}) copy-start(bf16[48,1024]{1,0:T(8,128)(2,1)} %cot_ref.3) | copy-start | bytes 294916
  50.7 2.6 %collective-permute-start.10 = (f32[24,512]{1,0:T(8,128)S(1)}, f32[24,512]{1,0:T(8,128)S(1)}, u32[]{:S(2)}, u32[]{:S(2)}) collective-permute-start(f32[24,512]{1,0:T(8,128)S(1)} %get-tuple-element.45), channel_id=1, source_target_pairs={{0,4},{4,0},{8,12},{12,8},{16,20},{20,16},{24,28},{28,24},{32,36},... | collective-permute-start | bytes 147464 | tf_op jit(solution)/shard_map/ppermute | solution.py:260
  53.3 3.0 %collective-permute-start.11 = (f32[24,512]{1,0:T(8,128)S(1)}, f32[24,512]{1,0:T(8,128)S(1)}, u32[]{:S(2)}, u32[]{:S(2)}) collective-permute-start(f32[24,512]{1,0:T(8,128)S(1)} %add.58), channel_id=1, source_target_pairs={{0,32},{4,36},{8,40},{12,44},{16,48},{20,52},{24,56},{28,60},{32,0... | collective-permute-start | bytes 147464 | tf_op jit(solution)/shard_map/ppermute | solution.py:260
  56.3 4.6 %collective-permute-start.14 = (f32[24,512]{1,0:T(8,128)S(1)}, f32[24,512]{1,0:T(8,128)S(1)}, u32[]{:S(2)}, u32[]{:S(2)}) collective-permute-start(f32[24,512]{1,0:T(8,128)S(1)} %add.59), channel_id=1, source_target_pairs={{0,16},{4,20},{8,24},{12,28},{16,0},{20,4},{24,8},{28,12},{32,48},... | collective-permute-start | bytes 147464 | tf_op jit(solution)/shard_map/ppermute | solution.py:260
  56.8 4.6 %collective-permute-start.13 = (f32[24,512]{1,0:T(8,128)S(1)}, f32[24,512]{1,0:T(8,128)S(1)}, u32[]{:S(2)}, u32[]{:S(2)}) collective-permute-start(f32[24,512]{1,0:T(8,128)S(1)} %add.59), channel_id=1, source_target_pairs={{0,24},{4,28},{8,16},{12,20},{16,8},{20,12},{24,0},{28,4},{32,56},... | collective-permute-start | bytes 147464 | tf_op jit(solution)/shard_map/ppermute | solution.py:260
  58.3 3.1 %collective-permute-start.12 = (f32[24,512]{1,0:T(8,128)S(1)}, f32[24,512]{1,0:T(8,128)S(1)}, u32[]{:S(2)}, u32[]{:S(2)}) collective-permute-start(f32[24,512]{1,0:T(8,128)S(1)} %add.59), channel_id=1, source_target_pairs={{0,8},{4,12},{8,0},{12,4},{16,24},{20,28},{24,16},{28,20},{32,40},... | collective-permute-start | bytes 147464 | tf_op jit(solution)/shard_map/ppermute | solution.py:260
  61.4 14.9 %copy-start.2 = (bf16[48,48]{1,0:T(8,128)(2,1)S(1)}, bf16[48,48]{1,0:T(8,128)(2,1)}, u32[]{:S(2)}) copy-start(bf16[48,48]{1,0:T(8,128)(2,1)} %in_ref.3) | copy-start | bytes 13828
  61.4 14.9 %copy-start.3 = (bf16[48,48]{1,0:T(8,128)(2,1)S(1)}, bf16[48,48]{1,0:T(8,128)(2,1)}, u32[]{:S(2)}) copy-start(bf16[48,48]{1,0:T(8,128)(2,1)} %outf_ref.3) | copy-start | bytes 13828
  61.4 6.9 %collective-permute-start.17 = (f32[24,512]{1,0:T(8,128)S(1)}, f32[24,512]{1,0:T(8,128)S(1)}, u32[]{:S(2)}, u32[]{:S(2)}) collective-permute-start(f32[24,512]{1,0:T(8,128)S(1)} %add_add_fusion.1), channel_id=1, source_target_pairs={{0,128},{4,132},{8,136},{12,140},{16,144},{20,148},{24,152},{28,15... | collective-permute-start | bytes 147464 | tf_op jit(solution)/shard_map/ppermute | solution.py:260
  66.5 5.4 %collective-permute-start.16 = (f32[24,512]{1,0:T(8,128)S(1)}, f32[24,512]{1,0:T(8,128)S(1)}, u32[]{:S(2)}, u32[]{:S(2)}) collective-permute-start(f32[24,512]{1,0:T(8,128)S(1)} %add_add_fusion.1), channel_id=1, source_target_pairs={{0,192},{4,196},{8,200},{12,204},{16,208},{20,212},{24,216},{28,22... | collective-permute-start | bytes 147464 | tf_op jit(solution)/shard_map/ppermute | solution.py:260
  66.6 5.4 %collective-permute-start.15 = (f32[24,512]{1,0:T(8,128)S(1)}, f32[24,512]{1,0:T(8,128)S(1)}, u32[]{:S(2)}, u32[]{:S(2)}) collective-permute-start(f32[24,512]{1,0:T(8,128)S(1)} %add_add_fusion.1), channel_id=1, source_target_pairs={{0,64},{4,68},{8,72},{12,76},{16,80},{20,84},{24,88},{28,92},{32,9... | collective-permute-start | bytes 147464 | tf_op jit(solution)/shard_map/ppermute | solution.py:260
  71.9 5.3 %collective-permute-start.18 = (f32[24,512]{1,0:T(8,128)S(1)}, f32[24,512]{1,0:T(8,128)S(1)}, u32[]{:S(2)}, u32[]{:S(2)}) collective-permute-start(f32[24,512]{1,0:T(8,128)S(1)} %add_add_fusion.refs_0_), channel_id=1, source_target_pairs={{0,4},{4,0},{8,12},{12,8},{16,20},{20,16},{24,28},{28,24},{32,36},... | collective-permute-start | bytes 147464 | tf_op jit(solution)/shard_map/ppermute | solution.py:260

commit v10 on v9

--- a/solution.py
+++ b/solution.py
@@ -267,10 +267,18 @@
     )
 
 
+def from_z(block, even, odd):
+    count = lax.axis_size("leaf")
+    return lax.ppermute(
+        block, "leaf", [((i + 8 * (odd if i // 8 % 2 else even)) % count, i) for i in range(count)]
+    )
+
+
 def leaf_sum(mine, give):
     mine = mine + crossed(give, 1)
-    for masks in ((8,), (2, 6, 4), (16, 48, 32)):
+    for masks in ((8,), (2, 6, 4)):
         mine = mine + sum(crossed(mine, mask) for mask in masks)
+    mine = mine + sum(from_z(mine, even, odd) for even, odd in ((-1, 1), (2, -2), (-3, 3)))
     return mine, crossed(mine, 1)
 
 

time: 78.2 us -> 77.8 us (level)
  waiting for transfers between devices: 24.6 us -> 22.8 us
  starting transfers between devices: 33.8 us -> 35.1 us
    ppermute x0 -> x3, starting transfers between devices: none -> 7.78 us  [from_z(): lax.ppermute(block, 'leaf', [((i + 8 * (odd if i // 8 % 2 else even)) % c...]
    ppermute x11 -> x8, starting transfers between devices: 18.3 us -> 11.8 us  [crossed(): lax.ppermute(block, 'leaf', [(i, i ^ mask) for i in range(lax.axis_size('...]
    ppermute x11 -> x8, waiting for transfers between devices: 12.3 us -> 8.06 us  [crossed(): lax.ppermute(block, 'leaf', [(i, i ^ mask) for i in range(lax.axis_size('...]
    ppermute x0 -> x3, waiting for transfers between devices: none -> 2.56 us  [from_z(): lax.ppermute(block, 'leaf', [((i + 8 * (odd if i // 8 % 2 else even)) % c...]
where the time goes in v10:
time: 77.8 us; the launch traced here: 77.7 us
  starting transfers between devices  35.1 us (45%)
  waiting for transfers between devices  22.8 us (29%)
  Pallas kernels  18.1 us (23%)
  between operations  0.83 us (1%)
    ppermute x8, starting transfers between devices, crossed(): lax.ppermute(block, 'leaf', [(i, i ^ mask) for i in range(lax.axis_size('...  11.8 us
    ppermute x6, waiting for transfers between devices, shifted(): lax.ppermute(block, axis, [(i, (i + distance) % count) for i in range(cou...  10.1 us
    ppermute x8, waiting for transfers between devices, crossed(): lax.ppermute(block, 'leaf', [(i, i ^ mask) for i in range(lax.axis_size('...  8.06 us
    ppermute x6, starting transfers between devices, shifted(): lax.ppermute(block, axis, [(i, (i + distance) % count) for i in range(cou...  8.06 us
    ppermute x3, starting transfers between devices, from_z(): lax.ppermute(block, 'leaf', [((i + 8 * (odd if i // 8 % 2 else even)) % c...  7.78 us
    ppermute x2, starting transfers between devices, outward(): lax.ppermute(block, 'leaf', [(i, (i + (2 * chips if i % 2 == 0 else -2 *...  7.42 us
    pallas_call x1, Pallas kernels, body(): pl.pallas_call(scatter_kernel, out_shape=[struct((rank, rows), BF), struc...  5.98 us
    pallas_call x1, Pallas kernels, body(): pl.pallas_call(far_gather_kernel, out_shape=[struct((rank, rows), F32), s...  4.08 us
  transfers between devices with their start and end apart: 19, of which 13 were waited for; matrix products, arithmetic and copies ran while one was open for 0% of the time, Pallas kernels for 6%

profile of v10, /device:TPU:1, one launch (start us, length us, event | category | flops | bytes accessed | tf_op | source)
XLA Modules:
  0.0 77.7 jit_solution(13433639532659499613)
XLA Ops:
  0.6 2.2 %project.1 = (f32[64,1024]{1,0:T(8,128)}, bf16[64,1024]{1,0:T(8,128)(2,1)}, bf16[64,1024]{1,0:T(8,128)(2,1)}, bf16[64,1024]{1,0:T(8,128)(2,1)}) custom-call(bf16[48,1024]{1,0:T(8,128)(2,1)} %feat_ref.3, bf16[48,48]{1,0:T(8,128)(2,1)} %in_ref.3, bf16[48,1024]{1,0:T(8,128)(2,1)} %cot_ref.3, bf16[48,48]{1,0:T(8,128)(2,1)} %outf_ref.3, s32[1,1024]{1,0:T(1,128)} %bitcast.9), custom_call_target="tpu_custom_call" | custom-call | tf_op jit(solution)/shard_map/project/pallas_call | solution.py:300
  2.8 2.1 %collective-permute-start = (bf16[64,1024]{1,0:T(8,128)(2,1)}, bf16[64,1024]{1,0:T(8,128)(2,1)S(1)}, u32[]{:S(2)}, u32[]{:S(2)}) collective-permute-start(bf16[64,1024]{1,0:T(8,128)(2,1)} %get-tuple-element.28), channel_id=1, source_target_pairs={{0,1},{1,2},{2,3},{3,0},{4,5},{5,6},{6,7},{7,4},{8,9},{9,10},{10,1... | collective-permute-start | bytes 393224 | tf_op jit(solution)/shard_map/ppermute | solution.py:256
  5.0 1.5 %collective-permute-start.1 = (bf16[64,1024]{1,0:T(8,128)(2,1)}, bf16[64,1024]{1,0:T(8,128)(2,1)S(1)}, u32[]{:S(2)}, u32[]{:S(2)}) collective-permute-start(bf16[64,1024]{1,0:T(8,128)(2,1)} %get-tuple-element.29), channel_id=1, source_target_pairs={{0,3},{1,0},{2,1},{3,2},{4,7},{5,4},{6,5},{7,6},{8,11},{9,8},{10,9... | collective-permute-start | bytes 393224 | tf_op jit(solution)/shard_map/ppermute | solution.py:256
  6.5 1.6 %collective-permute-start.2 = (bf16[64,1024]{1,0:T(8,128)(2,1)}, bf16[64,1024]{1,0:T(8,128)(2,1)S(1)}, u32[]{:S(2)}, u32[]{:S(2)}) collective-permute-start(bf16[64,1024]{1,0:T(8,128)(2,1)} %get-tuple-element.30), channel_id=1, source_target_pairs={{0,2},{1,3},{2,0},{3,1},{4,6},{5,7},{6,4},{7,5},{8,10},{9,11},{10,... | collective-permute-start | bytes 393224 | tf_op jit(solution)/shard_map/ppermute | solution.py:256
  8.1 0.8 %collective-permute-done.p1 = bf16[64,1024]{1,0:T(8,128)(2,1)S(1)} collective-permute-done((bf16[64,1024]{1,0:T(8,128)(2,1)}, bf16[64,1024]{1,0:T(8,128)(2,1)S(1)}, u32[]{:S(2)}, u32[]{:S(2)}) %collective-permute-start) | collective-permute-done | bytes 131104 | tf_op jit(solution)/shard_map/ppermute | solution.py:256
  9.0 4.0 %collective-permute-done.2.p3 = bf16[64,1024]{1,0:T(8,128)(2,1)S(1)} collective-permute-done((bf16[64,1024]{1,0:T(8,128)(2,1)}, bf16[64,1024]{1,0:T(8,128)(2,1)S(1)}, u32[]{:S(2)}, u32[]{:S(2)}) %collective-permute-start.2) | collective-permute-done | bytes 131104 | tf_op jit(solution)/shard_map/ppermute | solution.py:256
  13.0 6.0 %scatter.1 = (bf16[48,1024]{1,0:T(8,128)(2,1)S(1)}, f32[16,1024]{1,0:T(8,128)S(1)}, f32[48,1024]{1,0:T(8,128)S(1)}, bf16[96,1024]{1,0:T(8,128)(2,1)S(1)}) custom-call(s32[8,8]{1,0:T(8,128)S(1)} %bitcast.6, f32[64,1024]{1,0:T(8,128)S(1)} %copy-done.4, bf16[64,1024]{1,0:T(8,128)(2,1)S(1)} %collective-permute-done.p1, ...), custom_call_target="tpu_custom_call" | custom-call | flops 5000000000 | bytes 1048576 | tf_op jit(solution)/shard_map/scatter/pallas_call | solution.py:310
  19.0 3.1 %collective-permute-start.3 = (bf16[96,1024]{1,0:T(8,128)(2,1)S(1)}, bf16[96,1024]{1,0:T(8,128)(2,1)S(1)}, u32[]{:S(2)}, u32[]{:S(2)}) collective-permute-start(bf16[96,1024]{1,0:T(8,128)(2,1)S(1)} %get-tuple-element.31), channel_id=1, source_target_pairs={{0,4},{4,0},{8,12},{12,8},{16,20},{20,16},{24,28},{28,24},{32,36},... | collective-permute-start | bytes 589832 | tf_op jit(solution)/shard_map/ppermute | solution.py:260
  22.1 1.1 %collective-permute-done.3 = bf16[96,1024]{1,0:T(8,128)(2,1)S(1)} collective-permute-done((bf16[96,1024]{1,0:T(8,128)(2,1)S(1)}, bf16[96,1024]{1,0:T(8,128)(2,1)S(1)}, u32[]{:S(2)}, u32[]{:S(2)}) %collective-permute-start.3) | collective-permute-done | bytes 196640 | tf_op jit(solution)/shard_map/ppermute | solution.py:260
  23.2 6.9 %collective-permute-start.5 = (bf16[64,1024]{1,0:T(8,128)(2,1)S(1)}, bf16[64,1024]{1,0:T(8,128)(2,1)S(1)}, u32[]{:S(2)}, u32[]{:S(2)}) collective-permute-start(bf16[64,1024]{1,0:T(8,128)(2,1)S(1)} %get-tuple-element.54), channel_id=1, source_target_pairs={{0,8},{4,252},{8,16},{12,4},{16,24},{20,12},{24,32},{28,20},{32,40... | collective-permute-start | bytes 393224 | tf_op jit(solution)/shard_map/ppermute | solution.py:265
  30.6 3.2 %near_gather.1.base_ref = bf16[432,1024]{1,0:T(8,128)(2,1)S(1)} custom-call(s32[8,8]{1,0:T(8,128)S(1)} %bitcast.7, bf16[16,1024]{1,0:T(8,128)(2,1)S(1)} %slice.51.own_ref, bf16[16,1024]{1,0:T(8,128)(2,1)S(1)} %get-tuple-element.52.pair_ref, s32[27,1024]{1,0:T(8,128)S(1)} %copy-done.5), custom_call_target="tpu_custom_call" | custom-call | flops 5000000000 | bytes 1048576 | tf_op jit(solution)/shard_map/near_gather/pallas_call | solution.py:336
  33.8 2.1 %collective-permute-done.4 = bf16[64,1024]{1,0:T(8,128)(2,1)S(1)} collective-permute-done((bf16[64,1024]{1,0:T(8,128)(2,1)S(1)}, bf16[64,1024]{1,0:T(8,128)(2,1)S(1)}, u32[]{:S(2)}, u32[]{:S(2)}) %collective-permute-start.4) | collective-permute-done | bytes 131104 | tf_op jit(solution)/shard_map/ppermute | solution.py:265
  36.6 0.8 %collective-permute-done.6.cross_ref = bf16[80,1024]{1,0:T(8,128)(2,1)S(1)} collective-permute-done((bf16[80,1024]{1,0:T(8,128)(2,1)S(1)}, bf16[80,1024]{1,0:T(8,128)(2,1)S(1)}, u32[]{:S(2)}, u32[]{:S(2)}) %collective-permute-start.6) | collective-permute-done | bytes 163872 | tf_op jit(solution)/shard_map/ppermute | solution.py:260
  37.4 4.1 %far_gather.1 = (f32[48,1024]{1,0:T(8,128)S(1)}, bf16[512,1024]{1,0:T(8,128)(2,1)S(1)}) custom-call(s32[8,8]{1,0:T(8,128)S(1)} %bitcast.8, bf16[432,1024]{1,0:T(8,128)(2,1)S(1)} %near_gather.1.base_ref, bf16[32,1024]{1,0:T(8,128)(2,1)S(1)} %slice.60.near_ref, bf16[32,1024]{1,0:T(8,128)(2,1)S(1)} %slice.61.far_ref, ...), custom_call_target="tpu_custom_call" | custom-call | flops 5000000000 | bytes 1048576 | tf_op jit(solution)/shard_map/far_gather/pallas_call | solution.py:353
  41.6 0.9 %collective-permute-start.9 = (bf16[64,1024]{1,0:T(8,128)(2,1)S(1)}, bf16[64,1024]{1,0:T(8,128)(2,1)S(1)}, u32[]{:S(2)}, u32[]{:S(2)}) collective-permute-start(bf16[64,1024]{1,0:T(8,128)(2,1)S(1)} %pad_maximum_fusion.4.e0), channel_id=1, source_target_pairs={{0,1},{1,2},{2,3},{3,0},{4,5},{5,6},{6,7},{7,4},{8,9},{9,10},{10,1... | collective-permute-start | bytes 393224 | tf_op jit(solution)/shard_map/ppermute | solution.py:256
  42.5 1.8 %collective-permute-start.8 = (bf16[64,1024]{1,0:T(8,128)(2,1)S(1)}, bf16[64,1024]{1,0:T(8,128)(2,1)S(1)}, u32[]{:S(2)}, u32[]{:S(2)}) collective-permute-start(bf16[64,1024]{1,0:T(8,128)(2,1)S(1)} %pad_maximum_fusion.4.e0), channel_id=1, source_target_pairs={{0,3},{1,0},{2,1},{3,2},{4,7},{5,4},{6,5},{7,6},{8,11},{9,8},{10,9... | collective-permute-start | bytes 393224 | tf_op jit(solution)/shard_map/ppermute | solution.py:256
  44.9 3.0 %collective-permute-done.9.e1 = bf16[64,1024]{1,0:T(8,128)(2,1)S(1)} collective-permute-done((bf16[64,1024]{1,0:T(8,128)(2,1)S(1)}, bf16[64,1024]{1,0:T(8,128)(2,1)S(1)}, u32[]{:S(2)}, u32[]{:S(2)}) %collective-permute-start.9) | collective-permute-done | bytes 131104 | tf_op jit(solution)/shard_map/ppermute | solution.py:256
  47.8 2.3 %collective-permute-done.7.e2 = bf16[64,1024]{1,0:T(8,128)(2,1)S(1)} collective-permute-done((bf16[64,1024]{1,0:T(8,128)(2,1)S(1)}, bf16[64,1024]{1,0:T(8,128)(2,1)S(1)}, u32[]{:S(2)}, u32[]{:S(2)}) %collective-permute-start.7) | collective-permute-done | bytes 131104 | tf_op jit(solution)/shard_map/ppermute | solution.py:256
  50.2 0.6 sums.1
  50.7 1.7 %collective-permute-start.10 = (f32[24,512]{1,0:T(8,128)S(1)}, f32[24,512]{1,0:T(8,128)S(1)}, u32[]{:S(2)}, u32[]{:S(2)}) collective-permute-start(f32[24,512]{1,0:T(8,128)S(1)} %get-tuple-element.45), channel_id=1, source_target_pairs={{0,4},{4,0},{8,12},{12,8},{16,20},{20,16},{24,28},{28,24},{32,36},... | collective-permute-start | bytes 147464 | tf_op jit(solution)/shard_map/ppermute | solution.py:260
  52.4 0.9 %collective-permute-done.10 = f32[24,512]{1,0:T(8,128)S(1)} collective-permute-done((f32[24,512]{1,0:T(8,128)S(1)}, f32[24,512]{1,0:T(8,128)S(1)}, u32[]{:S(2)}, u32[]{:S(2)}) %collective-permute-start.10) | collective-permute-done | bytes 49184 | tf_op jit(solution)/shard_map/ppermute | solution.py:260
  53.4 2.9 %collective-permute-done.11 = f32[24,512]{1,0:T(8,128)S(1)} collective-permute-done((f32[24,512]{1,0:T(8,128)S(1)}, f32[24,512]{1,0:T(8,128)S(1)}, u32[]{:S(2)}, u32[]{:S(2)}) %collective-permute-start.11) | collective-permute-done | bytes 49184 | tf_op jit(solution)/shard_map/ppermute | solution.py:260
  56.8 1.4 %collective-permute-start.13 = (f32[24,512]{1,0:T(8,128)S(1)}, f32[24,512]{1,0:T(8,128)S(1)}, u32[]{:S(2)}, u32[]{:S(2)}) collective-permute-start(f32[24,512]{1,0:T(8,128)S(1)} %add.59), channel_id=1, source_target_pairs={{0,24},{4,28},{8,16},{12,20},{16,8},{20,12},{24,0},{28,4},{32,56},... | collective-permute-start | bytes 147464 | tf_op jit(solution)/shard_map/ppermute | solution.py:260
  58.3 0.8 %collective-permute-start.12 = (f32[24,512]{1,0:T(8,128)S(1)}, f32[24,512]{1,0:T(8,128)S(1)}, u32[]{:S(2)}, u32[]{:S(2)}) collective-permute-start(f32[24,512]{1,0:T(8,128)S(1)} %add.59), channel_id=1, source_target_pairs={{0,8},{4,12},{8,0},{12,4},{16,24},{20,28},{24,16},{28,20},{32,40},... | collective-permute-start | bytes 147464 | tf_op jit(solution)/shard_map/ppermute | solution.py:260
  59.1 1.8 %collective-permute-done.14 = f32[24,512]{1,0:T(8,128)S(1)} collective-permute-done((f32[24,512]{1,0:T(8,128)S(1)}, f32[24,512]{1,0:T(8,128)S(1)}, u32[]{:S(2)}, u32[]{:S(2)}) %collective-permute-start.14) | collective-permute-done | bytes 49184 | tf_op jit(solution)/shard_map/ppermute | solution.py:260
  61.4 4.5 %collective-permute-start.17 = (f32[24,512]{1,0:T(8,128)S(1)}, f32[24,512]{1,0:T(8,128)S(1)}, u32[]{:S(2)}, u32[]{:S(2)}) collective-permute-start(f32[24,512]{1,0:T(8,128)S(1)} %add_add_fusion.1), channel_id=1, source_target_pairs={{160,0},{164,4},{168,8},{172,12},{176,16},{180,20},{184,24},{188,2... | collective-permute-start | bytes 147464 | tf_op jit(solution)/shard_map/ppermute | solution.py:272
  66.3 3.0 %collective-permute-start.15 = (f32[24,512]{1,0:T(8,128)S(1)}, f32[24,512]{1,0:T(8,128)S(1)}, u32[]{:S(2)}, u32[]{:S(2)}) collective-permute-start(f32[24,512]{1,0:T(8,128)S(1)} %add_add_fusion.1), channel_id=1, source_target_pairs={{224,0},{228,4},{232,8},{236,12},{240,16},{244,20},{248,24},{252,2... | collective-permute-start | bytes 147464 | tf_op jit(solution)/shard_map/ppermute | solution.py:272
  69.2 0.6 collective-permute-done.16
  69.8 2.0 %collective-permute-done.15 = f32[24,512]{1,0:T(8,128)S(1)} collective-permute-done((f32[24,512]{1,0:T(8,128)S(1)}, f32[24,512]{1,0:T(8,128)S(1)}, u32[]{:S(2)}, u32[]{:S(2)}) %collective-permute-start.15) | collective-permute-done | bytes 49184 | tf_op jit(solution)/shard_map/ppermute | solution.py:272
  71.8 4.2 %collective-permute-start.18 = (f32[24,512]{1,0:T(8,128)S(1)}, f32[24,512]{1,0:T(8,128)S(1)}, u32[]{:S(2)}, u32[]{:S(2)}) collective-permute-start(f32[24,512]{1,0:T(8,128)S(1)} %add_add_fusion.refs_0_), channel_id=1, source_target_pairs={{0,4},{4,0},{8,12},{12,8},{16,20},{20,16},{24,28},{28,24},{32,36},... | collective-permute-start | bytes 147464 | tf_op jit(solution)/shard_map/ppermute | solution.py:260
  76.0 0.8 %outputs.1 = (bf16[48,1024]{1,0:T(8,128)(2,1)}, bf16[48,1024]{1,0:T(8,128)(2,1)}) custom-call(bf16[48,1024]{1,0:T(8,128)(2,1)S(1)} %get-tuple-element.40.rows_ref, bf16[48,1024]{1,0:T(8,128)(2,1)S(1)} %get-tuple-element.41.mixed_ref, bf16[48,48]{1,0:T(8,128)(2,1)S(1)} %copy-done.2, bf16[48,48]{1,0:T(8,128)(2,1)S(1)} %copy-done.3), custom_call_target="tpu_custom_call" | custom-call | flops 500000000 | bytes 1048576 | tf_op jit(solution)/shard_map/outputs/pallas_call | solution.py:385
  76.9 0.8 %unpack.1 = (f32[48,48]{1,0:T(8,128)}, f32[12,27,48]{2,1,0:T(8,128)}, f32[48,48]{1,0:T(8,128)}) custom-call(f32[24,512]{1,0:T(8,128)S(1)} %add_add_fusion.refs_0_, f32[24,512]{1,0:T(8,128)S(1)} %collective-permute-done.18.refs_1_), custom_call_target="tpu_custom_call" | custom-call | tf_op jit(solution)/shard_map/unpack/pallas_call | solution.py:397
  (50 shorter events, 3.4 us)
Async XLA Ops:
  0.6 7.4 %copy-start.7 = (bf16[27,12,48]{2,0,1:T(8,128)(2,1)S(1)}, bf16[27,12,48]{2,0,1:T(8,128)(2,1)}, u32[]{:S(2)}) copy-start(bf16[27,12,48]{2,0,1:T(8,128)(2,1)} %param.10) | copy-start | bytes 93316
  2.8 10.2 %copy-start.4 = (f32[64,1024]{1,0:T(8,128)S(1)}, f32[64,1024]{1,0:T(8,128)}, u32[]{:S(2)}) copy-start(f32[64,1024]{1,0:T(8,128)} %get-tuple-element.27.p0) | copy-start | bytes 786436
  2.8 6.1 %collective-permute-start = (bf16[64,1024]{1,0:T(8,128)(2,1)}, bf16[64,1024]{1,0:T(8,128)(2,1)S(1)}, u32[]{:S(2)}, u32[]{:S(2)}) collective-permute-start(bf16[64,1024]{1,0:T(8,128)(2,1)} %get-tuple-element.28), channel_id=1, source_target_pairs={{0,1},{1,2},{2,3},{3,0},{4,5},{5,6},{6,7},{7,4},{8,9},{9,10},{10,1... | collective-permute-start | bytes 393224 | tf_op jit(solution)/shard_map/ppermute | solution.py:256
  5.0 4.0 %collective-permute-start.1 = (bf16[64,1024]{1,0:T(8,128)(2,1)}, bf16[64,1024]{1,0:T(8,128)(2,1)S(1)}, u32[]{:S(2)}, u32[]{:S(2)}) collective-permute-start(bf16[64,1024]{1,0:T(8,128)(2,1)} %get-tuple-element.29), channel_id=1, source_target_pairs={{0,3},{1,0},{2,1},{3,2},{4,7},{5,4},{6,5},{7,6},{8,11},{9,8},{10,9... | collective-permute-start | bytes 393224 | tf_op jit(solution)/shard_map/ppermute | solution.py:256
  6.5 6.5 %collective-permute-start.2 = (bf16[64,1024]{1,0:T(8,128)(2,1)}, bf16[64,1024]{1,0:T(8,128)(2,1)S(1)}, u32[]{:S(2)}, u32[]{:S(2)}) collective-permute-start(bf16[64,1024]{1,0:T(8,128)(2,1)} %get-tuple-element.30), channel_id=1, source_target_pairs={{0,2},{1,3},{2,0},{3,1},{4,6},{5,7},{6,4},{7,5},{8,10},{9,11},{10,... | collective-permute-start | bytes 393224 | tf_op jit(solution)/shard_map/ppermute | solution.py:256
  8.1 4.9 %copy-start.5 = (s32[27,1024]{1,0:T(8,128)S(1)}, s32[27,1024]{1,0:T(8,128)}, u32[]{:S(2)}) copy-start(s32[27,1024]{1,0:T(8,128)} %nbr_ref.5) | copy-start | bytes 331780
  8.1 4.9 %copy-start.6 = (s32[1,8,8]{2,1,0:T(8,128)S(1)}, s32[1,8,8]{2,1,0:T(8,128)}, u32[]{:S(2)}) copy-start(s32[1,8,8]{2,1,0:T(8,128)} %param.13) | copy-start | bytes 772
  19.0 4.1 %collective-permute-start.3 = (bf16[96,1024]{1,0:T(8,128)(2,1)S(1)}, bf16[96,1024]{1,0:T(8,128)(2,1)S(1)}, u32[]{:S(2)}, u32[]{:S(2)}) collective-permute-start(bf16[96,1024]{1,0:T(8,128)(2,1)S(1)} %get-tuple-element.31), channel_id=1, source_target_pairs={{0,4},{4,0},{8,12},{12,8},{16,20},{20,16},{24,28},{28,24},{32,36},... | collective-permute-start | bytes 589832 | tf_op jit(solution)/shard_map/ppermute | solution.py:260
  23.2 10.6 %collective-permute-start.5 = (bf16[64,1024]{1,0:T(8,128)(2,1)S(1)}, bf16[64,1024]{1,0:T(8,128)(2,1)S(1)}, u32[]{:S(2)}, u32[]{:S(2)}) collective-permute-start(bf16[64,1024]{1,0:T(8,128)(2,1)S(1)} %get-tuple-element.54), channel_id=1, source_target_pairs={{0,8},{4,252},{8,16},{12,4},{16,24},{20,12},{24,32},{28,20},{32,40... | collective-permute-start | bytes 393224 | tf_op jit(solution)/shard_map/ppermute | solution.py:265
  30.1 5.8 %collective-permute-start.4 = (bf16[64,1024]{1,0:T(8,128)(2,1)S(1)}, bf16[64,1024]{1,0:T(8,128)(2,1)S(1)}, u32[]{:S(2)}, u32[]{:S(2)}) collective-permute-start(bf16[64,1024]{1,0:T(8,128)(2,1)S(1)} %get-tuple-element.55), channel_id=1, source_target_pairs={{0,16},{4,244},{8,24},{12,252},{16,32},{20,4},{24,40},{28,12},{32,... | collective-permute-start | bytes 393224 | tf_op jit(solution)/shard_map/ppermute | solution.py:265
  35.9 0.7 copy-start.8
  35.9 1.5 %collective-permute-start.6 = (bf16[80,1024]{1,0:T(8,128)(2,1)S(1)}, bf16[80,1024]{1,0:T(8,128)(2,1)S(1)}, u32[]{:S(2)}, u32[]{:S(2)}) collective-permute-start(bf16[80,1024]{1,0:T(8,128)(2,1)S(1)} %pad_maximum_fusion), channel_id=1, source_target_pairs={{0,4},{4,0},{8,12},{12,8},{16,20},{20,16},{24,28},{28,24},{32,36},... | collective-permute-start | bytes 491528 | tf_op jit(solution)/shard_map/ppermute | solution.py:260
  41.6 6.2 %collective-permute-start.9 = (bf16[64,1024]{1,0:T(8,128)(2,1)S(1)}, bf16[64,1024]{1,0:T(8,128)(2,1)S(1)}, u32[]{:S(2)}, u32[]{:S(2)}) collective-permute-start(bf16[64,1024]{1,0:T(8,128)(2,1)S(1)} %pad_maximum_fusion.4.e0), channel_id=1, source_target_pairs={{0,1},{1,2},{2,3},{3,0},{4,5},{5,6},{6,7},{7,4},{8,9},{9,10},{10,1... | collective-permute-start | bytes 393224 | tf_op jit(solution)/shard_map/ppermute | solution.py:256
  42.5 5.3 %collective-permute-start.8 = (bf16[64,1024]{1,0:T(8,128)(2,1)S(1)}, bf16[64,1024]{1,0:T(8,128)(2,1)S(1)}, u32[]{:S(2)}, u32[]{:S(2)}) collective-permute-start(bf16[64,1024]{1,0:T(8,128)(2,1)S(1)} %pad_maximum_fusion.4.e0), channel_id=1, source_target_pairs={{0,3},{1,0},{2,1},{3,2},{4,7},{5,4},{6,5},{7,6},{8,11},{9,8},{10,9... | collective-permute-start | bytes 393224 | tf_op jit(solution)/shard_map/ppermute | solution.py:256
  44.3 5.8 %collective-permute-start.7 = (bf16[64,1024]{1,0:T(8,128)(2,1)S(1)}, bf16[64,1024]{1,0:T(8,128)(2,1)S(1)}, u32[]{:S(2)}, u32[]{:S(2)}) collective-permute-start(bf16[64,1024]{1,0:T(8,128)(2,1)S(1)} %pad_maximum_fusion.4.e0), channel_id=1, source_target_pairs={{0,2},{1,3},{2,0},{3,1},{4,6},{5,7},{6,4},{7,5},{8,10},{9,11},{10,... | collective-permute-start | bytes 393224 | tf_op jit(solution)/shard_map/ppermute | solution.py:256
  44.4 5.7 %copy-start = (bf16[48,1024]{1,0:T(8,128)(2,1)S(1)}, bf16[48,1024]{1,0:T(8,128)(2,1)}, u32[]{:S(2)}) copy-start(bf16[48,1024]{1,0:T(8,128)(2,1)} %feat_ref.3) | copy-start | bytes 294916
  44.4 5.7 %copy-start.1 = (bf16[48,1024]{1,0:T(8,128)(2,1)S(1)}, bf16[48,1024]{1,0:T(8,128)(2,1)}, u32[]{:S(2)}) copy-start(bf16[48,1024]{1,0:T(8,128)(2,1)} %cot_ref.3) | copy-start | bytes 294916
  50.7 2.6 %collective-permute-start.10 = (f32[24,512]{1,0:T(8,128)S(1)}, f32[24,512]{1,0:T(8,128)S(1)}, u32[]{:S(2)}, u32[]{:S(2)}) collective-permute-start(f32[24,512]{1,0:T(8,128)S(1)} %get-tuple-element.45), channel_id=1, source_target_pairs={{0,4},{4,0},{8,12},{12,8},{16,20},{20,16},{24,28},{28,24},{32,36},... | collective-permute-start | bytes 147464 | tf_op jit(solution)/shard_map/ppermute | solution.py:260
  53.3 3.0 %collective-permute-start.11 = (f32[24,512]{1,0:T(8,128)S(1)}, f32[24,512]{1,0:T(8,128)S(1)}, u32[]{:S(2)}, u32[]{:S(2)}) collective-permute-start(f32[24,512]{1,0:T(8,128)S(1)} %add.58), channel_id=1, source_target_pairs={{0,32},{4,36},{8,40},{12,44},{16,48},{20,52},{24,56},{28,60},{32,0... | collective-permute-start | bytes 147464 | tf_op jit(solution)/shard_map/ppermute | solution.py:260
  56.3 4.6 %collective-permute-start.14 = (f32[24,512]{1,0:T(8,128)S(1)}, f32[24,512]{1,0:T(8,128)S(1)}, u32[]{:S(2)}, u32[]{:S(2)}) collective-permute-start(f32[24,512]{1,0:T(8,128)S(1)} %add.59), channel_id=1, source_target_pairs={{0,16},{4,20},{8,24},{12,28},{16,0},{20,4},{24,8},{28,12},{32,48},... | collective-permute-start | bytes 147464 | tf_op jit(solution)/shard_map/ppermute | solution.py:260
  56.8 4.6 %collective-permute-start.13 = (f32[24,512]{1,0:T(8,128)S(1)}, f32[24,512]{1,0:T(8,128)S(1)}, u32[]{:S(2)}, u32[]{:S(2)}) collective-permute-start(f32[24,512]{1,0:T(8,128)S(1)} %add.59), channel_id=1, source_target_pairs={{0,24},{4,28},{8,16},{12,20},{16,8},{20,12},{24,0},{28,4},{32,56},... | collective-permute-start | bytes 147464 | tf_op jit(solution)/shard_map/ppermute | solution.py:260
  58.3 3.1 %collective-permute-start.12 = (f32[24,512]{1,0:T(8,128)S(1)}, f32[24,512]{1,0:T(8,128)S(1)}, u32[]{:S(2)}, u32[]{:S(2)}) collective-permute-start(f32[24,512]{1,0:T(8,128)S(1)} %add.59), channel_id=1, source_target_pairs={{0,8},{4,12},{8,0},{12,4},{16,24},{20,28},{24,16},{28,20},{32,40},... | collective-permute-start | bytes 147464 | tf_op jit(solution)/shard_map/ppermute | solution.py:260
  61.4 14.6 %copy-start.2 = (bf16[48,48]{1,0:T(8,128)(2,1)S(1)}, bf16[48,48]{1,0:T(8,128)(2,1)}, u32[]{:S(2)}) copy-start(bf16[48,48]{1,0:T(8,128)(2,1)} %in_ref.3) | copy-start | bytes 13828
  61.4 14.5 %copy-start.3 = (bf16[48,48]{1,0:T(8,128)(2,1)S(1)}, bf16[48,48]{1,0:T(8,128)(2,1)}, u32[]{:S(2)}) copy-start(bf16[48,48]{1,0:T(8,128)(2,1)} %outf_ref.3) | copy-start | bytes 13828
  61.4 7.8 %collective-permute-start.17 = (f32[24,512]{1,0:T(8,128)S(1)}, f32[24,512]{1,0:T(8,128)S(1)}, u32[]{:S(2)}, u32[]{:S(2)}) collective-permute-start(f32[24,512]{1,0:T(8,128)S(1)} %add_add_fusion.1), channel_id=1, source_target_pairs={{160,0},{164,4},{168,8},{172,12},{176,16},{180,20},{184,24},{188,2... | collective-permute-start | bytes 147464 | tf_op jit(solution)/shard_map/ppermute | solution.py:272
  66.0 3.8 %collective-permute-start.16 = (f32[24,512]{1,0:T(8,128)S(1)}, f32[24,512]{1,0:T(8,128)S(1)}, u32[]{:S(2)}, u32[]{:S(2)}) collective-permute-start(f32[24,512]{1,0:T(8,128)S(1)} %add_add_fusion.1), channel_id=1, source_target_pairs={{64,0},{68,4},{72,8},{76,12},{80,16},{84,20},{88,24},{92,28},{224,... | collective-permute-start | bytes 147464 | tf_op jit(solution)/shard_map/ppermute | solution.py:272
  66.3 5.5 %collective-permute-start.15 = (f32[24,512]{1,0:T(8,128)S(1)}, f32[24,512]{1,0:T(8,128)S(1)}, u32[]{:S(2)}, u32[]{:S(2)}) collective-permute-start(f32[24,512]{1,0:T(8,128)S(1)} %add_add_fusion.1), channel_id=1, source_target_pairs={{224,0},{228,4},{232,8},{236,12},{240,16},{244,20},{248,24},{252,2... | collective-permute-start | bytes 147464 | tf_op jit(solution)/shard_map/ppermute | solution.py:272
  71.8 5.1 %collective-permute-start.18 = (f32[24,512]{1,0:T(8,128)S(1)}, f32[24,512]{1,0:T(8,128)S(1)}, u32[]{:S(2)}, u32[]{:S(2)}) collective-permute-start(f32[24,512]{1,0:T(8,128)S(1)} %add_add_fusion.refs_0_), channel_id=1, source_target_pairs={{0,4},{4,0},{8,12},{12,8},{16,20},{20,16},{24,28},{28,24},{32,36},... | collective-permute-start | bytes 147464 | tf_op jit(solution)/shard_map/ppermute | solution.py:260

commit v11 on v10

--- a/solution.py
+++ b/solution.py
@@ -77,36 +77,49 @@
     gm_ref[...] = grad_mixed
     terms_ref[...] = dot(core_ref[...], grad_mixed).astype(BF)
     acc_ref[...] = jnp.zeros_like(acc_ref)
-
-    def step(k, carry):
+    offsets, rows = nbr_ref.shape
+    middle = offsets // 2
+    copies = 4
+    tall = core_ref.shape[0] // offsets
+    width = tall // copies
+    own_tiles = rows // LOW
+    near = halo_ref.shape[0]
+    per_peer = halo_ref.shape[1] * 64 // LOW
+    groups = (own_tiles + near * per_peer) // copies
+    spare = jnp.zeros((acc_ref.shape[0] - groups * tall, rows), BF)
+    nth = (lax.broadcasted_iota(jnp.int32, (tall, rows), 0) // width).astype(F32)
+
+    def step(i, carry):
+        k = i + (i >= middle)
         index = nbr_ref[pl.ds(k, 1), :]
         onehot = low_onehot(index & (LOW - 1))
-        high = jnp.broadcast_to((index >> 8).astype(F32), (SLAB, rows)).astype(BF)
-        terms = terms_ref[pl.ds(pl.multiple_of(k * SLAB, SLAB), SLAB), :]
-        spread = jnp.concatenate(
-            [jnp.where(high == jnp.full((), t, BF), terms, jnp.zeros((), BF)) for t in range(tiles)], 0
-        )
-        acc_ref[...] += dot(spread, onehot, NT)
+        high = (jnp.broadcast_to((index >> 8).astype(F32), (tall, rows)) - nth).astype(BF)
+        terms = terms_ref[pl.ds(pl.multiple_of(k * tall, tall), tall), :]
+        spread = [
+            jnp.where(high == jnp.full((), g * copies, BF), terms, jnp.zeros((), BF)) for g in range(groups)
+        ]
+        acc_ref[...] += dot(jnp.concatenate(spread + [spare], 0), onehot, NT)
         return carry
 
-    offsets = nbr_ref.shape[0]
-    middle = offsets // 2
-    lax.fori_loop(0, offsets - 1, lambda i, carry: step(i + (i >= middle), carry), 0, unroll=13)
+    lax.fori_loop(0, offsets - 1, step, 0, unroll=13)
 
     def tile(t):
-        return acc_ref[pl.ds(pl.multiple_of(t * SLAB, SLAB), SLAB), :]
-
-    own_tiles = rows // LOW
-    itself = terms_ref[middle * SLAB : (middle + 1) * SLAB, :].astype(F32)
-    own_ref[...] = jnp.concatenate([tile(t) for t in range(own_tiles)], 1) + itself
-    near = halo_ref.shape[0]
-    per_peer = (tiles - own_tiles) // near
-    blank = jnp.zeros((SLAB, rows - per_peer * LOW), F32)
-    for view in range(near):
-        slot = mirrored(core_bit(), view, near)
+        return acc_ref[t * width : (t + 1) * width, :]
+
+    pad = jnp.zeros((SLAB - width, rows), F32)
+    itself = terms_ref[middle * tall : middle * tall + SLAB, :].astype(F32)
+    own = jnp.concatenate([tile(t) for t in range(own_tiles)], 1) + itself[:width]
+    own_ref[...] = jnp.concatenate([own, pad], 0)
+    blank = jnp.zeros((width, rows - per_peer * LOW), F32)
+    blocks = []
+    for slot in range(near):
         start = own_tiles + slot * per_peer
         window = jnp.concatenate([tile(start + i) for i in range(per_peer)] + [blank], 1)
-        block = pltpu.roll(window, first_octant(halo_ref, slot), 1)
+        window = jnp.concatenate([window, pad], 0)
+        blocks.append(pltpu.roll(window, first_octant(halo_ref, slot), 1))
+    first_core = core_bit() == 0
+    for view in range(near):
+        block = jnp.where(first_core, blocks[view], blocks[near - 1 - view])
         if view < 5:
             cross_ref[(view + 1) * SLAB : (view + 2) * SLAB, :] = block.astype(BF)
         else:
@@ -278,7 +291,7 @@
     mine = mine + crossed(give, 1)
     for masks in ((8,), (2, 6, 4)):
         mine = mine + sum(crossed(mine, mask) for mask in masks)
-    mine = mine + sum(from_z(mine, even, odd) for even, odd in ((-1, 1), (2, -2), (-3, 3)))
+    mine = mine + sum(from_z(mine, even, odd) for even, odd in ((-3, 3), (2, -2), (-1, 1)))
     return mine, crossed(mine, 1)
 
 
@@ -295,6 +308,7 @@
     keep = row_mask.reshape(1, rows)
     halo = halo_blocks[0]
     core_rows = jnp.pad(core, ((0, 0), (0, SLAB - width), (0, 0))).reshape(offsets * SLAB, rank)
+    core_copies = jnp.tile(core[:, None], (1, 4, 1, 1)).reshape(offsets * 4 * width, rank)
     estimate = pl.CostEstimate(flops=5 * 10**9, bytes_accessed=2**20, transcendentals=0)
 
     own_payload, *payload = pl.pallas_call(
@@ -312,11 +326,11 @@
         out_shape=[struct((rank, rows), BF), struct((SLAB, rows), F32), triple, struct((6 * SLAB, rows), BF)],
         in_specs=[SMEM] + [VMEM] * 6,
         out_specs=[VMEM] * 4,
-        scratch_shapes=[pltpu.VMEM((offsets * SLAB, rows), BF), pltpu.VMEM((table_rows, LOW), F32)],
+        scratch_shapes=[pltpu.VMEM((offsets * 4 * width, rows), BF), pltpu.VMEM((256, LOW), F32)],
         compiler_params=ROOMY,
         cost_estimate=estimate,
         name="scatter",
-    )(halo, own_payload, arrived[1], arrived[3], arrived[2], core_rows, neighbours)
+    )(halo, own_payload, arrived[1], arrived[3], arrived[2], core_copies, neighbours)
 
     def slabs_of(block, first, last):
         return block[first * SLAB : last * SLAB]

time: 77.8 us -> 77.9 us (level)
  waiting for transfers between devices: 22.8 us -> 24.8 us
  starting transfers between devices: 35.1 us -> 33.3 us
    ppermute x3, waiting for transfers between devices: 2.56 us -> 4.94 us  [from_z(): lax.ppermute(block, 'leaf', [((i + 8 * (odd if i // 8 % 2 else even)) % c...]
    ppermute x3, starting transfers between devices: 7.78 us -> 5.81 us  [from_z(): lax.ppermute(block, 'leaf', [((i + 8 * (odd if i // 8 % 2 else even)) % c...]
where the time goes in v11:
time: 77.9 us; the launch traced here: 77.8 us
  starting transfers between devices  33.3 us (43%)
  waiting for transfers between devices  24.8 us (32%)
  Pallas kernels  17.7 us (23%)
  local copies, waits for them, and re-layouts  0.9 us (1%)
  between operations  0.84 us (1%)
    ppermute x8, starting transfers between devices, crossed(): lax.ppermute(block, 'leaf', [(i, i ^ mask) for i in range(lax.axis_size('...  11.9 us
    ppermute x6, waiting for transfers between devices, shifted(): lax.ppermute(block, axis, [(i, (i + distance) % count) for i in range(cou...  9.79 us
    ppermute x6, starting transfers between devices, shifted(): lax.ppermute(block, axis, [(i, (i + distance) % count) for i in range(cou...  8.21 us
    ppermute x8, waiting for transfers between devices, crossed(): lax.ppermute(block, 'leaf', [(i, i ^ mask) for i in range(lax.axis_size('...  8.03 us
    ppermute x2, starting transfers between devices, outward(): lax.ppermute(block, 'leaf', [(i, (i + (2 * chips if i % 2 == 0 else -2 *...  7.42 us
    ppermute x3, starting transfers between devices, from_z(): lax.ppermute(block, 'leaf', [((i + 8 * (odd if i // 8 % 2 else even)) % c...  5.81 us
    pallas_call x1, Pallas kernels, body(): pl.pallas_call(scatter_kernel, out_shape=[struct((rank, rows), BF), struc...  5.57 us
    ppermute x3, waiting for transfers between devices, from_z(): lax.ppermute(block, 'leaf', [((i + 8 * (odd if i // 8 % 2 else even)) % c...  4.94 us
  transfers between devices with their start and end apart: 19, of which 13 were waited for; matrix products, arithmetic and copies ran while one was open for 0% of the time, Pallas kernels for 6%

profile of v11, /device:TPU:1, one launch (start us, length us, event | category | flops | bytes accessed | tf_op | source)
XLA Modules:
  0.0 77.8 jit_solution(599315627632595721)
XLA Ops:
  0.6 2.2 %project.1 = (f32[64,1024]{1,0:T(8,128)}, bf16[64,1024]{1,0:T(8,128)(2,1)}, bf16[64,1024]{1,0:T(8,128)(2,1)}, bf16[64,1024]{1,0:T(8,128)(2,1)}) custom-call(bf16[48,1024]{1,0:T(8,128)(2,1)} %feat_ref.3, bf16[48,48]{1,0:T(8,128)(2,1)} %in_ref.3, bf16[48,1024]{1,0:T(8,128)(2,1)} %cot_ref.3, bf16[48,48]{1,0:T(8,128)(2,1)} %outf_ref.3, s32[1,1024]{1,0:T(1,128)} %bitcast.10), custom_call_target="tpu_custom_call" | custom-call | tf_op jit(solution)/shard_map/project/pallas_call | solution.py:314
  2.8 2.1 %collective-permute-start = (bf16[64,1024]{1,0:T(8,128)(2,1)}, bf16[64,1024]{1,0:T(8,128)(2,1)S(1)}, u32[]{:S(2)}, u32[]{:S(2)}) collective-permute-start(bf16[64,1024]{1,0:T(8,128)(2,1)} %get-tuple-element.28), channel_id=1, source_target_pairs={{0,1},{1,2},{2,3},{3,0},{4,5},{5,6},{6,7},{7,4},{8,9},{9,10},{10,1... | collective-permute-start | bytes 393224 | tf_op jit(solution)/shard_map/ppermute | solution.py:269
  5.0 1.4 %collective-permute-start.1 = (bf16[64,1024]{1,0:T(8,128)(2,1)}, bf16[64,1024]{1,0:T(8,128)(2,1)S(1)}, u32[]{:S(2)}, u32[]{:S(2)}) collective-permute-start(bf16[64,1024]{1,0:T(8,128)(2,1)} %get-tuple-element.29), channel_id=1, source_target_pairs={{0,3},{1,0},{2,1},{3,2},{4,7},{5,4},{6,5},{7,6},{8,11},{9,8},{10,9... | collective-permute-start | bytes 393224 | tf_op jit(solution)/shard_map/ppermute | solution.py:269
  6.4 1.6 %collective-permute-start.2 = (bf16[64,1024]{1,0:T(8,128)(2,1)}, bf16[64,1024]{1,0:T(8,128)(2,1)S(1)}, u32[]{:S(2)}, u32[]{:S(2)}) collective-permute-start(bf16[64,1024]{1,0:T(8,128)(2,1)} %get-tuple-element.30), channel_id=1, source_target_pairs={{0,2},{1,3},{2,0},{3,1},{4,6},{5,7},{6,4},{7,5},{8,10},{9,11},{10,... | collective-permute-start | bytes 393224 | tf_op jit(solution)/shard_map/ppermute | solution.py:269
  8.3 0.6 collective-permute-done.p1
  9.0 4.0 %collective-permute-done.2.p3 = bf16[64,1024]{1,0:T(8,128)(2,1)S(1)} collective-permute-done((bf16[64,1024]{1,0:T(8,128)(2,1)}, bf16[64,1024]{1,0:T(8,128)(2,1)S(1)}, u32[]{:S(2)}, u32[]{:S(2)}) %collective-permute-start.2) | collective-permute-done | bytes 131104 | tf_op jit(solution)/shard_map/ppermute | solution.py:269
  13.0 5.6 %scatter.1 = (bf16[48,1024]{1,0:T(8,128)(2,1)S(1)}, f32[16,1024]{1,0:T(8,128)S(1)}, f32[48,1024]{1,0:T(8,128)S(1)}, bf16[96,1024]{1,0:T(8,128)(2,1)S(1)}) custom-call(s32[8,8]{1,0:T(8,128)S(1)} %bitcast.7, f32[64,1024]{1,0:T(8,128)S(1)} %copy-done.4, bf16[64,1024]{1,0:T(8,128)(2,1)S(1)} %collective-permute-done.p1, ...), custom_call_target="tpu_custom_call" | custom-call | flops 5000000000 | bytes 1048576 | tf_op jit(solution)/shard_map/scatter/pallas_call | solution.py:324
  18.6 3.1 %collective-permute-start.3 = (bf16[96,1024]{1,0:T(8,128)(2,1)S(1)}, bf16[96,1024]{1,0:T(8,128)(2,1)S(1)}, u32[]{:S(2)}, u32[]{:S(2)}) collective-permute-start(bf16[96,1024]{1,0:T(8,128)(2,1)S(1)} %get-tuple-element.31), channel_id=1, source_target_pairs={{0,4},{4,0},{8,12},{12,8},{16,20},{20,16},{24,28},{28,24},{32,36},... | collective-permute-start | bytes 589832 | tf_op jit(solution)/shard_map/ppermute | solution.py:273
  21.7 1.1 %collective-permute-done.3 = bf16[96,1024]{1,0:T(8,128)(2,1)S(1)} collective-permute-done((bf16[96,1024]{1,0:T(8,128)(2,1)S(1)}, bf16[96,1024]{1,0:T(8,128)(2,1)S(1)}, u32[]{:S(2)}, u32[]{:S(2)}) %collective-permute-start.3) | collective-permute-done | bytes 196640 | tf_op jit(solution)/shard_map/ppermute | solution.py:273
  22.8 6.9 %collective-permute-start.5 = (bf16[64,1024]{1,0:T(8,128)(2,1)S(1)}, bf16[64,1024]{1,0:T(8,128)(2,1)S(1)}, u32[]{:S(2)}, u32[]{:S(2)}) collective-permute-start(bf16[64,1024]{1,0:T(8,128)(2,1)S(1)} %get-tuple-element.54), channel_id=1, source_target_pairs={{0,8},{4,252},{8,16},{12,4},{16,24},{20,12},{24,32},{28,20},{32,40... | collective-permute-start | bytes 393224 | tf_op jit(solution)/shard_map/ppermute | solution.py:278
  30.2 3.2 %near_gather.1.base_ref = bf16[432,1024]{1,0:T(8,128)(2,1)S(1)} custom-call(s32[8,8]{1,0:T(8,128)S(1)} %bitcast.8, bf16[16,1024]{1,0:T(8,128)(2,1)S(1)} %slice.51.own_ref, bf16[16,1024]{1,0:T(8,128)(2,1)S(1)} %get-tuple-element.52.pair_ref, s32[27,1024]{1,0:T(8,128)S(1)} %copy-done.5), custom_call_target="tpu_custom_call" | custom-call | flops 5000000000 | bytes 1048576 | tf_op jit(solution)/shard_map/near_gather/pallas_call | solution.py:350
  33.4 2.1 %collective-permute-done.4 = bf16[64,1024]{1,0:T(8,128)(2,1)S(1)} collective-permute-done((bf16[64,1024]{1,0:T(8,128)(2,1)S(1)}, bf16[64,1024]{1,0:T(8,128)(2,1)S(1)}, u32[]{:S(2)}, u32[]{:S(2)}) %collective-permute-start.4) | collective-permute-done | bytes 131104 | tf_op jit(solution)/shard_map/ppermute | solution.py:278
  36.2 0.8 %collective-permute-done.6.cross_ref = bf16[80,1024]{1,0:T(8,128)(2,1)S(1)} collective-permute-done((bf16[80,1024]{1,0:T(8,128)(2,1)S(1)}, bf16[80,1024]{1,0:T(8,128)(2,1)S(1)}, u32[]{:S(2)}, u32[]{:S(2)}) %collective-permute-start.6) | collective-permute-done | bytes 163872 | tf_op jit(solution)/shard_map/ppermute | solution.py:273
  37.0 4.1 %far_gather.1 = (f32[48,1024]{1,0:T(8,128)S(1)}, bf16[512,1024]{1,0:T(8,128)(2,1)S(1)}) custom-call(s32[8,8]{1,0:T(8,128)S(1)} %bitcast.9, bf16[432,1024]{1,0:T(8,128)(2,1)S(1)} %near_gather.1.base_ref, bf16[32,1024]{1,0:T(8,128)(2,1)S(1)} %slice.60.near_ref, bf16[32,1024]{1,0:T(8,128)(2,1)S(1)} %slice.61.far_ref, ...), custom_call_target="tpu_custom_call" | custom-call | flops 5000000000 | bytes 1048576 | tf_op jit(solution)/shard_map/far_gather/pallas_call | solution.py:367
  41.2 0.9 %collective-permute-start.9 = (bf16[64,1024]{1,0:T(8,128)(2,1)S(1)}, bf16[64,1024]{1,0:T(8,128)(2,1)S(1)}, u32[]{:S(2)}, u32[]{:S(2)}) collective-permute-start(bf16[64,1024]{1,0:T(8,128)(2,1)S(1)} %pad_maximum_fusion.4.e0), channel_id=1, source_target_pairs={{0,1},{1,2},{2,3},{3,0},{4,5},{5,6},{6,7},{7,4},{8,9},{9,10},{10,1... | collective-permute-start | bytes 393224 | tf_op jit(solution)/shard_map/ppermute | solution.py:269
  42.1 1.8 %collective-permute-start.8 = (bf16[64,1024]{1,0:T(8,128)(2,1)S(1)}, bf16[64,1024]{1,0:T(8,128)(2,1)S(1)}, u32[]{:S(2)}, u32[]{:S(2)}) collective-permute-start(bf16[64,1024]{1,0:T(8,128)(2,1)S(1)} %pad_maximum_fusion.4.e0), channel_id=1, source_target_pairs={{0,3},{1,0},{2,1},{3,2},{4,7},{5,4},{6,5},{7,6},{8,11},{9,8},{10,9... | collective-permute-start | bytes 393224 | tf_op jit(solution)/shard_map/ppermute | solution.py:269
  44.6 2.8 %collective-permute-done.9.e1 = bf16[64,1024]{1,0:T(8,128)(2,1)S(1)} collective-permute-done((bf16[64,1024]{1,0:T(8,128)(2,1)S(1)}, bf16[64,1024]{1,0:T(8,128)(2,1)S(1)}, u32[]{:S(2)}, u32[]{:S(2)}) %collective-permute-start.9) | collective-permute-done | bytes 131104 | tf_op jit(solution)/shard_map/ppermute | solution.py:269
  47.4 2.3 %collective-permute-done.7.e2 = bf16[64,1024]{1,0:T(8,128)(2,1)S(1)} collective-permute-done((bf16[64,1024]{1,0:T(8,128)(2,1)S(1)}, bf16[64,1024]{1,0:T(8,128)(2,1)S(1)}, u32[]{:S(2)}, u32[]{:S(2)}) %collective-permute-start.7) | collective-permute-done | bytes 131104 | tf_op jit(solution)/shard_map/ppermute | solution.py:269
  50.3 1.7 %collective-permute-start.10 = (f32[24,512]{1,0:T(8,128)S(1)}, f32[24,512]{1,0:T(8,128)S(1)}, u32[]{:S(2)}, u32[]{:S(2)}) collective-permute-start(f32[24,512]{1,0:T(8,128)S(1)} %get-tuple-element.45), channel_id=1, source_target_pairs={{0,4},{4,0},{8,12},{12,8},{16,20},{20,16},{24,28},{28,24},{32,36},... | collective-permute-start | bytes 147464 | tf_op jit(solution)/shard_map/ppermute | solution.py:273
  52.0 0.9 %collective-permute-done.10 = f32[24,512]{1,0:T(8,128)S(1)} collective-permute-done((f32[24,512]{1,0:T(8,128)S(1)}, f32[24,512]{1,0:T(8,128)S(1)}, u32[]{:S(2)}, u32[]{:S(2)}) %collective-permute-start.10) | collective-permute-done | bytes 49184 | tf_op jit(solution)/shard_map/ppermute | solution.py:273
  53.0 2.9 %collective-permute-done.11 = f32[24,512]{1,0:T(8,128)S(1)} collective-permute-done((f32[24,512]{1,0:T(8,128)S(1)}, f32[24,512]{1,0:T(8,128)S(1)}, u32[]{:S(2)}, u32[]{:S(2)}) %collective-permute-start.11) | collective-permute-done | bytes 49184 | tf_op jit(solution)/shard_map/ppermute | solution.py:273
  56.4 1.4 %collective-permute-start.13 = (f32[24,512]{1,0:T(8,128)S(1)}, f32[24,512]{1,0:T(8,128)S(1)}, u32[]{:S(2)}, u32[]{:S(2)}) collective-permute-start(f32[24,512]{1,0:T(8,128)S(1)} %add.59), channel_id=1, source_target_pairs={{0,24},{4,28},{8,16},{12,20},{16,8},{20,12},{24,0},{28,4},{32,56},... | collective-permute-start | bytes 147464 | tf_op jit(solution)/shard_map/ppermute | solution.py:273
  57.9 0.8 %collective-permute-start.12 = (f32[24,512]{1,0:T(8,128)S(1)}, f32[24,512]{1,0:T(8,128)S(1)}, u32[]{:S(2)}, u32[]{:S(2)}) collective-permute-start(f32[24,512]{1,0:T(8,128)S(1)} %add.59), channel_id=1, source_target_pairs={{0,8},{4,12},{8,0},{12,4},{16,24},{20,28},{24,16},{28,20},{32,40},... | collective-permute-start | bytes 147464 | tf_op jit(solution)/shard_map/ppermute | solution.py:273
  58.7 1.8 %collective-permute-done.14 = f32[24,512]{1,0:T(8,128)S(1)} collective-permute-done((f32[24,512]{1,0:T(8,128)S(1)}, f32[24,512]{1,0:T(8,128)S(1)}, u32[]{:S(2)}, u32[]{:S(2)}) %collective-permute-start.14) | collective-permute-done | bytes 49184 | tf_op jit(solution)/shard_map/ppermute | solution.py:273
  61.0 3.6 %collective-permute-start.17 = (f32[24,512]{1,0:T(8,128)S(1)}, f32[24,512]{1,0:T(8,128)S(1)}, u32[]{:S(2)}, u32[]{:S(2)}) collective-permute-start(f32[24,512]{1,0:T(8,128)S(1)} %add_add_fusion.1), channel_id=1, source_target_pairs={{224,0},{228,4},{232,8},{236,12},{240,16},{244,20},{248,24},{252,2... | collective-permute-start | bytes 147464 | tf_op jit(solution)/shard_map/ppermute | solution.py:285
  64.7 1.2 %collective-permute-start.16 = (f32[24,512]{1,0:T(8,128)S(1)}, f32[24,512]{1,0:T(8,128)S(1)}, u32[]{:S(2)}, u32[]{:S(2)}) collective-permute-start(f32[24,512]{1,0:T(8,128)S(1)} %add_add_fusion.1), channel_id=1, source_target_pairs={{64,0},{68,4},{72,8},{76,12},{80,16},{84,20},{88,24},{92,28},{224,... | collective-permute-start | bytes 147464 | tf_op jit(solution)/shard_map/ppermute | solution.py:285
  65.9 1.0 %collective-permute-start.15 = (f32[24,512]{1,0:T(8,128)S(1)}, f32[24,512]{1,0:T(8,128)S(1)}, u32[]{:S(2)}, u32[]{:S(2)}) collective-permute-start(f32[24,512]{1,0:T(8,128)S(1)} %add_add_fusion.1), channel_id=1, source_target_pairs={{160,0},{164,4},{168,8},{172,12},{176,16},{180,20},{184,24},{188,2... | collective-permute-start | bytes 147464 | tf_op jit(solution)/shard_map/ppermute | solution.py:285
  66.9 2.0 %collective-permute-done.16 = f32[24,512]{1,0:T(8,128)S(1)} collective-permute-done((f32[24,512]{1,0:T(8,128)S(1)}, f32[24,512]{1,0:T(8,128)S(1)}, u32[]{:S(2)}, u32[]{:S(2)}) %collective-permute-start.16) | collective-permute-done | bytes 49184 | tf_op jit(solution)/shard_map/ppermute | solution.py:285
  68.8 3.0 %collective-permute-done.15 = f32[24,512]{1,0:T(8,128)S(1)} collective-permute-done((f32[24,512]{1,0:T(8,128)S(1)}, f32[24,512]{1,0:T(8,128)S(1)}, u32[]{:S(2)}, u32[]{:S(2)}) %collective-permute-start.15) | collective-permute-done | bytes 49184 | tf_op jit(solution)/shard_map/ppermute | solution.py:285
  71.8 4.2 %collective-permute-start.18 = (f32[24,512]{1,0:T(8,128)S(1)}, f32[24,512]{1,0:T(8,128)S(1)}, u32[]{:S(2)}, u32[]{:S(2)}) collective-permute-start(f32[24,512]{1,0:T(8,128)S(1)} %add_add_fusion.refs_0_), channel_id=1, source_target_pairs={{0,4},{4,0},{8,12},{12,8},{16,20},{20,16},{24,28},{28,24},{32,36},... | collective-permute-start | bytes 147464 | tf_op jit(solution)/shard_map/ppermute | solution.py:273
  76.0 0.8 %outputs.1 = (bf16[48,1024]{1,0:T(8,128)(2,1)}, bf16[48,1024]{1,0:T(8,128)(2,1)}) custom-call(bf16[48,1024]{1,0:T(8,128)(2,1)S(1)} %get-tuple-element.40.rows_ref, bf16[48,1024]{1,0:T(8,128)(2,1)S(1)} %get-tuple-element.41.mixed_ref, bf16[48,48]{1,0:T(8,128)(2,1)S(1)} %copy-done.2, bf16[48,48]{1,0:T(8,128)(2,1)S(1)} %copy-done.3), custom_call_target="tpu_custom_call" | custom-call | flops 500000000 | bytes 1048576 | tf_op jit(solution)/shard_map/outputs/pallas_call | solution.py:399
  76.9 0.8 %unpack.1 = (f32[48,48]{1,0:T(8,128)}, f32[12,27,48]{2,1,0:T(8,128)}, f32[48,48]{1,0:T(8,128)}) custom-call(f32[24,512]{1,0:T(8,128)S(1)} %add_add_fusion.refs_0_, f32[24,512]{1,0:T(8,128)S(1)} %collective-permute-done.18.refs_1_), custom_call_target="tpu_custom_call" | custom-call | tf_op jit(solution)/shard_map/unpack/pallas_call | solution.py:411
  (52 shorter events, 4.0 us)
Async XLA Ops:
  0.6 7.4 %copy-start.7 = (bf16[27,12,48]{2,0,1:T(8,128)(2,1)S(1)}, bf16[27,12,48]{2,0,1:T(8,128)(2,1)}, u32[]{:S(2)}) copy-start(bf16[27,12,48]{2,0,1:T(8,128)(2,1)} %param.10) | copy-start | bytes 93316
  2.8 6.1 %collective-permute-start = (bf16[64,1024]{1,0:T(8,128)(2,1)}, bf16[64,1024]{1,0:T(8,128)(2,1)S(1)}, u32[]{:S(2)}, u32[]{:S(2)}) collective-permute-start(bf16[64,1024]{1,0:T(8,128)(2,1)} %get-tuple-element.28), channel_id=1, source_target_pairs={{0,1},{1,2},{2,3},{3,0},{4,5},{5,6},{6,7},{7,4},{8,9},{9,10},{10,1... | collective-permute-start | bytes 393224 | tf_op jit(solution)/shard_map/ppermute | solution.py:269
  5.0 4.0 %collective-permute-start.1 = (bf16[64,1024]{1,0:T(8,128)(2,1)}, bf16[64,1024]{1,0:T(8,128)(2,1)S(1)}, u32[]{:S(2)}, u32[]{:S(2)}) collective-permute-start(bf16[64,1024]{1,0:T(8,128)(2,1)} %get-tuple-element.29), channel_id=1, source_target_pairs={{0,3},{1,0},{2,1},{3,2},{4,7},{5,4},{6,5},{7,6},{8,11},{9,8},{10,9... | collective-permute-start | bytes 393224 | tf_op jit(solution)/shard_map/ppermute | solution.py:269
  6.4 6.6 %collective-permute-start.2 = (bf16[64,1024]{1,0:T(8,128)(2,1)}, bf16[64,1024]{1,0:T(8,128)(2,1)S(1)}, u32[]{:S(2)}, u32[]{:S(2)}) collective-permute-start(bf16[64,1024]{1,0:T(8,128)(2,1)} %get-tuple-element.30), channel_id=1, source_target_pairs={{0,2},{1,3},{2,0},{3,1},{4,6},{5,7},{6,4},{7,5},{8,10},{9,11},{10,... | collective-permute-start | bytes 393224 | tf_op jit(solution)/shard_map/ppermute | solution.py:269
  8.1 4.8 %copy-start.4 = (f32[64,1024]{1,0:T(8,128)S(1)}, f32[64,1024]{1,0:T(8,128)}, u32[]{:S(2)}) copy-start(f32[64,1024]{1,0:T(8,128)} %get-tuple-element.27.p0) | copy-start | bytes 786436
  8.2 4.8 %copy-start.5 = (s32[27,1024]{1,0:T(8,128)S(1)}, s32[27,1024]{1,0:T(8,128)}, u32[]{:S(2)}) copy-start(s32[27,1024]{1,0:T(8,128)} %nbr_ref.5) | copy-start | bytes 331780
  8.2 4.8 %copy-start.6 = (s32[1,8,8]{2,1,0:T(8,128)S(1)}, s32[1,8,8]{2,1,0:T(8,128)}, u32[]{:S(2)}) copy-start(s32[1,8,8]{2,1,0:T(8,128)} %param.13) | copy-start | bytes 772
  18.6 4.2 %collective-permute-start.3 = (bf16[96,1024]{1,0:T(8,128)(2,1)S(1)}, bf16[96,1024]{1,0:T(8,128)(2,1)S(1)}, u32[]{:S(2)}, u32[]{:S(2)}) collective-permute-start(bf16[96,1024]{1,0:T(8,128)(2,1)S(1)} %get-tuple-element.31), channel_id=1, source_target_pairs={{0,4},{4,0},{8,12},{12,8},{16,20},{20,16},{24,28},{28,24},{32,36},... | collective-permute-start | bytes 589832 | tf_op jit(solution)/shard_map/ppermute | solution.py:273
  22.8 10.6 %collective-permute-start.5 = (bf16[64,1024]{1,0:T(8,128)(2,1)S(1)}, bf16[64,1024]{1,0:T(8,128)(2,1)S(1)}, u32[]{:S(2)}, u32[]{:S(2)}) collective-permute-start(bf16[64,1024]{1,0:T(8,128)(2,1)S(1)} %get-tuple-element.54), channel_id=1, source_target_pairs={{0,8},{4,252},{8,16},{12,4},{16,24},{20,12},{24,32},{28,20},{32,40... | collective-permute-start | bytes 393224 | tf_op jit(solution)/shard_map/ppermute | solution.py:278
  29.7 5.8 %collective-permute-start.4 = (bf16[64,1024]{1,0:T(8,128)(2,1)S(1)}, bf16[64,1024]{1,0:T(8,128)(2,1)S(1)}, u32[]{:S(2)}, u32[]{:S(2)}) collective-permute-start(bf16[64,1024]{1,0:T(8,128)(2,1)S(1)} %get-tuple-element.55), channel_id=1, source_target_pairs={{0,16},{4,244},{8,24},{12,252},{16,32},{20,4},{24,40},{28,12},{32,... | collective-permute-start | bytes 393224 | tf_op jit(solution)/shard_map/ppermute | solution.py:278
  35.5 0.7 copy-start.8
  35.5 1.5 %collective-permute-start.6 = (bf16[80,1024]{1,0:T(8,128)(2,1)S(1)}, bf16[80,1024]{1,0:T(8,128)(2,1)S(1)}, u32[]{:S(2)}, u32[]{:S(2)}) collective-permute-start(bf16[80,1024]{1,0:T(8,128)(2,1)S(1)} %pad_maximum_fusion), channel_id=1, source_target_pairs={{0,4},{4,0},{8,12},{12,8},{16,20},{20,16},{24,28},{28,24},{32,36},... | collective-permute-start | bytes 491528 | tf_op jit(solution)/shard_map/ppermute | solution.py:273
  41.2 6.2 %collective-permute-start.9 = (bf16[64,1024]{1,0:T(8,128)(2,1)S(1)}, bf16[64,1024]{1,0:T(8,128)(2,1)S(1)}, u32[]{:S(2)}, u32[]{:S(2)}) collective-permute-start(bf16[64,1024]{1,0:T(8,128)(2,1)S(1)} %pad_maximum_fusion.4.e0), channel_id=1, source_target_pairs={{0,1},{1,2},{2,3},{3,0},{4,5},{5,6},{6,7},{7,4},{8,9},{9,10},{10,1... | collective-permute-start | bytes 393224 | tf_op jit(solution)/shard_map/ppermute | solution.py:269
  42.1 5.3 %collective-permute-start.8 = (bf16[64,1024]{1,0:T(8,128)(2,1)S(1)}, bf16[64,1024]{1,0:T(8,128)(2,1)S(1)}, u32[]{:S(2)}, u32[]{:S(2)}) collective-permute-start(bf16[64,1024]{1,0:T(8,128)(2,1)S(1)} %pad_maximum_fusion.4.e0), channel_id=1, source_target_pairs={{0,3},{1,0},{2,1},{3,2},{4,7},{5,4},{6,5},{7,6},{8,11},{9,8},{10,9... | collective-permute-start | bytes 393224 | tf_op jit(solution)/shard_map/ppermute | solution.py:269
  43.9 5.8 %collective-permute-start.7 = (bf16[64,1024]{1,0:T(8,128)(2,1)S(1)}, bf16[64,1024]{1,0:T(8,128)(2,1)S(1)}, u32[]{:S(2)}, u32[]{:S(2)}) collective-permute-start(bf16[64,1024]{1,0:T(8,128)(2,1)S(1)} %pad_maximum_fusion.4.e0), channel_id=1, source_target_pairs={{0,2},{1,3},{2,0},{3,1},{4,6},{5,7},{6,4},{7,5},{8,10},{9,11},{10,... | collective-permute-start | bytes 393224 | tf_op jit(solution)/shard_map/ppermute | solution.py:269
  44.2 5.6 %copy-start = (bf16[48,1024]{1,0:T(8,128)(2,1)S(1)}, bf16[48,1024]{1,0:T(8,128)(2,1)}, u32[]{:S(2)}) copy-start(bf16[48,1024]{1,0:T(8,128)(2,1)} %feat_ref.3) | copy-start | bytes 294916
  44.2 5.6 %copy-start.1 = (bf16[48,1024]{1,0:T(8,128)(2,1)S(1)}, bf16[48,1024]{1,0:T(8,128)(2,1)}, u32[]{:S(2)}) copy-start(bf16[48,1024]{1,0:T(8,128)(2,1)} %cot_ref.3) | copy-start | bytes 294916
  50.3 2.6 %collective-permute-start.10 = (f32[24,512]{1,0:T(8,128)S(1)}, f32[24,512]{1,0:T(8,128)S(1)}, u32[]{:S(2)}, u32[]{:S(2)}) collective-permute-start(f32[24,512]{1,0:T(8,128)S(1)} %get-tuple-element.45), channel_id=1, source_target_pairs={{0,4},{4,0},{8,12},{12,8},{16,20},{20,16},{24,28},{28,24},{32,36},... | collective-permute-start | bytes 147464 | tf_op jit(solution)/shard_map/ppermute | solution.py:273
  52.9 3.0 %collective-permute-start.11 = (f32[24,512]{1,0:T(8,128)S(1)}, f32[24,512]{1,0:T(8,128)S(1)}, u32[]{:S(2)}, u32[]{:S(2)}) collective-permute-start(f32[24,512]{1,0:T(8,128)S(1)} %add.58), channel_id=1, source_target_pairs={{0,32},{4,36},{8,40},{12,44},{16,48},{20,52},{24,56},{28,60},{32,0... | collective-permute-start | bytes 147464 | tf_op jit(solution)/shard_map/ppermute | solution.py:273
  55.9 4.6 %collective-permute-start.14 = (f32[24,512]{1,0:T(8,128)S(1)}, f32[24,512]{1,0:T(8,128)S(1)}, u32[]{:S(2)}, u32[]{:S(2)}) collective-permute-start(f32[24,512]{1,0:T(8,128)S(1)} %add.59), channel_id=1, source_target_pairs={{0,16},{4,20},{8,24},{12,28},{16,0},{20,4},{24,8},{28,12},{32,48},... | collective-permute-start | bytes 147464 | tf_op jit(solution)/shard_map/ppermute | solution.py:273
  56.4 4.6 %collective-permute-start.13 = (f32[24,512]{1,0:T(8,128)S(1)}, f32[24,512]{1,0:T(8,128)S(1)}, u32[]{:S(2)}, u32[]{:S(2)}) collective-permute-start(f32[24,512]{1,0:T(8,128)S(1)} %add.59), channel_id=1, source_target_pairs={{0,24},{4,28},{8,16},{12,20},{16,8},{20,12},{24,0},{28,4},{32,56},... | collective-permute-start | bytes 147464 | tf_op jit(solution)/shard_map/ppermute | solution.py:273
  57.9 3.1 %collective-permute-start.12 = (f32[24,512]{1,0:T(8,128)S(1)}, f32[24,512]{1,0:T(8,128)S(1)}, u32[]{:S(2)}, u32[]{:S(2)}) collective-permute-start(f32[24,512]{1,0:T(8,128)S(1)} %add.59), channel_id=1, source_target_pairs={{0,8},{4,12},{8,0},{12,4},{16,24},{20,28},{24,16},{28,20},{32,40},... | collective-permute-start | bytes 147464 | tf_op jit(solution)/shard_map/ppermute | solution.py:273
  61.0 15.0 %copy-start.2 = (bf16[48,48]{1,0:T(8,128)(2,1)S(1)}, bf16[48,48]{1,0:T(8,128)(2,1)}, u32[]{:S(2)}) copy-start(bf16[48,48]{1,0:T(8,128)(2,1)} %in_ref.3) | copy-start | bytes 13828
  61.0 15.0 %copy-start.3 = (bf16[48,48]{1,0:T(8,128)(2,1)S(1)}, bf16[48,48]{1,0:T(8,128)(2,1)}, u32[]{:S(2)}) copy-start(bf16[48,48]{1,0:T(8,128)(2,1)} %outf_ref.3) | copy-start | bytes 13828
  61.0 5.8 %collective-permute-start.17 = (f32[24,512]{1,0:T(8,128)S(1)}, f32[24,512]{1,0:T(8,128)S(1)}, u32[]{:S(2)}, u32[]{:S(2)}) collective-permute-start(f32[24,512]{1,0:T(8,128)S(1)} %add_add_fusion.1), channel_id=1, source_target_pairs={{224,0},{228,4},{232,8},{236,12},{240,16},{244,20},{248,24},{252,2... | collective-permute-start | bytes 147464 | tf_op jit(solution)/shard_map/ppermute | solution.py:285
  64.7 4.1 %collective-permute-start.16 = (f32[24,512]{1,0:T(8,128)S(1)}, f32[24,512]{1,0:T(8,128)S(1)}, u32[]{:S(2)}, u32[]{:S(2)}) collective-permute-start(f32[24,512]{1,0:T(8,128)S(1)} %add_add_fusion.1), channel_id=1, source_target_pairs={{64,0},{68,4},{72,8},{76,12},{80,16},{84,20},{88,24},{92,28},{224,... | collective-permute-start | bytes 147464 | tf_op jit(solution)/shard_map/ppermute | solution.py:285
  65.9 5.9 %collective-permute-start.15 = (f32[24,512]{1,0:T(8,128)S(1)}, f32[24,512]{1,0:T(8,128)S(1)}, u32[]{:S(2)}, u32[]{:S(2)}) collective-permute-start(f32[24,512]{1,0:T(8,128)S(1)} %add_add_fusion.1), channel_id=1, source_target_pairs={{160,0},{164,4},{168,8},{172,12},{176,16},{180,20},{184,24},{188,2... | collective-permute-start | bytes 147464 | tf_op jit(solution)/shard_map/ppermute | solution.py:285
  71.8 5.1 %collective-permute-start.18 = (f32[24,512]{1,0:T(8,128)S(1)}, f32[24,512]{1,0:T(8,128)S(1)}, u32[]{:S(2)}, u32[]{:S(2)}) collective-permute-start(f32[24,512]{1,0:T(8,128)S(1)} %add_add_fusion.refs_0_), channel_id=1, source_target_pairs={{0,4},{4,0},{8,12},{12,8},{16,20},{20,16},{24,28},{28,24},{32,36},... | collective-permute-start | bytes 147464 | tf_op jit(solution)/shard_map/ppermute | solution.py:273

commit v12 on v11

--- a/solution.py
+++ b/solution.py
@@ -291,7 +291,7 @@
     mine = mine + crossed(give, 1)
     for masks in ((8,), (2, 6, 4)):
         mine = mine + sum(crossed(mine, mask) for mask in masks)
-    mine = mine + sum(from_z(mine, even, odd) for even, odd in ((-3, 3), (2, -2), (-1, 1)))
+    mine = mine + sum(from_z(mine, even, odd) for even, odd in ((-1, 1), (2, -2), (-3, 3)))
     return mine, crossed(mine, 1)
 
 

time: 77.9 us -> 77.4 us (level)
  waiting for transfers between devices: 24.8 us -> 22.4 us
  starting transfers between devices: 33.3 us -> 35.3 us
    ppermute x3, waiting for transfers between devices: 4.94 us -> 2.49 us  [from_z(): lax.ppermute(block, 'leaf', [((i + 8 * (odd if i // 8 % 2 else even)) % c...]
    ppermute x3, starting transfers between devices: 5.81 us -> 8.06 us  [from_z(): lax.ppermute(block, 'leaf', [((i + 8 * (odd if i // 8 % 2 else even)) % c...]
where the time goes in v12:
time: 77.4 us; the launch traced here: 77.3 us
  starting transfers between devices  35.3 us (46%)
  waiting for transfers between devices  22.4 us (29%)
  Pallas kernels  17.7 us (23%)
  local copies, waits for them, and re-layouts  0.9 us (1%)
  between operations  0.84 us (1%)
    ppermute x8, starting transfers between devices, crossed(): lax.ppermute(block, 'leaf', [(i, i ^ mask) for i in range(lax.axis_size('...  11.6 us
    ppermute x6, waiting for transfers between devices, shifted(): lax.ppermute(block, axis, [(i, (i + distance) % count) for i in range(cou...  9.79 us
    ppermute x6, starting transfers between devices, shifted(): lax.ppermute(block, axis, [(i, (i + distance) % count) for i in range(cou...  8.21 us
    ppermute x3, starting transfers between devices, from_z(): lax.ppermute(block, 'leaf', [((i + 8 * (odd if i // 8 % 2 else even)) % c...  8.06 us
    ppermute x8, waiting for transfers between devices, crossed(): lax.ppermute(block, 'leaf', [(i, i ^ mask) for i in range(lax.axis_size('...  8.02 us
    ppermute x2, starting transfers between devices, outward(): lax.ppermute(block, 'leaf', [(i, (i + (2 * chips if i % 2 == 0 else -2 *...  7.42 us
    pallas_call x1, Pallas kernels, body(): pl.pallas_call(scatter_kernel, out_shape=[struct((rank, rows), BF), struc...  5.57 us
    pallas_call x1, Pallas kernels, body(): pl.pallas_call(far_gather_kernel, out_shape=[struct((rank, rows), F32), s...  4.08 us
  transfers between devices with their start and end apart: 19, of which 13 were waited for; matrix products, arithmetic and copies ran while one was open for 0% of the time, Pallas kernels for 6%

profile of v12, /device:TPU:1, one launch (start us, length us, event | category | flops | bytes accessed | tf_op | source)
XLA Modules:
  0.0 77.3 jit_solution(10610023613306978266)
XLA Ops:
  0.6 2.2 %project.1 = (f32[64,1024]{1,0:T(8,128)}, bf16[64,1024]{1,0:T(8,128)(2,1)}, bf16[64,1024]{1,0:T(8,128)(2,1)}, bf16[64,1024]{1,0:T(8,128)(2,1)}) custom-call(bf16[48,1024]{1,0:T(8,128)(2,1)} %feat_ref.3, bf16[48,48]{1,0:T(8,128)(2,1)} %in_ref.3, bf16[48,1024]{1,0:T(8,128)(2,1)} %cot_ref.3, bf16[48,48]{1,0:T(8,128)(2,1)} %outf_ref.3, s32[1,1024]{1,0:T(1,128)} %bitcast.10), custom_call_target="tpu_custom_call" | custom-call | tf_op jit(solution)/shard_map/project/pallas_call | solution.py:314
  2.8 2.1 %collective-permute-start = (bf16[64,1024]{1,0:T(8,128)(2,1)}, bf16[64,1024]{1,0:T(8,128)(2,1)S(1)}, u32[]{:S(2)}, u32[]{:S(2)}) collective-permute-start(bf16[64,1024]{1,0:T(8,128)(2,1)} %get-tuple-element.28), channel_id=1, source_target_pairs={{0,1},{1,2},{2,3},{3,0},{4,5},{5,6},{6,7},{7,4},{8,9},{9,10},{10,1... | collective-permute-start | bytes 393224 | tf_op jit(solution)/shard_map/ppermute | solution.py:269
  5.0 1.4 %collective-permute-start.1 = (bf16[64,1024]{1,0:T(8,128)(2,1)}, bf16[64,1024]{1,0:T(8,128)(2,1)S(1)}, u32[]{:S(2)}, u32[]{:S(2)}) collective-permute-start(bf16[64,1024]{1,0:T(8,128)(2,1)} %get-tuple-element.29), channel_id=1, source_target_pairs={{0,3},{1,0},{2,1},{3,2},{4,7},{5,4},{6,5},{7,6},{8,11},{9,8},{10,9... | collective-permute-start | bytes 393224 | tf_op jit(solution)/shard_map/ppermute | solution.py:269
  6.4 1.6 %collective-permute-start.2 = (bf16[64,1024]{1,0:T(8,128)(2,1)}, bf16[64,1024]{1,0:T(8,128)(2,1)S(1)}, u32[]{:S(2)}, u32[]{:S(2)}) collective-permute-start(bf16[64,1024]{1,0:T(8,128)(2,1)} %get-tuple-element.30), channel_id=1, source_target_pairs={{0,2},{1,3},{2,0},{3,1},{4,6},{5,7},{6,4},{7,5},{8,10},{9,11},{10,... | collective-permute-start | bytes 393224 | tf_op jit(solution)/shard_map/ppermute | solution.py:269
  8.3 0.6 collective-permute-done.p1
  9.0 4.0 %collective-permute-done.2.p3 = bf16[64,1024]{1,0:T(8,128)(2,1)S(1)} collective-permute-done((bf16[64,1024]{1,0:T(8,128)(2,1)}, bf16[64,1024]{1,0:T(8,128)(2,1)S(1)}, u32[]{:S(2)}, u32[]{:S(2)}) %collective-permute-start.2) | collective-permute-done | bytes 131104 | tf_op jit(solution)/shard_map/ppermute | solution.py:269
  13.0 5.6 %scatter.1 = (bf16[48,1024]{1,0:T(8,128)(2,1)S(1)}, f32[16,1024]{1,0:T(8,128)S(1)}, f32[48,1024]{1,0:T(8,128)S(1)}, bf16[96,1024]{1,0:T(8,128)(2,1)S(1)}) custom-call(s32[8,8]{1,0:T(8,128)S(1)} %bitcast.7, f32[64,1024]{1,0:T(8,128)S(1)} %copy-done.4, bf16[64,1024]{1,0:T(8,128)(2,1)S(1)} %collective-permute-done.p1, ...), custom_call_target="tpu_custom_call" | custom-call | flops 5000000000 | bytes 1048576 | tf_op jit(solution)/shard_map/scatter/pallas_call | solution.py:324
  18.6 3.1 %collective-permute-start.3 = (bf16[96,1024]{1,0:T(8,128)(2,1)S(1)}, bf16[96,1024]{1,0:T(8,128)(2,1)S(1)}, u32[]{:S(2)}, u32[]{:S(2)}) collective-permute-start(bf16[96,1024]{1,0:T(8,128)(2,1)S(1)} %get-tuple-element.31), channel_id=1, source_target_pairs={{0,4},{4,0},{8,12},{12,8},{16,20},{20,16},{24,28},{28,24},{32,36},... | collective-permute-start | bytes 589832 | tf_op jit(solution)/shard_map/ppermute | solution.py:273
  21.7 1.1 %collective-permute-done.3 = bf16[96,1024]{1,0:T(8,128)(2,1)S(1)} collective-permute-done((bf16[96,1024]{1,0:T(8,128)(2,1)S(1)}, bf16[96,1024]{1,0:T(8,128)(2,1)S(1)}, u32[]{:S(2)}, u32[]{:S(2)}) %collective-permute-start.3) | collective-permute-done | bytes 196640 | tf_op jit(solution)/shard_map/ppermute | solution.py:273
  22.8 6.9 %collective-permute-start.5 = (bf16[64,1024]{1,0:T(8,128)(2,1)S(1)}, bf16[64,1024]{1,0:T(8,128)(2,1)S(1)}, u32[]{:S(2)}, u32[]{:S(2)}) collective-permute-start(bf16[64,1024]{1,0:T(8,128)(2,1)S(1)} %get-tuple-element.54), channel_id=1, source_target_pairs={{0,8},{4,252},{8,16},{12,4},{16,24},{20,12},{24,32},{28,20},{32,40... | collective-permute-start | bytes 393224 | tf_op jit(solution)/shard_map/ppermute | solution.py:278
  30.2 3.2 %near_gather.1.base_ref = bf16[432,1024]{1,0:T(8,128)(2,1)S(1)} custom-call(s32[8,8]{1,0:T(8,128)S(1)} %bitcast.8, bf16[16,1024]{1,0:T(8,128)(2,1)S(1)} %slice.51.own_ref, bf16[16,1024]{1,0:T(8,128)(2,1)S(1)} %get-tuple-element.52.pair_ref, s32[27,1024]{1,0:T(8,128)S(1)} %copy-done.5), custom_call_target="tpu_custom_call" | custom-call | flops 5000000000 | bytes 1048576 | tf_op jit(solution)/shard_map/near_gather/pallas_call | solution.py:350
  33.4 2.1 %collective-permute-done.4 = bf16[64,1024]{1,0:T(8,128)(2,1)S(1)} collective-permute-done((bf16[64,1024]{1,0:T(8,128)(2,1)S(1)}, bf16[64,1024]{1,0:T(8,128)(2,1)S(1)}, u32[]{:S(2)}, u32[]{:S(2)}) %collective-permute-start.4) | collective-permute-done | bytes 131104 | tf_op jit(solution)/shard_map/ppermute | solution.py:278
  35.6 0.6 copy-done.8
  36.2 0.8 %collective-permute-done.6.cross_ref = bf16[80,1024]{1,0:T(8,128)(2,1)S(1)} collective-permute-done((bf16[80,1024]{1,0:T(8,128)(2,1)S(1)}, bf16[80,1024]{1,0:T(8,128)(2,1)S(1)}, u32[]{:S(2)}, u32[]{:S(2)}) %collective-permute-start.6) | collective-permute-done | bytes 163872 | tf_op jit(solution)/shard_map/ppermute | solution.py:273
  37.0 4.1 %far_gather.1 = (f32[48,1024]{1,0:T(8,128)S(1)}, bf16[512,1024]{1,0:T(8,128)(2,1)S(1)}) custom-call(s32[8,8]{1,0:T(8,128)S(1)} %bitcast.9, bf16[432,1024]{1,0:T(8,128)(2,1)S(1)} %near_gather.1.base_ref, bf16[32,1024]{1,0:T(8,128)(2,1)S(1)} %slice.60.near_ref, bf16[32,1024]{1,0:T(8,128)(2,1)S(1)} %slice.61.far_ref, ...), custom_call_target="tpu_custom_call" | custom-call | flops 5000000000 | bytes 1048576 | tf_op jit(solution)/shard_map/far_gather/pallas_call | solution.py:367
  41.2 0.9 %collective-permute-start.9 = (bf16[64,1024]{1,0:T(8,128)(2,1)S(1)}, bf16[64,1024]{1,0:T(8,128)(2,1)S(1)}, u32[]{:S(2)}, u32[]{:S(2)}) collective-permute-start(bf16[64,1024]{1,0:T(8,128)(2,1)S(1)} %pad_maximum_fusion.4.e0), channel_id=1, source_target_pairs={{0,1},{1,2},{2,3},{3,0},{4,5},{5,6},{6,7},{7,4},{8,9},{9,10},{10,1... | collective-permute-start | bytes 393224 | tf_op jit(solution)/shard_map/ppermute | solution.py:269
  42.1 1.8 %collective-permute-start.8 = (bf16[64,1024]{1,0:T(8,128)(2,1)S(1)}, bf16[64,1024]{1,0:T(8,128)(2,1)S(1)}, u32[]{:S(2)}, u32[]{:S(2)}) collective-permute-start(bf16[64,1024]{1,0:T(8,128)(2,1)S(1)} %pad_maximum_fusion.4.e0), channel_id=1, source_target_pairs={{0,3},{1,0},{2,1},{3,2},{4,7},{5,4},{6,5},{7,6},{8,11},{9,8},{10,9... | collective-permute-start | bytes 393224 | tf_op jit(solution)/shard_map/ppermute | solution.py:269
  44.6 2.8 %collective-permute-done.9.e1 = bf16[64,1024]{1,0:T(8,128)(2,1)S(1)} collective-permute-done((bf16[64,1024]{1,0:T(8,128)(2,1)S(1)}, bf16[64,1024]{1,0:T(8,128)(2,1)S(1)}, u32[]{:S(2)}, u32[]{:S(2)}) %collective-permute-start.9) | collective-permute-done | bytes 131104 | tf_op jit(solution)/shard_map/ppermute | solution.py:269
  47.4 2.3 %collective-permute-done.7.e2 = bf16[64,1024]{1,0:T(8,128)(2,1)S(1)} collective-permute-done((bf16[64,1024]{1,0:T(8,128)(2,1)S(1)}, bf16[64,1024]{1,0:T(8,128)(2,1)S(1)}, u32[]{:S(2)}, u32[]{:S(2)}) %collective-permute-start.7) | collective-permute-done | bytes 131104 | tf_op jit(solution)/shard_map/ppermute | solution.py:269
  49.8 0.6 sums.1
  50.3 1.7 %collective-permute-start.10 = (f32[24,512]{1,0:T(8,128)S(1)}, f32[24,512]{1,0:T(8,128)S(1)}, u32[]{:S(2)}, u32[]{:S(2)}) collective-permute-start(f32[24,512]{1,0:T(8,128)S(1)} %get-tuple-element.45), channel_id=1, source_target_pairs={{0,4},{4,0},{8,12},{12,8},{16,20},{20,16},{24,28},{28,24},{32,36},... | collective-permute-start | bytes 147464 | tf_op jit(solution)/shard_map/ppermute | solution.py:273
  52.0 0.9 %collective-permute-done.10 = f32[24,512]{1,0:T(8,128)S(1)} collective-permute-done((f32[24,512]{1,0:T(8,128)S(1)}, f32[24,512]{1,0:T(8,128)S(1)}, u32[]{:S(2)}, u32[]{:S(2)}) %collective-permute-start.10) | collective-permute-done | bytes 49184 | tf_op jit(solution)/shard_map/ppermute | solution.py:273
  53.0 2.9 %collective-permute-done.11 = f32[24,512]{1,0:T(8,128)S(1)} collective-permute-done((f32[24,512]{1,0:T(8,128)S(1)}, f32[24,512]{1,0:T(8,128)S(1)}, u32[]{:S(2)}, u32[]{:S(2)}) %collective-permute-start.11) | collective-permute-done | bytes 49184 | tf_op jit(solution)/shard_map/ppermute | solution.py:273
  56.4 1.4 %collective-permute-start.13 = (f32[24,512]{1,0:T(8,128)S(1)}, f32[24,512]{1,0:T(8,128)S(1)}, u32[]{:S(2)}, u32[]{:S(2)}) collective-permute-start(f32[24,512]{1,0:T(8,128)S(1)} %add.59), channel_id=1, source_target_pairs={{0,24},{4,28},{8,16},{12,20},{16,8},{20,12},{24,0},{28,4},{32,56},... | collective-permute-start | bytes 147464 | tf_op jit(solution)/shard_map/ppermute | solution.py:273
  57.9 0.8 %collective-permute-start.12 = (f32[24,512]{1,0:T(8,128)S(1)}, f32[24,512]{1,0:T(8,128)S(1)}, u32[]{:S(2)}, u32[]{:S(2)}) collective-permute-start(f32[24,512]{1,0:T(8,128)S(1)} %add.59), channel_id=1, source_target_pairs={{0,8},{4,12},{8,0},{12,4},{16,24},{20,28},{24,16},{28,20},{32,40},... | collective-permute-start | bytes 147464 | tf_op jit(solution)/shard_map/ppermute | solution.py:273
  58.7 1.8 %collective-permute-done.14 = f32[24,512]{1,0:T(8,128)S(1)} collective-permute-done((f32[24,512]{1,0:T(8,128)S(1)}, f32[24,512]{1,0:T(8,128)S(1)}, u32[]{:S(2)}, u32[]{:S(2)}) %collective-permute-start.14) | collective-permute-done | bytes 49184 | tf_op jit(solution)/shard_map/ppermute | solution.py:273
  61.0 4.5 %collective-permute-start.17 = (f32[24,512]{1,0:T(8,128)S(1)}, f32[24,512]{1,0:T(8,128)S(1)}, u32[]{:S(2)}, u32[]{:S(2)}) collective-permute-start(f32[24,512]{1,0:T(8,128)S(1)} %add_add_fusion.1), channel_id=1, source_target_pairs={{160,0},{164,4},{168,8},{172,12},{176,16},{180,20},{184,24},{188,2... | collective-permute-start | bytes 147464 | tf_op jit(solution)/shard_map/ppermute | solution.py:285
  65.8 3.3 %collective-permute-start.15 = (f32[24,512]{1,0:T(8,128)S(1)}, f32[24,512]{1,0:T(8,128)S(1)}, u32[]{:S(2)}, u32[]{:S(2)}) collective-permute-start(f32[24,512]{1,0:T(8,128)S(1)} %add_add_fusion.1), channel_id=1, source_target_pairs={{224,0},{228,4},{232,8},{236,12},{240,16},{244,20},{248,24},{252,2... | collective-permute-start | bytes 147464 | tf_op jit(solution)/shard_map/ppermute | solution.py:285
  69.4 2.2 %collective-permute-done.15 = f32[24,512]{1,0:T(8,128)S(1)} collective-permute-done((f32[24,512]{1,0:T(8,128)S(1)}, f32[24,512]{1,0:T(8,128)S(1)}, u32[]{:S(2)}, u32[]{:S(2)}) %collective-permute-start.15) | collective-permute-done | bytes 49184 | tf_op jit(solution)/shard_map/ppermute | solution.py:285
  71.6 3.9 %collective-permute-start.18 = (f32[24,512]{1,0:T(8,128)S(1)}, f32[24,512]{1,0:T(8,128)S(1)}, u32[]{:S(2)}, u32[]{:S(2)}) collective-permute-start(f32[24,512]{1,0:T(8,128)S(1)} %add_add_fusion.refs_0_), channel_id=1, source_target_pairs={{0,4},{4,0},{8,12},{12,8},{16,20},{20,16},{24,28},{28,24},{32,36},... | collective-permute-start | bytes 147464 | tf_op jit(solution)/shard_map/ppermute | solution.py:273
  75.6 0.8 %outputs.1 = (bf16[48,1024]{1,0:T(8,128)(2,1)}, bf16[48,1024]{1,0:T(8,128)(2,1)}) custom-call(bf16[48,1024]{1,0:T(8,128)(2,1)S(1)} %get-tuple-element.40.rows_ref, bf16[48,1024]{1,0:T(8,128)(2,1)S(1)} %get-tuple-element.41.mixed_ref, bf16[48,48]{1,0:T(8,128)(2,1)S(1)} %copy-done.2, bf16[48,48]{1,0:T(8,128)(2,1)S(1)} %copy-done.3), custom_call_target="tpu_custom_call" | custom-call | flops 500000000 | bytes 1048576 | tf_op jit(solution)/shard_map/outputs/pallas_call | solution.py:399
  76.5 0.8 %unpack.1 = (f32[48,48]{1,0:T(8,128)}, f32[12,27,48]{2,1,0:T(8,128)}, f32[48,48]{1,0:T(8,128)}) custom-call(f32[24,512]{1,0:T(8,128)S(1)} %add_add_fusion.refs_0_, f32[24,512]{1,0:T(8,128)S(1)} %collective-permute-done.18.refs_1_), custom_call_target="tpu_custom_call" | custom-call | tf_op jit(solution)/shard_map/unpack/pallas_call | solution.py:411
  (52 shorter events, 3.5 us)
Async XLA Ops:
  0.6 7.4 %copy-start.7 = (bf16[27,12,48]{2,0,1:T(8,128)(2,1)S(1)}, bf16[27,12,48]{2,0,1:T(8,128)(2,1)}, u32[]{:S(2)}) copy-start(bf16[27,12,48]{2,0,1:T(8,128)(2,1)} %param.10) | copy-start | bytes 93316
  2.8 6.1 %collective-permute-start = (bf16[64,1024]{1,0:T(8,128)(2,1)}, bf16[64,1024]{1,0:T(8,128)(2,1)S(1)}, u32[]{:S(2)}, u32[]{:S(2)}) collective-permute-start(bf16[64,1024]{1,0:T(8,128)(2,1)} %get-tuple-element.28), channel_id=1, source_target_pairs={{0,1},{1,2},{2,3},{3,0},{4,5},{5,6},{6,7},{7,4},{8,9},{9,10},{10,1... | collective-permute-start | bytes 393224 | tf_op jit(solution)/shard_map/ppermute | solution.py:269
  5.0 4.0 %collective-permute-start.1 = (bf16[64,1024]{1,0:T(8,128)(2,1)}, bf16[64,1024]{1,0:T(8,128)(2,1)S(1)}, u32[]{:S(2)}, u32[]{:S(2)}) collective-permute-start(bf16[64,1024]{1,0:T(8,128)(2,1)} %get-tuple-element.29), channel_id=1, source_target_pairs={{0,3},{1,0},{2,1},{3,2},{4,7},{5,4},{6,5},{7,6},{8,11},{9,8},{10,9... | collective-permute-start | bytes 393224 | tf_op jit(solution)/shard_map/ppermute | solution.py:269
  6.4 6.6 %collective-permute-start.2 = (bf16[64,1024]{1,0:T(8,128)(2,1)}, bf16[64,1024]{1,0:T(8,128)(2,1)S(1)}, u32[]{:S(2)}, u32[]{:S(2)}) collective-permute-start(bf16[64,1024]{1,0:T(8,128)(2,1)} %get-tuple-element.30), channel_id=1, source_target_pairs={{0,2},{1,3},{2,0},{3,1},{4,6},{5,7},{6,4},{7,5},{8,10},{9,11},{10,... | collective-permute-start | bytes 393224 | tf_op jit(solution)/shard_map/ppermute | solution.py:269
  8.1 4.8 %copy-start.4 = (f32[64,1024]{1,0:T(8,128)S(1)}, f32[64,1024]{1,0:T(8,128)}, u32[]{:S(2)}) copy-start(f32[64,1024]{1,0:T(8,128)} %get-tuple-element.27.p0) | copy-start | bytes 786436
  8.2 4.8 %copy-start.5 = (s32[27,1024]{1,0:T(8,128)S(1)}, s32[27,1024]{1,0:T(8,128)}, u32[]{:S(2)}) copy-start(s32[27,1024]{1,0:T(8,128)} %nbr_ref.5) | copy-start | bytes 331780
  8.2 4.8 %copy-start.6 = (s32[1,8,8]{2,1,0:T(8,128)S(1)}, s32[1,8,8]{2,1,0:T(8,128)}, u32[]{:S(2)}) copy-start(s32[1,8,8]{2,1,0:T(8,128)} %param.13) | copy-start | bytes 772
  18.6 4.2 %collective-permute-start.3 = (bf16[96,1024]{1,0:T(8,128)(2,1)S(1)}, bf16[96,1024]{1,0:T(8,128)(2,1)S(1)}, u32[]{:S(2)}, u32[]{:S(2)}) collective-permute-start(bf16[96,1024]{1,0:T(8,128)(2,1)S(1)} %get-tuple-element.31), channel_id=1, source_target_pairs={{0,4},{4,0},{8,12},{12,8},{16,20},{20,16},{24,28},{28,24},{32,36},... | collective-permute-start | bytes 589832 | tf_op jit(solution)/shard_map/ppermute | solution.py:273
  22.8 10.6 %collective-permute-start.5 = (bf16[64,1024]{1,0:T(8,128)(2,1)S(1)}, bf16[64,1024]{1,0:T(8,128)(2,1)S(1)}, u32[]{:S(2)}, u32[]{:S(2)}) collective-permute-start(bf16[64,1024]{1,0:T(8,128)(2,1)S(1)} %get-tuple-element.54), channel_id=1, source_target_pairs={{0,8},{4,252},{8,16},{12,4},{16,24},{20,12},{24,32},{28,20},{32,40... | collective-permute-start | bytes 393224 | tf_op jit(solution)/shard_map/ppermute | solution.py:278
  29.7 5.8 %collective-permute-start.4 = (bf16[64,1024]{1,0:T(8,128)(2,1)S(1)}, bf16[64,1024]{1,0:T(8,128)(2,1)S(1)}, u32[]{:S(2)}, u32[]{:S(2)}) collective-permute-start(bf16[64,1024]{1,0:T(8,128)(2,1)S(1)} %get-tuple-element.55), channel_id=1, source_target_pairs={{0,16},{4,244},{8,24},{12,252},{16,32},{20,4},{24,40},{28,12},{32,... | collective-permute-start | bytes 393224 | tf_op jit(solution)/shard_map/ppermute | solution.py:278
  35.5 0.7 copy-start.8
  35.5 1.5 %collective-permute-start.6 = (bf16[80,1024]{1,0:T(8,128)(2,1)S(1)}, bf16[80,1024]{1,0:T(8,128)(2,1)S(1)}, u32[]{:S(2)}, u32[]{:S(2)}) collective-permute-start(bf16[80,1024]{1,0:T(8,128)(2,1)S(1)} %pad_maximum_fusion), channel_id=1, source_target_pairs={{0,4},{4,0},{8,12},{12,8},{16,20},{20,16},{24,28},{28,24},{32,36},... | collective-permute-start | bytes 491528 | tf_op jit(solution)/shard_map/ppermute | solution.py:273
  41.2 6.2 %collective-permute-start.9 = (bf16[64,1024]{1,0:T(8,128)(2,1)S(1)}, bf16[64,1024]{1,0:T(8,128)(2,1)S(1)}, u32[]{:S(2)}, u32[]{:S(2)}) collective-permute-start(bf16[64,1024]{1,0:T(8,128)(2,1)S(1)} %pad_maximum_fusion.4.e0), channel_id=1, source_target_pairs={{0,1},{1,2},{2,3},{3,0},{4,5},{5,6},{6,7},{7,4},{8,9},{9,10},{10,1... | collective-permute-start | bytes 393224 | tf_op jit(solution)/shard_map/ppermute | solution.py:269
  42.1 5.3 %collective-permute-start.8 = (bf16[64,1024]{1,0:T(8,128)(2,1)S(1)}, bf16[64,1024]{1,0:T(8,128)(2,1)S(1)}, u32[]{:S(2)}, u32[]{:S(2)}) collective-permute-start(bf16[64,1024]{1,0:T(8,128)(2,1)S(1)} %pad_maximum_fusion.4.e0), channel_id=1, source_target_pairs={{0,3},{1,0},{2,1},{3,2},{4,7},{5,4},{6,5},{7,6},{8,11},{9,8},{10,9... | collective-permute-start | bytes 393224 | tf_op jit(solution)/shard_map/ppermute | solution.py:269
  43.9 5.8 %collective-permute-start.7 = (bf16[64,1024]{1,0:T(8,128)(2,1)S(1)}, bf16[64,1024]{1,0:T(8,128)(2,1)S(1)}, u32[]{:S(2)}, u32[]{:S(2)}) collective-permute-start(bf16[64,1024]{1,0:T(8,128)(2,1)S(1)} %pad_maximum_fusion.4.e0), channel_id=1, source_target_pairs={{0,2},{1,3},{2,0},{3,1},{4,6},{5,7},{6,4},{7,5},{8,10},{9,11},{10,... | collective-permute-start | bytes 393224 | tf_op jit(solution)/shard_map/ppermute | solution.py:269
  44.2 5.6 %copy-start = (bf16[48,1024]{1,0:T(8,128)(2,1)S(1)}, bf16[48,1024]{1,0:T(8,128)(2,1)}, u32[]{:S(2)}) copy-start(bf16[48,1024]{1,0:T(8,128)(2,1)} %feat_ref.3) | copy-start | bytes 294916
  44.2 5.6 %copy-start.1 = (bf16[48,1024]{1,0:T(8,128)(2,1)S(1)}, bf16[48,1024]{1,0:T(8,128)(2,1)}, u32[]{:S(2)}) copy-start(bf16[48,1024]{1,0:T(8,128)(2,1)} %cot_ref.3) | copy-start | bytes 294916
  50.3 2.6 %collective-permute-start.10 = (f32[24,512]{1,0:T(8,128)S(1)}, f32[24,512]{1,0:T(8,128)S(1)}, u32[]{:S(2)}, u32[]{:S(2)}) collective-permute-start(f32[24,512]{1,0:T(8,128)S(1)} %get-tuple-element.45), channel_id=1, source_target_pairs={{0,4},{4,0},{8,12},{12,8},{16,20},{20,16},{24,28},{28,24},{32,36},... | collective-permute-start | bytes 147464 | tf_op jit(solution)/shard_map/ppermute | solution.py:273
  52.9 3.0 %collective-permute-start.11 = (f32[24,512]{1,0:T(8,128)S(1)}, f32[24,512]{1,0:T(8,128)S(1)}, u32[]{:S(2)}, u32[]{:S(2)}) collective-permute-start(f32[24,512]{1,0:T(8,128)S(1)} %add.58), channel_id=1, source_target_pairs={{0,32},{4,36},{8,40},{12,44},{16,48},{20,52},{24,56},{28,60},{32,0... | collective-permute-start | bytes 147464 | tf_op jit(solution)/shard_map/ppermute | solution.py:273
  55.9 4.6 %collective-permute-start.14 = (f32[24,512]{1,0:T(8,128)S(1)}, f32[24,512]{1,0:T(8,128)S(1)}, u32[]{:S(2)}, u32[]{:S(2)}) collective-permute-start(f32[24,512]{1,0:T(8,128)S(1)} %add.59), channel_id=1, source_target_pairs={{0,16},{4,20},{8,24},{12,28},{16,0},{20,4},{24,8},{28,12},{32,48},... | collective-permute-start | bytes 147464 | tf_op jit(solution)/shard_map/ppermute | solution.py:273
  56.4 4.6 %collective-permute-start.13 = (f32[24,512]{1,0:T(8,128)S(1)}, f32[24,512]{1,0:T(8,128)S(1)}, u32[]{:S(2)}, u32[]{:S(2)}) collective-permute-start(f32[24,512]{1,0:T(8,128)S(1)} %add.59), channel_id=1, source_target_pairs={{0,24},{4,28},{8,16},{12,20},{16,8},{20,12},{24,0},{28,4},{32,56},... | collective-permute-start | bytes 147464 | tf_op jit(solution)/shard_map/ppermute | solution.py:273
  57.9 3.1 %collective-permute-start.12 = (f32[24,512]{1,0:T(8,128)S(1)}, f32[24,512]{1,0:T(8,128)S(1)}, u32[]{:S(2)}, u32[]{:S(2)}) collective-permute-start(f32[24,512]{1,0:T(8,128)S(1)} %add.59), channel_id=1, source_target_pairs={{0,8},{4,12},{8,0},{12,4},{16,24},{20,28},{24,16},{28,20},{32,40},... | collective-permute-start | bytes 147464 | tf_op jit(solution)/shard_map/ppermute | solution.py:273
  61.0 14.5 %copy-start.2 = (bf16[48,48]{1,0:T(8,128)(2,1)S(1)}, bf16[48,48]{1,0:T(8,128)(2,1)}, u32[]{:S(2)}) copy-start(bf16[48,48]{1,0:T(8,128)(2,1)} %in_ref.3) | copy-start | bytes 13828
  61.0 14.5 %copy-start.3 = (bf16[48,48]{1,0:T(8,128)(2,1)S(1)}, bf16[48,48]{1,0:T(8,128)(2,1)}, u32[]{:S(2)}) copy-start(bf16[48,48]{1,0:T(8,128)(2,1)} %outf_ref.3) | copy-start | bytes 13828
  61.0 8.1 %collective-permute-start.17 = (f32[24,512]{1,0:T(8,128)S(1)}, f32[24,512]{1,0:T(8,128)S(1)}, u32[]{:S(2)}, u32[]{:S(2)}) collective-permute-start(f32[24,512]{1,0:T(8,128)S(1)} %add_add_fusion.1), channel_id=1, source_target_pairs={{160,0},{164,4},{168,8},{172,12},{176,16},{180,20},{184,24},{188,2... | collective-permute-start | bytes 147464 | tf_op jit(solution)/shard_map/ppermute | solution.py:285
  65.6 3.8 %collective-permute-start.16 = (f32[24,512]{1,0:T(8,128)S(1)}, f32[24,512]{1,0:T(8,128)S(1)}, u32[]{:S(2)}, u32[]{:S(2)}) collective-permute-start(f32[24,512]{1,0:T(8,128)S(1)} %add_add_fusion.1), channel_id=1, source_target_pairs={{64,0},{68,4},{72,8},{76,12},{80,16},{84,20},{88,24},{92,28},{224,... | collective-permute-start | bytes 147464 | tf_op jit(solution)/shard_map/ppermute | solution.py:285
  65.8 5.8 %collective-permute-start.15 = (f32[24,512]{1,0:T(8,128)S(1)}, f32[24,512]{1,0:T(8,128)S(1)}, u32[]{:S(2)}, u32[]{:S(2)}) collective-permute-start(f32[24,512]{1,0:T(8,128)S(1)} %add_add_fusion.1), channel_id=1, source_target_pairs={{224,0},{228,4},{232,8},{236,12},{240,16},{244,20},{248,24},{252,2... | collective-permute-start | bytes 147464 | tf_op jit(solution)/shard_map/ppermute | solution.py:285
  71.6 4.8 %collective-permute-start.18 = (f32[24,512]{1,0:T(8,128)S(1)}, f32[24,512]{1,0:T(8,128)S(1)}, u32[]{:S(2)}, u32[]{:S(2)}) collective-permute-start(f32[24,512]{1,0:T(8,128)S(1)} %add_add_fusion.refs_0_), channel_id=1, source_target_pairs={{0,4},{4,0},{8,12},{12,8},{16,20},{20,16},{24,28},{28,24},{32,36},... | collective-permute-start | bytes 147464 | tf_op jit(solution)/shard_map/ppermute | solution.py:273

commit v13 on v12

--- a/solution.py
+++ b/solution.py
@@ -291,7 +291,7 @@
     mine = mine + crossed(give, 1)
     for masks in ((8,), (2, 6, 4)):
         mine = mine + sum(crossed(mine, mask) for mask in masks)
-    mine = mine + sum(from_z(mine, even, odd) for even, odd in ((-1, 1), (2, -2), (-3, 3)))
+    mine = mine + sum(from_z(mine, even, odd) for even, odd in ((2, -2), (-1, 1), (-3, 3)))
     return mine, crossed(mine, 1)
 
 

time: 77.4 us -> 76.2 us (0.984)
  starting transfers between devices: 35.3 us -> 32.7 us
  waiting for transfers between devices: 22.4 us -> 23.8 us
    ppermute x3, starting transfers between devices: 8.06 us -> 4.91 us  [from_z(): lax.ppermute(block, 'leaf', [((i + 8 * (odd if i // 8 % 2 else even)) % c...]
    ppermute x3, waiting for transfers between devices: 2.49 us -> 3.94 us  [from_z(): lax.ppermute(block, 'leaf', [((i + 8 * (odd if i // 8 % 2 else even)) % c...]
  transfers between devices with their start and end apart: 19 -> 19, of which waited for: 13 -> 14; matrix products, arithmetic and copies ran while one was open for 0% -> 0% of each run, Pallas kernels for 6% -> 6%
where the time goes in v13:
time: 76.2 us; the launch traced here: 76.1 us
  starting transfers between devices  32.7 us (43%)
  waiting for transfers between devices  23.8 us (31%)
  Pallas kernels  17.7 us (23%)
  local copies, waits for them, and re-layouts  0.9 us (1%)
  between operations  0.84 us (1%)
    ppermute x8, starting transfers between devices, crossed(): lax.ppermute(block, 'leaf', [(i, i ^ mask) for i in range(lax.axis_size('...  12.1 us
    ppermute x6, waiting for transfers between devices, shifted(): lax.ppermute(block, axis, [(i, (i + distance) % count) for i in range(cou...  9.79 us
    ppermute x6, starting transfers between devices, shifted(): lax.ppermute(block, axis, [(i, (i + distance) % count) for i in range(cou...  8.21 us
    ppermute x8, waiting for transfers between devices, crossed(): lax.ppermute(block, 'leaf', [(i, i ^ mask) for i in range(lax.axis_size('...  8.02 us
    ppermute x2, starting transfers between devices, outward(): lax.ppermute(block, 'leaf', [(i, (i + (2 * chips if i % 2 == 0 else -2 *...  7.42 us
    pallas_call x1, Pallas kernels, body(): pl.pallas_call(scatter_kernel, out_shape=[struct((rank, rows), BF), struc...  5.57 us
    ppermute x3, starting transfers between devices, from_z(): lax.ppermute(block, 'leaf', [((i + 8 * (odd if i // 8 % 2 else even)) % c...  4.91 us
    pallas_call x1, Pallas kernels, body(): pl.pallas_call(far_gather_kernel, out_shape=[struct((rank, rows), F32), s...  4.08 us
  transfers between devices with their start and end apart: 19, of which 14 were waited for; matrix products, arithmetic and copies ran while one was open for 0% of the time, Pallas kernels for 6%

profile of v13, /device:TPU:1, one launch (start us, length us, event | category | flops | bytes accessed | tf_op | source)
XLA Modules:
  0.0 76.1 jit_solution(681513463014080663)
XLA Ops:
  0.6 2.2 %project.1 = (f32[64,1024]{1,0:T(8,128)}, bf16[64,1024]{1,0:T(8,128)(2,1)}, bf16[64,1024]{1,0:T(8,128)(2,1)}, bf16[64,1024]{1,0:T(8,128)(2,1)}) custom-call(bf16[48,1024]{1,0:T(8,128)(2,1)} %feat_ref.3, bf16[48,48]{1,0:T(8,128)(2,1)} %in_ref.3, bf16[48,1024]{1,0:T(8,128)(2,1)} %cot_ref.3, bf16[48,48]{1,0:T(8,128)(2,1)} %outf_ref.3, s32[1,1024]{1,0:T(1,128)} %bitcast.10), custom_call_target="tpu_custom_call" | custom-call | tf_op jit(solution)/shard_map/project/pallas_call | solution.py:314
  2.8 2.1 %collective-permute-start = (bf16[64,1024]{1,0:T(8,128)(2,1)}, bf16[64,1024]{1,0:T(8,128)(2,1)S(1)}, u32[]{:S(2)}, u32[]{:S(2)}) collective-permute-start(bf16[64,1024]{1,0:T(8,128)(2,1)} %get-tuple-element.28), channel_id=1, source_target_pairs={{0,1},{1,2},{2,3},{3,0},{4,5},{5,6},{6,7},{7,4},{8,9},{9,10},{10,1... | collective-permute-start | bytes 393224 | tf_op jit(solution)/shard_map/ppermute | solution.py:269
  5.0 1.4 %collective-permute-start.1 = (bf16[64,1024]{1,0:T(8,128)(2,1)}, bf16[64,1024]{1,0:T(8,128)(2,1)S(1)}, u32[]{:S(2)}, u32[]{:S(2)}) collective-permute-start(bf16[64,1024]{1,0:T(8,128)(2,1)} %get-tuple-element.29), channel_id=1, source_target_pairs={{0,3},{1,0},{2,1},{3,2},{4,7},{5,4},{6,5},{7,6},{8,11},{9,8},{10,9... | collective-permute-start | bytes 393224 | tf_op jit(solution)/shard_map/ppermute | solution.py:269
  6.4 1.6 %collective-permute-start.2 = (bf16[64,1024]{1,0:T(8,128)(2,1)}, bf16[64,1024]{1,0:T(8,128)(2,1)S(1)}, u32[]{:S(2)}, u32[]{:S(2)}) collective-permute-start(bf16[64,1024]{1,0:T(8,128)(2,1)} %get-tuple-element.30), channel_id=1, source_target_pairs={{0,2},{1,3},{2,0},{3,1},{4,6},{5,7},{6,4},{7,5},{8,10},{9,11},{10,... | collective-permute-start | bytes 393224 | tf_op jit(solution)/shard_map/ppermute | solution.py:269
  8.3 0.6 collective-permute-done.p1
  9.0 4.0 %collective-permute-done.2.p3 = bf16[64,1024]{1,0:T(8,128)(2,1)S(1)} collective-permute-done((bf16[64,1024]{1,0:T(8,128)(2,1)}, bf16[64,1024]{1,0:T(8,128)(2,1)S(1)}, u32[]{:S(2)}, u32[]{:S(2)}) %collective-permute-start.2) | collective-permute-done | bytes 131104 | tf_op jit(solution)/shard_map/ppermute | solution.py:269
  13.0 5.6 %scatter.1 = (bf16[48,1024]{1,0:T(8,128)(2,1)S(1)}, f32[16,1024]{1,0:T(8,128)S(1)}, f32[48,1024]{1,0:T(8,128)S(1)}, bf16[96,1024]{1,0:T(8,128)(2,1)S(1)}) custom-call(s32[8,8]{1,0:T(8,128)S(1)} %bitcast.7, f32[64,1024]{1,0:T(8,128)S(1)} %copy-done.4, bf16[64,1024]{1,0:T(8,128)(2,1)S(1)} %collective-permute-done.p1, ...), custom_call_target="tpu_custom_call" | custom-call | flops 5000000000 | bytes 1048576 | tf_op jit(solution)/shard_map/scatter/pallas_call | solution.py:324
  18.6 3.1 %collective-permute-start.3 = (bf16[96,1024]{1,0:T(8,128)(2,1)S(1)}, bf16[96,1024]{1,0:T(8,128)(2,1)S(1)}, u32[]{:S(2)}, u32[]{:S(2)}) collective-permute-start(bf16[96,1024]{1,0:T(8,128)(2,1)S(1)} %get-tuple-element.31), channel_id=1, source_target_pairs={{0,4},{4,0},{8,12},{12,8},{16,20},{20,16},{24,28},{28,24},{32,36},... | collective-permute-start | bytes 589832 | tf_op jit(solution)/shard_map/ppermute | solution.py:273
  21.7 1.1 %collective-permute-done.3 = bf16[96,1024]{1,0:T(8,128)(2,1)S(1)} collective-permute-done((bf16[96,1024]{1,0:T(8,128)(2,1)S(1)}, bf16[96,1024]{1,0:T(8,128)(2,1)S(1)}, u32[]{:S(2)}, u32[]{:S(2)}) %collective-permute-start.3) | collective-permute-done | bytes 196640 | tf_op jit(solution)/shard_map/ppermute | solution.py:273
  22.8 6.9 %collective-permute-start.5 = (bf16[64,1024]{1,0:T(8,128)(2,1)S(1)}, bf16[64,1024]{1,0:T(8,128)(2,1)S(1)}, u32[]{:S(2)}, u32[]{:S(2)}) collective-permute-start(bf16[64,1024]{1,0:T(8,128)(2,1)S(1)} %get-tuple-element.54), channel_id=1, source_target_pairs={{0,8},{4,252},{8,16},{12,4},{16,24},{20,12},{24,32},{28,20},{32,40... | collective-permute-start | bytes 393224 | tf_op jit(solution)/shard_map/ppermute | solution.py:278
  30.2 3.2 %near_gather.1.base_ref = bf16[432,1024]{1,0:T(8,128)(2,1)S(1)} custom-call(s32[8,8]{1,0:T(8,128)S(1)} %bitcast.8, bf16[16,1024]{1,0:T(8,128)(2,1)S(1)} %slice.51.own_ref, bf16[16,1024]{1,0:T(8,128)(2,1)S(1)} %get-tuple-element.52.pair_ref, s32[27,1024]{1,0:T(8,128)S(1)} %copy-done.5), custom_call_target="tpu_custom_call" | custom-call | flops 5000000000 | bytes 1048576 | tf_op jit(solution)/shard_map/near_gather/pallas_call | solution.py:350
  33.4 2.1 %collective-permute-done.4 = bf16[64,1024]{1,0:T(8,128)(2,1)S(1)} collective-permute-done((bf16[64,1024]{1,0:T(8,128)(2,1)S(1)}, bf16[64,1024]{1,0:T(8,128)(2,1)S(1)}, u32[]{:S(2)}, u32[]{:S(2)}) %collective-permute-start.4) | collective-permute-done | bytes 131104 | tf_op jit(solution)/shard_map/ppermute | solution.py:278
  35.6 0.6 copy-done.8
  36.2 0.8 %collective-permute-done.6.cross_ref = bf16[80,1024]{1,0:T(8,128)(2,1)S(1)} collective-permute-done((bf16[80,1024]{1,0:T(8,128)(2,1)S(1)}, bf16[80,1024]{1,0:T(8,128)(2,1)S(1)}, u32[]{:S(2)}, u32[]{:S(2)}) %collective-permute-start.6) | collective-permute-done | bytes 163872 | tf_op jit(solution)/shard_map/ppermute | solution.py:273
  37.0 4.1 %far_gather.1 = (f32[48,1024]{1,0:T(8,128)S(1)}, bf16[512,1024]{1,0:T(8,128)(2,1)S(1)}) custom-call(s32[8,8]{1,0:T(8,128)S(1)} %bitcast.9, bf16[432,1024]{1,0:T(8,128)(2,1)S(1)} %near_gather.1.base_ref, bf16[32,1024]{1,0:T(8,128)(2,1)S(1)} %slice.60.near_ref, bf16[32,1024]{1,0:T(8,128)(2,1)S(1)} %slice.61.far_ref, ...), custom_call_target="tpu_custom_call" | custom-call | flops 5000000000 | bytes 1048576 | tf_op jit(solution)/shard_map/far_gather/pallas_call | solution.py:367
  41.2 0.9 %collective-permute-start.9 = (bf16[64,1024]{1,0:T(8,128)(2,1)S(1)}, bf16[64,1024]{1,0:T(8,128)(2,1)S(1)}, u32[]{:S(2)}, u32[]{:S(2)}) collective-permute-start(bf16[64,1024]{1,0:T(8,128)(2,1)S(1)} %pad_maximum_fusion.4.e0), channel_id=1, source_target_pairs={{0,1},{1,2},{2,3},{3,0},{4,5},{5,6},{6,7},{7,4},{8,9},{9,10},{10,1... | collective-permute-start | bytes 393224 | tf_op jit(solution)/shard_map/ppermute | solution.py:269
  42.1 1.8 %collective-permute-start.8 = (bf16[64,1024]{1,0:T(8,128)(2,1)S(1)}, bf16[64,1024]{1,0:T(8,128)(2,1)S(1)}, u32[]{:S(2)}, u32[]{:S(2)}) collective-permute-start(bf16[64,1024]{1,0:T(8,128)(2,1)S(1)} %pad_maximum_fusion.4.e0), channel_id=1, source_target_pairs={{0,3},{1,0},{2,1},{3,2},{4,7},{5,4},{6,5},{7,6},{8,11},{9,8},{10,9... | collective-permute-start | bytes 393224 | tf_op jit(solution)/shard_map/ppermute | solution.py:269
  44.6 2.8 %collective-permute-done.9.e1 = bf16[64,1024]{1,0:T(8,128)(2,1)S(1)} collective-permute-done((bf16[64,1024]{1,0:T(8,128)(2,1)S(1)}, bf16[64,1024]{1,0:T(8,128)(2,1)S(1)}, u32[]{:S(2)}, u32[]{:S(2)}) %collective-permute-start.9) | collective-permute-done | bytes 131104 | tf_op jit(solution)/shard_map/ppermute | solution.py:269
  47.4 2.3 %collective-permute-done.7.e2 = bf16[64,1024]{1,0:T(8,128)(2,1)S(1)} collective-permute-done((bf16[64,1024]{1,0:T(8,128)(2,1)S(1)}, bf16[64,1024]{1,0:T(8,128)(2,1)S(1)}, u32[]{:S(2)}, u32[]{:S(2)}) %collective-permute-start.7) | collective-permute-done | bytes 131104 | tf_op jit(solution)/shard_map/ppermute | solution.py:269
  49.8 0.6 sums.1
  50.3 1.7 %collective-permute-start.10 = (f32[24,512]{1,0:T(8,128)S(1)}, f32[24,512]{1,0:T(8,128)S(1)}, u32[]{:S(2)}, u32[]{:S(2)}) collective-permute-start(f32[24,512]{1,0:T(8,128)S(1)} %get-tuple-element.45), channel_id=1, source_target_pairs={{0,4},{4,0},{8,12},{12,8},{16,20},{20,16},{24,28},{28,24},{32,36},... | collective-permute-start | bytes 147464 | tf_op jit(solution)/shard_map/ppermute | solution.py:273
  52.0 0.9 %collective-permute-done.10 = f32[24,512]{1,0:T(8,128)S(1)} collective-permute-done((f32[24,512]{1,0:T(8,128)S(1)}, f32[24,512]{1,0:T(8,128)S(1)}, u32[]{:S(2)}, u32[]{:S(2)}) %collective-permute-start.10) | collective-permute-done | bytes 49184 | tf_op jit(solution)/shard_map/ppermute | solution.py:273
  53.0 2.9 %collective-permute-done.11 = f32[24,512]{1,0:T(8,128)S(1)} collective-permute-done((f32[24,512]{1,0:T(8,128)S(1)}, f32[24,512]{1,0:T(8,128)S(1)}, u32[]{:S(2)}, u32[]{:S(2)}) %collective-permute-start.11) | collective-permute-done | bytes 49184 | tf_op jit(solution)/shard_map/ppermute | solution.py:273
  56.4 1.4 %collective-permute-start.13 = (f32[24,512]{1,0:T(8,128)S(1)}, f32[24,512]{1,0:T(8,128)S(1)}, u32[]{:S(2)}, u32[]{:S(2)}) collective-permute-start(f32[24,512]{1,0:T(8,128)S(1)} %add.59), channel_id=1, source_target_pairs={{0,24},{4,28},{8,16},{12,20},{16,8},{20,12},{24,0},{28,4},{32,56},... | collective-permute-start | bytes 147464 | tf_op jit(solution)/shard_map/ppermute | solution.py:273
  57.9 0.8 %collective-permute-start.12 = (f32[24,512]{1,0:T(8,128)S(1)}, f32[24,512]{1,0:T(8,128)S(1)}, u32[]{:S(2)}, u32[]{:S(2)}) collective-permute-start(f32[24,512]{1,0:T(8,128)S(1)} %add.59), channel_id=1, source_target_pairs={{0,8},{4,12},{8,0},{12,4},{16,24},{20,28},{24,16},{28,20},{32,40},... | collective-permute-start | bytes 147464 | tf_op jit(solution)/shard_map/ppermute | solution.py:273
  58.7 1.8 %collective-permute-done.14 = f32[24,512]{1,0:T(8,128)S(1)} collective-permute-done((f32[24,512]{1,0:T(8,128)S(1)}, f32[24,512]{1,0:T(8,128)S(1)}, u32[]{:S(2)}, u32[]{:S(2)}) %collective-permute-start.14) | collective-permute-done | bytes 49184 | tf_op jit(solution)/shard_map/ppermute | solution.py:273
  61.0 4.5 %collective-permute-start.17 = (f32[24,512]{1,0:T(8,128)S(1)}, f32[24,512]{1,0:T(8,128)S(1)}, u32[]{:S(2)}, u32[]{:S(2)}) collective-permute-start(f32[24,512]{1,0:T(8,128)S(1)} %add_add_fusion.1), channel_id=1, source_target_pairs={{160,0},{164,4},{168,8},{172,12},{176,16},{180,20},{184,24},{188,2... | collective-permute-start | bytes 147464 | tf_op jit(solution)/shard_map/ppermute | solution.py:285
  66.0 1.1 %collective-permute-done.17 = f32[24,512]{1,0:T(8,128)S(1)} collective-permute-done((f32[24,512]{1,0:T(8,128)S(1)}, f32[24,512]{1,0:T(8,128)S(1)}, u32[]{:S(2)}, u32[]{:S(2)}) %collective-permute-start.17) | collective-permute-done | bytes 49184 | tf_op jit(solution)/shard_map/ppermute | solution.py:285
  67.1 2.6 %collective-permute-done.16 = f32[24,512]{1,0:T(8,128)S(1)} collective-permute-done((f32[24,512]{1,0:T(8,128)S(1)}, f32[24,512]{1,0:T(8,128)S(1)}, u32[]{:S(2)}, u32[]{:S(2)}) %collective-permute-start.16) | collective-permute-done | bytes 49184 | tf_op jit(solution)/shard_map/ppermute | solution.py:285
  69.9 4.4 %collective-permute-start.18 = (f32[24,512]{1,0:T(8,128)S(1)}, f32[24,512]{1,0:T(8,128)S(1)}, u32[]{:S(2)}, u32[]{:S(2)}) collective-permute-start(f32[24,512]{1,0:T(8,128)S(1)} %add_add_fusion.refs_0_), channel_id=1, source_target_pairs={{0,4},{4,0},{8,12},{12,8},{16,20},{20,16},{24,28},{28,24},{32,36},... | collective-permute-start | bytes 147464 | tf_op jit(solution)/shard_map/ppermute | solution.py:273
  74.4 0.8 %outputs.1 = (bf16[48,1024]{1,0:T(8,128)(2,1)}, bf16[48,1024]{1,0:T(8,128)(2,1)}) custom-call(bf16[48,1024]{1,0:T(8,128)(2,1)S(1)} %get-tuple-element.40.rows_ref, bf16[48,1024]{1,0:T(8,128)(2,1)S(1)} %get-tuple-element.41.mixed_ref, bf16[48,48]{1,0:T(8,128)(2,1)S(1)} %copy-done.2, bf16[48,48]{1,0:T(8,128)(2,1)S(1)} %copy-done.3), custom_call_target="tpu_custom_call" | custom-call | flops 500000000 | bytes 1048576 | tf_op jit(solution)/shard_map/outputs/pallas_call | solution.py:399
  75.2 0.8 %unpack.1 = (f32[48,48]{1,0:T(8,128)}, f32[12,27,48]{2,1,0:T(8,128)}, f32[48,48]{1,0:T(8,128)}) custom-call(f32[24,512]{1,0:T(8,128)S(1)} %add_add_fusion.refs_0_, f32[24,512]{1,0:T(8,128)S(1)} %collective-permute-done.18.refs_1_), custom_call_target="tpu_custom_call" | custom-call | tf_op jit(solution)/shard_map/unpack/pallas_call | solution.py:411
  (52 shorter events, 3.5 us)
Async XLA Ops:
  0.6 7.4 %copy-start.7 = (bf16[27,12,48]{2,0,1:T(8,128)(2,1)S(1)}, bf16[27,12,48]{2,0,1:T(8,128)(2,1)}, u32[]{:S(2)}) copy-start(bf16[27,12,48]{2,0,1:T(8,128)(2,1)} %param.10) | copy-start | bytes 93316
  2.8 6.1 %collective-permute-start = (bf16[64,1024]{1,0:T(8,128)(2,1)}, bf16[64,1024]{1,0:T(8,128)(2,1)S(1)}, u32[]{:S(2)}, u32[]{:S(2)}) collective-permute-start(bf16[64,1024]{1,0:T(8,128)(2,1)} %get-tuple-element.28), channel_id=1, source_target_pairs={{0,1},{1,2},{2,3},{3,0},{4,5},{5,6},{6,7},{7,4},{8,9},{9,10},{10,1... | collective-permute-start | bytes 393224 | tf_op jit(solution)/shard_map/ppermute | solution.py:269
  5.0 4.0 %collective-permute-start.1 = (bf16[64,1024]{1,0:T(8,128)(2,1)}, bf16[64,1024]{1,0:T(8,128)(2,1)S(1)}, u32[]{:S(2)}, u32[]{:S(2)}) collective-permute-start(bf16[64,1024]{1,0:T(8,128)(2,1)} %get-tuple-element.29), channel_id=1, source_target_pairs={{0,3},{1,0},{2,1},{3,2},{4,7},{5,4},{6,5},{7,6},{8,11},{9,8},{10,9... | collective-permute-start | bytes 393224 | tf_op jit(solution)/shard_map/ppermute | solution.py:269
  6.4 6.6 %collective-permute-start.2 = (bf16[64,1024]{1,0:T(8,128)(2,1)}, bf16[64,1024]{1,0:T(8,128)(2,1)S(1)}, u32[]{:S(2)}, u32[]{:S(2)}) collective-permute-start(bf16[64,1024]{1,0:T(8,128)(2,1)} %get-tuple-element.30), channel_id=1, source_target_pairs={{0,2},{1,3},{2,0},{3,1},{4,6},{5,7},{6,4},{7,5},{8,10},{9,11},{10,... | collective-permute-start | bytes 393224 | tf_op jit(solution)/shard_map/ppermute | solution.py:269
  8.1 4.8 %copy-start.4 = (f32[64,1024]{1,0:T(8,128)S(1)}, f32[64,1024]{1,0:T(8,128)}, u32[]{:S(2)}) copy-start(f32[64,1024]{1,0:T(8,128)} %get-tuple-element.27.p0) | copy-start | bytes 786436
  8.2 4.8 %copy-start.5 = (s32[27,1024]{1,0:T(8,128)S(1)}, s32[27,1024]{1,0:T(8,128)}, u32[]{:S(2)}) copy-start(s32[27,1024]{1,0:T(8,128)} %nbr_ref.5) | copy-start | bytes 331780
  8.2 4.8 %copy-start.6 = (s32[1,8,8]{2,1,0:T(8,128)S(1)}, s32[1,8,8]{2,1,0:T(8,128)}, u32[]{:S(2)}) copy-start(s32[1,8,8]{2,1,0:T(8,128)} %param.13) | copy-start | bytes 772
  18.6 4.2 %collective-permute-start.3 = (bf16[96,1024]{1,0:T(8,128)(2,1)S(1)}, bf16[96,1024]{1,0:T(8,128)(2,1)S(1)}, u32[]{:S(2)}, u32[]{:S(2)}) collective-permute-start(bf16[96,1024]{1,0:T(8,128)(2,1)S(1)} %get-tuple-element.31), channel_id=1, source_target_pairs={{0,4},{4,0},{8,12},{12,8},{16,20},{20,16},{24,28},{28,24},{32,36},... | collective-permute-start | bytes 589832 | tf_op jit(solution)/shard_map/ppermute | solution.py:273
  22.8 10.6 %collective-permute-start.5 = (bf16[64,1024]{1,0:T(8,128)(2,1)S(1)}, bf16[64,1024]{1,0:T(8,128)(2,1)S(1)}, u32[]{:S(2)}, u32[]{:S(2)}) collective-permute-start(bf16[64,1024]{1,0:T(8,128)(2,1)S(1)} %get-tuple-element.54), channel_id=1, source_target_pairs={{0,8},{4,252},{8,16},{12,4},{16,24},{20,12},{24,32},{28,20},{32,40... | collective-permute-start | bytes 393224 | tf_op jit(solution)/shard_map/ppermute | solution.py:278
  29.7 5.8 %collective-permute-start.4 = (bf16[64,1024]{1,0:T(8,128)(2,1)S(1)}, bf16[64,1024]{1,0:T(8,128)(2,1)S(1)}, u32[]{:S(2)}, u32[]{:S(2)}) collective-permute-start(bf16[64,1024]{1,0:T(8,128)(2,1)S(1)} %get-tuple-element.55), channel_id=1, source_target_pairs={{0,16},{4,244},{8,24},{12,252},{16,32},{20,4},{24,40},{28,12},{32,... | collective-permute-start | bytes 393224 | tf_op jit(solution)/shard_map/ppermute | solution.py:278
  35.5 0.7 copy-start.8
  35.5 1.5 %collective-permute-start.6 = (bf16[80,1024]{1,0:T(8,128)(2,1)S(1)}, bf16[80,1024]{1,0:T(8,128)(2,1)S(1)}, u32[]{:S(2)}, u32[]{:S(2)}) collective-permute-start(bf16[80,1024]{1,0:T(8,128)(2,1)S(1)} %pad_maximum_fusion), channel_id=1, source_target_pairs={{0,4},{4,0},{8,12},{12,8},{16,20},{20,16},{24,28},{28,24},{32,36},... | collective-permute-start | bytes 491528 | tf_op jit(solution)/shard_map/ppermute | solution.py:273
  41.2 6.2 %collective-permute-start.9 = (bf16[64,1024]{1,0:T(8,128)(2,1)S(1)}, bf16[64,1024]{1,0:T(8,128)(2,1)S(1)}, u32[]{:S(2)}, u32[]{:S(2)}) collective-permute-start(bf16[64,1024]{1,0:T(8,128)(2,1)S(1)} %pad_maximum_fusion.4.e0), channel_id=1, source_target_pairs={{0,1},{1,2},{2,3},{3,0},{4,5},{5,6},{6,7},{7,4},{8,9},{9,10},{10,1... | collective-permute-start | bytes 393224 | tf_op jit(solution)/shard_map/ppermute | solution.py:269
  42.1 5.3 %collective-permute-start.8 = (bf16[64,1024]{1,0:T(8,128)(2,1)S(1)}, bf16[64,1024]{1,0:T(8,128)(2,1)S(1)}, u32[]{:S(2)}, u32[]{:S(2)}) collective-permute-start(bf16[64,1024]{1,0:T(8,128)(2,1)S(1)} %pad_maximum_fusion.4.e0), channel_id=1, source_target_pairs={{0,3},{1,0},{2,1},{3,2},{4,7},{5,4},{6,5},{7,6},{8,11},{9,8},{10,9... | collective-permute-start | bytes 393224 | tf_op jit(solution)/shard_map/ppermute | solution.py:269
  43.9 5.8 %collective-permute-start.7 = (bf16[64,1024]{1,0:T(8,128)(2,1)S(1)}, bf16[64,1024]{1,0:T(8,128)(2,1)S(1)}, u32[]{:S(2)}, u32[]{:S(2)}) collective-permute-start(bf16[64,1024]{1,0:T(8,128)(2,1)S(1)} %pad_maximum_fusion.4.e0), channel_id=1, source_target_pairs={{0,2},{1,3},{2,0},{3,1},{4,6},{5,7},{6,4},{7,5},{8,10},{9,11},{10,... | collective-permute-start | bytes 393224 | tf_op jit(solution)/shard_map/ppermute | solution.py:269
  44.2 5.6 %copy-start = (bf16[48,1024]{1,0:T(8,128)(2,1)S(1)}, bf16[48,1024]{1,0:T(8,128)(2,1)}, u32[]{:S(2)}) copy-start(bf16[48,1024]{1,0:T(8,128)(2,1)} %feat_ref.3) | copy-start | bytes 294916
  44.2 5.6 %copy-start.1 = (bf16[48,1024]{1,0:T(8,128)(2,1)S(1)}, bf16[48,1024]{1,0:T(8,128)(2,1)}, u32[]{:S(2)}) copy-start(bf16[48,1024]{1,0:T(8,128)(2,1)} %cot_ref.3) | copy-start | bytes 294916
  50.3 2.6 %collective-permute-start.10 = (f32[24,512]{1,0:T(8,128)S(1)}, f32[24,512]{1,0:T(8,128)S(1)}, u32[]{:S(2)}, u32[]{:S(2)}) collective-permute-start(f32[24,512]{1,0:T(8,128)S(1)} %get-tuple-element.45), channel_id=1, source_target_pairs={{0,4},{4,0},{8,12},{12,8},{16,20},{20,16},{24,28},{28,24},{32,36},... | collective-permute-start | bytes 147464 | tf_op jit(solution)/shard_map/ppermute | solution.py:273
  52.9 3.0 %collective-permute-start.11 = (f32[24,512]{1,0:T(8,128)S(1)}, f32[24,512]{1,0:T(8,128)S(1)}, u32[]{:S(2)}, u32[]{:S(2)}) collective-permute-start(f32[24,512]{1,0:T(8,128)S(1)} %add.58), channel_id=1, source_target_pairs={{0,32},{4,36},{8,40},{12,44},{16,48},{20,52},{24,56},{28,60},{32,0... | collective-permute-start | bytes 147464 | tf_op jit(solution)/shard_map/ppermute | solution.py:273
  55.9 4.6 %collective-permute-start.14 = (f32[24,512]{1,0:T(8,128)S(1)}, f32[24,512]{1,0:T(8,128)S(1)}, u32[]{:S(2)}, u32[]{:S(2)}) collective-permute-start(f32[24,512]{1,0:T(8,128)S(1)} %add.59), channel_id=1, source_target_pairs={{0,16},{4,20},{8,24},{12,28},{16,0},{20,4},{24,8},{28,12},{32,48},... | collective-permute-start | bytes 147464 | tf_op jit(solution)/shard_map/ppermute | solution.py:273
  56.4 4.6 %collective-permute-start.13 = (f32[24,512]{1,0:T(8,128)S(1)}, f32[24,512]{1,0:T(8,128)S(1)}, u32[]{:S(2)}, u32[]{:S(2)}) collective-permute-start(f32[24,512]{1,0:T(8,128)S(1)} %add.59), channel_id=1, source_target_pairs={{0,24},{4,28},{8,16},{12,20},{16,8},{20,12},{24,0},{28,4},{32,56},... | collective-permute-start | bytes 147464 | tf_op jit(solution)/shard_map/ppermute | solution.py:273
  57.9 3.1 %collective-permute-start.12 = (f32[24,512]{1,0:T(8,128)S(1)}, f32[24,512]{1,0:T(8,128)S(1)}, u32[]{:S(2)}, u32[]{:S(2)}) collective-permute-start(f32[24,512]{1,0:T(8,128)S(1)} %add.59), channel_id=1, source_target_pairs={{0,8},{4,12},{8,0},{12,4},{16,24},{20,28},{24,16},{28,20},{32,40},... | collective-permute-start | bytes 147464 | tf_op jit(solution)/shard_map/ppermute | solution.py:273
  61.0 13.3 %copy-start.2 = (bf16[48,48]{1,0:T(8,128)(2,1)S(1)}, bf16[48,48]{1,0:T(8,128)(2,1)}, u32[]{:S(2)}) copy-start(bf16[48,48]{1,0:T(8,128)(2,1)} %in_ref.3) | copy-start | bytes 13828
  61.0 13.3 %copy-start.3 = (bf16[48,48]{1,0:T(8,128)(2,1)S(1)}, bf16[48,48]{1,0:T(8,128)(2,1)}, u32[]{:S(2)}) copy-start(bf16[48,48]{1,0:T(8,128)(2,1)} %outf_ref.3) | copy-start | bytes 13828
  61.0 6.0 %collective-permute-start.17 = (f32[24,512]{1,0:T(8,128)S(1)}, f32[24,512]{1,0:T(8,128)S(1)}, u32[]{:S(2)}, u32[]{:S(2)}) collective-permute-start(f32[24,512]{1,0:T(8,128)S(1)} %add_add_fusion.1), channel_id=1, source_target_pairs={{160,0},{164,4},{168,8},{172,12},{176,16},{180,20},{184,24},{188,2... | collective-permute-start | bytes 147464 | tf_op jit(solution)/shard_map/ppermute | solution.py:285
  65.6 4.2 %collective-permute-start.16 = (f32[24,512]{1,0:T(8,128)S(1)}, f32[24,512]{1,0:T(8,128)S(1)}, u32[]{:S(2)}, u32[]{:S(2)}) collective-permute-start(f32[24,512]{1,0:T(8,128)S(1)} %add_add_fusion.1), channel_id=1, source_target_pairs={{224,0},{228,4},{232,8},{236,12},{240,16},{244,20},{248,24},{252,2... | collective-permute-start | bytes 147464 | tf_op jit(solution)/shard_map/ppermute | solution.py:285
  65.6 4.3 %collective-permute-start.15 = (f32[24,512]{1,0:T(8,128)S(1)}, f32[24,512]{1,0:T(8,128)S(1)}, u32[]{:S(2)}, u32[]{:S(2)}) collective-permute-start(f32[24,512]{1,0:T(8,128)S(1)} %add_add_fusion.1), channel_id=1, source_target_pairs={{64,0},{68,4},{72,8},{76,12},{80,16},{84,20},{88,24},{92,28},{224,... | collective-permute-start | bytes 147464 | tf_op jit(solution)/shard_map/ppermute | solution.py:285
  69.9 5.3 %collective-permute-start.18 = (f32[24,512]{1,0:T(8,128)S(1)}, f32[24,512]{1,0:T(8,128)S(1)}, u32[]{:S(2)}, u32[]{:S(2)}) collective-permute-start(f32[24,512]{1,0:T(8,128)S(1)} %add_add_fusion.refs_0_), channel_id=1, source_target_pairs={{0,4},{4,0},{8,12},{12,8},{16,20},{20,16},{24,28},{28,24},{32,36},... | collective-permute-start | bytes 147464 | tf_op jit(solution)/shard_map/ppermute | solution.py:273
